TPU v7x, 32 devices: a whole 2x2x4 slice. The times are simulated.
32 devices in a mesh: walker: 8 (over z, y), orb: 4 (over x, core).
Axes of the slice: x: 2, y: 2, z: 4, core: 2. Of those that a mesh axis runs over, the one named last changes fastest.
Arguments:
- positions: float32 [64, 3, 512], P('walker'), may hold values from 0 to 24
- inverse: float32 [64, 512, 512], P('walker', 'orb')
- spline_table: bfloat16 [512, 13824], P('orb'), may hold values from -6 to 6
- gaussian: float32 [64, 3, 64], P('walker'), may hold values from -4 to 4
- accepted: int32 [64, 64], P('walker'), may hold values 0 or 1
- block_order: int32 [32], replicated, may hold values from 0 to 31, each once
- parent: int32 [64], P('walker'), may hold values from 0 to 63, as said below
Outputs:
- new_positions: float32 [64, 3, 512], P('walker')
- new_inverse: float32 [64, 512, 512], P('walker', 'orb')
Inputs may be any that keep to these rules, and one draw needn't show every extreme that they name: Walkers s and parent[s] lie in the same group of 8 (one index of walker) except for 3 to 6 walkers of each group, exactly 6 in some group; a group takes at most 1 parents from any one other group, exactly 1 from some. A parent may be named several times or not at all.
All inputs are finite; a program needn't handle non-finite values. No bound on the sum of `accepted` on one device may be relied on, other than what follows from the above.
Results may differ from a plain program's by a relative error of at most 0.0004.
Values may be sent and summed in bfloat16 or wider, within the bound.
No kernel may reach another device: no remote copies, remote signals or barrier semaphores. Data moves between devices by JAX's collectives and lax.ppermute only.
A program may use at most 128 MiB of HBM per device.

v0:
```python
import jax
import jax.numpy as jnp
from jax import lax
from jax.sharding import PartitionSpec as P

GRID = 24
K = 16
NMOVE = 4
CAP = 1


TAU = 0.25
ROOT_TAU = 0.5


def spline_weights(coords):
    floors = jnp.floor(coords)
    within = coords - floors
    remain = 1.0 - within
    square = within * within
    cubed = square * within
    values = jnp.stack(
        [
            remain * remain * remain / 6.0,
            (3.0 * cubed - 6.0 * square + 4.0) / 6.0,
            (-3.0 * cubed + 3.0 * square + 3.0 * within + 1.0) / 6.0,
            cubed / 6.0,
        ]
    )
    slopes = jnp.stack(
        [
            -0.5 * remain * remain,
            1.5 * square - 2.0 * within,
            -1.5 * square + within + 0.5,
            0.5 * square,
        ]
    )
    return (floors.astype(jnp.int32) - 1, values, slopes)


def evaluate(table_rows, coords, with_slopes):
    corner, values, slopes = spline_weights(coords)
    shifts = jnp.arange(4, dtype=jnp.int32)
    indices = jnp.mod(corner[None, :, :] + shifts[:, None, None], GRID)
    along_x = indices[:, 0]
    along_y = indices[:, 1]
    along_z = indices[:, 2]
    points = (
        along_x[:, None, None] * (GRID * GRID)
        + along_y[None, :, None] * GRID
        + along_z[None, None, :]
    ).reshape(64, -1)
    value_x = values[:, 0][:, None, None]
    value_y = values[:, 1][None, :, None]
    value_z = values[:, 2][None, None, :]
    plain = (value_x * value_y * value_z).reshape(64, -1)
    if with_slopes:
        slope_x = (slopes[:, 0][:, None, None] * value_y * value_z).reshape(64, -1)
        slope_y = (value_x * slopes[:, 1][None, :, None] * value_z).reshape(64, -1)
        slope_z = (value_x * value_y * slopes[:, 2][None, None, :]).reshape(64, -1)
        weights = jnp.stack([plain, slope_x, slope_y, slope_z])
    else:
        weights = plain[None]
    gathered = jnp.take(table_rows, points, axis=1).astype(jnp.float32)
    return jnp.einsum("rne,cne->cre", gathered, weights, precision=lax.Precision.HIGHEST)


def blocked_sweep(
    table_rows, positions, inverse, gaussian, accepted, block_order, drift_total, column_total
):
    walkers = positions.shape[0]
    for sweep_step in range(NMOVE):
        offset = block_order[sweep_step] * K
        current = lax.dynamic_slice_in_dim(positions, offset, K, 2)
        columns = lax.dynamic_slice_in_dim(inverse, offset, K, 2)
        coords = jnp.transpose(current, (1, 0, 2)).reshape(3, walkers * K)
        pieces = evaluate(table_rows, coords, True)
        orbitals = pieces.shape[1]
        slopes = pieces[1:].reshape(3, orbitals, walkers, K)
        drifts = drift_total(
            jnp.einsum("djwk,wjk->wdk", slopes, columns, precision=lax.Precision.HIGHEST)
        )
        speeds = jnp.sum(drifts * drifts, axis=1, keepdims=True)
        capped = drifts / jnp.sqrt(1.0 + TAU * speeds)
        jitter = lax.slice_in_dim(gaussian, sweep_step * K, sweep_step * K + K, axis=2)
        decide = lax.slice_in_dim(accepted, sweep_step * K, sweep_step * K + K, axis=1)[:, None, :]
        proposal = current + decide * (TAU * capped + ROOT_TAU * jitter)
        new_coords = jnp.transpose(proposal, (1, 0, 2)).reshape(3, walkers * K)
        fresh_vals = evaluate(table_rows, new_coords, False)[0]
        change = (fresh_vals - pieces[0]).reshape(orbitals, walkers, K)
        updates = column_total(
            jnp.einsum("jwk,wjn->wkn", change, inverse, precision=lax.Precision.HIGHEST)
        )
        inverse = inverse - jnp.einsum(
            "wjk,wkn->wjn", columns, updates, precision=lax.Precision.HIGHEST
        )
        positions = lax.dynamic_update_slice_in_dim(positions, proposal, offset, 2)
    return (positions, inverse)


def unchanged(partial_sum):
    return partial_sum


def advance(spline_table, positions, inverse, gaussian, decided, block_order):
    shards = lax.axis_size("orb")
    share = positions.shape[0] // shards
    first = lax.axis_index("orb") * share
    whole_table = lax.all_gather(spline_table, "orb", axis=0, tiled=True)
    own_inverse = lax.all_to_all(inverse, "orb", split_axis=0, concat_axis=1, tiled=True)
    own_positions = lax.dynamic_slice_in_dim(positions, first, share, 0)
    own_gaussian = lax.dynamic_slice_in_dim(gaussian, first, share, 0)
    own_decided = lax.dynamic_slice_in_dim(decided, first, share, 0)
    swept_pos, swept_inv = blocked_sweep(
        whole_table,
        own_positions,
        own_inverse,
        own_gaussian,
        own_decided,
        block_order,
        unchanged,
        unchanged,
    )
    back_inverse = lax.all_to_all(swept_inv, "orb", split_axis=1, concat_axis=0, tiled=True)
    back_positions = lax.all_gather(swept_pos, "orb", axis=0, tiled=True)
    result = (back_positions, back_inverse)
    return result


def routing(everyone, own_parent, width, myself):
    groups = everyone.shape[0] // width
    listing = everyone.reshape(groups, width)
    source = listing // width
    within = listing % width
    target = lax.broadcasted_iota(jnp.int32, (groups, width), 0)
    mine = jnp.logical_and(source == myself, target != myself)
    ranks = jnp.cumsum(mine.astype(jnp.int32), axis=1) - 1
    places = lax.broadcasted_iota(jnp.int32, (groups, CAP, width), 1)
    chosen = jnp.logical_and(mine[:, None, :], ranks[:, None, :] == places)
    sending = jnp.sum(jnp.where(chosen, within[:, None, :], 0), axis=2).reshape(groups * CAP)
    anchor = own_parent // width
    earlier = lax.broadcasted_iota(jnp.int32, (width, width), 1) < lax.broadcasted_iota(
        jnp.int32, (width, width), 0
    )
    same_anchor = anchor[None, :] == anchor[:, None]
    order_rank = jnp.sum(jnp.logical_and(same_anchor, earlier).astype(jnp.int32), axis=1)
    picking = jnp.where(anchor == myself, own_parent % width, width + anchor * CAP + order_rank)
    return (sending, picking)


def outgoing(holding, sending, groups):
    return jnp.take(holding, sending, axis=0).reshape((groups, CAP) + holding.shape[1:])


def arrive(holding, received, picking):
    candidates = jnp.concatenate([holding, received.reshape((-1,) + holding.shape[1:])], axis=0)
    return jnp.take(candidates, picking, axis=0)


def local(positions, inverse, spline_table, gaussian, accepted, block_order, parent):
    myself = lax.axis_index("walker")
    groups = lax.axis_size("walker")
    width = positions.shape[0]
    everyone = lax.all_gather(parent, "walker", axis=0, tiled=True)
    sending, picking = routing(everyone, parent, width, myself)
    decided = accepted.astype(jnp.float32)
    swept_pos, swept_inv = advance(spline_table, positions, inverse, gaussian, decided, block_order)
    got_pos, got_inv = (
        lax.all_to_all(
            outgoing(swept_pos, sending, groups), "walker", split_axis=0, concat_axis=0, tiled=True
        ),
        lax.all_to_all(
            outgoing(swept_inv, sending, groups), "walker", split_axis=0, concat_axis=0, tiled=True
        ),
    )
    new_positions = arrive(swept_pos, got_pos, picking)
    new_inverse = arrive(swept_inv, got_inv, picking)
    return (new_positions, new_inverse)


def solution(mesh):
    return jax.shard_map(
        local,
        mesh=mesh,
        in_specs=(
            P("walker", None, None),
            P("walker", "orb", None),
            P("orb", None),
            P("walker", None, None),
            P("walker", None),
            P(),
            P("walker"),
        ),
        out_specs=(P("walker", None, None), P("walker", "orb", None)),
        check_vma=False,
    )
```

profile of v0, /device:TPU:0, one launch (start us, length us, event | category | flops | bytes accessed | tf_op | source)
XLA Modules:
  0.0 409.9 jit_solution(3382808491043756039)
XLA Ops:
  7.2 6.0 %copy.226 = bf16[128,13824]{0,1:T(8,128)(2,1)} copy(bf16[128,13824]{1,0:T(8,128)(2,1)} %param.11) | data formatting | bytes 7077888 | tf_op args[2]
  13.3 4.4 %all-to-all-start = ((f32[8,128,512]{2,1,0:T(8,128)}), f32[8,128,512]{2,1,0:T(8,128)S(1)}, u32[]{:S(2)}, u32[]{:S(2)}) async-start(f32[8,128,512]{2,1,0:T(8,128)} %param.10), calls=%async_computation | async-start | bytes 4194304 | tf_op jit(solution)/shard_map/all_to_all | solution.py:110
  17.6 0.7 fusion.197
  21.9 0.7 constant_dynamic-slice_fusion.6
  22.6 0.6 fusion.196
  23.2 34.9 %all-to-all-done = f32[8,128,512]{2,1,0:T(8,128)S(1)} async-done(((f32[8,128,512]{2,1,0:T(8,128)}), f32[8,128,512]{2,1,0:T(8,128)S(1)}, u32[]{:S(2)}, u32[]{:S(2)}) %all-to-all-start) | async-done | bytes 2097184 | tf_op jit(solution)/shard_map/all_to_all | solution.py:110
  58.3 1.3 copy-done.8
  59.6 0.2 dynamic-slice_bitcast_fusion.3
  60.0 63.1 %all-gather.2.cloned.1.call-done = bf16[512,13824]{0,1:T(8,128)(2,1)} async-done(((bf16[128,13824]{0,1:T(8,128)(2,1)}), bf16[512,13824]{0,1:T(8,128)(2,1)}) %all-gather.2.cloned.1.call-update) | async-done | bytes 14155792 | tf_op jit(solution)/shard_map/all_gather | solution.py:109
  123.1 14.4 %gather_fusion.4 = bf16[2048,512]{1,0:T(8,128)(2,1)S(1)} fusion(bf16[512,13824]{0,1:T(8,128)(2,1)} %all-gather.2.cloned.1.call-done, s32[2048]{0:T(1024)S(1)} %broadcast_clamp_fusion.7), kind=kCustom, calls=%fused_computation.clone | custom fusion | bytes 4202496 | tf_op jit(solution)/shard_map/jit(_take)/gather | solution.py:64
  137.5 3.2 fusion.21
  141.3 0.4 dynamic_update_slice.12
  142.4 14.4 %gather_fusion.5 = bf16[2048,512]{1,0:T(8,128)(2,1)S(1)} fusion(bf16[512,13824]{0,1:T(8,128)(2,1)} %all-gather.2.cloned.1.call-done, s32[2048]{0:T(1024)S(1)} %broadcast_clamp_fusion.6), kind=kCustom, calls=%fused_computation.1.clone | custom fusion | bytes 4202496 | tf_op jit(solution)/shard_map/jit(_take)/gather | solution.py:64
  156.8 0.7 select_bitcast_fusion.3
  157.5 3.0 fusion.15
  160.6 1.1 fusion.198
  161.7 1.8 convolution_subtract_fusion.3
  163.6 1.3 copy-done.4
  164.9 0.2 dynamic-slice_bitcast_fusion.2
  165.9 14.4 %gather_fusion.6 = bf16[2048,512]{1,0:T(8,128)(2,1)S(1)} fusion(bf16[512,13824]{0,1:T(8,128)(2,1)} %all-gather.2.cloned.1.call-done, s32[2048]{0:T(1024)S(1)} %broadcast_clamp_fusion.5), kind=kCustom, calls=%fused_computation.2.clone | custom fusion | bytes 4202496 | tf_op jit(solution)/shard_map/jit(_take)/gather | solution.py:64
  180.4 3.2 fusion.24
  184.2 0.9 dynamic_update_slice.13
  185.7 14.4 %gather_fusion.7 = bf16[2048,512]{1,0:T(8,128)(2,1)S(1)} fusion(bf16[512,13824]{0,1:T(8,128)(2,1)} %all-gather.2.cloned.1.call-done, s32[2048]{0:T(1024)S(1)} %broadcast_clamp_fusion.4), kind=kCustom, calls=%fused_computation.3.clone | custom fusion | bytes 4202496 | tf_op jit(solution)/shard_map/jit(_take)/gather | solution.py:64
  200.1 0.5 select_bitcast_fusion.2
  200.6 3.0 fusion.13
  203.7 1.1 fusion.199
  204.8 1.8 convolution_subtract_fusion.2
  206.7 1.3 copy-done.2
  209.0 14.4 %gather_fusion.8 = bf16[2048,512]{1,0:T(8,128)(2,1)S(1)} fusion(bf16[512,13824]{0,1:T(8,128)(2,1)} %all-gather.2.cloned.1.call-done, s32[2048]{0:T(1024)S(1)} %broadcast_clamp_fusion.3), kind=kCustom, calls=%fused_computation.4.clone | custom fusion | bytes 4202496 | tf_op jit(solution)/shard_map/jit(_take)/gather | solution.py:64
  223.5 3.4 fusion.27
  227.3 0.4 dynamic_update_slice.14
  228.4 14.4 %gather_fusion.9 = bf16[2048,512]{1,0:T(8,128)(2,1)S(1)} fusion(bf16[512,13824]{0,1:T(8,128)(2,1)} %all-gather.2.cloned.1.call-done, s32[2048]{0:T(1024)S(1)} %broadcast_clamp_fusion.2), kind=kCustom, calls=%fused_computation.5.clone | custom fusion | bytes 4202496 | tf_op jit(solution)/shard_map/jit(_take)/gather | solution.py:64
  242.9 0.5 select_bitcast_fusion.1
  243.4 3.0 fusion.11
  246.4 1.1 fusion.200
  247.6 1.8 convolution_subtract_fusion.1
  249.4 1.3 copy-done.6
  251.8 14.4 %gather_fusion.10 = bf16[2048,512]{1,0:T(8,128)(2,1)S(1)} fusion(bf16[512,13824]{0,1:T(8,128)(2,1)} %all-gather.2.cloned.1.call-done, s32[2048]{0:T(1024)S(1)} %broadcast_clamp_fusion.1), kind=kCustom, calls=%fused_computation.6.clone | custom fusion | bytes 4202496 | tf_op jit(solution)/shard_map/jit(_take)/gather | solution.py:64
  266.2 3.4 fusion.30
  270.6 14.4 %gather_fusion.11 = bf16[2048,512]{1,0:T(8,128)(2,1)S(1)} fusion(bf16[512,13824]{0,1:T(8,128)(2,1)} %all-gather.2.cloned.1.call-done, s32[2048]{0:T(1024)S(1)} %broadcast_clamp_fusion), kind=kCustom, calls=%fused_computation.7.clone | custom fusion | bytes 4202496 | tf_op jit(solution)/shard_map/jit(_take)/gather | solution.py:64
  285.1 0.5 select_bitcast_fusion
  285.5 3.0 fusion.9
  288.6 1.1 fusion.201
  289.7 1.8 convolution_subtract_fusion
  291.6 2.9 copy.271
  294.5 3.7 all-to-all-start.2
  298.3 0.6 dynamic-slice
  299.6 0.2 dynamic-update-slice
  299.8 12.4 %all-reduce = s32[64]{0:T(128)S(1)} all-reduce(s32[64]{0:T(128)S(1)} %dynamic-update-slice), channel_id=1, replica_groups=mesh['walker'=8,'orb'=4] {'walker'}, use_global_device_ids=true, to_apply=%add | all-reduce | flops 64 | bytes 512
  312.9 12.2 %all_gather.10 = f32[8,3,512]{2,1,0:T(4,128)S(1)} all-gather(f32[2,3,512]{2,1,0:T(4,128)S(1)} %dynamic_update_slice.15), channel_id=1, replica_groups=mesh['walker'=8,'orb'=4] {'orb'}, dimensions={0}, use_global_device_ids=true | all-gather | bytes 61440 | tf_op jit(solution)/shard_map/all_gather | solution.py:125
  325.1 0.6 gather_fusion
  325.8 0.7 copy.265
  326.5 6.9 %all-to-all-start.1 = ((f32[8,1,3,512]{3,1,2,0:T(1,128)}), f32[8,1,3,512]{3,1,2,0:T(1,128)S(1)}, u32[]{:S(2)}, u32[]{:S(2)}) async-start(f32[8,1,3,512]{3,1,2,0:T(1,128)} %copy.265), calls=%async_computation.1 | async-start | bytes 98304 | tf_op jit(solution)/shard_map/all_to_all | solution.py:169
  333.4 0.4 copy.272
  334.0 2.0 gather_fusion.2
  336.0 3.3 fusion
  339.3 0.9 all-to-all-done.1
  340.2 5.1 %all-to-all-start.3 = ((f32[8,1,128,512]{3,2,1,0:T(8,128)}), f32[8,1,128,512]{3,2,1,0:T(8,128)}, u32[]{:S(2)}, u32[]{:S(2)}) async-start(f32[8,1,128,512]{3,2,1,0:T(8,128)} %fusion), calls=%async_computation.3 | async-start | bytes 4194304 | tf_op jit(solution)/shard_map/all_to_all | solution.py:172
  345.6 0.6 gather_fusion.1
  346.3 0.6 copy.275
  347.0 46.6 %all-to-all-done.3 = f32[8,1,128,512]{3,2,1,0:T(8,128)} async-done(((f32[8,1,128,512]{3,2,1,0:T(8,128)}), f32[8,1,128,512]{3,2,1,0:T(8,128)}, u32[]{:S(2)}, u32[]{:S(2)}) %all-to-all-start.3) | async-done | bytes 2097184 | tf_op jit(solution)/shard_map/all_to_all | solution.py:172
  393.6 4.3 %pad_maximum_fusion = f32[16,128,512]{2,1,0:T(8,128)} fusion(f32[8,128,512]{2,1,0:T(8,128)} %bitcast.166, f32[8,128,512]{2,1,0:T(8,128)S(1)} %bitcast.299), kind=kLoop, calls=%fused_computation.12 | loop fusion | flops 1048576 | bytes 8388608 | tf_op jit(solution)/shard_map/concatenate | solution.py:156
  397.9 2.9 gather_fusion.3
  400.8 1.8 broadcast_select_fusion
  (261 shorter events, 9.7 us)
Async XLA Ops:
  7.2 11.8 %copy-start = (f32[8,3,512]{2,0,1:T(8,128)S(1)}, f32[8,3,512]{2,0,1:T(8,128)}, u32[]{:S(2)}) copy-start(f32[8,3,512]{2,0,1:T(8,128)} %param.9) | copy-start | bytes 147460
  7.2 115.9 %all-gather.2.cloned.1.call-start = ((), (), s32[]{:S(2)}) async-start(), calls=%async_computation.4 | async-start | bytes 17694720 | tf_op jit(solution)/shard_map/all_gather | solution.py:109
  13.2 4.4 %copy-start.12 = (s32[32]{0:T(128)S(1)}, s32[32]{0:T(128)}, u32[]{:S(2)}) copy-start(s32[32]{0:T(128)} %param.14) | copy-start | bytes 388
  13.2 8.6 %copy-start.13 = (s32[8,64]{1,0:T(8,128)S(1)}, s32[8,64]{1,0:T(8,128)}, u32[]{:S(2)}) copy-start(s32[8,64]{1,0:T(8,128)} %param.13) | copy-start | bytes 6148
  13.3 8.6 %copy-start.10 = (f32[8,3,64]{2,0,1:T(8,128)S(1)}, f32[8,3,64]{2,0,1:T(8,128)}, u32[]{:S(2)}) copy-start(f32[8,3,64]{2,0,1:T(8,128)} %param.12) | copy-start | bytes 18436
  13.3 44.8 %all-to-all-start = ((f32[8,128,512]{2,1,0:T(8,128)}), f32[8,128,512]{2,1,0:T(8,128)S(1)}, u32[]{:S(2)}, u32[]{:S(2)}) async-start(f32[8,128,512]{2,1,0:T(8,128)} %param.10), calls=%async_computation | async-start | bytes 4194304 | tf_op jit(solution)/shard_map/all_to_all | solution.py:110
  58.3 1.3 copy-start.8
  157.5 3.1 copy-start.9
  163.6 1.3 copy-start.4
  200.6 3.1 copy-start.5
  206.7 1.3 copy-start.2
  243.3 3.1 copy-start.3
  249.4 1.3 copy-start.6
  266.2 3.8 copy-start.11
  266.2 3.8 copy-start.14
  285.5 3.1 copy-start.7
  294.5 3.8 copy-start.16
  294.5 5.0 %copy-start.15 = (s32[8]{0:T(128)S(1)}, s32[8]{0:T(128)}, u32[]{:S(2)}) copy-start(s32[8]{0:T(128)} %param.15) | copy-start | bytes 100
  294.5 31.9 %all-to-all-start.2 = ((f32[2,512,512]{2,0,1:T(2,128)}), f32[2,512,512]{2,0,1:T(2,128)S(1)}, u32[]{:S(2)}, u32[]{:S(2)}) async-start(f32[2,512,512]{2,0,1:T(2,128)} %copy.271), calls=%async_computation.2 | async-start | bytes 4194304 | tf_op jit(solution)/shard_map/all_to_all | solution.py:124
  326.5 13.7 %all-to-all-start.1 = ((f32[8,1,3,512]{3,1,2,0:T(1,128)}), f32[8,1,3,512]{3,1,2,0:T(1,128)S(1)}, u32[]{:S(2)}, u32[]{:S(2)}) async-start(f32[8,1,3,512]{3,1,2,0:T(1,128)} %copy.265), calls=%async_computation.1 | async-start | bytes 98304 | tf_op jit(solution)/shard_map/all_to_all | solution.py:169
  340.2 53.4 %all-to-all-start.3 = ((f32[8,1,128,512]{3,2,1,0:T(8,128)}), f32[8,1,128,512]{3,2,1,0:T(8,128)}, u32[]{:S(2)}, u32[]{:S(2)}) async-start(f32[8,1,128,512]{3,2,1,0:T(8,128)} %fusion), calls=%async_computation.3 | async-start | bytes 4194304 | tf_op jit(solution)/shard_map/all_to_all | solution.py:172
  397.9 4.6 %copy-start.1 = (f32[8,3,512]{2,0,1:T(8,128)S(1)}, f32[8,3,512]{2,0,1:T(8,128)}, u32[]{:S(2)}) copy-start(f32[8,3,512]{2,0,1:T(8,128)} %param.9) | copy-start | bytes 147460
Sparse Core Ops, SparseCore 0:
  13.3 109.7 all-gather.1
where the time goes:
time: 417 us; the launch traced here: 410 us
  local copies, waits for them, and re-layouts  149 us (36%)
  waiting for transfers between devices  146 us (35%)
  matrix products  37 us (9%)
  blocking collectives  24.7 us (6%)
  starting transfers between devices  20.2 us (5%)
  between operations  19.1 us (5%)
  other arithmetic  14.7 us (4%)
    gather x8, local copies, waits for them, and re-layouts, evaluate(): gathered = jnp.take(table_rows, points, axis=1).astype(jnp.float32)  116 us
    all_gather x1, waiting for transfers between devices, advance(): whole_table = lax.all_gather(spline_table, 'orb', axis=0, tiled=True)  63.1 us
    all_to_all x1, waiting for transfers between devices, local(): lax.all_to_all(outgoing(swept_inv, sending, groups), 'walker', split_axis...  46.6 us
    all_to_all x1, waiting for transfers between devices, advance(): lax.all_to_all(inverse, 'orb', split_axis=0, concat_axis=1, tiled=True)  34.9 us
    dot_general x8, matrix products, evaluate(): jnp.einsum('rne,cne->cre', gathered, weights, precision=lax.Precision.HIG...  25.2 us
    unnamed x53, local copies, waits for them, and re-layouts  14.3 us
    unnamed x1, blocking collectives  12.4 us
    all_gather x1, blocking collectives, advance(): back_positions = lax.all_gather(swept_pos, 'orb', axis=0, tiled=True)  12.2 us
  transfers between devices with their start and end apart: 5, of which 4 were waited for; matrix products, arithmetic and copies ran while one was open for 3% of the time, Pallas kernels for 0%

commit v1 on v0

v1 whole, which is shorter than its diff:
```python
import functools

import jax
import jax.numpy as jnp
from jax import lax
from jax.experimental import pallas as pl
from jax.experimental.pallas import tpu as pltpu
from jax.sharding import PartitionSpec as P

GRID = 24
PLANE = GRID * GRID
WIDE = 640
K = 16
NMOVE = 4
MOVED = K * NMOVE
CAP = 1
TAU = 0.25
ROOT_TAU = 0.5
F32 = jnp.float32
BF16 = jnp.bfloat16
HIGHEST = lax.Precision.HIGHEST
VMEM = pl.BlockSpec(memory_space=pltpu.VMEM)
LIMIT = 24 * 2**20


def axis_weights(u, with_slopes):
    floors = jnp.floor(u)
    t = u - floors
    remain = 1.0 - t
    square = t * t
    cubed = square * t
    values = (
        remain * remain * remain / 6.0,
        (3.0 * cubed - 6.0 * square + 4.0) / 6.0,
        (-3.0 * cubed + 3.0 * square + 3.0 * t + 1.0) / 6.0,
        cubed / 6.0,
    )
    lanes = u.shape[1]
    line = lax.broadcasted_iota(jnp.int32, (GRID, lanes), 0)
    step = line - (floors.astype(jnp.int32) - 1)
    step = jnp.where(step < 0, step + GRID, step)
    step = jnp.where(step < 0, step + GRID, step)
    step = jnp.where(step >= GRID, step - GRID, step)

    def spread(weights):
        out = jnp.zeros((GRID, lanes), F32)
        for a in range(4):
            out = jnp.where(step == a, jnp.broadcast_to(weights[a], (GRID, lanes)), out)
        return out

    if not with_slopes:
        return spread(values), None
    slopes = (
        -0.5 * remain * remain,
        1.5 * square - 2.0 * t,
        -1.5 * square + t + 0.5,
        0.5 * square,
    )
    return spread(values), spread(slopes)


def halves(first, second):
    product = jnp.concatenate([first[y : y + 1, :] * second for y in range(GRID)], axis=0)
    high = product.astype(BF16)
    return [high, (product - high.astype(F32)).astype(BF16)]


def fill(even_ref, odd_ref, pieces):
    lanes = pieces[0].shape[1]
    pad = jnp.zeros((WIDE - PLANE, lanes), BF16)
    for i, piece in enumerate(pieces):
        at = slice(i * lanes, (i + 1) * lanes)
        even_ref[0:PLANE, at] = piece
        even_ref[PLANE:WIDE, at] = pad
        odd_ref[0 : WIDE - PLANE, at] = pad
        odd_ref[WIDE - PLANE : WIDE, at] = piece


def plane_pair(table_ref, pair, even_ref, odd_ref):
    start = pl.multiple_of(pair * 2 * PLANE, 128)
    even = table_ref[:, pl.ds(start, WIDE)]
    start = pl.multiple_of(pair * 2 * PLANE + 2 * PLANE - WIDE, 128)
    odd = table_ref[:, pl.ds(start, WIDE)]
    return (
        jnp.dot(even, even_ref[...], preferred_element_type=F32),
        jnp.dot(odd, odd_ref[...], preferred_element_type=F32),
    )


def slopes_kernel(state_ref, table_ref, phi_ref, grad_ref, even_ref, odd_ref, wx_ref, sx_ref):
    n = state_ref.shape[1]
    wx, sx = axis_weights(state_ref[0:1, :], True)
    wy, sy = axis_weights(state_ref[1:2, :], True)
    wz, sz = axis_weights(state_ref[2:3, :], True)
    wx_ref[...] = wx
    sx_ref[...] = sx
    fill(even_ref, odd_ref, halves(wy, wz) + halves(sy, wz) + halves(wy, sz))
    phi_ref[...] = jnp.zeros_like(phi_ref)
    grad_ref[...] = jnp.zeros_like(grad_ref)

    def body(pair, carry):
        both = plane_pair(table_ref, pair, even_ref, odd_ref)
        for plane, x in zip(both, (2 * pair, 2 * pair + 1)):
            w = wx_ref[pl.ds(x, 1), :]
            s = sx_ref[pl.ds(x, 1), :]
            base = plane[:, 0:n] + plane[:, n : 2 * n]
            phi_ref[...] += w * base
            grad_ref[:, 0:n] += s * base
            grad_ref[:, n : 2 * n] += w * (plane[:, 2 * n : 3 * n] + plane[:, 3 * n : 4 * n])
            grad_ref[:, 2 * n : 3 * n] += w * (plane[:, 4 * n : 5 * n] + plane[:, 5 * n : 6 * n])
        return carry

    lax.fori_loop(0, GRID // 2, body, 0, unroll=4)


def slopes_call(state, table):
    orbitals = table.shape[0]
    n = state.shape[1]
    return pl.pallas_call(
        slopes_kernel,
        name="slopes",
        out_shape=(
            jax.ShapeDtypeStruct((orbitals, n), F32),
            jax.ShapeDtypeStruct((orbitals, 3 * n), F32),
        ),
        in_specs=[VMEM, VMEM],
        out_specs=(VMEM, VMEM),
        scratch_shapes=[
            pltpu.VMEM((WIDE, 6 * n), BF16),
            pltpu.VMEM((WIDE, 6 * n), BF16),
            pltpu.VMEM((GRID, n), F32),
            pltpu.VMEM((GRID, n), F32),
        ],
        compiler_params=pltpu.CompilerParams(vmem_limit_bytes=LIMIT),
    )(state, table)


def dot(a, b):
    return jnp.dot(a, b, precision=HIGHEST, preferred_element_type=F32)


def dot_nt(a, b):
    return lax.dot_general(
        a, b, (((1,), (1,)), ((), ())), precision=HIGHEST, preferred_element_type=F32
    )


def own_lanes(n, walker):
    lane = lax.broadcasted_iota(jnp.int32, (MOVED, n), 1)
    return jnp.logical_and(lane >= walker * K, lane < (walker + 1) * K)


def fold(big):
    n = big.shape[1]
    total = jnp.zeros((MOVED, n), F32)
    for w in range(n // K):
        total = jnp.where(own_lanes(n, w), big[w * MOVED : (w + 1) * MOVED, :], total)
    return total


def unit(block, n):
    row = lax.broadcasted_iota(jnp.int32, (MOVED, n), 0)
    lane = lax.broadcasted_iota(jnp.int32, (MOVED, n), 1)
    return jnp.where(row - block * K == lane % K, 1.0, 0.0).astype(F32)


def tree(parts):
    while len(parts) > 1:
        parts = [parts[i] + parts[i + 1] for i in range(0, len(parts), 2)]
    return parts[0]


def total(refs):
    return tree([ref[...] for ref in refs])


def drift_kernel(first, vm_ref, grad_ref, out_ref):
    n = grad_ref.shape[1] // 3
    for d in range(3):
        q = fold(dot(vm_ref[...], grad_ref[:, d * n : (d + 1) * n]))
        if first:
            out_ref[d : d + 1, :] = jnp.sum(q * unit(0, n), axis=0, keepdims=True)
        else:
            out_ref[d * MOVED : (d + 1) * MOVED, :] = q
    if first:
        out_ref[3:8, :] = jnp.zeros((5, n), F32)


def drift_call(first, vm, grad):
    n = grad.shape[1] // 3
    return pl.pallas_call(
        functools.partial(drift_kernel, first),
        name="drift",
        out_shape=jax.ShapeDtypeStruct((8 if first else 3 * MOVED, n), F32),
        in_specs=[VMEM, VMEM],
        out_specs=VMEM,
        compiler_params=pltpu.CompilerParams(vmem_limit_bytes=LIMIT),
    )(vm, grad)


def absorb(block, s, y_all, l_all, t):
    n = s.shape[1]
    u = s - fold(dot(y_all, s))
    r = unit(block, n) - fold(dot(l_all, s))

    def spread(x):
        return jnp.concatenate(
            [jnp.where(own_lanes(n, w), x, 0.0) for w in range(n // K)], axis=0
        )

    return y_all + dot_nt(spread(u), t), l_all + dot_nt(spread(r), t)


def step_kernel(block, shards, *refs):
    refs = list(refs)
    s_parts = [refs.pop(0) for _ in range(shards)]
    if block:
        q_parts = [refs.pop(0) for _ in range(shards)]
        y_ref, l_ref, t_ref = [refs.pop(0) for _ in range(3)]
    state_ref, phi_ref, vm_ref, table_ref = [refs.pop(0) for _ in range(4)]
    s_ref, moved_ref, d_ref, y_out, l_out, t_out = [refs.pop(0) for _ in range(6)]
    even_ref, odd_ref, wx_ref = refs
    n = state_ref.shape[1]
    if block == 0:
        drifts = total(s_parts)[0:3, :]
        t_out[...] = unit(0, n)
        y_out[...] = jnp.zeros_like(y_out)
        l_out[...] = jnp.zeros_like(l_out)
    else:
        y_all, l_all = absorb(block - 1, total(s_parts), y_ref[...], l_ref[...], t_ref[...])
        y_out[...] = y_all
        l_out[...] = l_all
        rows = jnp.concatenate(
            [
                y_all[w * MOVED + block * K : w * MOVED + (block + 1) * K, :]
                for w in range(n // K)
            ],
            axis=0,
        )
        t = unit(block, n) - jnp.transpose(rows)
        t_out[...] = t
        q = total(q_parts)
        drifts = jnp.concatenate(
            [
                jnp.sum(q[d * MOVED : (d + 1) * MOVED, :] * t, axis=0, keepdims=True)
                for d in range(3)
            ],
            axis=0,
        )
    speeds = jnp.sum(drifts * drifts, axis=0, keepdims=True)
    capped = drifts / jnp.sqrt(1.0 + TAU * speeds)
    moved = state_ref[0:3, :] + state_ref[6:7, :] * (TAU * capped + ROOT_TAU * state_ref[3:6, :])
    moved_ref[0:3, :] = moved
    moved_ref[3:8, :] = jnp.zeros((5, n), F32)
    wx, _ = axis_weights(moved[0:1, :], False)
    wy, _ = axis_weights(moved[1:2, :], False)
    wz, _ = axis_weights(moved[2:3, :], False)
    wx_ref[...] = wx
    fill(even_ref, odd_ref, halves(wy, wz))
    d_ref[...] = jnp.zeros_like(d_ref)

    def body(pair, carry):
        both = plane_pair(table_ref, pair, even_ref, odd_ref)
        for plane, x in zip(both, (2 * pair, 2 * pair + 1)):
            d_ref[...] += wx_ref[pl.ds(x, 1), :] * (plane[:, 0:n] + plane[:, n : 2 * n])
        return carry

    lax.fori_loop(0, GRID // 2, body, 0, unroll=4)
    change = d_ref[...] - phi_ref[...]
    d_ref[...] = change
    s_ref[...] = fold(dot(vm_ref[...], change))


def step_call(block, s_parts, q_parts, carried, state, phi, vm, table):
    n = state.shape[1]
    rows, orbitals = vm.shape
    operands = [*s_parts, *q_parts, *carried, state, phi, vm, table]
    shapes = [(MOVED, n), (8, n), (orbitals, n), (rows, MOVED), (rows, MOVED), (MOVED, n)]
    return pl.pallas_call(
        functools.partial(step_kernel, block, len(s_parts)),
        name="step",
        out_shape=tuple(jax.ShapeDtypeStruct(shape, F32) for shape in shapes),
        in_specs=[VMEM] * len(operands),
        out_specs=(VMEM,) * len(shapes),
        scratch_shapes=[
            pltpu.VMEM((WIDE, 2 * n), BF16),
            pltpu.VMEM((WIDE, 2 * n), BF16),
            pltpu.VMEM((GRID, n), F32),
        ],
        compiler_params=pltpu.CompilerParams(vmem_limit_bytes=LIMIT),
    )(*operands)


def last_kernel(shards, *refs):
    y_ref, l_ref, t_ref, vm_ref, out_ref = refs[shards:]
    n = t_ref.shape[1]
    _, l_all = absorb(NMOVE - 1, total(refs[:shards]), y_ref[...], l_ref[...], t_ref[...])
    for w in range(n // K):
        at = slice(w * MOVED, (w + 1) * MOVED)
        out_ref[w] = jnp.transpose(dot(l_all[at, :], vm_ref[at, :]))


def last_call(s_parts, carried, vm):
    rows, orbitals = vm.shape
    return pl.pallas_call(
        functools.partial(last_kernel, len(s_parts)),
        name="last",
        out_shape=jax.ShapeDtypeStruct((rows // MOVED, orbitals, MOVED), F32),
        in_specs=[VMEM] * (len(s_parts) + 4),
        out_specs=VMEM,
        compiler_params=pltpu.CompilerParams(vmem_limit_bytes=LIMIT),
    )(*s_parts, *carried, vm)


def sums_kernel(*refs):
    v_ref, out_ref = refs[NMOVE:]
    change = jnp.concatenate([jnp.transpose(ref[...]) for ref in refs[:NMOVE]], axis=0)
    n = refs[0].shape[1]
    for w in range(n // K):
        own = jnp.concatenate(
            [change[b * n + w * K : b * n + (w + 1) * K, :] for b in range(NMOVE)], axis=0
        )
        out_ref[w] = dot(own, v_ref[w])


def sums_call(changes, inverse):
    walkers, _, electrons = inverse.shape
    return pl.pallas_call(
        sums_kernel,
        name="sums",
        out_shape=jax.ShapeDtypeStruct((walkers, MOVED, electrons), F32),
        in_specs=[VMEM] * (NMOVE + 1),
        out_specs=VMEM,
        compiler_params=pltpu.CompilerParams(vmem_limit_bytes=LIMIT),
    )(*changes, inverse)


def update_kernel(v_ref, factor_ref, sums_ref, out_ref):
    out_ref[0] = v_ref[0] - dot(factor_ref[0], sums_ref[0])


def update_call(inverse, factor, sums):
    walkers, orbitals, electrons = inverse.shape
    return pl.pallas_call(
        update_kernel,
        name="update",
        grid=(walkers,),
        out_shape=jax.ShapeDtypeStruct(inverse.shape, F32),
        in_specs=[
            pl.BlockSpec((1, orbitals, electrons), lambda w: (w, 0, 0)),
            pl.BlockSpec((1, orbitals, MOVED), lambda w: (w, 0, 0)),
            pl.BlockSpec((1, MOVED, electrons), lambda w: (w, 0, 0)),
        ],
        out_specs=pl.BlockSpec((1, orbitals, electrons), lambda w: (w, 0, 0)),
        compiler_params=pltpu.CompilerParams(vmem_limit_bytes=LIMIT),
    )(inverse, factor, sums)


def exchange(part, axis):
    size = lax.axis_size(axis)
    others = [
        lax.ppermute(part, axis, [(i, i ^ k) for i in range(size)]) for k in range(1, size)
    ]
    return [part, *others]


def routing(everyone, own_parent, width, myself):
    groups = everyone.shape[0] // width
    listing = everyone.reshape(groups, width)
    source = listing // width
    within = listing % width
    target = lax.broadcasted_iota(jnp.int32, (groups, width), 0)
    mine = jnp.logical_and(source == myself, target != myself)
    sending = jnp.sum(jnp.where(mine, within, 0), axis=1)
    anchor = own_parent // width
    picking = jnp.where(anchor == myself, own_parent % width, width + anchor)
    return sending, picking


def fetch(holding, sending, picking):
    outgoing = jnp.take(holding, sending, axis=0)
    received = lax.all_to_all(outgoing, "walker", split_axis=0, concat_axis=0, tiled=True)
    return jnp.take(jnp.concatenate([holding, received], axis=0), picking, axis=0)


def local(positions, inverse, spline_table, gaussian, accepted, block_order, parent):
    myself = lax.axis_index("walker")
    walkers, _, electrons = positions.shape
    orbitals = inverse.shape[1]
    n = walkers * K
    columns = (block_order[:NMOVE, None] * K + jnp.arange(K, dtype=jnp.int32)).reshape(MOVED)
    chosen = (
        columns[:, None] == lax.broadcasted_iota(jnp.int32, (MOVED, electrons), 1)
    ).astype(F32)

    moving = jnp.einsum("wdn,mn->wdm", positions, chosen, precision=HIGHEST)
    info = jnp.concatenate(
        [
            moving,
            gaussian,
            accepted.astype(F32)[:, None, :],
            jnp.broadcast_to(parent.astype(F32)[:, None, None], (walkers, 1, MOVED)),
        ],
        axis=1,
    )
    everyone = lax.all_gather(info, "walker", axis=0, tiled=True)
    sending, picking = routing(everyone[:, 7, 0].astype(jnp.int32), parent, walkers, myself)
    states = jnp.take(everyone, parent, axis=0)
    states = jnp.transpose(states.reshape(walkers, 8, NMOVE, K), (2, 1, 0, 3))
    states = states.reshape(NMOVE, 8, n)

    own_vm = jnp.einsum("mn,wjn->wmj", chosen, inverse, precision=HIGHEST)
    vm = fetch(own_vm, sending, picking).reshape(walkers * MOVED, orbitals)
    whole = fetch(inverse, sending, picking)
    all_positions = lax.all_gather(positions, "walker", axis=0, tiled=True)
    resting = jnp.take(all_positions, parent, axis=0)

    evals = [slopes_call(states[b], spline_table) for b in range(NMOVE)]
    s_parts = exchange(drift_call(True, vm, evals[0][1]), "orb")
    q_parts = [[]] + [
        exchange(drift_call(False, vm, evals[b][1]), "orb") for b in range(1, NMOVE)
    ]
    carried = []
    moved = []
    changes = []
    for b in range(NMOVE):
        s, new, change, *carried = step_call(
            b, s_parts, q_parts[b], carried, states[b], evals[b][0], vm, spline_table
        )
        moved.append(new[0:3].reshape(3, walkers, K))
        changes.append(change)
        s_parts = exchange(s, "orb")
    factor = last_call(s_parts, carried, vm)
    sums = lax.psum(sums_call(changes, whole), "orb")
    new_inverse = update_call(whole, factor, sums)

    fresh = jnp.transpose(jnp.stack(moved), (2, 1, 0, 3)).reshape(walkers, 3, MOVED)
    placed = jnp.einsum("wdm,mn->wdn", fresh, chosen, precision=HIGHEST)
    touched = jnp.sum(chosen, axis=0) > 0.0
    return jnp.where(touched, placed, resting), new_inverse


def solution(mesh):
    return jax.shard_map(
        local,
        mesh=mesh,
        in_specs=(
            P("walker", None, None),
            P("walker", "orb", None),
            P("orb", None),
            P("walker", None, None),
            P("walker", None),
            P(),
            P("walker"),
        ),
        out_specs=(P("walker", None, None), P("walker", "orb", None)),
        check_vma=False,
    )
```

time: 417 us -> 262 us (0.63); the launches traced: 410 us -> 261 us
  waiting for transfers between devices: 146 us -> 35 us
  local copies, waits for them, and re-layouts: 149 us -> 45.3 us
  Pallas kernels: 0 us -> 50.3 us
  blocking collectives: 24.7 us -> 64.1 us
  matrix products: 37 us -> 4.69 us
  starting transfers between devices: 20.2 us -> 26.6 us
  other arithmetic: 14.7 us -> 19.9 us
  between operations: 19.1 us -> 14.7 us
    gather x12 -> x7, local copies, waits for them, and re-layouts: 122 us -> 15.2 us  [the longest x2 6.63 us: fetch(): jnp.take(jnp.concatenate([holding, received], axis=0), picking, axis=0)]
    all_to_all x4 -> x2, waiting for transfers between devices: 82.4 us -> 3.13 us  [fetch(): lax.all_to_all(outgoing, 'walker', split_axis=0, concat_axis=0, tiled=True)]
    all_gather x1 -> x0, waiting for transfers between devices: 63.1 us -> none  [advance(): whole_table = lax.all_gather(spline_table, 'orb', axis=0, tiled=True)]
    all_gather x1 -> x2, blocking collectives: 12.2 us -> 64.1 us  [the longest x1 32.6 us: local(): everyone = lax.all_gather(info, 'walker', axis=0, tiled=True)]
    pallas_call x0 -> x15, Pallas kernels: none -> 50.3 us  [the longest x4 19.4 us: slopes_call(): pl.pallas_call(slopes_kernel, name='slopes', out_shape=(jax.ShapeDtypeStr...]
    dot_general x16 -> x3, matrix products: 37 us -> 4.69 us  [the longest x1 2.83 us: local(): own_vm = jnp.einsum('mn,wjn->wmj', chosen, inverse, precision=HIGHEST)]
    psum x0 -> x1, waiting for transfers between devices: none -> 28.4 us  [local(): sums = lax.psum(sums_call(changes, whole), 'orb')]
    ppermute x0 -> x24, starting transfers between devices: none -> 16.7 us  [exchange(): lax.ppermute(part, axis, [(i, i ^ k) for i in range(size)])]
  transfers between devices with their start and end apart: 5 -> 27, of which waited for: 4 -> 6; matrix products, arithmetic and copies ran while one was open for 3% -> 10% of each run, Pallas kernels for 0% -> 17%
where the time goes in v1:
time: 262 us; the launch traced here: 261 us
  blocking collectives  64.1 us (24%)
  Pallas kernels  50.3 us (19%)
  local copies, waits for them, and re-layouts  45.3 us (17%)
  waiting for transfers between devices  35 us (13%)
  starting transfers between devices  26.6 us (10%)
  other arithmetic  19.9 us (8%)
  between operations  14.7 us (6%)
  matrix products  4.69 us (2%)
    all_gather x1, blocking collectives, local(): everyone = lax.all_gather(info, 'walker', axis=0, tiled=True)  32.6 us
    all_gather x1, blocking collectives, local(): all_positions = lax.all_gather(positions, 'walker', axis=0, tiled=True)  31.5 us
    psum x1, waiting for transfers between devices, local(): sums = lax.psum(sums_call(changes, whole), 'orb')  28.4 us
    unnamed x138, local copies, waits for them, and re-layouts  22.4 us
    pallas_call x4, Pallas kernels, slopes_call(): pl.pallas_call(slopes_kernel, name='slopes', out_shape=(jax.ShapeDtypeStr...  19.4 us
    pallas_call x4, Pallas kernels, step_call(): pl.pallas_call(functools.partial(step_kernel, block, len(s_parts)), name=...  17.7 us
    ppermute x24, starting transfers between devices, exchange(): lax.ppermute(part, axis, [(i, i ^ k) for i in range(size)])  16.7 us
    all_to_all x2, starting transfers between devices, fetch(): lax.all_to_all(outgoing, 'walker', split_axis=0, concat_axis=0, tiled=True)  9.94 us
  transfers between devices with their start and end apart: 27, of which 6 were waited for; matrix products, arithmetic and copies ran while one was open for 10% of the time, Pallas kernels for 17%

profile of v1, /device:TPU:0, one launch (start us, length us, event | category | flops | bytes accessed | tf_op | source)
XLA Modules:
  0.0 260.6 jit_solution(2777744129021232116)
XLA Ops:
  7.8 1.2 compare_select_fusion.4
  9.9 1.0 convolution_bitcast_fusion.1
  11.8 32.6 %all_gather.6 = f32[64,8,64]{2,0,1:T(8,128)S(1)} all-gather(f32[8,8,64]{2,0,1:T(8,128)S(1)} %pad_maximum_fusion.2), channel_id=1, replica_groups=mesh['walker'=8,'orb'=4] {'walker'}, dimensions={0}, use_global_device_ids=true | all-gather | bytes 147456 | tf_op jit(solution)/shard_map/all_gather | solution.py:406
  45.1 2.8 %convolution_bitcast_fusion = f32[8,64,128]{2,1,0:T(8,128)S(1)} fusion(f32[8,128,512]{2,1,0:T(8,128)} %param.8, s32[64]{0:T(128)S(1)} %add.79), kind=kOutput, calls=%fused_computation.7 | convolution fusion | flops 402685952 | bytes 2359552 | tf_op jit(solution)/shard_map/mn,wjn->wmj/dot_general | solution.py:412
  48.5 0.8 broadcast_select_fusion.2
  49.3 5.6 %all-to-all-start = ((f32[8,64,128]{2,1,0:T(8,128)}), f32[8,64,128]{2,1,0:T(8,128)}, u32[]{:S(2)}, u32[]{:S(2)}) async-start(f32[8,64,128]{2,1,0:T(8,128)} %broadcast_select_fusion.2), calls=%async_computation | async-start | bytes 524288 | tf_op jit(solution)/shard_map/all_to_all | solution.py:382
  54.9 2.0 gather_fusion.4
  56.9 3.3 %broadcast_select_fusion.1 = f32[8,128,512]{2,1,0:T(8,128)} fusion(f32[8,128,512]{2,1,0:T(8,128)} %gather_fusion.4, pred[8]{0:T(512)(128)(4,1)S(1)} %compare_and_fusion.1), kind=kLoop, calls=%fused_computation.11 | loop fusion | flops 524288 | bytes 4194312 | tf_op jit(solution)/shard_map/jit(_take)/select_n | solution.py:381
  60.2 3.1 %all-to-all-done = f32[8,64,128]{2,1,0:T(8,128)} async-done(((f32[8,64,128]{2,1,0:T(8,128)}), f32[8,64,128]{2,1,0:T(8,128)}, u32[]{:S(2)}, u32[]{:S(2)}) %all-to-all-start) | async-done | bytes 262176 | tf_op jit(solution)/shard_map/all_to_all | solution.py:382
  63.3 4.4 %all-to-all-start.1 = ((f32[8,128,512]{2,1,0:T(8,128)}), f32[8,128,512]{2,1,0:T(8,128)}, u32[]{:S(2)}, u32[]{:S(2)}) async-start(f32[8,128,512]{2,1,0:T(8,128)} %broadcast_select_fusion.1), calls=%async_computation.1 | async-start | bytes 4194304 | tf_op jit(solution)/shard_map/all_to_all | solution.py:382
  67.7 1.8 copy.16
  70.9 2.1 gather_fusion.2
  73.0 1.5 gather.32
  74.6 1.0 fusion
  76.2 0.8 squeeze.8.state_ref.refs_4_
  77.0 5.0 %slopes.4 = (f32[128,128]{1,0:T(8,128)S(1)}, f32[128,384]{1,0:T(8,128)S(1)}) custom-call(f32[8,128]{1,0:T(8,128)S(1)} %squeeze.8.state_ref.refs_4_, bf16[128,13824]{1,0:T(8,128)(2,1)S(1)} %copy-done), custom_call_target="tpu_custom_call" | custom-call | tf_op jit(solution)/shard_map/slopes/pallas_call | solution.py:119
  83.3 1.8 pad_maximum_fusion.1
  85.1 2.3 gather_fusion.1
  87.4 1.1 bitcast_select_fusion.vm_ref.refs_6_.refs_13_.refs_7_
  88.5 1.0 copy-done.21
  90.4 1.6 collective-permute-start.1
  92.3 1.2 collective-permute-done.2.refs_3_
  94.1 0.8 copy-done.31
  94.9 2.9 %step.4 = (f32[64,128]{1,0:T(8,128)}, f32[8,128]{1,0:T(8,128)S(1)}, f32[128,128]{1,0:T(8,128)S(1)}, f32[512,64]{1,0:T(8,128)S(1)}, f32[512,64]{1,0:T(8,128)S(1)}, /*index=5*/f32[64,128]{1,0:T(8,128)S(1)}) custom-call(f32[8,128]{1,0:T(8,128)S(1)} %drift.4.refs_0_, f32[8,128]{1,0:T(8,128)S(1)} %collective-permute-done.refs_1_, ...), custom_call_target="tpu_custom_call" | custom-call | tf_op jit(solution)/shard_map/step/pallas_call | solution.py:279
  100.5 0.9 collective-permute-start.5
  101.4 1.5 collective-permute-start.4
  102.9 0.8 squeeze.18.state_ref.refs_11_
  103.8 4.8 %slopes.5 = (f32[128,128]{1,0:T(8,128)S(1)}, f32[128,384]{1,0:T(8,128)S(1)}) custom-call(f32[8,128]{1,0:T(8,128)S(1)} %squeeze.18.state_ref.refs_11_, bf16[128,13824]{1,0:T(8,128)(2,1)S(1)} %copy-done), custom_call_target="tpu_custom_call" | custom-call | tf_op jit(solution)/shard_map/slopes/pallas_call | solution.py:119
  109.2 1.4 drift.5.refs_4_
  111.3 1.5 collective-permute-start.7
  112.8 0.8 squeeze.19.state_ref.refs_11_
  113.6 4.8 %slopes.6 = (f32[128,128]{1,0:T(8,128)S(1)}, f32[128,384]{1,0:T(8,128)S(1)}) custom-call(f32[8,128]{1,0:T(8,128)S(1)} %squeeze.19.state_ref.refs_11_, bf16[128,13824]{1,0:T(8,128)(2,1)S(1)} %copy-done), custom_call_target="tpu_custom_call" | custom-call | tf_op jit(solution)/shard_map/slopes/pallas_call | solution.py:119
  119.0 1.4 drift.6.refs_4_
  121.1 1.5 collective-permute-start.13
  122.6 0.8 squeeze.20.state_ref.refs_11_
  123.4 4.8 %slopes.7 = (f32[128,128]{1,0:T(8,128)S(1)}, f32[128,384]{1,0:T(8,128)S(1)}) custom-call(f32[8,128]{1,0:T(8,128)S(1)} %squeeze.20.state_ref.refs_11_, bf16[128,13824]{1,0:T(8,128)(2,1)S(1)} %copy-done), custom_call_target="tpu_custom_call" | custom-call | tf_op jit(solution)/shard_map/slopes/pallas_call | solution.py:119
  128.3 1.4 drift.7.refs_4_
  130.4 4.9 %step.5 = (f32[64,128]{1,0:T(8,128)S(1)}, f32[8,128]{1,0:T(8,128)S(1)}, f32[128,128]{1,0:T(8,128)S(1)}, f32[512,64]{1,0:T(8,128)S(1)}, f32[512,64]{1,0:T(8,128)S(1)}, /*index=5*/f32[64,128]{1,0:T(8,128)S(1)}) custom-call(f32[64,128]{1,0:T(8,128)} %get-tuple-element.37.refs_0_, f32[64,128]{1,0:T(8,128)} %collective-permute-done.3.refs_1_, ...), custom_call_target="tpu_custom_call" | custom-call | tf_op jit(solution)/shard_map/step/pallas_call | solution.py:279
  135.4 1.2 collective-permute-start.11
  137.3 31.5 %all_gather.7 = f32[64,3,512]{2,0,1:T(8,128)S(1)} all-gather(f32[8,3,512]{2,0,1:T(8,128)S(1)} %copy-done.57), channel_id=1, replica_groups=mesh['walker'=8,'orb'=4] {'walker'}, dimensions={0}, use_global_device_ids=true | all-gather | bytes 442368 | tf_op jit(solution)/shard_map/all_gather | solution.py:415
  168.8 1.2 collective-permute-start.19
  170.0 5.2 %step.6 = (f32[64,128]{1,0:T(8,128)}, f32[8,128]{1,0:T(8,128)S(1)}, f32[128,128]{1,0:T(8,128)S(1)}, f32[512,64]{1,0:T(8,128)S(1)}, f32[512,64]{1,0:T(8,128)S(1)}, /*index=5*/f32[64,128]{1,0:T(8,128)S(1)}) custom-call(f32[64,128]{1,0:T(8,128)S(1)} %get-tuple-element.44.refs_0_, f32[64,128]{1,0:T(8,128)S(1)} %collective-permute-done.9.refs_1_, ...), custom_call_target="tpu_custom_call" | custom-call | tf_op jit(solution)/shard_map/step/pallas_call | solution.py:279
  177.9 0.9 collective-permute-start.17
  178.8 1.2 collective-permute-start.16
  181.3 1.1 copy.19
  182.4 2.4 gather_fusion.3
  184.8 0.9 copy-done.5
  185.7 0.9 copy-done.13
  186.7 0.9 copy-done.15
  187.6 0.9 copy-done.23
  188.5 0.8 copy-done.25
  190.1 4.6 %step.7 = (f32[64,128]{1,0:T(8,128)S(1)}, f32[8,128]{1,0:T(8,128)S(1)}, f32[128,128]{1,0:T(8,128)S(1)}, f32[512,64]{1,0:T(8,128)S(1)}, f32[512,64]{1,0:T(8,128)S(1)}, /*index=5*/f32[64,128]{1,0:T(8,128)S(1)}) custom-call(f32[64,128]{1,0:T(8,128)} %get-tuple-element.51.refs_0_, f32[64,128]{1,0:T(8,128)} %collective-permute-done.15.refs_1_, ...), custom_call_target="tpu_custom_call" | custom-call | tf_op jit(solution)/shard_map/step/pallas_call | solution.py:279
  198.1 4.9 %pad_maximum_fusion = f32[16,128,512]{2,1,0:T(8,128)} fusion(f32[8,128,512]{2,1,0:T(8,128)} %all-to-all-done.1, f32[8,128,512]{2,1,0:T(8,128)} %param.8), kind=kLoop, calls=%fused_computation.6 | loop fusion | flops 1048576 | bytes 8388608 | tf_op jit(solution)/shard_map/concatenate | solution.py:383
  202.9 4.3 %gather_fusion.5 = f32[8,128,512]{2,1,0:T(8,128)} fusion(f32[16,128,512]{2,1,0:T(8,128)} %pad_maximum_fusion, s32[1024]{0:T(1024)} %copy-done.59), kind=kCustom, calls=%fused_computation.5 | custom fusion | bytes 4194336 | tf_op jit(solution)/shard_map/jit(_take)/gather | solution.py:383
  207.2 2.0 broadcast_select_fusion.refs_4_.v_ref
  209.4 2.1 sums.1
  211.8 1.0 collective-permute-start.23
  212.8 1.2 collective-permute-start.22
  214.2 0.9 convolution_select_fusion
  215.2 1.5 collective-permute-done.22.refs_2_
  218.1 1.4 last.1.factor_ref
  219.5 28.4 %all-reduce.2.cloned.1.call-done.sums_ref = f32[8,64,512]{2,1,0:T(8,128)} async-done(((f32[8,64,512]{2,1,0:T(8,128)}), f32[8,64,512]{2,1,0:T(8,128)}) %all-reduce.2.cloned.1.call-update) | async-done | bytes 1048592 | tf_op jit(solution)/shard_map/psum | solution.py:434
  247.9 1.2 copy-done.7
  249.1 4.6 %update.1 = f32[8,128,512]{2,1,0:T(8,128)} custom-call(f32[8,128,512]{2,1,0:T(8,128)S(1)} %broadcast_select_fusion.refs_4_.v_ref, f32[8,128,64]{2,1,0:T(8,128)S(1)} %last.1.factor_ref, f32[8,64,512]{2,1,0:T(8,128)S(1)} %copy-done.7), custom_call_target="tpu_custom_call" | custom-call | tf_op jit(solution)/shard_map/update/pallas_call | solution.py:344
  (202 shorter events, 25.3 us)
Async XLA Ops:
  9.2 35.9 %copy-start.61 = (s32[64]{0:T(128)}, s32[64]{0:T(128)S(1)}, u32[]{:S(2)}) copy-start(s32[64]{0:T(128)S(1)} %add.79) | copy-start | bytes 772
  11.8 43.1 %copy-start.52 = (f32[8,128,512]{2,1,0:T(8,128)S(1)}, f32[8,128,512]{2,1,0:T(8,128)}, u32[]{:S(2)}) copy-start(f32[8,128,512]{2,1,0:T(8,128)} %param.8) | copy-start | bytes 6291460
  48.0 9.0 %copy-start.53 = (f32[8,64,128]{2,1,0:T(8,128)}, f32[8,64,128]{2,1,0:T(8,128)S(1)}, u32[]{:S(2)}) copy-start(f32[8,64,128]{2,1,0:T(8,128)S(1)} %convolution_bitcast_fusion) | copy-start | bytes 786436
  49.3 14.0 %all-to-all-start = ((f32[8,64,128]{2,1,0:T(8,128)}), f32[8,64,128]{2,1,0:T(8,128)}, u32[]{:S(2)}, u32[]{:S(2)}) async-start(f32[8,64,128]{2,1,0:T(8,128)} %broadcast_select_fusion.2), calls=%async_computation | async-start | bytes 524288 | tf_op jit(solution)/shard_map/all_to_all | solution.py:382
  60.2 9.4 %copy-start.68 = (s32[8]{0:T(128)S(1)}, s32[8]{0:T(128)}, u32[]{:S(2)}) copy-start(s32[8]{0:T(128)} %param.13) | copy-start | bytes 100
  60.2 16.8 %copy-start = (bf16[128,13824]{1,0:T(8,128)(2,1)S(1)}, bf16[128,13824]{1,0:T(8,128)(2,1)}, u32[]{:S(2)}) copy-start(bf16[128,13824]{1,0:T(8,128)(2,1)} %refs_14_.5) | copy-start | bytes 10616836
  63.3 134.7 %all-to-all-start.1 = ((f32[8,128,512]{2,1,0:T(8,128)}), f32[8,128,512]{2,1,0:T(8,128)}, u32[]{:S(2)}, u32[]{:S(2)}) async-start(f32[8,128,512]{2,1,0:T(8,128)} %broadcast_select_fusion.1), calls=%async_computation.1 | async-start | bytes 4194304 | tf_op jit(solution)/shard_map/all_to_all | solution.py:382
  67.7 180.2 %all-reduce.2.cloned.1.call-start = ((), (), s32[]{:S(2)}) async-start(), calls=%async_computation.2 | async-start | bytes 2097152 | tf_op jit(solution)/shard_map/psum | solution.py:434
  69.6 6.6 %copy-start.64 = (pred[8]{0:T(512)(128)(4,1)}, pred[8]{0:T(512)(128)(4,1)S(1)}, u32[]{:S(2)}) copy-start(pred[8]{0:T(512)(128)(4,1)S(1)} %get-tuple-element.72) | copy-start | bytes 28
  70.9 11.1 %copy-start.60 = (s32[1024]{0:T(1024)}, s32[1024]{0:T(1024)S(1)}, u32[]{:S(2)}) copy-start(s32[1024]{0:T(1024)S(1)} %pad_clamp_fusion) | copy-start | bytes 12292
  77.0 6.3 %copy-start.54 = (f32[8,64,128]{2,1,0:T(8,128)S(1)}, f32[8,64,128]{2,1,0:T(8,128)}, u32[]{:S(2)}) copy-start(f32[8,64,128]{2,1,0:T(8,128)} %copy-done.53) | copy-start | bytes 786436
  83.3 10.8 %copy-start.59 = (s32[1024]{0:T(1024)}, s32[1024]{0:T(1024)S(1)}, u32[]{:S(2)}) copy-start(s32[1024]{0:T(1024)S(1)} %pad_clamp_fusion.1) | copy-start | bytes 12292
  88.5 9.4 %copy-start.1 = (f32[512,128]{1,0:T(8,128)}, f32[512,128]{1,0:T(8,128)S(1)}, u32[]{:S(2)}) copy-start(f32[512,128]{1,0:T(8,128)S(1)} %bitcast_select_fusion.vm_ref.refs_6_.refs_13_.refs_7_) | copy-start | bytes 786436
  90.3 3.1 %collective-permute-start.2 = (f32[8,128]{1,0:T(8,128)S(1)}, f32[8,128]{1,0:T(8,128)S(1)}, u32[]{:S(2)}, u32[]{:S(2)}) collective-permute-start(f32[8,128]{1,0:T(8,128)S(1)} %drift.4.refs_0_), channel_id=1, source_target_pairs={{0,3},{1,2},{2,1},{3,0},{4,7},{5,6},{6,5},{7,4},{8,11},{9,10},{10,... | collective-permute-start | bytes 12296 | tf_op jit(solution)/shard_map/ppermute | solution.py:362
  90.4 3.7 %collective-permute-start.1 = (f32[8,128]{1,0:T(8,128)S(1)}, f32[8,128]{1,0:T(8,128)S(1)}, u32[]{:S(2)}, u32[]{:S(2)}) collective-permute-start(f32[8,128]{1,0:T(8,128)S(1)} %drift.4.refs_0_), channel_id=1, source_target_pairs={{0,2},{1,3},{2,0},{3,1},{4,6},{5,7},{6,4},{7,5},{8,10},{9,11},{10,... | collective-permute-start | bytes 12296 | tf_op jit(solution)/shard_map/ppermute | solution.py:362
  92.0 2.1 collective-permute-start
  100.5 12.2 %collective-permute-start.5 = (f32[64,128]{1,0:T(8,128)}, f32[64,128]{1,0:T(8,128)}, u32[]{:S(2)}, u32[]{:S(2)}) collective-permute-start(f32[64,128]{1,0:T(8,128)} %get-tuple-element.37.refs_0_), channel_id=1, source_target_pairs={{0,3},{1,2},{2,1},{3,0},{4,7},{5,6},{6,5},{7,4},{8,11},{9,10},{10,... | collective-permute-start | bytes 98312 | tf_op jit(solution)/shard_map/ppermute | solution.py:362
  101.4 19.0 %collective-permute-start.4 = (f32[64,128]{1,0:T(8,128)}, f32[64,128]{1,0:T(8,128)}, u32[]{:S(2)}, u32[]{:S(2)}) collective-permute-start(f32[64,128]{1,0:T(8,128)} %get-tuple-element.37.refs_0_), channel_id=1, source_target_pairs={{0,2},{1,3},{2,0},{3,1},{4,6},{5,7},{6,4},{7,5},{8,10},{9,11},{10,... | collective-permute-start | bytes 98312 | tf_op jit(solution)/shard_map/ppermute | solution.py:362
  102.9 18.1 %collective-permute-start.3 = (f32[64,128]{1,0:T(8,128)}, f32[64,128]{1,0:T(8,128)}, u32[]{:S(2)}, u32[]{:S(2)}) collective-permute-start(f32[64,128]{1,0:T(8,128)} %get-tuple-element.37.refs_0_), channel_id=1, source_target_pairs={{0,1},{1,0},{2,3},{3,2},{4,5},{5,4},{6,7},{7,6},{8,9},{9,8},{10,11... | collective-permute-start | bytes 98312 | tf_op jit(solution)/shard_map/ppermute | solution.py:362
  103.8 5.4 %copy-start.2 = (f32[512,128]{1,0:T(8,128)S(1)}, f32[512,128]{1,0:T(8,128)}, u32[]{:S(2)}) copy-start(f32[512,128]{1,0:T(8,128)} %copy-done.1) | copy-start | bytes 786436
  110.6 19.1 %collective-permute-start.8 = (f32[192,128]{1,0:T(8,128)}, f32[192,128]{1,0:T(8,128)}, u32[]{:S(2)}, u32[]{:S(2)}) collective-permute-start(f32[192,128]{1,0:T(8,128)} %drift.5.refs_4_), channel_id=1, source_target_pairs={{0,3},{1,2},{2,1},{3,0},{4,7},{5,6},{6,5},{7,4},{8,11},{9,10},{10,... | collective-permute-start | bytes 294920 | tf_op jit(solution)/shard_map/ppermute | solution.py:362
  111.3 18.5 %collective-permute-start.7 = (f32[192,128]{1,0:T(8,128)}, f32[192,128]{1,0:T(8,128)}, u32[]{:S(2)}, u32[]{:S(2)}) collective-permute-start(f32[192,128]{1,0:T(8,128)} %drift.5.refs_4_), channel_id=1, source_target_pairs={{0,2},{1,3},{2,0},{3,1},{4,6},{5,7},{6,4},{7,5},{8,10},{9,11},{10,... | collective-permute-start | bytes 294920 | tf_op jit(solution)/shard_map/ppermute | solution.py:362
  112.8 17.6 %collective-permute-start.6 = (f32[192,128]{1,0:T(8,128)}, f32[192,128]{1,0:T(8,128)}, u32[]{:S(2)}, u32[]{:S(2)}) collective-permute-start(f32[192,128]{1,0:T(8,128)} %drift.5.refs_4_), channel_id=1, source_target_pairs={{0,1},{1,0},{2,3},{3,2},{4,5},{5,4},{6,7},{7,6},{8,9},{9,8},{10,11... | collective-permute-start | bytes 294920 | tf_op jit(solution)/shard_map/ppermute | solution.py:362
  113.6 5.4 %copy-start.3 = (f32[512,128]{1,0:T(8,128)S(1)}, f32[512,128]{1,0:T(8,128)}, u32[]{:S(2)}) copy-start(f32[512,128]{1,0:T(8,128)} %copy-done.1) | copy-start | bytes 786436
  120.4 16.2 %collective-permute-start.14 = (f32[192,128]{1,0:T(8,128)}, f32[192,128]{1,0:T(8,128)}, u32[]{:S(2)}, u32[]{:S(2)}) collective-permute-start(f32[192,128]{1,0:T(8,128)} %drift.6.refs_4_), channel_id=1, source_target_pairs={{0,3},{1,2},{2,1},{3,0},{4,7},{5,6},{6,5},{7,4},{8,11},{9,10},{10,... | collective-permute-start | bytes 294920 | tf_op jit(solution)/shard_map/ppermute | solution.py:362
  121.1 16.1 %collective-permute-start.13 = (f32[192,128]{1,0:T(8,128)}, f32[192,128]{1,0:T(8,128)}, u32[]{:S(2)}, u32[]{:S(2)}) collective-permute-start(f32[192,128]{1,0:T(8,128)} %drift.6.refs_4_), channel_id=1, source_target_pairs={{0,2},{1,3},{2,0},{3,1},{4,6},{5,7},{6,4},{7,5},{8,10},{9,11},{10,... | collective-permute-start | bytes 294920 | tf_op jit(solution)/shard_map/ppermute | solution.py:362
  123.4 4.9 %copy-start.4 = (f32[512,128]{1,0:T(8,128)S(1)}, f32[512,128]{1,0:T(8,128)}, u32[]{:S(2)}) copy-start(f32[512,128]{1,0:T(8,128)} %copy-done.1) | copy-start | bytes 786436
  123.4 7.0 %copy-start.9 = (f32[512,64]{1,0:T(8,128)S(1)}, f32[512,64]{1,0:T(8,128)}, u32[]{:S(2)}) copy-start(f32[512,64]{1,0:T(8,128)} %copy-done.8) | copy-start | bytes 393220
  123.4 7.0 %copy-start.11 = (f32[512,64]{1,0:T(8,128)S(1)}, f32[512,64]{1,0:T(8,128)}, u32[]{:S(2)}) copy-start(f32[512,64]{1,0:T(8,128)} %copy-done.10) | copy-start | bytes 393220
  123.4 7.0 %copy-start.29 = (f32[128,128]{1,0:T(8,128)S(1)}, f32[128,128]{1,0:T(8,128)}, u32[]{:S(2)}) copy-start(f32[128,128]{1,0:T(8,128)} %copy-done.28) | copy-start | bytes 196612
  123.4 7.0 %copy-start.41 = (f32[64,128]{1,0:T(8,128)S(1)}, f32[64,128]{1,0:T(8,128)}, u32[]{:S(2)}) copy-start(f32[64,128]{1,0:T(8,128)} %copy-done.40) | copy-start | bytes 98308
  128.3 7.1 %copy-start.24 = (f32[128,128]{1,0:T(8,128)}, f32[128,128]{1,0:T(8,128)S(1)}, u32[]{:S(2)}) copy-start(f32[128,128]{1,0:T(8,128)S(1)} %get-tuple-element.56.refs_12_) | copy-start | bytes 196612
  129.7 39.1 %collective-permute-start.12 = (f32[192,128]{1,0:T(8,128)}, f32[192,128]{1,0:T(8,128)S(1)}, u32[]{:S(2)}, u32[]{:S(2)}) collective-permute-start(f32[192,128]{1,0:T(8,128)} %drift.6.refs_4_), channel_id=1, source_target_pairs={{0,1},{1,0},{2,3},{3,2},{4,5},{5,4},{6,7},{7,6},{8,9},{9,8},{10,11... | collective-permute-start | bytes 294920 | tf_op jit(solution)/shard_map/ppermute | solution.py:362
  129.7 50.3 %collective-permute-start.20 = (f32[192,128]{1,0:T(8,128)}, f32[192,128]{1,0:T(8,128)S(1)}, u32[]{:S(2)}, u32[]{:S(2)}) collective-permute-start(f32[192,128]{1,0:T(8,128)} %drift.7.refs_4_), channel_id=1, source_target_pairs={{0,3},{1,2},{2,1},{3,0},{4,7},{5,6},{6,5},{7,4},{8,11},{9,10},{10,... | collective-permute-start | bytes 294920 | tf_op jit(solution)/shard_map/ppermute | solution.py:362
  130.4 6.9 %copy-start.57 = (f32[8,3,512]{2,0,1:T(8,128)S(1)}, f32[8,3,512]{2,0,1:T(8,128)}, u32[]{:S(2)}) copy-start(f32[8,3,512]{2,0,1:T(8,128)} %param.7) | copy-start | bytes 147460
  130.4 39.6 %copy-start.27 = (f32[128,128]{1,0:T(8,128)S(1)}, f32[128,128]{1,0:T(8,128)}, u32[]{:S(2)}) copy-start(f32[128,128]{1,0:T(8,128)} %copy-done.26) | copy-start | bytes 196612
  135.4 39.9 %copy-start.34 = (f32[128,128]{1,0:T(8,128)}, f32[128,128]{1,0:T(8,128)S(1)}, u32[]{:S(2)}) copy-start(f32[128,128]{1,0:T(8,128)S(1)} %get-tuple-element.63.refs_1_) | copy-start | bytes 196612
  135.4 39.8 %copy-start.50 = (f32[8,128]{1,0:T(8,128)}, f32[8,128]{1,0:T(8,128)S(1)}, u32[]{:S(2)}) copy-start(f32[8,128]{1,0:T(8,128)S(1)} %get-tuple-element.43) | copy-start | bytes 12292
  135.4 34.6 %collective-permute-start.11 = (f32[64,128]{1,0:T(8,128)S(1)}, f32[64,128]{1,0:T(8,128)S(1)}, u32[]{:S(2)}, u32[]{:S(2)}) collective-permute-start(f32[64,128]{1,0:T(8,128)S(1)} %get-tuple-element.44.refs_0_), channel_id=1, source_target_pairs={{0,3},{1,2},{2,1},{3,0},{4,7},{5,6},{6,5},{7,4},{8,11},{9,10},{10,... | collective-permute-start | bytes 98312 | tf_op jit(solution)/shard_map/ppermute | solution.py:362
  136.6 33.3 %collective-permute-start.10 = (f32[64,128]{1,0:T(8,128)S(1)}, f32[64,128]{1,0:T(8,128)S(1)}, u32[]{:S(2)}, u32[]{:S(2)}) collective-permute-start(f32[64,128]{1,0:T(8,128)S(1)} %get-tuple-element.44.refs_0_), channel_id=1, source_target_pairs={{0,2},{1,3},{2,0},{3,1},{4,6},{5,7},{6,4},{7,5},{8,10},{9,11},{10,... | collective-permute-start | bytes 98312 | tf_op jit(solution)/shard_map/ppermute | solution.py:362
  137.2 32.8 %collective-permute-start.9 = (f32[64,128]{1,0:T(8,128)S(1)}, f32[64,128]{1,0:T(8,128)S(1)}, u32[]{:S(2)}, u32[]{:S(2)}) collective-permute-start(f32[64,128]{1,0:T(8,128)S(1)} %get-tuple-element.44.refs_0_), channel_id=1, source_target_pairs={{0,1},{1,0},{2,3},{3,2},{4,5},{5,4},{6,7},{7,6},{8,9},{9,8},{10,11... | collective-permute-start | bytes 98312 | tf_op jit(solution)/shard_map/ppermute | solution.py:362
  168.8 15.9 %collective-permute-start.19 = (f32[192,128]{1,0:T(8,128)}, f32[192,128]{1,0:T(8,128)}, u32[]{:S(2)}, u32[]{:S(2)}) collective-permute-start(f32[192,128]{1,0:T(8,128)} %drift.7.refs_4_), channel_id=1, source_target_pairs={{0,2},{1,3},{2,0},{3,1},{4,6},{5,7},{6,4},{7,5},{8,10},{9,11},{10,... | collective-permute-start | bytes 294920 | tf_op jit(solution)/shard_map/ppermute | solution.py:362
  170.0 14.8 %collective-permute-start.18 = (f32[192,128]{1,0:T(8,128)}, f32[192,128]{1,0:T(8,128)}, u32[]{:S(2)}, u32[]{:S(2)}) collective-permute-start(f32[192,128]{1,0:T(8,128)} %drift.7.refs_4_), channel_id=1, source_target_pairs={{0,1},{1,0},{2,3},{3,2},{4,5},{5,4},{6,7},{7,6},{8,9},{9,8},{10,11... | collective-permute-start | bytes 294920 | tf_op jit(solution)/shard_map/ppermute | solution.py:362
  170.0 10.6 %copy-start.62 = (s32[64]{0:T(128)S(1)}, s32[64]{0:T(128)}, u32[]{:S(2)}) copy-start(s32[64]{0:T(128)} %copy-done.61) | copy-start | bytes 772
  177.9 6.9 %collective-permute-start.17 = (f32[64,128]{1,0:T(8,128)}, f32[64,128]{1,0:T(8,128)}, u32[]{:S(2)}, u32[]{:S(2)}) collective-permute-start(f32[64,128]{1,0:T(8,128)} %get-tuple-element.51.refs_0_), channel_id=1, source_target_pairs={{0,3},{1,2},{2,1},{3,0},{4,7},{5,6},{6,5},{7,4},{8,11},{9,10},{10,... | collective-permute-start | bytes 98312 | tf_op jit(solution)/shard_map/ppermute | solution.py:362
  178.8 5.9 %collective-permute-start.16 = (f32[64,128]{1,0:T(8,128)}, f32[64,128]{1,0:T(8,128)}, u32[]{:S(2)}, u32[]{:S(2)}) collective-permute-start(f32[64,128]{1,0:T(8,128)} %get-tuple-element.51.refs_0_), channel_id=1, source_target_pairs={{0,2},{1,3},{2,0},{3,1},{4,6},{5,7},{6,4},{7,5},{8,10},{9,11},{10,... | collective-permute-start | bytes 98312 | tf_op jit(solution)/shard_map/ppermute | solution.py:362
  180.6 4.1 %collective-permute-start.15 = (f32[64,128]{1,0:T(8,128)}, f32[64,128]{1,0:T(8,128)}, u32[]{:S(2)}, u32[]{:S(2)}) collective-permute-start(f32[64,128]{1,0:T(8,128)} %get-tuple-element.51.refs_0_), channel_id=1, source_target_pairs={{0,1},{1,0},{2,3},{3,2},{4,5},{5,4},{6,7},{7,6},{8,9},{9,8},{10,11... | collective-permute-start | bytes 98312 | tf_op jit(solution)/shard_map/ppermute | solution.py:362
  202.9 4.3 %copy-start.67 = (pred[8]{0:T(512)(128)(4,1)S(1)}, pred[8]{0:T(512)(128)(4,1)}, u32[]{:S(2)}) copy-start(pred[8]{0:T(512)(128)(4,1)} %copy-done.66) | copy-start | bytes 28
  207.2 2.0 copy-start.35
  207.2 2.1 copy-start.37
  207.2 2.1 copy-start.39
  209.3 2.2 copy-start.58
  209.3 2.3 copy-start.51
  209.3 2.5 copy-start.45
  209.3 4.8 %copy-start.56 = (f32[8,3,512]{2,1,0:T(4,128)S(1)}, f32[8,3,512]{2,1,0:T(4,128)}, u32[]{:S(2)}) copy-start(f32[8,3,512]{2,1,0:T(4,128)} %gather_fusion.3) | copy-start | bytes 147460
  209.3 4.8 %copy-start.63 = (s32[64]{0:T(128)S(1)}, s32[64]{0:T(128)}, u32[]{:S(2)}) copy-start(s32[64]{0:T(128)} %copy-done.61) | copy-start | bytes 772
  209.4 4.8 %copy-start.65 = (pred[8]{0:T(512)(128)(4,1)S(1)}, pred[8]{0:T(512)(128)(4,1)}, u32[]{:S(2)}) copy-start(pred[8]{0:T(512)(128)(4,1)} %copy-done.64) | copy-start | bytes 28
  209.4 7.9 %copy-start.6 = (f32[512,128]{1,0:T(8,128)S(1)}, f32[512,128]{1,0:T(8,128)}, u32[]{:S(2)}) copy-start(f32[512,128]{1,0:T(8,128)} %copy-done.1) | copy-start | bytes 786436
  209.4 7.9 %copy-start.17 = (f32[512,64]{1,0:T(8,128)S(1)}, f32[512,64]{1,0:T(8,128)}, u32[]{:S(2)}) copy-start(f32[512,64]{1,0:T(8,128)} %copy-done.16) | copy-start | bytes 393220
  209.4 7.9 %copy-start.19 = (f32[512,64]{1,0:T(8,128)S(1)}, f32[512,64]{1,0:T(8,128)}, u32[]{:S(2)}) copy-start(f32[512,64]{1,0:T(8,128)} %copy-done.18) | copy-start | bytes 393220
  209.4 7.9 %copy-start.47 = (f32[64,128]{1,0:T(8,128)S(1)}, f32[64,128]{1,0:T(8,128)}, u32[]{:S(2)}) copy-start(f32[64,128]{1,0:T(8,128)} %copy-done.46) | copy-start | bytes 98308
  211.8 3.4 %collective-permute-start.23 = (f32[64,128]{1,0:T(8,128)S(1)}, f32[64,128]{1,0:T(8,128)S(1)}, u32[]{:S(2)}, u32[]{:S(2)}) collective-permute-start(f32[64,128]{1,0:T(8,128)S(1)} %copy-done.45), channel_id=1, source_target_pairs={{0,3},{1,2},{2,1},{3,0},{4,7},{5,6},{6,5},{7,4},{8,11},{9,10},{10,... | collective-permute-start | bytes 98312 | tf_op jit(solution)/shard_map/ppermute | solution.py:362
  212.8 3.9 %collective-permute-start.22 = (f32[64,128]{1,0:T(8,128)S(1)}, f32[64,128]{1,0:T(8,128)S(1)}, u32[]{:S(2)}, u32[]{:S(2)}) collective-permute-start(f32[64,128]{1,0:T(8,128)S(1)} %copy-done.45), channel_id=1, source_target_pairs={{0,2},{1,3},{2,0},{3,1},{4,6},{5,7},{6,4},{7,5},{8,10},{9,11},{10,... | collective-permute-start | bytes 98312 | tf_op jit(solution)/shard_map/ppermute | solution.py:362
  213.9 2.7 %collective-permute-start.21 = (f32[64,128]{1,0:T(8,128)S(1)}, f32[64,128]{1,0:T(8,128)S(1)}, u32[]{:S(2)}, u32[]{:S(2)}) collective-permute-start(f32[64,128]{1,0:T(8,128)S(1)} %copy-done.45), channel_id=1, source_target_pairs={{0,1},{1,0},{2,3},{3,2},{4,5},{5,4},{6,7},{7,6},{8,9},{9,8},{10,11... | collective-permute-start | bytes 98312 | tf_op jit(solution)/shard_map/ppermute | solution.py:362
  (32 other events, 24.8 us)
Sparse Core Ops, SparseCore 0:
  211.6 36.1 all-reduce.1

commit v2 on v1

v2 whole, which is shorter than its diff:
```python
import functools

import jax
import jax.numpy as jnp
from jax import lax
from jax.experimental import pallas as pl
from jax.experimental.pallas import tpu as pltpu
from jax.sharding import PartitionSpec as P

GRID = 24
PLANE = GRID * GRID
WIDE = 640
UNROLL = 4
K = 16
NMOVE = 4
MOVED = K * NMOVE
CAP = 1
TAU = 0.25
ROOT_TAU = 0.5
F32 = jnp.float32
BF16 = jnp.bfloat16
LEVELS = 32767.0
HIGHEST = lax.Precision.HIGHEST
VMEM = pl.BlockSpec(memory_space=pltpu.VMEM)
SMEM = pl.BlockSpec(memory_space=pltpu.SMEM)
LIMIT = 16 * 2**20


def axis_weights(u, with_slopes):
    floors = jnp.floor(u)
    t = u - floors
    remain = 1.0 - t
    square = t * t
    cubed = square * t
    values = (
        remain * remain * remain / 6.0,
        (3.0 * cubed - 6.0 * square + 4.0) / 6.0,
        (-3.0 * cubed + 3.0 * square + 3.0 * t + 1.0) / 6.0,
        cubed / 6.0,
    )
    lanes = u.shape[1]
    line = lax.broadcasted_iota(jnp.int32, (GRID, lanes), 0)
    step = line - (floors.astype(jnp.int32) - 1)
    step = jnp.where(step < 0, step + GRID, step)
    step = jnp.where(step < 0, step + GRID, step)
    step = jnp.where(step >= GRID, step - GRID, step)

    def spread(weights):
        out = jnp.zeros((GRID, lanes), F32)
        for a in range(4):
            out = jnp.where(step == a, jnp.broadcast_to(weights[a], (GRID, lanes)), out)
        return out

    if not with_slopes:
        return spread(values), None
    slopes = (
        -0.5 * remain * remain,
        1.5 * square - 2.0 * t,
        -1.5 * square + t + 0.5,
        0.5 * square,
    )
    return spread(values), spread(slopes)


def halves(first, second):
    product = jnp.concatenate([first[y : y + 1, :] * second for y in range(GRID)], axis=0)
    high = product.astype(BF16)
    return [high, (product - high.astype(F32)).astype(BF16)]


def fill(even_ref, odd_ref, pieces):
    lanes = pieces[0].shape[1]
    pad = jnp.zeros((WIDE - PLANE, lanes), BF16)
    for i, piece in enumerate(pieces):
        at = slice(i * lanes, (i + 1) * lanes)
        even_ref[0:PLANE, at] = piece
        even_ref[PLANE:WIDE, at] = pad
        odd_ref[0 : WIDE - PLANE, at] = pad
        odd_ref[WIDE - PLANE : WIDE, at] = piece


def plane_pair(table_ref, pair, even_ref, odd_ref):
    start = pl.multiple_of(pair * 2 * PLANE, 128)
    even = table_ref[:, pl.ds(start, WIDE)]
    start = pl.multiple_of(pair * 2 * PLANE + 2 * PLANE - WIDE, 128)
    odd = table_ref[:, pl.ds(start, WIDE)]
    return (
        jnp.dot(even, even_ref[...], preferred_element_type=F32),
        jnp.dot(odd, odd_ref[...], preferred_element_type=F32),
    )


def slopes_kernel(state_ref, table_ref, phi_ref, grad_ref, even_ref, odd_ref, wx_ref, sx_ref):
    n = state_ref.shape[1]
    wx, sx = axis_weights(state_ref[0:1, :], True)
    wy, sy = axis_weights(state_ref[1:2, :], True)
    wz, sz = axis_weights(state_ref[2:3, :], True)
    wx_ref[...] = wx
    sx_ref[...] = sx
    fill(even_ref, odd_ref, halves(wy, wz) + halves(sy, wz) + halves(wy, sz))
    phi_ref[...] = jnp.zeros_like(phi_ref)
    grad_ref[...] = jnp.zeros_like(grad_ref)

    def body(pair, carry):
        even, odd = plane_pair(table_ref, pair, even_ref, odd_ref)
        w0, w1 = wx_ref[pl.ds(2 * pair, 1), :], wx_ref[pl.ds(2 * pair + 1, 1), :]
        s0, s1 = sx_ref[pl.ds(2 * pair, 1), :], sx_ref[pl.ds(2 * pair + 1, 1), :]

        def both(i):
            at, to = slice(2 * i * n, (2 * i + 1) * n), slice((2 * i + 1) * n, (2 * i + 2) * n)
            return even[:, at] + even[:, to], odd[:, at] + odd[:, to]

        e, o = both(0)
        phi_ref[...] += w0 * e + w1 * o
        grad_ref[:, 0:n] += s0 * e + s1 * o
        for d in (1, 2):
            e, o = both(d)
            grad_ref[:, d * n : (d + 1) * n] += w0 * e + w1 * o
        return carry

    lax.fori_loop(0, GRID // 2, body, 0, unroll=UNROLL)


def slopes_call(state, table):
    orbitals = table.shape[0]
    n = state.shape[1]
    return pl.pallas_call(
        slopes_kernel,
        name="slopes",
        out_shape=(
            jax.ShapeDtypeStruct((orbitals, n), F32),
            jax.ShapeDtypeStruct((orbitals, 3 * n), F32),
        ),
        in_specs=[VMEM, VMEM],
        out_specs=(VMEM, VMEM),
        scratch_shapes=[
            pltpu.VMEM((WIDE, 6 * n), BF16),
            pltpu.VMEM((WIDE, 6 * n), BF16),
            pltpu.VMEM((GRID, n), F32),
            pltpu.VMEM((GRID, n), F32),
        ],
        compiler_params=pltpu.CompilerParams(vmem_limit_bytes=LIMIT),
    )(state, table)


def dot(a, b):
    return jnp.dot(a, b, precision=HIGHEST, preferred_element_type=F32)


def dot_nt(a, b):
    return lax.dot_general(
        a, b, (((1,), (1,)), ((), ())), precision=HIGHEST, preferred_element_type=F32
    )


def own_lanes(n, walker):
    lane = lax.broadcasted_iota(jnp.int32, (MOVED, n), 1)
    return jnp.logical_and(lane >= walker * K, lane < (walker + 1) * K)


def fold(big):
    n = big.shape[1]
    total = jnp.zeros((MOVED, n), F32)
    for w in range(n // K):
        total = jnp.where(own_lanes(n, w), big[w * MOVED : (w + 1) * MOVED, :], total)
    return total


def unit(block, n):
    row = lax.broadcasted_iota(jnp.int32, (MOVED, n), 0)
    lane = lax.broadcasted_iota(jnp.int32, (MOVED, n), 1)
    return jnp.where(row - block * K == lane % K, 1.0, 0.0).astype(F32)


def tree(parts):
    while len(parts) > 1:
        parts = [parts[i] + parts[i + 1] for i in range(0, len(parts), 2)]
    return parts[0]


def total(refs):
    return tree([ref[...] for ref in refs])


def params(limit=LIMIT):
    return pltpu.CompilerParams(vmem_limit_bytes=limit)


def parent_of(meta_ref, walkers, w):
    parent = meta_ref[w]
    group = parent // walkers
    here = group == meta_ref[walkers + NMOVE]
    return here, jnp.where(here, parent % walkers, 0), jnp.where(here, 0, group)


def block_lanes(x, block):
    lane = lax.broadcasted_iota(jnp.int32, x.shape, 1)
    kept = jnp.where(lane // K == block, x, 0.0)
    return tree([kept[:, i : i + 128] for i in range(0, x.shape[1], 128)])


def roll(x, shift):
    if isinstance(shift, int):
        shift = shift % 128
        return x if shift == 0 else pltpu.roll(x, shift, 1)
    return pltpu.roll(x, lax.rem(shift + 1024, 128), 1)


def pack_kernel(meta_ref, pos_ref, gauss_ref, acc_ref, out_ref):
    walkers = pos_ref.shape[0]
    half = jnp.zeros((3, MOVED), F32)
    lane = lax.broadcasted_iota(jnp.int32, (1, 128), 1)
    for w in range(walkers):
        line = jnp.concatenate([half, gauss_ref[w]], axis=1)
        for b in range(NMOVE):
            block = meta_ref[walkers + b]
            line = line + roll(block_lanes(pos_ref[w], block), (b - block) * K)
        decided = acc_ref[w : w + 1, :].astype(F32)
        decided = jnp.concatenate([decided, jnp.zeros((1, 128 - MOVED), F32)], axis=1)
        decided = jnp.where(lane < MOVED, decided, meta_ref[w].astype(F32))
        for g in range(out_ref.shape[0]):
            out_ref[g, 4 * w : 4 * w + 3, :] = line
            out_ref[g, 4 * w + 3 : 4 * w + 4, :] = decided


def pack_call(meta, positions, gaussian, accepted, groups):
    walkers = positions.shape[0]
    return pl.pallas_call(
        pack_kernel,
        name="pack",
        out_shape=jax.ShapeDtypeStruct((groups, 4 * walkers, 128), F32),
        in_specs=[SMEM, VMEM, VMEM, VMEM],
        out_specs=VMEM,
        compiler_params=params(),
    )(meta, positions, gaussian, accepted)


def columns_kernel(meta_ref, v_ref, pos_ref, out_ref, code_ref):
    walkers = meta_ref.shape[0] - NMOVE - 1
    v = v_ref[0]
    orbitals, electrons = v.shape
    row = lax.broadcasted_iota(jnp.int32, (K, electrons), 0)
    column = lax.broadcasted_iota(jnp.int32, (K, electrons), 1)
    chosen = jnp.concatenate(
        [
            jnp.where(column - meta_ref[walkers + b] * K == row, 1.0, 0.0).astype(F32)
            for b in range(NMOVE)
        ],
        axis=0,
    )
    out_ref[0, 0:MOVED, :] = dot_nt(chosen, v)
    size = jnp.abs(v)
    scale = jnp.max(size, axis=0, keepdims=True)
    at = MOVED
    for line in [scale] + [pos_ref[0, d : d + 1, :] for d in range(3)]:
        for i in range(0, electrons, orbitals):
            out_ref[0, at : at + 1, :] = line[:, i : i + orbitals]
            at += 1
    step = jnp.where(scale > 0.0, LEVELS / jnp.sqrt(jnp.where(scale > 0.0, scale, 1.0)), 0.0)
    level = jnp.minimum(jnp.floor(jnp.sqrt(size) * step + 0.5), LEVELS)
    code_ref[0] = jnp.where(v < 0.0, -level, level).astype(jnp.int32).astype(jnp.int16)


def payload_rows(orbitals, electrons):
    return MOVED + 4 * electrons // orbitals


def columns_call(meta, inverse, positions):
    walkers, orbitals, electrons = inverse.shape
    rows = payload_rows(orbitals, electrons)
    return pl.pallas_call(
        columns_kernel,
        name="columns",
        grid_spec=pltpu.PrefetchScalarGridSpec(
            num_scalar_prefetch=1,
            grid=(walkers,),
            in_specs=[
                pl.BlockSpec((1, orbitals, electrons), lambda w, m: (w, 0, 0)),
                pl.BlockSpec((1, 3, electrons), lambda w, m: (w, 0, 0)),
            ],
            out_specs=(
                pl.BlockSpec((1, rows, orbitals), lambda w, m: (w, 0, 0)),
                pl.BlockSpec((1, orbitals, electrons), lambda w, m: (w, 0, 0)),
            ),
        ),
        out_shape=(
            jax.ShapeDtypeStruct((walkers, rows, orbitals), F32),
            jax.ShapeDtypeStruct(inverse.shape, jnp.int16),
        ),
        compiler_params=params(),
    )(meta, inverse, positions)


def route_kernel(meta_ref, info_ref, own_ref, states_ref, out_ref, sending_ref):
    walkers = own_ref.shape[0]
    groups = out_ref.shape[0]
    me = meta_ref[walkers + NMOVE]
    lane = lax.broadcasted_iota(jnp.int32, (4, 128), 1)
    lines = [info_ref[pl.ds(4 * meta_ref[w], 4), :] for w in range(walkers)]
    for b in range(NMOVE):
        for half in range(2):
            total = jnp.zeros((4, 128), F32)
            for w in range(walkers):
                moved = roll(lines[w], (w - b) * K - half * MOVED)
                total = jnp.where(lane // K == w, moved, total)
            states_ref[b, 4 * half : 4 * half + 4, :] = total
    for g in range(groups):
        wanted = jnp.zeros((1, 128), jnp.int32)
        for s in range(walkers):
            row = 4 * (g * walkers + s) + 3
            parent = info_ref[row : row + 1, :].astype(jnp.int32)
            parent = jnp.where(lane[0:1] < MOVED, pltpu.roll(parent, 128 - MOVED, 1), parent)
            within = parent - me * walkers
            wanted = jnp.where(
                jnp.logical_and(within >= 0, within < walkers), within, wanted
            )
        wanted = jnp.where(me == g, 0, wanted)
        sending_ref[g : g + 1, :] = wanted
        picked = wanted[:, 0 : own_ref.shape[2]]
        total = own_ref[0]
        for w in range(1, walkers):
            total = jnp.where(picked == w, own_ref[w], total)
        out_ref[g] = total


def route_call(meta, info, own):
    walkers, rows, orbitals = own.shape
    groups = info.shape[0] // (4 * walkers)
    return pl.pallas_call(
        route_kernel,
        name="route",
        out_shape=(
            jax.ShapeDtypeStruct((NMOVE, 8, 128), F32),
            jax.ShapeDtypeStruct((groups, rows, orbitals), F32),
            jax.ShapeDtypeStruct((groups, 128), jnp.int32),
        ),
        in_specs=[SMEM, VMEM, VMEM],
        out_specs=(VMEM, VMEM, VMEM),
        compiler_params=params(),
    )(meta, info, own)


def select_kernel(meta_ref, own_ref, got_ref, grad_ref, vm_ref, out_ref):
    walkers = own_ref.shape[0]
    for w in range(walkers):
        here, place, group = parent_of(meta_ref, walkers, w)
        vm_ref[w * MOVED : (w + 1) * MOVED, :] = jnp.where(
            here, own_ref[place, 0:MOVED, :], got_ref[group, 0:MOVED, :]
        )
    n = grad_ref.shape[1] // 3
    for d in range(3):
        q = fold(dot(vm_ref[...], grad_ref[:, d * n : (d + 1) * n]))
        out_ref[d : d + 1, :] = jnp.sum(q * unit(0, n), axis=0, keepdims=True)
    out_ref[3:8, :] = jnp.zeros((5, n), F32)


def select_call(meta, own, got, grad):
    walkers, _, orbitals = own.shape
    n = grad.shape[1] // 3
    return pl.pallas_call(
        select_kernel,
        name="select",
        out_shape=(
            jax.ShapeDtypeStruct((walkers * MOVED, orbitals), F32),
            jax.ShapeDtypeStruct((8, n), F32),
        ),
        in_specs=[SMEM, VMEM, VMEM, VMEM],
        out_specs=(VMEM, VMEM),
        compiler_params=params(),
    )(meta, own, got, grad)


def drift_kernel(vm_ref, grad_ref, out_ref):
    n = grad_ref.shape[1] // 3
    rows = out_ref.shape[0] // 3
    for d in range(3):
        q = fold(dot(vm_ref[...], grad_ref[:, d * n : (d + 1) * n]))
        out_ref[d * rows : (d + 1) * rows, :] = q[0:rows, :]


def drift_call(block, vm, grad):
    n = grad.shape[1] // 3
    return pl.pallas_call(
        drift_kernel,
        name="drift",
        out_shape=jax.ShapeDtypeStruct((3 * (block + 1) * K, n), F32),
        in_specs=[VMEM, VMEM],
        out_specs=VMEM,
        compiler_params=params(),
    )(vm, grad)


def spread(x):
    n = x.shape[1]
    return jnp.concatenate([jnp.where(own_lanes(n, w), x, 0.0) for w in range(n // K)], axis=0)


def step_kernel(block, shards, *refs):
    refs = list(refs)
    s_parts = [refs.pop(0) for _ in range(shards)]
    if block:
        q_parts = [refs.pop(0) for _ in range(shards)]
        t_before = refs.pop(0)
    if block > 1:
        y_before = refs.pop(0)
    states_ref, phi_ref, vm_ref, table_ref = [refs.pop(0) for _ in range(4)]
    s_ref, moved_ref, d_ref, t_ref = [refs.pop(0) for _ in range(4)]
    y_ref = refs.pop(0) if block else None
    sum_ref, big_ref, even_ref, odd_ref, wx_ref = refs
    n = phi_ref.shape[1]
    state = states_ref[block]
    if block == 0:
        drifts = total(s_parts)[0:3, :]
        t_ref[...] = unit(0, n)
    else:
        s = total(s_parts)
        if block > 1:
            s_ref[...] = s
            big_ref[...] = dot(y_before[...], s_ref[...])
            s = s - fold(big_ref[...])
        s_ref[...] = s
        y_all = dot_nt(spread(s_ref[...]), t_before[...])
        if block > 1:
            y_all = y_all + y_before[...]
        y_ref[...] = y_all
        rows = jnp.concatenate(
            [
                y_ref[w * MOVED + block * K : w * MOVED + (block + 1) * K, :]
                for w in range(n // K)
            ],
            axis=0,
        )
        t_ref[...] = unit(block, n) - jnp.transpose(rows)
        t = t_ref[...]
        q = total(q_parts)
        size = q.shape[0] // 3
        drifts = jnp.concatenate(
            [
                jnp.sum(q[d * size : (d + 1) * size, :] * t[0:size, :], axis=0, keepdims=True)
                for d in range(3)
            ],
            axis=0,
        )
    speeds = jnp.sum(drifts * drifts, axis=0, keepdims=True)
    capped = drifts / jnp.sqrt(1.0 + TAU * speeds)
    moved = state[0:3, :] + state[3:4, :] * (TAU * capped + ROOT_TAU * state[4:7, :])
    moved_ref[0:3, :] = moved
    moved_ref[3:8, :] = jnp.zeros((5, n), F32)
    wx, _ = axis_weights(moved[0:1, :], False)
    wy, _ = axis_weights(moved[1:2, :], False)
    wz, _ = axis_weights(moved[2:3, :], False)
    wx_ref[...] = wx
    fill(even_ref, odd_ref, halves(wy, wz))
    sum_ref[...] = jnp.zeros_like(sum_ref)

    def body(pair, carry):
        even, odd = plane_pair(table_ref, pair, even_ref, odd_ref)
        w0, w1 = wx_ref[pl.ds(2 * pair, 1), :], wx_ref[pl.ds(2 * pair + 1, 1), :]
        sum_ref[...] += w0 * (even[:, 0:n] + even[:, n:]) + w1 * (odd[:, 0:n] + odd[:, n:])
        return carry

    lax.fori_loop(0, GRID // 2, body, 0, unroll=UNROLL)
    change = sum_ref[...] - phi_ref[...]
    d_ref[...] = jnp.transpose(change)
    s_ref[...] = fold(dot(vm_ref[...], change))


def step_call(block, s_parts, q_parts, carried, states, phi, vm, table):
    orbitals, n = phi.shape
    rows = vm.shape[0]
    operands = [*s_parts, *q_parts, *carried, states, phi, vm, table]
    shapes = [(MOVED, n), (8, n), (n, orbitals), (MOVED, n)] + [(rows, MOVED)] * (block > 0)
    return pl.pallas_call(
        functools.partial(step_kernel, block, len(s_parts)),
        name="step",
        out_shape=tuple(jax.ShapeDtypeStruct(shape, F32) for shape in shapes),
        in_specs=[VMEM] * len(operands),
        out_specs=(VMEM,) * len(shapes),
        scratch_shapes=[
            pltpu.VMEM((orbitals, n), F32),
            pltpu.VMEM((rows, n), F32),
            pltpu.VMEM((WIDE, 2 * n), BF16),
            pltpu.VMEM((WIDE, 2 * n), BF16),
            pltpu.VMEM((GRID, n), F32),
        ],
        compiler_params=params(),
    )(*operands)


def last_kernel(shards, *refs):
    l_all = None
    for block in range(NMOVE):
        t = refs[NMOVE * shards + block][...]
        r = unit(block, t.shape[1])
        if block:
            r = r - fold(dot(l_all, total(refs[block * shards : (block + 1) * shards])))
        more = dot_nt(spread(r), t)
        l_all = l_all + more if block else more
    vm_ref, out_ref = refs[NMOVE * (shards + 1) :]
    for w in range(out_ref.shape[0]):
        at = slice(w * MOVED, (w + 1) * MOVED)
        out_ref[w] = jnp.transpose(dot(l_all[at, :], vm_ref[at, :]))


def last_call(s_parts, ts, vm):
    rows, orbitals = vm.shape
    operands = [part for parts in s_parts for part in parts] + list(ts) + [vm]
    return pl.pallas_call(
        functools.partial(last_kernel, len(s_parts[0])),
        name="last",
        out_shape=jax.ShapeDtypeStruct((rows // MOVED, orbitals, MOVED), F32),
        in_specs=[VMEM] * len(operands),
        out_specs=VMEM,
        compiler_params=params(),
    )(*operands)


def assemble_kernel(meta_ref, own_ref, code_ref, got_ref, *refs):
    v_ref, out_ref = refs[NMOVE - 1 :]
    walkers = meta_ref.shape[0] - NMOVE - 1
    here, _, _ = parent_of(meta_ref, walkers, pl.program_id(0))
    _, orbitals, electrons = own_ref.shape
    scale = jnp.concatenate(
        [got_ref[0, MOVED + i : MOVED + i + 1, :] for i in range(electrons // orbitals)], axis=1
    )
    level = code_ref[0].astype(jnp.int32).astype(F32) * (1.0 / LEVELS)
    v = jnp.where(here, own_ref[0], level * jnp.abs(level) * scale)
    v_ref[0] = v
    change = jnp.concatenate([ref[...] for ref in refs[: NMOVE - 1]], axis=0)
    out_ref[0] = dot(change, v)


def assemble_call(meta, inverse, code, got, changes):
    walkers, orbitals, electrons = inverse.shape
    rows = got.shape[1]

    def near(w, m):
        return parent_of(m, walkers, w)[1], 0, 0

    def far(w, m):
        return parent_of(m, walkers, w)[2], 0, 0

    return pl.pallas_call(
        assemble_kernel,
        name="assemble",
        grid_spec=pltpu.PrefetchScalarGridSpec(
            num_scalar_prefetch=1,
            grid=(walkers,),
            in_specs=[
                pl.BlockSpec((1, orbitals, electrons), near),
                pl.BlockSpec((1, orbitals, electrons), far),
                pl.BlockSpec((1, rows, orbitals), far),
            ]
            + [pl.BlockSpec((K, orbitals), lambda w, m: (w, 0))] * (NMOVE - 1),
            out_specs=(
                pl.BlockSpec((1, orbitals, electrons), lambda w, m: (w, 0, 0)),
                pl.BlockSpec((1, (NMOVE - 1) * K, electrons), lambda w, m: (w, 0, 0)),
            ),
        ),
        out_shape=(
            jax.ShapeDtypeStruct(inverse.shape, F32),
            jax.ShapeDtypeStruct((walkers, (NMOVE - 1) * K, electrons), F32),
        ),
        compiler_params=params(),
    )(meta, inverse, code, got, *changes)


def sums_kernel(v_ref, change_ref, out_ref):
    out_ref[0] = dot(change_ref[...], v_ref[0])


def sums_call(inverse, change):
    walkers, orbitals, electrons = inverse.shape
    return pl.pallas_call(
        sums_kernel,
        name="sums",
        grid=(walkers,),
        out_shape=jax.ShapeDtypeStruct((walkers, K, electrons), F32),
        in_specs=[
            pl.BlockSpec((1, orbitals, electrons), lambda w: (w, 0, 0)),
            pl.BlockSpec((K, orbitals), lambda w: (w, 0)),
        ],
        out_specs=pl.BlockSpec((1, K, electrons), lambda w: (w, 0, 0)),
        compiler_params=params(),
    )(inverse, change)


def update_kernel(v_ref, factor_ref, first_ref, second_ref, out_ref):
    sums = jnp.concatenate([first_ref[0], second_ref[0]], axis=0)
    out_ref[0] = v_ref[0] - dot(factor_ref[0], sums)


def update_call(inverse, factor, first, second):
    walkers, orbitals, electrons = inverse.shape

    def per_walker(shape):
        return pl.BlockSpec((1, *shape[1:]), lambda w: (w, 0, 0))

    return pl.pallas_call(
        update_kernel,
        name="update",
        grid=(walkers,),
        out_shape=jax.ShapeDtypeStruct(inverse.shape, F32),
        in_specs=[per_walker(x.shape) for x in (inverse, factor, first, second)],
        out_specs=per_walker(inverse.shape),
        compiler_params=params(),
    )(inverse, factor, first, second)


def place_kernel(meta_ref, own_ref, got_ref, *refs):
    out_ref = refs[NMOVE]
    walkers, _, electrons = own_ref.shape
    width = got_ref.shape[2]
    parts = electrons // width
    lane = lax.broadcasted_iota(jnp.int32, (1, electrons), 1)
    for w in range(walkers):
        here, place, group = parent_of(meta_ref, walkers, w)
        lines = []
        for d in range(3):
            at = MOVED + (d + 1) * parts
            lines.append(
                jnp.concatenate(
                    [got_ref[group, at + i : at + i + 1, :] for i in range(parts)], axis=1
                )
            )
        line = jnp.where(here, own_ref[place], jnp.concatenate(lines, axis=0))
        for b in range(NMOVE):
            block = meta_ref[walkers + b]
            fresh = roll(refs[b][...], (block - w) * K)[0:3, :]
            fresh = jnp.concatenate([fresh] * (electrons // 128), axis=1)
            line = jnp.where(lane // K == block, fresh, line)
        out_ref[w] = line


def place_call(meta, positions, got, moved):
    return pl.pallas_call(
        place_kernel,
        name="place",
        out_shape=jax.ShapeDtypeStruct(positions.shape, F32),
        in_specs=[SMEM] + [VMEM] * (2 + NMOVE),
        out_specs=VMEM,
        compiler_params=params(),
    )(meta, positions, got, *moved)


def swap(x, axis, k):
    return lax.ppermute(x, axis, [(i, i ^ k) for i in range(lax.axis_size(axis))])


def exchange(part, axis):
    return [part] + [swap(part, axis, k) for k in range(1, lax.axis_size(axis))]


def add_up(part, axis):
    size = lax.axis_size(axis)
    half = part.shape[0] // 2
    low = lax.rem(lax.axis_index(axis), 2) == 0
    first, second = part[:half], part[half:]
    mine = jnp.where(low, first, second) + swap(jnp.where(low, second, first), axis, 1)
    k = 2
    while k < size:
        mine = mine + swap(mine, axis, k)
        k *= 2
    other = swap(mine, axis, 1)
    return jnp.concatenate([jnp.where(low, mine, other), jnp.where(low, other, mine)], axis=0)


def alltoall(x):
    return lax.all_to_all(x, "walker", split_axis=0, concat_axis=0, tiled=True)


def local(positions, inverse, spline_table, gaussian, accepted, block_order, parent):
    groups = lax.axis_size("walker")
    me = lax.axis_index("walker").astype(jnp.int32)
    meta = jnp.concatenate([parent, block_order[:NMOVE], me[None]])

    info = alltoall(pack_call(meta, positions, gaussian, accepted, groups))
    own, code = columns_call(meta, inverse, positions)
    states, outgoing, sending = route_call(meta, info.reshape(-1, 128), own)
    got = alltoall(outgoing)
    code = alltoall(code.at[sending[:, 0]].get(mode="promise_in_bounds"))

    evals = [slopes_call(states[b], spline_table) for b in range(NMOVE)]
    vm, first = select_call(meta, own, got, evals[0][1])
    s_parts = [exchange(first, "orb")]
    q_parts = [[]] + [
        exchange(drift_call(b, vm, evals[b][1]), "orb") for b in range(1, NMOVE)
    ]
    carried = []
    moved = []
    changes = []
    ts = []
    for b in range(NMOVE):
        s, new, change, t, *ys = step_call(
            b, s_parts[b], q_parts[b], carried, states, evals[b][0], vm, spline_table
        )
        carried = [t, *ys]
        ts.append(t)
        moved.append(new)
        changes.append(change)
        s_parts.append(exchange(s, "orb"))
        if b == NMOVE - 2:
            whole, sums = assemble_call(meta, inverse, code, got, changes)
            early = add_up(sums, "orb")
    late = add_up(sums_call(whole, changes[-1]), "orb")
    factor = last_call(s_parts[1:], ts, vm)
    return place_call(meta, positions, got, moved), update_call(whole, factor, early, late)


def solution(mesh):
    return jax.shard_map(
        local,
        mesh=mesh,
        in_specs=(
            P("walker", None, None),
            P("walker", "orb", None),
            P("orb", None),
            P("walker", None, None),
            P("walker", None),
            P(),
            P("walker"),
        ),
        out_specs=(P("walker", None, None), P("walker", "orb", None)),
        check_vma=False,
    )
```

time: 262 us -> 165 us (0.63)
  blocking collectives: 64.1 us -> 0 us
  other arithmetic: 19.9 us -> 1.97 us
  local copies, waits for them, and re-layouts: 45.3 us -> 27.5 us
  Pallas kernels: 50.3 us -> 65.3 us
  between operations: 14.7 us -> 1.23 us
  starting transfers between devices: 26.6 us -> 37.1 us
  matrix products: 4.69 us -> 0 us
  waiting for transfers between devices: 35 us -> 30.8 us
    all_gather x2 -> x0, blocking collectives: 64.1 us -> none  [the longest x1 32.6 us: local(): everyone = lax.all_gather(info, 'walker', axis=0, tiled=True)]
    psum x1 -> x0, waiting for transfers between devices: 28.4 us -> none  [local(): sums = lax.psum(sums_call(changes, whole), 'orb')]
    ppermute x24 -> x30, waiting for transfers between devices: 3.51 us -> 25 us  [swap(): lax.ppermute(x, axis, [(i, i ^ k) for i in range(lax.axis_size(axis))])]
    pallas_call x6 -> x11, Pallas kernels: 8.52 us -> 27.2 us  [the longest x1 6.21 us: assemble_call(): pl.pallas_call(assemble_kernel, name='assemble', grid_spec=pltpu.Prefetch...]
    gather x7 -> x1, local copies, waits for them, and re-layouts: 15.2 us -> 3.32 us  [local(): code = alltoall(code.at[sending[:, 0]].get(mode='promise_in_bounds'))]
    select_n x6 -> x5, other arithmetic: 8.42 us -> 0.3 us  [the longest x1 0.11 us: local(): code = alltoall(code.at[sending[:, 0]].get(mode='promise_in_bounds'))]
    all_to_all x2 -> x3, starting transfers between devices: 9.94 us -> 17.5 us  [alltoall(): return lax.all_to_all(x, 'walker', split_axis=0, concat_axis=0, tiled=True)]
    concatenate x3, other arithmetic: 7.38 us -> 0.87 us  [the longest x1 0.77 us: local(): meta = jnp.concatenate([parent, block_order[:NMOVE], me[None]])]
  transfers between devices with their start and end apart: 27 -> 33, of which waited for: 6 -> 12; matrix products, arithmetic and copies ran while one was open for 10% -> 3% of each run, Pallas kernels for 17% -> 31%
where the time goes in v2:
time: 165 us; the launch traced here: 164 us
  Pallas kernels  65.3 us (40%)
  starting transfers between devices  37.1 us (22%)
  waiting for transfers between devices  30.8 us (19%)
  local copies, waits for them, and re-layouts  27.5 us (17%)
  other arithmetic  1.97 us (1%)
    ppermute x30, waiting for transfers between devices, swap(): lax.ppermute(x, axis, [(i, i ^ k) for i in range(lax.axis_size(axis))])  25 us
    unnamed x115, local copies, waits for them, and re-layouts  23.6 us
    ppermute x30, starting transfers between devices, swap(): lax.ppermute(x, axis, [(i, i ^ k) for i in range(lax.axis_size(axis))])  19.5 us
    pallas_call x4, Pallas kernels, slopes_call(): pl.pallas_call(slopes_kernel, name='slopes', out_shape=(jax.ShapeDtypeStr...  19.4 us
    all_to_all x3, starting transfers between devices, alltoall(): return lax.all_to_all(x, 'walker', split_axis=0, concat_axis=0, tiled=True)  17.5 us
    pallas_call x4, Pallas kernels, step_call(): pl.pallas_call(functools.partial(step_kernel, block, len(s_parts)), name=...  14.1 us
    pallas_call x1, Pallas kernels, assemble_call(): pl.pallas_call(assemble_kernel, name='assemble', grid_spec=pltpu.Prefetch...  6.21 us
    all_to_all x3, waiting for transfers between devices, alltoall(): return lax.all_to_all(x, 'walker', split_axis=0, concat_axis=0, tiled=True)  5.78 us
  transfers between devices with their start and end apart: 33, of which 12 were waited for; matrix products, arithmetic and copies ran while one was open for 3% of the time, Pallas kernels for 31%

profile of v2, /device:TPU:0, one launch (start us, length us, event | category | flops | bytes accessed | tf_op | source)
XLA Modules:
  0.0 163.9 jit_solution(18166135430567716341)
XLA Ops:
  0.6 0.7 copy.15.gauss_ref
  1.3 0.8 copy.17.pos_ref.own_ref
  2.2 0.8 pad_add_fusion.meta_ref
  3.7 1.3 pack.1
  5.0 7.3 %all-to-all-start = ((f32[8,32,128]{2,1,0:T(8,128)}), f32[8,32,128]{2,1,0:T(8,128)}, u32[]{:S(2)}, u32[]{:S(2)}) async-start(f32[8,32,128]{2,1,0:T(8,128)} %pack.1), calls=%async_computation | async-start | bytes 262144 | tf_op jit(solution)/shard_map/all_to_all | solution.py:669
  12.3 1.6 copy-done.4
  13.9 0.8 copy-done.10
  14.7 5.2 %columns.1 = (f32[8,80,128]{2,1,0:T(8,128)S(1)}, s16[8,128,512]{2,1,0:T(8,128)(2,1)S(1)}) custom-call(s32[13]{0:T(128)S(1)} %pad_add_fusion.meta_ref, f32[8,128,512]{2,1,0:T(8,128)S(1)} %copy-done.4, f32[8,3,512]{2,1,0:T(4,128)S(1)} %copy-done.10), custom_call_target="tpu_custom_call" | custom-call | tf_op jit(solution)/shard_map/columns/pallas_call | solution.py:271
  19.9 1.0 copy-done.8
  21.5 1.9 %route.1 = (f32[4,8,128]{2,1,0:T(8,128)S(1)}, f32[8,80,128]{2,1,0:T(8,128)}, s32[8,128]{1,0:T(8,128)S(1)}) custom-call(s32[13]{0:T(128)S(1)} %copy-done.44, f32[256,128]{1,0:T(8,128)} %bitcast.1.info_ref, f32[8,80,128]{2,1,0:T(8,128)S(1)} %get-tuple-element.37.own_ref), custom_call_target="tpu_custom_call" | custom-call | tf_op jit(solution)/shard_map/route/pallas_call | solution.py:329
  23.4 6.0 %all-to-all-start.1 = ((f32[8,80,128]{2,1,0:T(8,128)}), f32[8,80,128]{2,1,0:T(8,128)}, u32[]{:S(2)}, u32[]{:S(2)}) async-start(f32[8,80,128]{2,1,0:T(8,128)} %get-tuple-element.38), calls=%async_computation.1 | async-start | bytes 655360 | tf_op jit(solution)/shard_map/all_to_all | solution.py:669
  30.1 3.3 %gather_fusion = s16[8,128,512]{2,1,0:T(8,128)(2,1)} fusion(s16[8,128,512]{2,1,0:T(8,128)(2,1)} %copy-done.8, s32[1024]{0:T(1024)} %pad_clamp_fusion), kind=kCustom, calls=%fused_computation | custom fusion | bytes 2097184 | tf_op jit(solution)/shard_map/gather | solution.py:681
  33.4 5.8 %all-to-all-done.1.got_ref = f32[8,80,128]{2,1,0:T(8,128)} async-done(((f32[8,80,128]{2,1,0:T(8,128)}), f32[8,80,128]{2,1,0:T(8,128)}, u32[]{:S(2)}, u32[]{:S(2)}) %all-to-all-start.1) | async-done | bytes 327712 | tf_op jit(solution)/shard_map/all_to_all | solution.py:669
  39.2 4.3 %all-to-all-start.2 = ((s16[8,128,512]{2,1,0:T(8,128)(2,1)}), s16[8,128,512]{2,1,0:T(8,128)(2,1)}, u32[]{:S(2)}, u32[]{:S(2)}) async-start(s16[8,128,512]{2,1,0:T(8,128)(2,1)} %gather_fusion), calls=%async_computation.2 | async-start | bytes 2097152 | tf_op jit(solution)/shard_map/all_to_all | solution.py:669
  44.1 4.8 %slopes.5 = (f32[128,128]{1,0:T(8,128)S(1)}, f32[128,384]{1,0:T(8,128)S(1)}) custom-call(f32[8,128]{1,0:T(8,128)S(1)} %get-tuple-element.82.state_ref, bf16[128,13824]{1,0:T(8,128)(2,1)S(1)} %copy-done), custom_call_target="tpu_custom_call" | custom-call | tf_op jit(solution)/shard_map/slopes/pallas_call | solution.py:127
  48.9 4.9 %slopes.4 = (f32[128,128]{1,0:T(8,128)S(1)}, f32[128,384]{1,0:T(8,128)S(1)}) custom-call(f32[8,128]{1,0:T(8,128)S(1)} %get-tuple-element.83.state_ref, bf16[128,13824]{1,0:T(8,128)(2,1)S(1)} %copy-done), custom_call_target="tpu_custom_call" | custom-call | tf_op jit(solution)/shard_map/slopes/pallas_call | solution.py:127
  53.8 1.7 %select.3 = (f32[512,128]{1,0:T(8,128)S(1)}, f32[8,128]{1,0:T(8,128)S(1)}) custom-call(s32[13]{0:T(128)S(1)} %copy-done.45, f32[8,80,128]{2,1,0:T(8,128)S(1)} %copy-done.7, f32[8,80,128]{2,1,0:T(8,128)} %all-to-all-done.1.got_ref, f32[128,384]{1,0:T(8,128)S(1)} %get-tuple-element.40.grad_ref), custom_call_target="tpu_custom_call" | custom-call | tf_op jit(solution)/shard_map/select/pallas_call | solution.py:360
  55.6 0.8 drift.3.refs_4_
  56.4 1.7 %collective-permute-start.2 = (f32[8,128]{1,0:T(8,128)S(1)}, f32[8,128]{1,0:T(8,128)S(1)}, u32[]{:S(2)}, u32[]{:S(2)}) collective-permute-start(f32[8,128]{1,0:T(8,128)S(1)} %get-tuple-element.41.refs_0_), channel_id=1, source_target_pairs={{0,3},{1,2},{2,1},{3,0},{4,7},{5,6},{6,5},{7,4},{8,11},{9,10},{10,... | collective-permute-start | bytes 12296 | tf_op jit(solution)/shard_map/ppermute | solution.py:647
  58.2 1.5 collective-permute-start.1
  59.7 0.8 collective-permute-done.2.refs_3_
  60.5 1.3 collective-permute-done.1.refs_2_
  61.8 2.4 %step.4 = (f32[64,128]{1,0:T(8,128)S(1)}, f32[8,128]{1,0:T(8,128)S(1)}, f32[128,128]{1,0:T(8,128)S(1)}, f32[64,128]{1,0:T(8,128)S(1)}) custom-call(f32[8,128]{1,0:T(8,128)S(1)} %get-tuple-element.41.refs_0_, f32[8,128]{1,0:T(8,128)S(1)} %collective-permute-done.refs_1_, f32[8,128]{1,0:T(8,128)S(1)} %collective-permute-done.1.refs_2_, ...), custom_call_target="tpu_custom_call" | custom-call | tf_op jit(solution)/shard_map/step/pallas_call | solution.py:473
  64.8 1.6 collective-permute-start.4
  66.7 4.9 %slopes.6 = (f32[128,128]{1,0:T(8,128)S(1)}, f32[128,384]{1,0:T(8,128)S(1)}) custom-call(f32[8,128]{1,0:T(8,128)S(1)} %get-tuple-element.81.state_ref, bf16[128,13824]{1,0:T(8,128)(2,1)S(1)} %copy-done), custom_call_target="tpu_custom_call" | custom-call | tf_op jit(solution)/shard_map/slopes/pallas_call | solution.py:127
  72.1 1.4 drift.4.refs_4_
  73.5 1.1 collective-permute-start.14
  74.6 0.8 collective-permute-start.7
  75.4 1.5 collective-permute-start.13
  76.9 2.8 %collective-permute-done.7.refs_6_ = f32[96,128]{1,0:T(8,128)S(1)} collective-permute-done((f32[96,128]{1,0:T(8,128)S(1)}, f32[96,128]{1,0:T(8,128)S(1)}, u32[]{:S(2)}, u32[]{:S(2)}) %collective-permute-start.7) | collective-permute-done | bytes 49184 | tf_op jit(solution)/shard_map/ppermute | solution.py:647
  79.7 3.5 %step.5 = (f32[64,128]{1,0:T(8,128)}, f32[8,128]{1,0:T(8,128)S(1)}, f32[128,128]{1,0:T(8,128)S(1)}, f32[64,128]{1,0:T(8,128)S(1)}, f32[512,64]{1,0:T(8,128)S(1)}) custom-call(f32[64,128]{1,0:T(8,128)S(1)} %get-tuple-element.45.refs_0_, f32[64,128]{1,0:T(8,128)S(1)} %collective-permute-done.3.refs_1_, f32[64,128]{1,0:T(8,128)S(1)} %collective-permute-done.4.refs_2_, ...), custom_call_target="tpu_custom_call" | custom-call | tf_op jit(solution)/shard_map/step/pallas_call | solution.py:473
  85.7 0.7 collective-permute-start.11
  88.2 1.4 collective-permute-done.11.refs_3_.refs_7_
  89.6 1.2 collective-permute-done.10.refs_2_.refs_6_
  90.8 0.9 copy-done.2
  91.7 0.9 copy-done.15
  92.7 0.8 copy-done.27
  93.5 0.9 copy-done.34
  94.3 0.8 copy-done.38
  95.2 4.5 %step.6 = (f32[64,128]{1,0:T(8,128)S(1)}, f32[8,128]{1,0:T(8,128)S(1)}, f32[128,128]{1,0:T(8,128)S(1)}, f32[64,128]{1,0:T(8,128)S(1)}, f32[512,64]{1,0:T(8,128)S(1)}) custom-call(f32[64,128]{1,0:T(8,128)} %get-tuple-element.50.refs_0_.refs_4_, f32[64,128]{1,0:T(8,128)} %collective-permute-done.9.refs_1_.refs_5_, ...), custom_call_target="tpu_custom_call" | custom-call | tf_op jit(solution)/shard_map/step/pallas_call | solution.py:473
  102.9 1.6 copy-done.5
  104.5 0.8 copy-done.36
  105.3 0.8 copy-done.40
  106.1 0.8 copy-done.42
  107.6 6.2 %assemble.1 = (f32[8,128,512]{2,1,0:T(8,128)S(1)}, f32[8,48,512]{2,1,0:T(8,128)S(1)}) custom-call(s32[13]{0:T(128)S(1)} %copy-done.46, f32[8,128,512]{2,1,0:T(8,128)S(1)} %copy-done.5, s16[8,128,512]{2,1,0:T(8,128)(2,1)} %all-to-all-done.2.code_ref, f32[8,80,128]{2,1,0:T(8,128)} %all-to-all-done.1.got_ref, f32[128,128]{1,0:T(8,128)S(1)} %copy-done.36, ...), custom_call_target="tpu_custom_call" | custom-call | tf_op jit(solution)/shard_map/assemble/pallas_call | solution.py:543
  114.0 4.8 %slopes.7 = (f32[128,128]{1,0:T(8,128)S(1)}, f32[128,384]{1,0:T(8,128)S(1)}) custom-call(f32[8,128]{1,0:T(8,128)S(1)} %copy-done.48, bf16[128,13824]{1,0:T(8,128)(2,1)S(1)} %copy-done), custom_call_target="tpu_custom_call" | custom-call | tf_op jit(solution)/shard_map/slopes/pallas_call | solution.py:127
  118.8 0.8 drift.5.refs_4_
  119.6 1.1 collective-permute-start.20
  120.7 1.1 collective-permute-start.19
  121.8 1.0 collective-permute-start.17
  122.8 1.3 collective-permute-done.20.refs_7_
  124.1 1.0 collective-permute-start.16
  125.2 2.0 %collective-permute-done.19.refs_6_ = f32[192,128]{1,0:T(8,128)S(1)} collective-permute-done((f32[192,128]{1,0:T(8,128)S(1)}, f32[192,128]{1,0:T(8,128)S(1)}, u32[]{:S(2)}, u32[]{:S(2)}) %collective-permute-start.19) | collective-permute-done | bytes 98336 | tf_op jit(solution)/shard_map/ppermute | solution.py:647
  127.2 1.1 collective-permute-done.16.refs_2_.refs_10_
  128.4 3.8 %step.7 = (f32[64,128]{1,0:T(8,128)S(1)}, f32[8,128]{1,0:T(8,128)S(1)}, f32[128,128]{1,0:T(8,128)S(1)}, f32[64,128]{1,0:T(8,128)S(1)}, f32[512,64]{1,0:T(8,128)}) custom-call(f32[64,128]{1,0:T(8,128)S(1)} %copy-done.30, f32[64,128]{1,0:T(8,128)S(1)} %collective-permute-done.15.refs_1_.refs_9_, f32[64,128]{1,0:T(8,128)S(1)} %collective-permute-done.16.refs_2_.refs_10_, ...), custom_call_target="tpu_custom_call" | custom-call | tf_op jit(solution)/shard_map/step/pallas_call | solution.py:473
  132.2 1.9 %sums.1 = f32[8,16,512]{2,1,0:T(8,128)S(1)} custom-call(f32[8,128,512]{2,1,0:T(8,128)S(1)} %get-tuple-element.67.v_ref, f32[128,128]{1,0:T(8,128)S(1)} %get-tuple-element.71.change_ref), custom_call_target="tpu_custom_call" | custom-call | tf_op jit(solution)/shard_map/sums/pallas_call | solution.py:574
  134.6 1.0 collective-permute-start.25
  135.7 1.1 collective-permute-start.28
  136.8 12.0 %collective-permute-done.28 = f32[4,16,512]{2,1,0:T(8,128)S(1)} collective-permute-done((f32[4,16,512]{2,1,0:T(8,128)S(1)}, f32[4,16,512]{2,1,0:T(8,128)S(1)}, u32[]{:S(2)}, u32[]{:S(2)}) %collective-permute-start.28) | collective-permute-done | bytes 131104 | tf_op jit(solution)/shard_map/ppermute | solution.py:647
  150.2 1.0 collective-permute-start.22
  151.5 1.2 place.1
  153.3 0.9 collective-permute-done.22.refs_14_
  154.2 4.8 %last.1.factor_ref = f32[8,128,64]{2,1,0:T(8,128)S(1)} custom-call(f32[64,128]{1,0:T(8,128)S(1)} %copy-done.17, f32[64,128]{1,0:T(8,128)S(1)} %copy-done.25, f32[64,128]{1,0:T(8,128)S(1)} %copy-done.23, f32[64,128]{1,0:T(8,128)S(1)} %copy-done.21, f32[64,128]{1,0:T(8,128)} %get-tuple-element.50.refs_0_.refs_4_, ...), custom_call_target="tpu_custom_call" | custom-call | tf_op jit(solution)/shard_map/last/pallas_call | solution.py:508
  159.3 4.6 %update.1 = f32[8,128,512]{2,1,0:T(8,128)} custom-call(f32[8,128,512]{2,1,0:T(8,128)S(1)} %get-tuple-element.67.v_ref, f32[8,128,64]{2,1,0:T(8,128)S(1)} %last.1.factor_ref, f32[8,48,512]{2,1,0:T(8,128)S(1)} %pad_maximum_fusion.first_ref, f32[8,16,512]{2,1,0:T(8,128)S(1)} %pad_maximum_fusion.1.second_ref), custom_call_target="tpu_custom_call" | custom-call | tf_op jit(solution)/shard_map/update/pallas_call | solution.py:599
  (152 shorter events, 15.4 us)
Async XLA Ops:
  2.2 2.8 %copy-start.9 = (f32[8,3,512]{2,1,0:T(4,128)}, f32[8,3,512]{2,1,0:T(4,128)S(1)}, u32[]{:S(2)}) copy-start(f32[8,3,512]{2,1,0:T(4,128)S(1)} %copy.17.pos_ref.own_ref) | copy-start | bytes 147460
  3.7 17.2 %copy-start.43 = (s32[13]{0:T(128)}, s32[13]{0:T(128)S(1)}, u32[]{:S(2)}) copy-start(s32[13]{0:T(128)S(1)} %pad_add_fusion.meta_ref) | copy-start | bytes 160
  5.0 15.9 %all-to-all-start = ((f32[8,32,128]{2,1,0:T(8,128)}), f32[8,32,128]{2,1,0:T(8,128)}, u32[]{:S(2)}, u32[]{:S(2)}) async-start(f32[8,32,128]{2,1,0:T(8,128)} %pack.1), calls=%async_computation | async-start | bytes 262144 | tf_op jit(solution)/shard_map/all_to_all | solution.py:669
  12.3 1.6 copy-start.4
  20.8 9.3 %copy-start.6 = (f32[8,80,128]{2,1,0:T(8,128)}, f32[8,80,128]{2,1,0:T(8,128)S(1)}, u32[]{:S(2)}) copy-start(f32[8,80,128]{2,1,0:T(8,128)S(1)} %get-tuple-element.37.own_ref) | copy-start | bytes 983044
  23.4 15.8 %all-to-all-start.1 = ((f32[8,80,128]{2,1,0:T(8,128)}), f32[8,80,128]{2,1,0:T(8,128)}, u32[]{:S(2)}, u32[]{:S(2)}) async-start(f32[8,80,128]{2,1,0:T(8,128)} %get-tuple-element.38), calls=%async_computation.1 | async-start | bytes 655360 | tf_op jit(solution)/shard_map/all_to_all | solution.py:669
  30.1 13.9 %copy-start = (bf16[128,13824]{1,0:T(8,128)(2,1)S(1)}, bf16[128,13824]{1,0:T(8,128)(2,1)}, u32[]{:S(2)}) copy-start(bf16[128,13824]{1,0:T(8,128)(2,1)} %refs_13_.3) | copy-start | bytes 10616836
  39.2 63.6 %all-to-all-start.2 = ((s16[8,128,512]{2,1,0:T(8,128)(2,1)}), s16[8,128,512]{2,1,0:T(8,128)(2,1)}, u32[]{:S(2)}, u32[]{:S(2)}) async-start(s16[8,128,512]{2,1,0:T(8,128)(2,1)} %gather_fusion), calls=%async_computation.2 | async-start | bytes 2097152 | tf_op jit(solution)/shard_map/all_to_all | solution.py:669
  48.9 4.9 %copy-start.7 = (f32[8,80,128]{2,1,0:T(8,128)S(1)}, f32[8,80,128]{2,1,0:T(8,128)}, u32[]{:S(2)}) copy-start(f32[8,80,128]{2,1,0:T(8,128)} %copy-done.6) | copy-start | bytes 983044
  48.9 4.9 %copy-start.45 = (s32[13]{0:T(128)S(1)}, s32[13]{0:T(128)}, u32[]{:S(2)}) copy-start(s32[13]{0:T(128)} %copy-done.43) | copy-start | bytes 160
  55.6 24.1 %copy-start.1 = (f32[512,128]{1,0:T(8,128)}, f32[512,128]{1,0:T(8,128)S(1)}, u32[]{:S(2)}) copy-start(f32[512,128]{1,0:T(8,128)S(1)} %get-tuple-element.43.refs_6_.vm_ref.refs_11_.refs_12_.refs_20_) | copy-start | bytes 786436
  56.4 20.6 %collective-permute-start.8 = (f32[96,128]{1,0:T(8,128)S(1)}, f32[96,128]{1,0:T(8,128)S(1)}, u32[]{:S(2)}, u32[]{:S(2)}) collective-permute-start(f32[96,128]{1,0:T(8,128)S(1)} %drift.3.refs_4_), channel_id=1, source_target_pairs={{0,3},{1,2},{2,1},{3,0},{4,7},{5,6},{6,5},{7,4},{8,11},{9,10},{10,... | collective-permute-start | bytes 147464 | tf_op jit(solution)/shard_map/ppermute | solution.py:647
  56.4 4.1 %collective-permute-start.2 = (f32[8,128]{1,0:T(8,128)S(1)}, f32[8,128]{1,0:T(8,128)S(1)}, u32[]{:S(2)}, u32[]{:S(2)}) collective-permute-start(f32[8,128]{1,0:T(8,128)S(1)} %get-tuple-element.41.refs_0_), channel_id=1, source_target_pairs={{0,3},{1,2},{2,1},{3,0},{4,7},{5,6},{6,5},{7,4},{8,11},{9,10},{10,... | collective-permute-start | bytes 12296 | tf_op jit(solution)/shard_map/ppermute | solution.py:647
  58.2 3.6 %collective-permute-start.1 = (f32[8,128]{1,0:T(8,128)S(1)}, f32[8,128]{1,0:T(8,128)S(1)}, u32[]{:S(2)}, u32[]{:S(2)}) collective-permute-start(f32[8,128]{1,0:T(8,128)S(1)} %get-tuple-element.41.refs_0_), channel_id=1, source_target_pairs={{0,2},{1,3},{2,0},{3,1},{4,6},{5,7},{6,4},{7,5},{8,10},{9,11},{10,... | collective-permute-start | bytes 12296 | tf_op jit(solution)/shard_map/ppermute | solution.py:647
  59.7 2.1 %collective-permute-start = (f32[8,128]{1,0:T(8,128)S(1)}, f32[8,128]{1,0:T(8,128)S(1)}, u32[]{:S(2)}, u32[]{:S(2)}) collective-permute-start(f32[8,128]{1,0:T(8,128)S(1)} %get-tuple-element.41.refs_0_), channel_id=1, source_target_pairs={{0,1},{1,0},{2,3},{3,2},{4,5},{5,4},{6,7},{7,6},{8,9},{9,8},{10,11... | collective-permute-start | bytes 12296 | tf_op jit(solution)/shard_map/ppermute | solution.py:647
  64.8 14.9 %copy-start.49 = (f32[8,128]{1,0:T(8,128)}, f32[8,128]{1,0:T(8,128)S(1)}, u32[]{:S(2)}) copy-start(f32[8,128]{1,0:T(8,128)S(1)} %get-tuple-element.44.refs_0_) | copy-start | bytes 12292
  64.8 18.4 %copy-start.16 = (f32[64,128]{1,0:T(8,128)}, f32[64,128]{1,0:T(8,128)S(1)}, u32[]{:S(2)}) copy-start(f32[64,128]{1,0:T(8,128)S(1)} %get-tuple-element.45.refs_0_) | copy-start | bytes 98308
  64.8 18.4 %copy-start.18 = (f32[64,128]{1,0:T(8,128)}, f32[64,128]{1,0:T(8,128)S(1)}, u32[]{:S(2)}) copy-start(f32[64,128]{1,0:T(8,128)S(1)} %get-tuple-element.47.refs_8_.refs_16_) | copy-start | bytes 98308
  64.8 9.8 %collective-permute-start.5 = (f32[64,128]{1,0:T(8,128)S(1)}, f32[64,128]{1,0:T(8,128)S(1)}, u32[]{:S(2)}, u32[]{:S(2)}) collective-permute-start(f32[64,128]{1,0:T(8,128)S(1)} %get-tuple-element.45.refs_0_), channel_id=1, source_target_pairs={{0,3},{1,2},{2,1},{3,0},{4,7},{5,6},{6,5},{7,4},{8,11},{9,10},{10,... | collective-permute-start | bytes 98312 | tf_op jit(solution)/shard_map/ppermute | solution.py:647
  64.8 10.6 %collective-permute-start.4 = (f32[64,128]{1,0:T(8,128)S(1)}, f32[64,128]{1,0:T(8,128)S(1)}, u32[]{:S(2)}, u32[]{:S(2)}) collective-permute-start(f32[64,128]{1,0:T(8,128)S(1)} %get-tuple-element.45.refs_0_), channel_id=1, source_target_pairs={{0,2},{1,3},{2,0},{3,1},{4,6},{5,7},{6,4},{7,5},{8,10},{9,11},{10,... | collective-permute-start | bytes 98312 | tf_op jit(solution)/shard_map/ppermute | solution.py:647
  66.4 9.0 %collective-permute-start.3 = (f32[64,128]{1,0:T(8,128)S(1)}, f32[64,128]{1,0:T(8,128)S(1)}, u32[]{:S(2)}, u32[]{:S(2)}) collective-permute-start(f32[64,128]{1,0:T(8,128)S(1)} %get-tuple-element.45.refs_0_), channel_id=1, source_target_pairs={{0,1},{1,0},{2,3},{3,2},{4,5},{5,4},{6,7},{7,6},{8,9},{9,8},{10,11... | collective-permute-start | bytes 98312 | tf_op jit(solution)/shard_map/ppermute | solution.py:647
  73.5 13.6 %collective-permute-start.14 = (f32[144,128]{1,0:T(8,128)}, f32[144,128]{1,0:T(8,128)S(1)}, u32[]{:S(2)}, u32[]{:S(2)}) collective-permute-start(f32[144,128]{1,0:T(8,128)} %drift.4.refs_4_), channel_id=1, source_target_pairs={{0,3},{1,2},{2,1},{3,0},{4,7},{5,6},{6,5},{7,4},{8,11},{9,10},{10,... | collective-permute-start | bytes 221192 | tf_op jit(solution)/shard_map/ppermute | solution.py:647
  74.6 8.5 %copy-start.20 = (f32[64,128]{1,0:T(8,128)}, f32[64,128]{1,0:T(8,128)S(1)}, u32[]{:S(2)}) copy-start(f32[64,128]{1,0:T(8,128)S(1)} %collective-permute-done.5.refs_3_) | copy-start | bytes 98308
  74.6 5.0 %collective-permute-start.7 = (f32[96,128]{1,0:T(8,128)S(1)}, f32[96,128]{1,0:T(8,128)S(1)}, u32[]{:S(2)}, u32[]{:S(2)}) collective-permute-start(f32[96,128]{1,0:T(8,128)S(1)} %drift.3.refs_4_), channel_id=1, source_target_pairs={{0,2},{1,3},{2,0},{3,1},{4,6},{5,7},{6,4},{7,5},{8,10},{9,11},{10,... | collective-permute-start | bytes 147464 | tf_op jit(solution)/shard_map/ppermute | solution.py:647
  75.4 7.8 %copy-start.22 = (f32[64,128]{1,0:T(8,128)}, f32[64,128]{1,0:T(8,128)S(1)}, u32[]{:S(2)}) copy-start(f32[64,128]{1,0:T(8,128)S(1)} %collective-permute-done.4.refs_2_) | copy-start | bytes 98308
  75.4 4.3 %collective-permute-start.6 = (f32[96,128]{1,0:T(8,128)S(1)}, f32[96,128]{1,0:T(8,128)S(1)}, u32[]{:S(2)}, u32[]{:S(2)}) collective-permute-start(f32[96,128]{1,0:T(8,128)S(1)} %drift.3.refs_4_), channel_id=1, source_target_pairs={{0,1},{1,0},{2,3},{3,2},{4,5},{5,4},{6,7},{7,6},{8,9},{9,8},{10,11... | collective-permute-start | bytes 147464 | tf_op jit(solution)/shard_map/ppermute | solution.py:647
  75.4 7.7 %copy-start.24 = (f32[64,128]{1,0:T(8,128)}, f32[64,128]{1,0:T(8,128)S(1)}, u32[]{:S(2)}) copy-start(f32[64,128]{1,0:T(8,128)S(1)} %collective-permute-done.3.refs_1_) | copy-start | bytes 98308
  75.4 12.8 %collective-permute-start.13 = (f32[144,128]{1,0:T(8,128)}, f32[144,128]{1,0:T(8,128)}, u32[]{:S(2)}, u32[]{:S(2)}) collective-permute-start(f32[144,128]{1,0:T(8,128)} %drift.4.refs_4_), channel_id=1, source_target_pairs={{0,2},{1,3},{2,0},{3,1},{4,6},{5,7},{6,4},{7,5},{8,10},{9,11},{10,... | collective-permute-start | bytes 221192 | tf_op jit(solution)/shard_map/ppermute | solution.py:647
  76.9 11.3 %collective-permute-start.12 = (f32[144,128]{1,0:T(8,128)}, f32[144,128]{1,0:T(8,128)}, u32[]{:S(2)}, u32[]{:S(2)}) collective-permute-start(f32[144,128]{1,0:T(8,128)} %drift.4.refs_4_), channel_id=1, source_target_pairs={{0,1},{1,0},{2,3},{3,2},{4,5},{5,4},{6,7},{7,6},{8,9},{9,8},{10,11... | collective-permute-start | bytes 221192 | tf_op jit(solution)/shard_map/ppermute | solution.py:647
  85.7 3.9 %collective-permute-start.11 = (f32[64,128]{1,0:T(8,128)}, f32[64,128]{1,0:T(8,128)}, u32[]{:S(2)}, u32[]{:S(2)}) collective-permute-start(f32[64,128]{1,0:T(8,128)} %get-tuple-element.50.refs_0_.refs_4_), channel_id=1, source_target_pairs={{0,3},{1,2},{2,1},{3,0},{4,7},{5,6},{6,5},{7,4},{8,11},{9,10},{10,... | collective-permute-start | bytes 98312 | tf_op jit(solution)/shard_map/ppermute | solution.py:647
  86.4 4.4 %collective-permute-start.10 = (f32[64,128]{1,0:T(8,128)}, f32[64,128]{1,0:T(8,128)}, u32[]{:S(2)}, u32[]{:S(2)}) collective-permute-start(f32[64,128]{1,0:T(8,128)} %get-tuple-element.50.refs_0_.refs_4_), channel_id=1, source_target_pairs={{0,2},{1,3},{2,0},{3,1},{4,6},{5,7},{6,4},{7,5},{8,10},{9,11},{10,... | collective-permute-start | bytes 98312 | tf_op jit(solution)/shard_map/ppermute | solution.py:647
  87.7 3.1 %collective-permute-start.9 = (f32[64,128]{1,0:T(8,128)}, f32[64,128]{1,0:T(8,128)}, u32[]{:S(2)}, u32[]{:S(2)}) collective-permute-start(f32[64,128]{1,0:T(8,128)} %get-tuple-element.50.refs_0_.refs_4_), channel_id=1, source_target_pairs={{0,1},{1,0},{2,3},{3,2},{4,5},{5,4},{6,7},{7,6},{8,9},{9,8},{10,11... | collective-permute-start | bytes 98312 | tf_op jit(solution)/shard_map/ppermute | solution.py:647
  102.9 1.6 copy-start.5
  107.6 6.4 %copy-start.48 = (f32[8,128]{1,0:T(8,128)S(1)}, f32[8,128]{1,0:T(8,128)}, u32[]{:S(2)}) copy-start(f32[8,128]{1,0:T(8,128)} %get-tuple-element.80.state_ref) | copy-start | bytes 12292
  113.8 5.0 %copy-start.3 = (f32[512,128]{1,0:T(8,128)S(1)}, f32[512,128]{1,0:T(8,128)}, u32[]{:S(2)}) copy-start(f32[512,128]{1,0:T(8,128)} %copy-done.1) | copy-start | bytes 786436
  113.9 7.9 %copy-start.30 = (f32[64,128]{1,0:T(8,128)S(1)}, f32[64,128]{1,0:T(8,128)}, u32[]{:S(2)}) copy-start(f32[64,128]{1,0:T(8,128)} %copy-done.29) | copy-start | bytes 98308
  113.9 14.5 %copy-start.13 = (f32[512,64]{1,0:T(8,128)S(1)}, f32[512,64]{1,0:T(8,128)}, u32[]{:S(2)}) copy-start(f32[512,64]{1,0:T(8,128)} %copy-done.12) | copy-start | bytes 393220
  113.9 14.5 %copy-start.32 = (f32[64,128]{1,0:T(8,128)S(1)}, f32[64,128]{1,0:T(8,128)}, u32[]{:S(2)}) copy-start(f32[64,128]{1,0:T(8,128)} %copy-done.31) | copy-start | bytes 98308
  113.9 20.6 %collective-permute-start.24 = (f32[4,48,512]{2,1,0:T(8,128)S(1)}, f32[4,48,512]{2,1,0:T(8,128)S(1)}, u32[]{:S(2)}, u32[]{:S(2)}) collective-permute-start(f32[4,48,512]{2,1,0:T(8,128)S(1)} %slice_select_fusion), channel_id=1, source_target_pairs={{0,1},{1,0},{2,3},{3,2},{4,5},{5,4},{6,7},{7,6},{8,9},{9,8},{10,11... | collective-permute-start | bytes 1179656 | tf_op jit(solution)/shard_map/ppermute | solution.py:647
  119.6 4.5 %collective-permute-start.20 = (f32[192,128]{1,0:T(8,128)S(1)}, f32[192,128]{1,0:T(8,128)S(1)}, u32[]{:S(2)}, u32[]{:S(2)}) collective-permute-start(f32[192,128]{1,0:T(8,128)S(1)} %drift.5.refs_4_), channel_id=1, source_target_pairs={{0,3},{1,2},{2,1},{3,0},{4,7},{5,6},{6,5},{7,4},{8,11},{9,10},{10,... | collective-permute-start | bytes 294920 | tf_op jit(solution)/shard_map/ppermute | solution.py:647
  120.7 6.5 %collective-permute-start.19 = (f32[192,128]{1,0:T(8,128)S(1)}, f32[192,128]{1,0:T(8,128)S(1)}, u32[]{:S(2)}, u32[]{:S(2)}) collective-permute-start(f32[192,128]{1,0:T(8,128)S(1)} %drift.5.refs_4_), channel_id=1, source_target_pairs={{0,2},{1,3},{2,0},{3,1},{4,6},{5,7},{6,4},{7,5},{8,10},{9,11},{10,... | collective-permute-start | bytes 294920 | tf_op jit(solution)/shard_map/ppermute | solution.py:647
  121.8 5.4 %collective-permute-start.18 = (f32[192,128]{1,0:T(8,128)S(1)}, f32[192,128]{1,0:T(8,128)S(1)}, u32[]{:S(2)}, u32[]{:S(2)}) collective-permute-start(f32[192,128]{1,0:T(8,128)S(1)} %drift.5.refs_4_), channel_id=1, source_target_pairs={{0,1},{1,0},{2,3},{3,2},{4,5},{5,4},{6,7},{7,6},{8,9},{9,8},{10,11... | collective-permute-start | bytes 294920 | tf_op jit(solution)/shard_map/ppermute | solution.py:647
  121.8 5.4 %collective-permute-start.17 = (f32[64,128]{1,0:T(8,128)S(1)}, f32[64,128]{1,0:T(8,128)S(1)}, u32[]{:S(2)}, u32[]{:S(2)}) collective-permute-start(f32[64,128]{1,0:T(8,128)S(1)} %copy-done.30), channel_id=1, source_target_pairs={{0,3},{1,2},{2,1},{3,0},{4,7},{5,6},{6,5},{7,4},{8,11},{9,10},{10,... | collective-permute-start | bytes 98312 | tf_op jit(solution)/shard_map/ppermute | solution.py:647
  124.1 4.2 %collective-permute-start.16 = (f32[64,128]{1,0:T(8,128)S(1)}, f32[64,128]{1,0:T(8,128)S(1)}, u32[]{:S(2)}, u32[]{:S(2)}) collective-permute-start(f32[64,128]{1,0:T(8,128)S(1)} %copy-done.30), channel_id=1, source_target_pairs={{0,2},{1,3},{2,0},{3,1},{4,6},{5,7},{6,4},{7,5},{8,10},{9,11},{10,... | collective-permute-start | bytes 98312 | tf_op jit(solution)/shard_map/ppermute | solution.py:647
  127.2 1.2 collective-permute-start.15
  134.1 17.3 %copy-start.11 = (f32[8,3,512]{2,1,0:T(4,128)S(1)}, f32[8,3,512]{2,1,0:T(4,128)}, u32[]{:S(2)}) copy-start(f32[8,3,512]{2,1,0:T(4,128)} %copy-done.9) | copy-start | bytes 147460
  134.1 17.3 %copy-start.47 = (s32[13]{0:T(128)S(1)}, s32[13]{0:T(128)}, u32[]{:S(2)}) copy-start(s32[13]{0:T(128)} %copy-done.43) | copy-start | bytes 160
  134.1 17.3 %copy-start.50 = (f32[8,128]{1,0:T(8,128)S(1)}, f32[8,128]{1,0:T(8,128)}, u32[]{:S(2)}) copy-start(f32[8,128]{1,0:T(8,128)} %copy-done.49) | copy-start | bytes 12292
  134.1 17.3 %copy-start.52 = (f32[8,128]{1,0:T(8,128)S(1)}, f32[8,128]{1,0:T(8,128)}, u32[]{:S(2)}) copy-start(f32[8,128]{1,0:T(8,128)} %copy-done.51) | copy-start | bytes 12292
  134.2 17.3 %copy-start.54 = (f32[8,128]{1,0:T(8,128)S(1)}, f32[8,128]{1,0:T(8,128)}, u32[]{:S(2)}) copy-start(f32[8,128]{1,0:T(8,128)} %copy-done.53) | copy-start | bytes 12292
  134.2 20.0 %copy-start.17 = (f32[64,128]{1,0:T(8,128)S(1)}, f32[64,128]{1,0:T(8,128)}, u32[]{:S(2)}) copy-start(f32[64,128]{1,0:T(8,128)} %copy-done.16) | copy-start | bytes 98308
  134.2 19.9 %copy-start.19 = (f32[64,128]{1,0:T(8,128)S(1)}, f32[64,128]{1,0:T(8,128)}, u32[]{:S(2)}) copy-start(f32[64,128]{1,0:T(8,128)} %copy-done.18) | copy-start | bytes 98308
  134.2 19.9 %copy-start.21 = (f32[64,128]{1,0:T(8,128)S(1)}, f32[64,128]{1,0:T(8,128)}, u32[]{:S(2)}) copy-start(f32[64,128]{1,0:T(8,128)} %copy-done.20) | copy-start | bytes 98308
  134.2 19.9 %copy-start.23 = (f32[64,128]{1,0:T(8,128)S(1)}, f32[64,128]{1,0:T(8,128)}, u32[]{:S(2)}) copy-start(f32[64,128]{1,0:T(8,128)} %copy-done.22) | copy-start | bytes 98308
  134.2 19.9 %copy-start.25 = (f32[64,128]{1,0:T(8,128)S(1)}, f32[64,128]{1,0:T(8,128)}, u32[]{:S(2)}) copy-start(f32[64,128]{1,0:T(8,128)} %copy-done.24) | copy-start | bytes 98308
  134.2 19.9 %copy-start.28 = (f32[64,128]{1,0:T(8,128)S(1)}, f32[64,128]{1,0:T(8,128)}, u32[]{:S(2)}) copy-start(f32[64,128]{1,0:T(8,128)} %copy-done.26) | copy-start | bytes 98308
  134.3 1.4 collective-permute-start.27
  134.6 14.3 %collective-permute-start.25 = (f32[4,48,512]{2,1,0:T(8,128)S(1)}, f32[4,48,512]{2,1,0:T(8,128)S(1)}, u32[]{:S(2)}, u32[]{:S(2)}) collective-permute-start(f32[4,48,512]{2,1,0:T(8,128)S(1)} %select_add_fusion), channel_id=1, source_target_pairs={{0,2},{1,3},{2,0},{3,1},{4,6},{5,7},{6,4},{7,5},{8,10},{9,11},{10,... | collective-permute-start | bytes 1179656 | tf_op jit(solution)/shard_map/ppermute | solution.py:647
  135.7 13.1 %collective-permute-start.28 = (f32[4,16,512]{2,1,0:T(8,128)S(1)}, f32[4,16,512]{2,1,0:T(8,128)S(1)}, u32[]{:S(2)}, u32[]{:S(2)}) collective-permute-start(f32[4,16,512]{2,1,0:T(8,128)S(1)} %select_add_fusion.1), channel_id=1, source_target_pairs={{0,2},{1,3},{2,0},{3,1},{4,6},{5,7},{6,4},{7,5},{8,10},{9,11},{10,... | collective-permute-start | bytes 393224 | tf_op jit(solution)/shard_map/ppermute | solution.py:647
  148.9 10.2 %collective-permute-start.29 = (f32[4,16,512]{2,1,0:T(8,128)S(1)}, f32[4,16,512]{2,1,0:T(8,128)S(1)}, u32[]{:S(2)}, u32[]{:S(2)}) collective-permute-start(f32[4,16,512]{2,1,0:T(8,128)S(1)} %add.20), channel_id=1, source_target_pairs={{0,1},{1,0},{2,3},{3,2},{4,5},{5,4},{6,7},{7,6},{8,9},{9,8},{10,11... | collective-permute-start | bytes 393224 | tf_op jit(solution)/shard_map/ppermute | solution.py:647
  149.0 10.1 %collective-permute-start.26 = (f32[4,48,512]{2,1,0:T(8,128)S(1)}, f32[4,48,512]{2,1,0:T(8,128)S(1)}, u32[]{:S(2)}, u32[]{:S(2)}) collective-permute-start(f32[4,48,512]{2,1,0:T(8,128)S(1)} %add.18), channel_id=1, source_target_pairs={{0,1},{1,0},{2,3},{3,2},{4,5},{5,4},{6,7},{7,6},{8,9},{9,8},{10,11... | collective-permute-start | bytes 1179656 | tf_op jit(solution)/shard_map/ppermute | solution.py:647
  149.6 3.7 %collective-permute-start.23 = (f32[64,128]{1,0:T(8,128)S(1)}, f32[64,128]{1,0:T(8,128)S(1)}, u32[]{:S(2)}, u32[]{:S(2)}) collective-permute-start(f32[64,128]{1,0:T(8,128)S(1)} %get-tuple-element.68.refs_12_), channel_id=1, source_target_pairs={{0,3},{1,2},{2,1},{3,0},{4,7},{5,6},{6,5},{7,4},{8,11},{9,10},{10,... | collective-permute-start | bytes 98312 | tf_op jit(solution)/shard_map/ppermute | solution.py:647
  150.2 3.9 %collective-permute-start.22 = (f32[64,128]{1,0:T(8,128)S(1)}, f32[64,128]{1,0:T(8,128)S(1)}, u32[]{:S(2)}, u32[]{:S(2)}) collective-permute-start(f32[64,128]{1,0:T(8,128)S(1)} %get-tuple-element.68.refs_12_), channel_id=1, source_target_pairs={{0,2},{1,3},{2,0},{3,1},{4,6},{5,7},{6,4},{7,5},{8,10},{9,11},{10,... | collective-permute-start | bytes 98312 | tf_op jit(solution)/shard_map/ppermute | solution.py:647
  151.3 2.9 %collective-permute-start.21 = (f32[64,128]{1,0:T(8,128)S(1)}, f32[64,128]{1,0:T(8,128)S(1)}, u32[]{:S(2)}, u32[]{:S(2)}) collective-permute-start(f32[64,128]{1,0:T(8,128)S(1)} %get-tuple-element.68.refs_12_), channel_id=1, source_target_pairs={{0,1},{1,0},{2,3},{3,2},{4,5},{5,4},{6,7},{7,6},{8,9},{9,8},{10,11... | collective-permute-start | bytes 98312 | tf_op jit(solution)/shard_map/ppermute | solution.py:647
  (25 other events, 18.2 us)

commit v3 on v2

v3 whole, which is shorter than its diff:
```python
import functools

import jax
import jax.numpy as jnp
from jax import lax
from jax.experimental import pallas as pl
from jax.experimental.pallas import tpu as pltpu
from jax.sharding import PartitionSpec as P

GRID = 24
PLANE = GRID * GRID
WIDE = 640
UNROLL = 12
K = 16
NMOVE = 4
MOVED = K * NMOVE
CAP = 1
TAU = 0.25
ROOT_TAU = 0.5
F32 = jnp.float32
BF16 = jnp.bfloat16
LEVELS = 32767.0
HIGHEST = lax.Precision.HIGHEST
VMEM = pl.BlockSpec(memory_space=pltpu.VMEM)
SMEM = pl.BlockSpec(memory_space=pltpu.SMEM)
ANY = pl.BlockSpec(memory_space=pl.ANY)
LIMIT = 16 * 2**20


def axis_weights(u, with_slopes):
    floors = jnp.floor(u)
    t = u - floors
    remain = 1.0 - t
    square = t * t
    cubed = square * t
    values = (
        remain * remain * remain / 6.0,
        (3.0 * cubed - 6.0 * square + 4.0) / 6.0,
        (-3.0 * cubed + 3.0 * square + 3.0 * t + 1.0) / 6.0,
        cubed / 6.0,
    )
    lanes = u.shape[1]
    line = lax.broadcasted_iota(jnp.int32, (GRID, lanes), 0)
    step = line - (floors.astype(jnp.int32) - 1)
    step = jnp.where(step < 0, step + GRID, step)
    step = jnp.where(step < 0, step + GRID, step)
    step = jnp.where(step >= GRID, step - GRID, step)

    def spread(weights):
        out = jnp.zeros((GRID, lanes), F32)
        for a in range(4):
            out = jnp.where(step == a, jnp.broadcast_to(weights[a], (GRID, lanes)), out)
        return out

    if not with_slopes:
        return spread(values), None
    slopes = (
        -0.5 * remain * remain,
        1.5 * square - 2.0 * t,
        -1.5 * square + t + 0.5,
        0.5 * square,
    )
    return spread(values), spread(slopes)


def halves(first, second):
    product = jnp.concatenate([first[y : y + 1, :] * second for y in range(GRID)], axis=0)
    high = product.astype(BF16)
    return [high, (product - high.astype(F32)).astype(BF16)]


def fill(even_ref, odd_ref, pieces):
    lanes = pieces[0].shape[1]
    pad = jnp.zeros((WIDE - PLANE, lanes), BF16)
    for i, piece in enumerate(pieces):
        at = slice(i * lanes, (i + 1) * lanes)
        even_ref[0:PLANE, at] = piece
        even_ref[PLANE:WIDE, at] = pad
        odd_ref[0 : WIDE - PLANE, at] = pad
        odd_ref[WIDE - PLANE : WIDE, at] = piece


def plane_pair(table_ref, pair, even_ref, odd_ref):
    start = pl.multiple_of(pair * 2 * PLANE, 128)
    even = table_ref[:, pl.ds(start, WIDE)]
    start = pl.multiple_of(pair * 2 * PLANE + 2 * PLANE - WIDE, 128)
    odd = table_ref[:, pl.ds(start, WIDE)]
    return (
        jnp.dot(even, even_ref[...], preferred_element_type=F32),
        jnp.dot(odd, odd_ref[...], preferred_element_type=F32),
    )


def slopes_kernel(state_ref, table_ref, phi_ref, grad_ref, even_ref, odd_ref, wx_ref, sx_ref):
    n = state_ref.shape[2]
    wx, sx = axis_weights(state_ref[0, 0:1, :], True)
    wy, sy = axis_weights(state_ref[0, 1:2, :], True)
    wz, sz = axis_weights(state_ref[0, 2:3, :], True)
    wx_ref[...] = wx
    sx_ref[...] = sx
    fill(even_ref, odd_ref, halves(wy, wz) + halves(sy, wz) + halves(wy, sz))
    phi_ref[...] = jnp.zeros_like(phi_ref)
    grad_ref[...] = jnp.zeros_like(grad_ref)

    def body(pair, carry):
        even, odd = plane_pair(table_ref, pair, even_ref, odd_ref)
        w0, w1 = wx_ref[pl.ds(2 * pair, 1), :], wx_ref[pl.ds(2 * pair + 1, 1), :]
        s0, s1 = sx_ref[pl.ds(2 * pair, 1), :], sx_ref[pl.ds(2 * pair + 1, 1), :]

        def both(i):
            at, to = slice(2 * i * n, (2 * i + 1) * n), slice((2 * i + 1) * n, (2 * i + 2) * n)
            return even[:, at] + even[:, to], odd[:, at] + odd[:, to]

        e, o = both(0)
        phi_ref[...] += w0 * e + w1 * o
        grad_ref[:, 0:n] += s0 * e + s1 * o
        for d in (1, 2):
            e, o = both(d)
            grad_ref[:, d * n : (d + 1) * n] += w0 * e + w1 * o
        return carry

    lax.fori_loop(0, GRID // 2, body, 0, unroll=UNROLL)


def slopes_call(states, table, blocks):
    orbitals = table.shape[0]
    n = states.shape[2]
    return pl.pallas_call(
        slopes_kernel,
        name="slopes",
        grid=(blocks,),
        out_shape=(
            jax.ShapeDtypeStruct((blocks * orbitals, n), F32),
            jax.ShapeDtypeStruct((blocks * orbitals, 3 * n), F32),
        ),
        in_specs=[pl.BlockSpec((1, 8, n), lambda b: (b, 0, 0)), VMEM],
        out_specs=(
            pl.BlockSpec((orbitals, n), lambda b: (b, 0)),
            pl.BlockSpec((orbitals, 3 * n), lambda b: (b, 0)),
        ),
        scratch_shapes=slopes_scratch(n),
        compiler_params=params(),
        cost_estimate=lasting(5 * blocks),
    )(states, table)


def slopes_scratch(n):
    return [
        pltpu.VMEM((WIDE, 6 * n), BF16),
        pltpu.VMEM((WIDE, 6 * n), BF16),
        pltpu.VMEM((GRID, n), F32),
        pltpu.VMEM((GRID, n), F32),
    ]


def later_kernel(block, states_ref, table_ref, vm_ref, phi_ref, q_ref, grad_ref, *scratch):
    slopes_kernel(states_ref.at[block : block + 1], table_ref, phi_ref, grad_ref, *scratch)
    drift_rows(block, vm_ref, grad_ref, q_ref, 0)


def later_call(block, states, table, vm):
    orbitals = table.shape[0]
    n = states.shape[2]
    return pl.pallas_call(
        functools.partial(later_kernel, block),
        name="later",
        out_shape=(
            jax.ShapeDtypeStruct((orbitals, n), F32),
            jax.ShapeDtypeStruct((drift_size(block), n), F32),
        ),
        in_specs=[VMEM] * 3,
        out_specs=(VMEM, VMEM),
        scratch_shapes=[pltpu.VMEM((orbitals, 3 * n), F32)] + slopes_scratch(n),
        compiler_params=params(),
        cost_estimate=lasting(6),
    )(states, table, vm)


def split(x):
    high = x.astype(BF16)
    return high, (x - high.astype(F32)).astype(BF16)


def product(a, b, dims):
    (a0, a1), (b0, b1) = split(a), split(b)

    def one(x, y):
        return lax.dot_general(x, y, (dims, ((), ())), preferred_element_type=F32)

    return one(a0, b0) + (one(a0, b1) + one(a1, b0))


def dot(a, b):
    return product(a, b, ((1,), (0,)))


def dot_nt(a, b):
    return product(a, b, ((1,), (1,)))


def own_lanes(n, walker):
    lane = lax.broadcasted_iota(jnp.int32, (MOVED, n), 1)
    return jnp.logical_and(lane >= walker * K, lane < (walker + 1) * K)


def fold(big):
    n = big.shape[1]
    total = jnp.zeros((MOVED, n), F32)
    for w in range(n // K):
        total = jnp.where(own_lanes(n, w), big[w * MOVED : (w + 1) * MOVED, :], total)
    return total


def unit(block, n):
    row = lax.broadcasted_iota(jnp.int32, (MOVED, n), 0)
    lane = lax.broadcasted_iota(jnp.int32, (MOVED, n), 1)
    return jnp.where(row - block * K == lane % K, 1.0, 0.0).astype(F32)


def tree(parts):
    while len(parts) > 1:
        parts = [parts[i] + parts[i + 1] for i in range(0, len(parts), 2)]
    return parts[0]


def total(refs):
    return tree([ref[...] for ref in refs])


def params():
    return pltpu.CompilerParams(vmem_limit_bytes=LIMIT)


def lasting(us):
    return pl.CostEstimate(flops=int(us * 1e9), bytes_accessed=0, transcendentals=0)


def parent_of(meta_ref, walkers, w):
    parent = meta_ref[w]
    group = parent // walkers
    here = group == meta_ref[walkers + NMOVE]
    return here, jnp.where(here, parent % walkers, 0), jnp.where(here, 0, group)


def block_lanes(x, block):
    lane = lax.broadcasted_iota(jnp.int32, x.shape, 1)
    kept = jnp.where(lane // K == block, x, 0.0)
    return tree([kept[:, i : i + 128] for i in range(0, x.shape[1], 128)])


def roll(x, shift):
    if isinstance(shift, int):
        shift = shift % 128
        return x if shift == 0 else pltpu.roll(x, shift, 1)
    return pltpu.roll(x, lax.rem(shift + 1024, 128), 1)


def moved_lanes(x, meta_ref, walkers):
    line = jnp.zeros((x.shape[0], 128), F32)
    for b in range(NMOVE):
        block = meta_ref[walkers + b]
        line = line + roll(block_lanes(x, block), (b - block) * K)
    return line


def pack_kernel(meta_ref, pos_ref, gauss_ref, acc_ref, out_ref):
    walkers = pos_ref.shape[1]
    half = jnp.zeros((walkers, 128 - MOVED), F32)
    lane = lax.broadcasted_iota(jnp.int32, (walkers, 128), 1)
    row = lax.broadcasted_iota(jnp.int32, (walkers, 128), 0)
    lines = []
    for d in range(3):
        line = moved_lanes(pos_ref[d], meta_ref, walkers)
        lines.append(line + jnp.concatenate([half, gauss_ref[d]], axis=1))
    parents = jnp.zeros((walkers, 128), jnp.int32)
    for w in range(walkers):
        parents = jnp.where(row == w, meta_ref[w], parents)
    decided = jnp.concatenate([acc_ref[...].astype(F32), half], axis=1)
    lines.append(jnp.where(lane < MOVED, decided, parents.astype(F32)))
    for g in range(out_ref.shape[0]):
        for d in range(4):
            out_ref[g, pl.ds(d, walkers, stride=4), :] = lines[d]


def pack_call(meta, positions, gaussian, accepted, groups):
    walkers = positions.shape[1]
    return pl.pallas_call(
        pack_kernel,
        name="pack",
        out_shape=jax.ShapeDtypeStruct((groups, 4 * walkers, 128), F32),
        in_specs=[SMEM, VMEM, VMEM, VMEM],
        out_specs=VMEM,
        compiler_params=params(),
        cost_estimate=lasting(1),
    )(meta, positions, gaussian, accepted)


def columns_kernel(meta_ref, v_ref, pos_ref, out_ref, code_ref):
    walkers = pos_ref.shape[1]
    v = v_ref[0]
    orbitals, electrons = v.shape
    out_ref[0, 0:MOVED, :] = jnp.transpose(moved_lanes(v, meta_ref, walkers))[0:MOVED, :]
    size = jnp.abs(v)
    scale = jnp.max(size, axis=0, keepdims=True)
    at = MOVED
    own = pl.ds(pl.program_id(0), 1)
    for line in [scale] + [pos_ref[d, own, :] for d in range(3)]:
        for i in range(0, electrons, orbitals):
            out_ref[0, at : at + 1, :] = line[:, i : i + orbitals]
            at += 1
    step = jnp.where(scale > 0.0, LEVELS / jnp.sqrt(jnp.where(scale > 0.0, scale, 1.0)), 0.0)
    level = jnp.minimum(jnp.floor(jnp.sqrt(size) * step + 0.5), LEVELS)
    code_ref[0] = jnp.where(v < 0.0, -level, level).astype(jnp.int32).astype(jnp.int16)


def payload_rows(orbitals, electrons):
    return MOVED + 4 * electrons // orbitals


def columns_call(meta, inverse, positions):
    walkers, orbitals, electrons = inverse.shape
    rows = payload_rows(orbitals, electrons)
    return pl.pallas_call(
        columns_kernel,
        name="columns",
        grid_spec=pltpu.PrefetchScalarGridSpec(
            num_scalar_prefetch=1,
            grid=(walkers,),
            in_specs=[
                pl.BlockSpec((1, orbitals, electrons), lambda w, m: (w, 0, 0)),
                pl.BlockSpec(positions.shape, lambda w, m: (0, 0, 0)),
            ],
            out_specs=(
                pl.BlockSpec((1, rows, orbitals), lambda w, m: (w, 0, 0)),
                pl.BlockSpec((1, orbitals, electrons), lambda w, m: (w, 0, 0)),
            ),
        ),
        out_shape=(
            jax.ShapeDtypeStruct((walkers, rows, orbitals), F32),
            jax.ShapeDtypeStruct(inverse.shape, jnp.int16),
        ),
        compiler_params=params(),
        cost_estimate=lasting(3),
    )(meta, inverse, positions)


def route_kernel(meta_ref, info_ref, own_ref, states_ref, out_ref, sending_ref):
    walkers = own_ref.shape[0]
    groups = out_ref.shape[0]
    me = meta_ref[walkers + NMOVE]
    lane = lax.broadcasted_iota(jnp.int32, (8, 128), 1)
    tiles = []
    for w in range(walkers):
        line = info_ref[pl.ds(4 * meta_ref[w], 4), :]
        tiles.append(jnp.concatenate([line, roll(line, 128 - MOVED)], axis=0))
    for b in range(NMOVE):
        state = jnp.zeros((8, 128), F32)
        for w in range(walkers):
            state = jnp.where(lane // K == w, roll(tiles[w], (w - b) * K), state)
        states_ref[b] = state
    for g in range(groups):
        wanted = jnp.zeros((1, 128), jnp.int32)
        for s in range(walkers):
            row = 4 * (g * walkers + s) + 3
            parent = info_ref[row : row + 1, :].astype(jnp.int32)
            parent = jnp.where(lane[0:1] < MOVED, pltpu.roll(parent, 128 - MOVED, 1), parent)
            within = parent - me * walkers
            wanted = jnp.where(
                jnp.logical_and(within >= 0, within < walkers), within, wanted
            )
        wanted = jnp.where(me == g, 0, wanted)
        sending_ref[g : g + 1, :] = wanted
        picked = wanted[:, 0 : own_ref.shape[2]]
        total = own_ref[0]
        for w in range(1, walkers):
            total = jnp.where(picked == w, own_ref[w], total)
        out_ref[g] = total


def route_call(meta, info, own):
    walkers, rows, orbitals = own.shape
    groups = info.shape[0] // (4 * walkers)
    return pl.pallas_call(
        route_kernel,
        name="route",
        out_shape=(
            jax.ShapeDtypeStruct((NMOVE, 8, 128), F32),
            jax.ShapeDtypeStruct((groups, rows, orbitals), F32),
            jax.ShapeDtypeStruct((groups, 128), jnp.int32),
        ),
        in_specs=[SMEM, VMEM, VMEM],
        out_specs=(VMEM, VMEM, VMEM),
        compiler_params=params(),
        cost_estimate=lasting(2),
    )(meta, info, own)


def outcode_kernel(meta_ref, sending_ref, code_ref, *refs):
    out_refs, sem = refs[:-1], refs[-1]
    me = meta_ref[meta_ref.shape[0] - 2]
    copies = []
    for k, out_ref in enumerate(out_refs, start=1):
        source = sending_ref[jnp.bitwise_xor(me, k), 0]
        copies.append(pltpu.make_async_copy(code_ref.at[source], out_ref, sem.at[k - 1]))
    for copy in copies:
        copy.start()
    for copy in copies:
        copy.wait()


def outcode_call(meta, sending, code):
    others = sending.shape[0] - 1
    return pl.pallas_call(
        outcode_kernel,
        name="outcode",
        out_shape=tuple(jax.ShapeDtypeStruct(code.shape[1:], code.dtype) for _ in range(others)),
        in_specs=[SMEM, SMEM, ANY],
        out_specs=(ANY,) * others,
        scratch_shapes=[pltpu.SemaphoreType.DMA((others,))],
        compiler_params=params(),
        cost_estimate=lasting(1),
    )(meta, sending, code)


def select_kernel(meta_ref, own_ref, got_ref, grad_ref, vm_ref, out_ref):
    walkers = own_ref.shape[0]
    for w in range(walkers):
        here, place, group = parent_of(meta_ref, walkers, w)
        vm_ref[w * MOVED : (w + 1) * MOVED, :] = jnp.where(
            here, own_ref[place, 0:MOVED, :], got_ref[group, 0:MOVED, :]
        )
    orbitals = own_ref.shape[2]
    drift_rows(0, vm_ref, grad_ref.at[0:orbitals], out_ref, 0)
    drift_rows(1, vm_ref, grad_ref.at[orbitals:], out_ref, drift_size(0))


def drift_size(block):
    return 8 + 3 * K * block


def drift_rows(block, vm_ref, grad_ref, out_ref, at):
    n = grad_ref.shape[1] // 3
    size = K * block
    out_ref[at + 3 : at + 8, :] = jnp.zeros((5, n), F32)
    for d in range(3):
        q = fold(dot(vm_ref[...], grad_ref[:, d * n : (d + 1) * n]))
        out_ref[at + d : at + d + 1, :] = jnp.sum(q * unit(block, n), axis=0, keepdims=True)
        if block:
            out_ref[at + 8 + d * size : at + 8 + (d + 1) * size, :] = q[0:size, :]


def drift_of(block, q, t):
    size = K * block
    lines = [q[0:3, :]]
    if block:
        lines[0] += jnp.concatenate(
            [
                jnp.sum(q[8 + d * size : 8 + (d + 1) * size, :] * t[0:size, :], axis=0)[None]
                for d in range(3)
            ],
            axis=0,
        )
    return lines[0]


def select_call(meta, own, got, grad):
    walkers, _, orbitals = own.shape
    n = grad.shape[1] // 3
    return pl.pallas_call(
        select_kernel,
        name="select",
        out_shape=(
            jax.ShapeDtypeStruct((walkers * MOVED, orbitals), F32),
            jax.ShapeDtypeStruct((drift_size(0) + drift_size(1), n), F32),
        ),
        in_specs=[SMEM, VMEM, VMEM, VMEM],
        out_specs=(VMEM, VMEM),
        compiler_params=params(),
        cost_estimate=lasting(2),
    )(meta, own, got, grad)


def spread(x):
    n = x.shape[1]
    return jnp.concatenate([jnp.where(own_lanes(n, w), x, 0.0) for w in range(n // K)], axis=0)


def step_kernel(block, shards, *refs):
    refs = list(refs)
    first_parts = [refs.pop(0) for _ in range(shards)] if block < 2 else []
    if block:
        s_parts = [refs.pop(0) for _ in range(shards)]
        t_before = refs.pop(0)
    if block > 1:
        q_parts = [refs.pop(0) for _ in range(shards)]
        y_before = refs.pop(0)
    states_ref, phi_ref, vm_ref, table_ref = [refs.pop(0) for _ in range(4)]
    s_ref, moved_ref, d_ref, t_ref = [refs.pop(0) for _ in range(4)]
    y_ref = refs.pop(0) if block else None
    sum_ref, big_ref, even_ref, odd_ref, wx_ref = refs
    orbitals, n = sum_ref.shape
    state = states_ref[block]
    if block == 0:
        t_ref[...] = unit(0, n)
        drifts = drift_of(0, tree([ref[0:8, :] for ref in first_parts]), None)
    else:
        s = total(s_parts)
        if block > 1:
            s_ref[...] = s
            big_ref[...] = dot(y_before[...], s_ref[...])
            s = s - fold(big_ref[...])
        s_ref[...] = s
        y_all = dot_nt(spread(s_ref[...]), t_before[...])
        if block > 1:
            y_all = y_all + y_before[...]
        y_ref[...] = y_all
        rows = jnp.concatenate(
            [
                y_ref[w * MOVED + block * K : w * MOVED + (block + 1) * K, :]
                for w in range(n // K)
            ],
            axis=0,
        )
        t_ref[...] = unit(block, n) - jnp.transpose(rows)
        if block == 1:
            q = tree([ref[drift_size(0) :, :] for ref in first_parts])
        else:
            q = total(q_parts)
        drifts = drift_of(block, q, t_ref[...])
    speeds = jnp.sum(drifts * drifts, axis=0, keepdims=True)
    capped = drifts / jnp.sqrt(1.0 + TAU * speeds)
    moved = state[0:3, :] + state[3:4, :] * (TAU * capped + ROOT_TAU * state[4:7, :])
    moved_ref[0:3, :] = moved
    moved_ref[3:8, :] = jnp.zeros((5, n), F32)
    wx, _ = axis_weights(moved[0:1, :], False)
    wy, _ = axis_weights(moved[1:2, :], False)
    wz, _ = axis_weights(moved[2:3, :], False)
    wx_ref[...] = wx
    fill(even_ref, odd_ref, halves(wy, wz))
    sum_ref[...] = jnp.zeros_like(sum_ref)

    def body(pair, carry):
        even, odd = plane_pair(table_ref, pair, even_ref, odd_ref)
        w0, w1 = wx_ref[pl.ds(2 * pair, 1), :], wx_ref[pl.ds(2 * pair + 1, 1), :]
        sum_ref[...] += w0 * (even[:, 0:n] + even[:, n:]) + w1 * (odd[:, 0:n] + odd[:, n:])
        return carry

    lax.fori_loop(0, GRID // 2, body, 0, unroll=UNROLL)
    at = block * orbitals if block < 2 else 0
    change = sum_ref[...] - phi_ref[at : at + orbitals, :]
    d_ref[...] = jnp.transpose(change)
    s_ref[...] = fold(dot(vm_ref[...], change))


def step_call(block, operands, states, phi, vm, table):
    orbitals, n = table.shape[0], states.shape[2]
    shards = lax.axis_size("orb")
    rows = vm.shape[0]
    operands = [*operands, states, phi, vm, table]
    shapes = [(MOVED, n), (8, n), (n, orbitals), (MOVED, n)] + [(rows, MOVED)] * (block > 0)
    return pl.pallas_call(
        functools.partial(step_kernel, block, shards),
        name="step",
        out_shape=tuple(jax.ShapeDtypeStruct(shape, F32) for shape in shapes),
        in_specs=[VMEM] * len(operands),
        out_specs=(VMEM,) * len(shapes),
        scratch_shapes=[
            pltpu.VMEM((orbitals, n), F32),
            pltpu.VMEM((rows, n), F32),
            pltpu.VMEM((WIDE, 2 * n), BF16),
            pltpu.VMEM((WIDE, 2 * n), BF16),
            pltpu.VMEM((GRID, n), F32),
        ],
        compiler_params=params(),
        cost_estimate=lasting(4),
    )(*operands)


def last_kernel(shards, *refs):
    l_all = None
    for block in range(NMOVE):
        t = refs[NMOVE * shards + block][...]
        r = unit(block, t.shape[1])
        if block:
            r = r - fold(dot(l_all, total(refs[block * shards : (block + 1) * shards])))
        more = dot_nt(spread(r), t)
        l_all = l_all + more if block else more
    vm_ref, out_ref = refs[NMOVE * (shards + 1) :]
    for w in range(out_ref.shape[0]):
        at = slice(w * MOVED, (w + 1) * MOVED)
        out_ref[w] = jnp.transpose(dot(l_all[at, :], vm_ref[at, :]))


def last_call(s_parts, ts, vm):
    rows, orbitals = vm.shape
    operands = [part for parts in s_parts for part in parts] + list(ts) + [vm]
    return pl.pallas_call(
        functools.partial(last_kernel, len(s_parts[0])),
        name="last",
        out_shape=jax.ShapeDtypeStruct((rows // MOVED, orbitals, MOVED), F32),
        in_specs=[VMEM] * len(operands),
        out_specs=VMEM,
        compiler_params=params(),
        cost_estimate=lasting(3),
    )(*operands)


def both_halves(meta_ref, walkers, i):
    parity = meta_ref[meta_ref.shape[0] - 1]
    half = walkers // 2
    return i + half * parity, i + half * (1 - parity)


def assemble_kernel(others, meta_ref, own_ref, got_ref, *refs):
    code_refs, change_refs = refs[:others], refs[others : others + NMOVE - 1]
    v_ref, mine_ref, give_ref, held_ref, sem = refs[others + NMOVE - 1 :]
    walkers, orbitals, electrons = own_ref.shape
    me = meta_ref[walkers + NMOVE]
    copies = [
        pltpu.make_async_copy(ref, held_ref.at[k], sem.at[k]) for k, ref in enumerate(code_refs)
    ]
    for copy in copies:
        copy.start()
    for copy in copies:
        copy.wait()

    def body(i, carry):
        for w, out_ref in zip(both_halves(meta_ref, walkers, i), (mine_ref, give_ref)):
            here, place, group = parent_of(meta_ref, walkers, w)
            scale = jnp.concatenate(
                [
                    got_ref[group, MOVED + j : MOVED + j + 1, :]
                    for j in range(electrons // orbitals)
                ],
                axis=1,
            )
            slot = jnp.where(here, 0, jnp.bitwise_xor(group, me) - 1)
            level = held_ref[slot].astype(jnp.int32).astype(F32) * (1.0 / LEVELS)
            v = jnp.where(here, own_ref[place], level * jnp.abs(level) * scale)
            v_ref[w] = v
            at = pl.ds(pl.multiple_of(w * K, K), K)
            change = jnp.concatenate([ref[at, :] for ref in change_refs], axis=0)
            out_ref[i] = dot(change, v)
        return carry

    lax.fori_loop(0, walkers // 2, body, 0)


def assemble_call(meta, inverse, got, codes, changes):
    walkers, orbitals, electrons = inverse.shape
    half = (walkers // 2, (NMOVE - 1) * K, electrons)
    return pl.pallas_call(
        functools.partial(assemble_kernel, len(codes)),
        name="assemble",
        out_shape=(
            jax.ShapeDtypeStruct(inverse.shape, F32),
            jax.ShapeDtypeStruct(half, F32),
            jax.ShapeDtypeStruct(half, F32),
        ),
        in_specs=[SMEM, VMEM, VMEM] + [ANY] * len(codes) + [VMEM] * len(changes),
        out_specs=(VMEM,) * 3,
        scratch_shapes=[
            pltpu.VMEM((len(codes), orbitals, electrons), jnp.int16),
            pltpu.SemaphoreType.DMA((len(codes),)),
        ],
        compiler_params=params(),
        cost_estimate=lasting(4),
    )(meta, inverse, got, *codes, *changes)


def sums_kernel(meta_ref, v_ref, change_ref, mine_ref, give_ref):
    walkers = v_ref.shape[0]

    def body(i, carry):
        for w, out_ref in zip(both_halves(meta_ref, walkers, i), (mine_ref, give_ref)):
            at = pl.ds(pl.multiple_of(w * K, K), K)
            out_ref[i] = dot(change_ref[at, :], v_ref[w])
        return carry

    lax.fori_loop(0, walkers // 2, body, 0)


def sums_call(meta, inverse, change):
    walkers, _, electrons = inverse.shape
    half = jax.ShapeDtypeStruct((walkers // 2, K, electrons), F32)
    return pl.pallas_call(
        sums_kernel,
        name="sums",
        out_shape=(half, half),
        in_specs=[SMEM, VMEM, VMEM],
        out_specs=(VMEM, VMEM),
        compiler_params=params(),
        cost_estimate=lasting(1),
    )(meta, inverse, change)


def update_kernel(meta_ref, v_ref, factor_ref, *refs):
    out_ref = refs[4]
    parity = meta_ref[meta_ref.shape[0] - 1]
    for half in range(2):
        own = parity == half
        sums = jnp.concatenate(
            [jnp.where(own, refs[i][0], refs[i + 1][0]) for i in (0, 2)], axis=0
        )
        out_ref[half, 0] = v_ref[half, 0] - dot(factor_ref[half, 0], sums)


def update_call(meta, inverse, factor, early, late):
    shape = inverse.shape
    half = shape[0] // 2

    def pair(x):
        return x.reshape(2, half, *x.shape[1:])

    def pair_spec(x):
        return pl.BlockSpec((2, 1, *x.shape[1:]), lambda i, m: (0, i, 0, 0))

    def half_spec(x):
        return pl.BlockSpec((1, *x.shape[1:]), lambda i, m: (i, 0, 0))

    sums = [*early, *late]
    return pl.pallas_call(
        update_kernel,
        name="update",
        grid_spec=pltpu.PrefetchScalarGridSpec(
            num_scalar_prefetch=1,
            grid=(half,),
            in_specs=[pair_spec(inverse), pair_spec(factor)] + [half_spec(x) for x in sums],
            out_specs=pair_spec(inverse),
        ),
        out_shape=jax.ShapeDtypeStruct((2, half, *shape[1:]), F32),
        compiler_params=params(),
        cost_estimate=lasting(3),
    )(meta, pair(inverse), pair(factor), *sums).reshape(shape)


def place_kernel(meta_ref, own_ref, got_ref, *refs):
    out_ref = refs[NMOVE]
    _, walkers, electrons = own_ref.shape
    parts = electrons // got_ref.shape[2]
    lane = lax.broadcasted_iota(jnp.int32, (1, electrons), 1)
    for w in range(walkers):
        here, place, group = parent_of(meta_ref, walkers, w)
        fresh = []
        for b in range(NMOVE):
            block = meta_ref[walkers + b]
            fresh.append((block, roll(refs[b][...], (block - w) * K)))
        for d in range(3):
            at = MOVED + (d + 1) * parts
            far = jnp.concatenate(
                [got_ref[group, at + i : at + i + 1, :] for i in range(parts)], axis=1
            )
            line = jnp.where(here, own_ref[d, pl.ds(place, 1), :], far)
            for block, moved in fresh:
                moved = jnp.concatenate([moved[d : d + 1, :]] * (electrons // 128), axis=1)
                line = jnp.where(lane // K == block, moved, line)
            out_ref[d, w : w + 1, :] = line


def place_call(meta, positions, got, moved):
    return pl.pallas_call(
        place_kernel,
        name="place",
        out_shape=jax.ShapeDtypeStruct(positions.shape, F32),
        in_specs=[SMEM] + [VMEM] * (2 + NMOVE),
        out_specs=VMEM,
        compiler_params=params(),
        cost_estimate=lasting(1),
    )(meta, positions, got, *moved)


def swap(x, axis, k):
    return lax.ppermute(x, axis, [(i, i ^ k) for i in range(lax.axis_size(axis))])


def exchange(part, axis):
    return [part] + [swap(part, axis, k) for k in range(1, lax.axis_size(axis))]


def add_up(mine, give, axis):
    size = lax.axis_size(axis)
    mine = mine + swap(give, axis, 1)
    k = 2
    while k < size:
        mine = mine + swap(mine, axis, k)
        k *= 2
    return mine, swap(mine, axis, 1)


def alltoall(x):
    return lax.all_to_all(x, "walker", split_axis=0, concat_axis=0, tiled=True)


def local(positions, inverse, spline_table, gaussian, accepted, block_order, parent):
    groups = lax.axis_size("walker")
    me = lax.axis_index("walker").astype(jnp.int32)
    parity = lax.rem(lax.axis_index("orb"), 2).astype(jnp.int32)
    meta = jnp.concatenate([parent, block_order[:NMOVE], me[None], parity[None]])
    positions = jnp.transpose(positions, (1, 0, 2))
    gaussian = jnp.transpose(gaussian, (1, 0, 2))

    info = alltoall(pack_call(meta, positions, gaussian, accepted, groups))
    own, code = columns_call(meta, inverse, positions)
    states, outgoing, sending = route_call(meta, info.reshape(-1, 128), own)
    got = alltoall(outgoing)
    codes = [
        swap(x, "walker", k + 1) for k, x in enumerate(outcode_call(meta, sending, code))
    ]
    phi, grad = slopes_call(states, spline_table, 2)
    vm, first = select_call(meta, own, got, grad)
    first = exchange(first, "orb")

    def step(b, operands, phi):
        return step_call(b, operands, states, phi, vm, spline_table)

    s0, new0, change0, t0 = step(0, first, phi)
    phi2, q2 = later_call(2, states, spline_table, vm)
    q2 = exchange(q2, "orb")
    s0 = exchange(s0, "orb")
    s1, new1, change1, t1, y = step(1, [*first, *s0, t0], phi)
    phi3, q3 = later_call(3, states, spline_table, vm)
    q3 = exchange(q3, "orb")
    s1 = exchange(s1, "orb")
    s2, new2, change2, t2, y = step(2, [*s1, t1, *q2, y], phi2)
    s2 = exchange(s2, "orb")
    whole, mine, give = assemble_call(meta, inverse, got, codes, [change0, change1, change2])
    early = add_up(mine, give, "orb")
    s3, new3, change3, t3, y = step(3, [*s2, t2, *q3, y], phi3)
    late = add_up(*sums_call(meta, whole, change3), "orb")
    s3 = exchange(s3, "orb")
    factor = last_call([s0, s1, s2, s3], [t0, t1, t2, t3], vm)
    new_positions = place_call(meta, positions, got, [new0, new1, new2, new3])
    new_inverse = update_call(meta, whole, factor, early, late)
    return jnp.transpose(new_positions, (1, 0, 2)), new_inverse


def solution(mesh):
    return jax.shard_map(
        local,
        mesh=mesh,
        in_specs=(
            P("walker", None, None),
            P("walker", "orb", None),
            P("orb", None),
            P("walker", None, None),
            P("walker", None),
            P(),
            P("walker"),
        ),
        out_specs=(P("walker", None, None), P("walker", "orb", None)),
        check_vma=False,
    )
```

time: 165 us -> 126 us (0.76)
  the two profiles are of different devices: /device:TPU:0 before, /device:TPU:18 now
where the time goes in v3:
time: 126 us
  Pallas kernels  47.9 us (38%)
  starting transfers between devices  37.8 us (30%)
  waiting for transfers between devices  28.6 us (23%)
  local copies, waits for them, and re-layouts  9.28 us (7%)
    ppermute x34, waiting for transfers between devices, swap(): lax.ppermute(x, axis, [(i, i ^ k) for i in range(lax.axis_size(axis))])  27.9 us
    ppermute x34, starting transfers between devices, swap(): lax.ppermute(x, axis, [(i, i ^ k) for i in range(lax.axis_size(axis))])  25.7 us
    all_to_all x2, starting transfers between devices, alltoall(): return lax.all_to_all(x, 'walker', split_axis=0, concat_axis=0, tiled=True)  12.1 us
    unnamed x28, local copies, waits for them, and re-layouts  9.28 us
    pallas_call x2, Pallas kernels, later_call(): pl.pallas_call(functools.partial(later_kernel, block), name='later', out_...  9.15 us
    pallas_call x4, Pallas kernels, step_call(): pl.pallas_call(functools.partial(step_kernel, block, shards), name='step'...  8.96 us
    pallas_call x1, Pallas kernels, slopes_call(): pl.pallas_call(slopes_kernel, name='slopes', grid=(blocks,), out_shape=(j...  8.18 us
    pallas_call x1, Pallas kernels, update_call(): pl.pallas_call(update_kernel, name='update', grid_spec=pltpu.PrefetchScal...  3.4 us
  transfers between devices with their start and end apart: 36, of which 11 were waited for; matrix products, arithmetic and copies ran while one was open for 0% of the time, Pallas kernels for 29%

profile of v3, /device:TPU:18, one launch (start us, length us, event | category | flops | bytes accessed | tf_op | source)
XLA Modules:
  0.0 125.5 jit_solution(8047626417079725430)
XLA Ops:
  0.6 0.9 pad_add_fusion.meta_ref
  1.5 0.8 copy-done.3
  2.3 0.7 copy-done.5
  3.1 0.7 copy-done.6
  3.7 1.3 %pack.1 = f32[8,32,128]{2,1,0:T(8,128)} custom-call(s32[14]{0:T(128)S(1)} %pad_add_fusion.meta_ref, f32[3,8,512]{2,1,0:T(8,128)S(1)} %bitcast.11, f32[3,8,64]{2,1,0:T(8,128)S(1)} %bitcast.14, s32[8,64]{1,0:T(8,128)S(1)} %copy-done.6), custom_call_target="tpu_custom_call" | custom-call | flops 1000000000 | tf_op jit(solution)/shard_map/pack/pallas_call | solution.py:287
  5.0 6.2 %all-to-all-start = ((f32[8,32,128]{2,1,0:T(8,128)}), f32[8,32,128]{2,1,0:T(8,128)S(1)}, u32[]{:S(2)}, u32[]{:S(2)}) async-start(f32[8,32,128]{2,1,0:T(8,128)} %pack.1), calls=%async_computation | async-start | bytes 262144 | tf_op jit(solution)/shard_map/all_to_all | solution.py:791
  11.2 3.4 %columns.1 = (f32[8,80,128]{2,1,0:T(8,128)S(1)}, s16[8,128,512]{2,1,0:T(8,128)(2,1)S(1)}) custom-call(s32[14]{0:T(128)S(1)} %pad_add_fusion.meta_ref, f32[8,128,512]{2,1,0:T(8,128)S(1)} %copy-done.2, f32[3,8,512]{2,1,0:T(8,128)S(1)} %bitcast.12), custom_call_target="tpu_custom_call" | custom-call | flops 3000000000 | tf_op jit(solution)/shard_map/columns/pallas_call | solution.py:323
  14.6 0.7 copy-done.9
  15.3 0.7 all-to-all-done
  16.0 1.0 copy-done.10
  17.0 1.6 %route.1 = (f32[4,8,128]{2,1,0:T(8,128)S(1)}, f32[8,80,128]{2,1,0:T(8,128)}, s32[8,128]{1,0:T(8,128)S(1)}) custom-call(s32[14]{0:T(128)S(1)} %pad_add_fusion.meta_ref, f32[256,128]{1,0:T(8,128)S(1)} %bitcast.10, f32[8,80,128]{2,1,0:T(8,128)S(1)} %copy-done.10), custom_call_target="tpu_custom_call" | custom-call | flops 2000000000 | tf_op jit(solution)/shard_map/route/pallas_call | solution.py:383
  18.6 5.9 %all-to-all-start.1 = ((f32[8,80,128]{2,1,0:T(8,128)}), f32[8,80,128]{2,1,0:T(8,128)S(1)}, u32[]{:S(2)}, u32[]{:S(2)}) async-start(f32[8,80,128]{2,1,0:T(8,128)} %get-tuple-element.46), calls=%async_computation.1 | async-start | bytes 655360 | tf_op jit(solution)/shard_map/all_to_all | solution.py:791
  24.5 2.0 %copy-done = bf16[128,13824]{1,0:T(8,128)(2,1)S(1)} copy-done((bf16[128,13824]{1,0:T(8,128)(2,1)S(1)}, bf16[128,13824]{1,0:T(8,128)(2,1)}, u32[]{:S(2)}) %copy-start) | copy-done | bytes 3538968
  26.5 8.2 %slopes.1 = (f32[256,128]{1,0:T(8,128)S(1)}, f32[256,384]{1,0:T(8,128)S(1)}) custom-call(f32[4,8,128]{2,1,0:T(8,128)S(1)} %get-tuple-element.47.state_ref.refs_4_.refs_9_.states_ref.refs_10_, bf16[128,13824]{1,0:T(8,128)(2,1)S(1)} %copy-done), custom_call_target="tpu_custom_call" | custom-call | flops 10000000000 | tf_op jit(solution)/shard_map/slopes/pallas_call | solution.py:128
  34.7 0.7 copy-done.7
  35.4 0.7 copy-done.12
  36.1 1.0 copy-done.8
  37.1 1.0 copy-done.11
  38.0 1.3 %select.3 = (f32[512,128]{1,0:T(8,128)S(1)}, f32[64,128]{1,0:T(8,128)S(1)}) custom-call(s32[14]{0:T(128)S(1)} %pad_add_fusion.meta_ref, f32[8,80,128]{2,1,0:T(8,128)S(1)} %copy-done.11, f32[8,80,128]{2,1,0:T(8,128)S(1)} %all-to-all-done.1.got_ref, f32[256,384]{1,0:T(8,128)S(1)} %copy-done.8), custom_call_target="tpu_custom_call" | custom-call | flops 2000000000 | tf_op jit(solution)/shard_map/select/pallas_call | solution.py:469
  39.5 0.6 collective-permute-start.1
  40.0 1.3 collective-permute-start
  41.3 2.0 %outcode.1 = (s16[128,512]{1,0:T(8,128)(2,1)S(1)}, s16[128,512]{1,0:T(8,128)(2,1)S(1)}, s16[128,512]{1,0:T(8,128)(2,1)S(1)}, s16[128,512]{1,0:T(8,128)(2,1)S(1)}...) custom-call(s32[14]{0:T(128)S(1)} %pad_add_fusion.meta_ref, ...), custom_call_target="tpu_custom_call" | custom-call | flops 1000000000 | tf_op jit(solution)/shard_map/outcode/pallas_call | solution.py:413
  43.4 1.5 %collective-permute-start.18 = (s16[128,512]{1,0:T(8,128)(2,1)S(1)}, s16[128,512]{1,0:T(8,128)(2,1)S(1)}, u32[]{:S(2)}, u32[]{:S(2)}) collective-permute-start(s16[128,512]{1,0:T(8,128)(2,1)S(1)} %get-tuple-element.70), channel_id=1, source_target_pairs={{0,4},{4,0},{8,12},{12,8},{16,20},{20,16},{24,28},{28,24},{1,5},{5... | collective-permute-start | bytes 393224 | tf_op jit(solution)/shard_map/ppermute | solution.py:773
  44.9 1.5 %collective-permute-start.19 = (s16[128,512]{1,0:T(8,128)(2,1)S(1)}, s16[128,512]{1,0:T(8,128)(2,1)S(1)}, u32[]{:S(2)}, u32[]{:S(2)}) collective-permute-start(s16[128,512]{1,0:T(8,128)(2,1)S(1)} %get-tuple-element.71), channel_id=1, source_target_pairs={{0,8},{4,12},{8,0},{12,4},{16,24},{20,28},{24,16},{28,20},{1,9},{5... | collective-permute-start | bytes 393224 | tf_op jit(solution)/shard_map/ppermute | solution.py:773
  46.4 1.8 %step.4 = (f32[64,128]{1,0:T(8,128)S(1)}, f32[8,128]{1,0:T(8,128)S(1)}, f32[128,128]{1,0:T(8,128)S(1)}, f32[64,128]{1,0:T(8,128)S(1)}) custom-call(f32[64,128]{1,0:T(8,128)S(1)} %get-tuple-element.49.refs_0_, f32[64,128]{1,0:T(8,128)S(1)} %collective-permute-done.refs_1_, f32[64,128]{1,0:T(8,128)S(1)} %collective-permute-done.1.refs_2_, ...), custom_call_target="tpu_custom_call" | custom-call | flops 4000000000 | tf_op jit(solution)/shard_map/step/pallas_call | solution.py:561
  48.3 1.1 collective-permute-start.4
  49.4 0.8 collective-permute-start.3
  50.2 4.6 %later.2 = (f32[128,128]{1,0:T(8,128)S(1)}, f32[104,128]{1,0:T(8,128)S(1)}) custom-call(f32[4,8,128]{2,1,0:T(8,128)S(1)} %get-tuple-element.47.state_ref.refs_4_.refs_9_.states_ref.refs_10_, bf16[128,13824]{1,0:T(8,128)(2,1)S(1)} %copy-done.1, f32[512,128]{1,0:T(8,128)S(1)} %get-tuple-element.51.refs_6_.refs_11_.vm_ref.refs_12_.refs_20_), custom_call_target="tpu_custom_call" | custom-call | flops 6000000000 | tf_op jit(solution)/shard_map/later/pallas_call | solution.py:164
  55.2 1.3 %collective-permute-start.10 = (f32[104,128]{1,0:T(8,128)S(1)}, f32[104,128]{1,0:T(8,128)S(1)}, u32[]{:S(2)}, u32[]{:S(2)}) collective-permute-start(f32[104,128]{1,0:T(8,128)S(1)} %get-tuple-element.58.refs_5_), channel_id=1, source_target_pairs={{0,2},{1,3},{2,0},{3,1},{4,6},{5,7},{6,4},{7,5},{8,10},{9,11},{10,... | collective-permute-start | bytes 159752 | tf_op jit(solution)/shard_map/ppermute | solution.py:773
  56.7 2.2 %step.5 = (f32[64,128]{1,0:T(8,128)S(1)}, f32[8,128]{1,0:T(8,128)S(1)}, f32[128,128]{1,0:T(8,128)S(1)}, f32[64,128]{1,0:T(8,128)S(1)}, f32[512,64]{1,0:T(8,128)S(1)}) custom-call(f32[64,128]{1,0:T(8,128)S(1)} %get-tuple-element.49.refs_0_, f32[64,128]{1,0:T(8,128)S(1)} %collective-permute-done.refs_1_, f32[64,128]{1,0:T(8,128)S(1)} %collective-permute-done.1.refs_2_, ...), custom_call_target="tpu_custom_call" | custom-call | flops 4000000000 | tf_op jit(solution)/shard_map/step/pallas_call | solution.py:561
  58.9 0.7 collective-permute-start.8
  59.6 1.3 %collective-permute-start.7 = (f32[64,128]{1,0:T(8,128)S(1)}, f32[64,128]{1,0:T(8,128)S(1)}, u32[]{:S(2)}, u32[]{:S(2)}) collective-permute-start(f32[64,128]{1,0:T(8,128)S(1)} %get-tuple-element.56.refs_0_.refs_4_), channel_id=1, source_target_pairs={{0,2},{1,3},{2,0},{3,1},{4,6},{5,7},{6,4},{7,5},{8,10},{9,11},{10,... | collective-permute-start | bytes 98312 | tf_op jit(solution)/shard_map/ppermute | solution.py:773
  60.9 0.6 collective-permute-start.20
  61.6 0.7 collective-permute-done.8.refs_3_.refs_7_
  62.3 3.0 %collective-permute-start.22 = (s16[128,512]{1,0:T(8,128)(2,1)S(1)}, s16[128,512]{1,0:T(8,128)(2,1)S(1)}, u32[]{:S(2)}, u32[]{:S(2)}) collective-permute-start(s16[128,512]{1,0:T(8,128)(2,1)S(1)} %get-tuple-element.74), channel_id=1, source_target_pairs={{0,20},{4,16},{8,28},{12,24},{16,4},{20,0},{24,12},{28,8},{1,21},{... | collective-permute-start | bytes 393224 | tf_op jit(solution)/shard_map/ppermute | solution.py:773
  65.4 0.5 collective-permute-start.23
  65.9 1.5 %collective-permute-start.24 = (s16[128,512]{1,0:T(8,128)(2,1)S(1)}, s16[128,512]{1,0:T(8,128)(2,1)S(1)}, u32[]{:S(2)}, u32[]{:S(2)}) collective-permute-start(s16[128,512]{1,0:T(8,128)(2,1)S(1)} %get-tuple-element.76), channel_id=1, source_target_pairs={{0,28},{4,24},{8,20},{12,16},{16,12},{20,8},{24,4},{28,0},{1,29},{... | collective-permute-start | bytes 393224 | tf_op jit(solution)/shard_map/ppermute | solution.py:773
  67.4 2.4 %step.6 = (f32[64,128]{1,0:T(8,128)S(1)}, f32[8,128]{1,0:T(8,128)S(1)}, f32[128,128]{1,0:T(8,128)S(1)}, f32[64,128]{1,0:T(8,128)S(1)}, f32[512,64]{1,0:T(8,128)S(1)}) custom-call(f32[64,128]{1,0:T(8,128)S(1)} %get-tuple-element.56.refs_0_.refs_4_, f32[64,128]{1,0:T(8,128)S(1)} %collective-permute-done.6.refs_1_.refs_5_, ...), custom_call_target="tpu_custom_call" | custom-call | flops 4000000000 | tf_op jit(solution)/shard_map/step/pallas_call | solution.py:561
  69.9 10.1 %collective-permute-done.22.refs_4_ = s16[128,512]{1,0:T(8,128)(2,1)S(1)} collective-permute-done((s16[128,512]{1,0:T(8,128)(2,1)S(1)}, s16[128,512]{1,0:T(8,128)(2,1)S(1)}, u32[]{:S(2)}, u32[]{:S(2)}) %collective-permute-start.22) | collective-permute-done | bytes 131104 | tf_op jit(solution)/shard_map/ppermute | solution.py:773
  80.0 5.3 %collective-permute-done.23.refs_5_ = s16[128,512]{1,0:T(8,128)(2,1)S(1)} collective-permute-done((s16[128,512]{1,0:T(8,128)(2,1)S(1)}, s16[128,512]{1,0:T(8,128)(2,1)S(1)}, u32[]{:S(2)}, u32[]{:S(2)}) %collective-permute-start.23) | collective-permute-done | bytes 131104 | tf_op jit(solution)/shard_map/ppermute | solution.py:773
  85.3 3.3 %collective-permute-done.24.refs_6_ = s16[128,512]{1,0:T(8,128)(2,1)S(1)} collective-permute-done((s16[128,512]{1,0:T(8,128)(2,1)S(1)}, s16[128,512]{1,0:T(8,128)(2,1)S(1)}, u32[]{:S(2)}, u32[]{:S(2)}) %collective-permute-start.24) | collective-permute-done | bytes 131104 | tf_op jit(solution)/shard_map/ppermute | solution.py:773
  88.6 3.4 %assemble.1 = (f32[8,128,512]{2,1,0:T(8,128)S(1)}, f32[4,48,512]{2,1,0:T(8,128)S(1)}, f32[4,48,512]{2,1,0:T(8,128)S(1)}) custom-call(s32[14]{0:T(128)S(1)} %pad_add_fusion.meta_ref, f32[8,128,512]{2,1,0:T(8,128)S(1)} %copy-done.2, f32[8,80,128]{2,1,0:T(8,128)S(1)} %all-to-all-done.1.got_ref, s16[128,512]{1,0:T(8,128)(2,1)S(1)} %collective-permute-done.18.refs_0_, ...), custom_call_target="tpu_custom_call" | custom-call | flops 4000000000 | tf_op jit(solution)/shard_map/assemble/pallas_call | solution.py:652
  92.0 4.6 %later.3 = (f32[128,128]{1,0:T(8,128)S(1)}, f32[152,128]{1,0:T(8,128)S(1)}) custom-call(f32[4,8,128]{2,1,0:T(8,128)S(1)} %get-tuple-element.47.state_ref.refs_4_.refs_9_.states_ref.refs_10_, bf16[128,13824]{1,0:T(8,128)(2,1)S(1)} %copy-done.1, f32[512,128]{1,0:T(8,128)S(1)} %get-tuple-element.51.refs_6_.refs_11_.vm_ref.refs_12_.refs_20_), custom_call_target="tpu_custom_call" | custom-call | flops 6000000000 | tf_op jit(solution)/shard_map/later/pallas_call | solution.py:164
  96.6 0.9 collective-permute-start.17
  97.5 1.3 %collective-permute-start.16 = (f32[152,128]{1,0:T(8,128)S(1)}, f32[152,128]{1,0:T(8,128)S(1)}, u32[]{:S(2)}, u32[]{:S(2)}) collective-permute-start(f32[152,128]{1,0:T(8,128)S(1)} %get-tuple-element.64.refs_5_), channel_id=1, source_target_pairs={{0,2},{1,3},{2,0},{3,1},{4,6},{5,7},{6,4},{7,5},{8,10},{9,11},{10,... | collective-permute-start | bytes 233480 | tf_op jit(solution)/shard_map/ppermute | solution.py:773
  98.8 0.9 collective-permute-start.14
  99.7 1.0 collective-permute-done.17.refs_8_
  100.7 0.8 collective-permute-start.13
  101.5 0.7 collective-permute-start.12
  102.3 1.0 collective-permute-done.16.refs_7_
  103.3 0.8 collective-permute-start.29
  104.1 0.8 collective-permute-done.13.refs_2_.refs_10_
  104.9 2.5 %step.7 = (f32[64,128]{1,0:T(8,128)S(1)}, f32[8,128]{1,0:T(8,128)S(1)}, f32[128,128]{1,0:T(8,128)S(1)}, f32[64,128]{1,0:T(8,128)S(1)}, f32[512,64]{1,0:T(8,128)}) custom-call(f32[64,128]{1,0:T(8,128)S(1)} %get-tuple-element.62.refs_0_.refs_8_, f32[64,128]{1,0:T(8,128)S(1)} %collective-permute-done.12.refs_1_.refs_9_, ...), custom_call_target="tpu_custom_call" | custom-call | flops 4000000000 | tf_op jit(solution)/shard_map/step/pallas_call | solution.py:561
  107.3 1.4 %sums.1 = (f32[4,16,512]{2,1,0:T(8,128)S(1)}, f32[4,16,512]{2,1,0:T(8,128)S(1)}) custom-call(s32[14]{0:T(128)S(1)} %pad_add_fusion.meta_ref, f32[8,128,512]{2,1,0:T(8,128)S(1)} %get-tuple-element.80.v_ref, f32[128,128]{1,0:T(8,128)S(1)} %get-tuple-element.85.change_ref), custom_call_target="tpu_custom_call" | custom-call | flops 1000000000 | tf_op jit(solution)/shard_map/sums/pallas_call | solution.py:686
  108.9 1.2 collective-permute-done.31
  110.2 0.9 collective-permute-start.32
  111.1 2.9 %collective-permute-done.29 = f32[4,48,512]{2,1,0:T(8,128)S(1)} collective-permute-done((f32[4,48,512]{2,1,0:T(8,128)S(1)}, f32[4,48,512]{2,1,0:T(8,128)S(1)}, u32[]{:S(2)}, u32[]{:S(2)}) %collective-permute-start.29) | collective-permute-done | bytes 393248 | tf_op jit(solution)/shard_map/ppermute | solution.py:773
  114.1 1.6 %collective-permute-start.27 = (f32[64,128]{1,0:T(8,128)S(1)}, f32[64,128]{1,0:T(8,128)S(1)}, u32[]{:S(2)}, u32[]{:S(2)}) collective-permute-start(f32[64,128]{1,0:T(8,128)S(1)} %get-tuple-element.81.refs_12_), channel_id=1, source_target_pairs={{0,3},{1,2},{2,1},{3,0},{4,7},{5,6},{6,5},{7,4},{8,11},{9,10},{10,... | collective-permute-start | bytes 98312 | tf_op jit(solution)/shard_map/ppermute | solution.py:773
  115.8 0.5 collective-permute-start.26
  116.3 1.4 %place.1 = f32[3,8,512]{2,1,0:T(8,128)} custom-call(s32[14]{0:T(128)S(1)} %pad_add_fusion.meta_ref, f32[3,8,512]{2,1,0:T(8,128)S(1)} %bitcast.13, f32[8,80,128]{2,1,0:T(8,128)S(1)} %all-to-all-done.1.got_ref, f32[8,128]{1,0:T(8,128)S(1)} %get-tuple-element.52.refs_0_, f32[8,128]{1,0:T(8,128)S(1)} %get-tuple-element.55.refs_1_, ...), custom_call_target="tpu_custom_call" | custom-call | flops 1000000000 | tf_op jit(solution)/shard_map/place/pallas_call | solution.py:761
  117.7 0.6 collective-permute-start.33
  118.3 1.4 %collective-permute-done.26.refs_14_ = f32[64,128]{1,0:T(8,128)S(1)} collective-permute-done((f32[64,128]{1,0:T(8,128)S(1)}, f32[64,128]{1,0:T(8,128)S(1)}, u32[]{:S(2)}, u32[]{:S(2)}) %collective-permute-start.26) | collective-permute-done | bytes 32800 | tf_op jit(solution)/shard_map/ppermute | solution.py:773
  119.7 2.4 %last.1 = f32[8,128,64]{2,1,0:T(8,128)S(1)} custom-call(f32[64,128]{1,0:T(8,128)S(1)} %get-tuple-element.53.refs_4_.refs_0_, f32[64,128]{1,0:T(8,128)S(1)} %collective-permute-done.3.refs_5_.refs_1_, f32[64,128]{1,0:T(8,128)S(1)} %collective-permute-done.4.refs_6_.refs_2_, f32[64,128]{1,0:T(8,128)S(1)} %collective-permute-done.5.refs_7_.refs_3_, ...), custom_call_target="tpu_custom_call" | custom-call | flops 3000000000 | tf_op jit(solution)/shard_map/last/pallas_call | solution.py:597
  122.1 3.4 %update.1 = f32[2,4,128,512]{3,2,1,0:T(8,128)} custom-call(s32[14]{0:T(128)S(1)} %pad_add_fusion.meta_ref, f32[2,4,128,512]{3,2,1,0:T(8,128)S(1)} %bitcast.15, f32[2,4,128,64]{3,2,1,0:T(8,128)S(1)} %bitcast.16, f32[4,48,512]{2,1,0:T(8,128)S(1)} %add.13.refs_0_, f32[4,48,512]{2,1,0:T(8,128)S(1)} %collective-permute-done.30.refs_1_, ...), custom_call_target="tpu_custom_call" | custom-call | flops 3000000000 | tf_op jit(solution)/shard_map/update/pallas_call | solution.py:722
  (58 shorter events, 1.4 us)
Async XLA Ops:
  0.6 10.6 %copy-start.2 = (f32[8,128,512]{2,1,0:T(8,128)S(1)}, f32[8,128,512]{2,1,0:T(8,128)}, u32[]{:S(2)}) copy-start(f32[8,128,512]{2,1,0:T(8,128)} %own_ref.1) | copy-start | bytes 6291460
  1.5 0.8 copy-start.3
  2.3 0.7 copy-start.5
  3.1 0.7 copy-start.6
  3.7 7.5 %copy-start.4 = (f32[8,3,512]{2,0,1:T(8,128)S(1)}, f32[8,3,512]{2,0,1:T(8,128)}, u32[]{:S(2)}) copy-start(f32[8,3,512]{2,0,1:T(8,128)} %param.7) | copy-start | bytes 147460
  5.0 11.0 %all-to-all-start = ((f32[8,32,128]{2,1,0:T(8,128)}), f32[8,32,128]{2,1,0:T(8,128)S(1)}, u32[]{:S(2)}, u32[]{:S(2)}) async-start(f32[8,32,128]{2,1,0:T(8,128)} %pack.1), calls=%async_computation | async-start | bytes 262144 | tf_op jit(solution)/shard_map/all_to_all | solution.py:791
  14.6 0.7 copy-start.9
  16.0 1.0 copy-start.10
  18.6 17.5 %all-to-all-start.1 = ((f32[8,80,128]{2,1,0:T(8,128)}), f32[8,80,128]{2,1,0:T(8,128)S(1)}, u32[]{:S(2)}, u32[]{:S(2)}) async-start(f32[8,80,128]{2,1,0:T(8,128)} %get-tuple-element.46), calls=%async_computation.1 | async-start | bytes 655360 | tf_op jit(solution)/shard_map/all_to_all | solution.py:791
  24.5 2.0 %copy-start = (bf16[128,13824]{1,0:T(8,128)(2,1)S(1)}, bf16[128,13824]{1,0:T(8,128)(2,1)}, u32[]{:S(2)}) copy-start(bf16[128,13824]{1,0:T(8,128)(2,1)} %refs_13_.3) | copy-start | bytes 10616836
  34.6 0.7 copy-start.7
  35.4 0.7 copy-start.12
  36.1 1.0 copy-start.8
  37.0 1.0 copy-start.11
  39.4 7.0 %copy-start.1 = (bf16[128,13824]{1,0:T(8,128)(2,1)S(1)}, bf16[128,13824]{1,0:T(8,128)(2,1)}, u32[]{:S(2)}) copy-start(bf16[128,13824]{1,0:T(8,128)(2,1)} %refs_13_.3) | copy-start | bytes 10616836
  39.4 7.0 %copy-start.13 = (f32[256,128]{1,0:T(8,128)S(1)}, f32[256,128]{1,0:T(8,128)}, u32[]{:S(2)}) copy-start(f32[256,128]{1,0:T(8,128)} %copy-done.12) | copy-start | bytes 393220
  39.4 7.0 %collective-permute-start.2 = (f32[64,128]{1,0:T(8,128)S(1)}, f32[64,128]{1,0:T(8,128)S(1)}, u32[]{:S(2)}, u32[]{:S(2)}) collective-permute-start(f32[64,128]{1,0:T(8,128)S(1)} %get-tuple-element.49.refs_0_), channel_id=1, source_target_pairs={{0,3},{1,2},{2,1},{3,0},{4,7},{5,6},{6,5},{7,4},{8,11},{9,10},{10,... | collective-permute-start | bytes 98312 | tf_op jit(solution)/shard_map/ppermute | solution.py:773
  39.5 6.9 %collective-permute-start.1 = (f32[64,128]{1,0:T(8,128)S(1)}, f32[64,128]{1,0:T(8,128)S(1)}, u32[]{:S(2)}, u32[]{:S(2)}) collective-permute-start(f32[64,128]{1,0:T(8,128)S(1)} %get-tuple-element.49.refs_0_), channel_id=1, source_target_pairs={{0,2},{1,3},{2,0},{3,1},{4,6},{5,7},{6,4},{7,5},{8,10},{9,11},{10,... | collective-permute-start | bytes 98312 | tf_op jit(solution)/shard_map/ppermute | solution.py:773
  40.0 6.3 %collective-permute-start = (f32[64,128]{1,0:T(8,128)S(1)}, f32[64,128]{1,0:T(8,128)S(1)}, u32[]{:S(2)}, u32[]{:S(2)}) collective-permute-start(f32[64,128]{1,0:T(8,128)S(1)} %get-tuple-element.49.refs_0_), channel_id=1, source_target_pairs={{0,1},{1,0},{2,3},{3,2},{4,5},{5,4},{6,7},{7,6},{8,9},{9,8},{10,11... | collective-permute-start | bytes 98312 | tf_op jit(solution)/shard_map/ppermute | solution.py:773
  43.4 15.6 %collective-permute-start.18 = (s16[128,512]{1,0:T(8,128)(2,1)S(1)}, s16[128,512]{1,0:T(8,128)(2,1)S(1)}, u32[]{:S(2)}, u32[]{:S(2)}) collective-permute-start(s16[128,512]{1,0:T(8,128)(2,1)S(1)} %get-tuple-element.70), channel_id=1, source_target_pairs={{0,4},{4,0},{8,12},{12,8},{16,20},{20,16},{24,28},{28,24},{1,5},{5... | collective-permute-start | bytes 393224 | tf_op jit(solution)/shard_map/ppermute | solution.py:773
  44.9 14.8 %collective-permute-start.19 = (s16[128,512]{1,0:T(8,128)(2,1)S(1)}, s16[128,512]{1,0:T(8,128)(2,1)S(1)}, u32[]{:S(2)}, u32[]{:S(2)}) collective-permute-start(s16[128,512]{1,0:T(8,128)(2,1)S(1)} %get-tuple-element.71), channel_id=1, source_target_pairs={{0,8},{4,12},{8,0},{12,4},{16,24},{20,28},{24,16},{28,20},{1,9},{5... | collective-permute-start | bytes 393224 | tf_op jit(solution)/shard_map/ppermute | solution.py:773
  48.2 6.5 %collective-permute-start.5 = (f32[64,128]{1,0:T(8,128)S(1)}, f32[64,128]{1,0:T(8,128)S(1)}, u32[]{:S(2)}, u32[]{:S(2)}) collective-permute-start(f32[64,128]{1,0:T(8,128)S(1)} %get-tuple-element.53.refs_4_.refs_0_), channel_id=1, source_target_pairs={{0,3},{1,2},{2,1},{3,0},{4,7},{5,6},{6,5},{7,4},{8,11},{9,10},{10,... | collective-permute-start | bytes 98312 | tf_op jit(solution)/shard_map/ppermute | solution.py:773
  48.3 6.9 %collective-permute-start.4 = (f32[64,128]{1,0:T(8,128)S(1)}, f32[64,128]{1,0:T(8,128)S(1)}, u32[]{:S(2)}, u32[]{:S(2)}) collective-permute-start(f32[64,128]{1,0:T(8,128)S(1)} %get-tuple-element.53.refs_4_.refs_0_), channel_id=1, source_target_pairs={{0,2},{1,3},{2,0},{3,1},{4,6},{5,7},{6,4},{7,5},{8,10},{9,11},{10,... | collective-permute-start | bytes 98312 | tf_op jit(solution)/shard_map/ppermute | solution.py:773
  49.4 7.1 %collective-permute-start.3 = (f32[64,128]{1,0:T(8,128)S(1)}, f32[64,128]{1,0:T(8,128)S(1)}, u32[]{:S(2)}, u32[]{:S(2)}) collective-permute-start(f32[64,128]{1,0:T(8,128)S(1)} %get-tuple-element.53.refs_4_.refs_0_), channel_id=1, source_target_pairs={{0,1},{1,0},{2,3},{3,2},{4,5},{5,4},{6,7},{7,6},{8,9},{9,8},{10,11... | collective-permute-start | bytes 98312 | tf_op jit(solution)/shard_map/ppermute | solution.py:773
  54.7 6.2 %collective-permute-start.11 = (f32[104,128]{1,0:T(8,128)S(1)}, f32[104,128]{1,0:T(8,128)S(1)}, u32[]{:S(2)}, u32[]{:S(2)}) collective-permute-start(f32[104,128]{1,0:T(8,128)S(1)} %get-tuple-element.58.refs_5_), channel_id=1, source_target_pairs={{0,3},{1,2},{2,1},{3,0},{4,7},{5,6},{6,5},{7,4},{8,11},{9,10},{10,... | collective-permute-start | bytes 159752 | tf_op jit(solution)/shard_map/ppermute | solution.py:773
  55.2 5.8 %collective-permute-start.10 = (f32[104,128]{1,0:T(8,128)S(1)}, f32[104,128]{1,0:T(8,128)S(1)}, u32[]{:S(2)}, u32[]{:S(2)}) collective-permute-start(f32[104,128]{1,0:T(8,128)S(1)} %get-tuple-element.58.refs_5_), channel_id=1, source_target_pairs={{0,2},{1,3},{2,0},{3,1},{4,6},{5,7},{6,4},{7,5},{8,10},{9,11},{10,... | collective-permute-start | bytes 159752 | tf_op jit(solution)/shard_map/ppermute | solution.py:773
  56.5 5.1 %collective-permute-start.9 = (f32[104,128]{1,0:T(8,128)S(1)}, f32[104,128]{1,0:T(8,128)S(1)}, u32[]{:S(2)}, u32[]{:S(2)}) collective-permute-start(f32[104,128]{1,0:T(8,128)S(1)} %get-tuple-element.58.refs_5_), channel_id=1, source_target_pairs={{0,1},{1,0},{2,3},{3,2},{4,5},{5,4},{6,7},{7,6},{8,9},{9,8},{10,11... | collective-permute-start | bytes 159752 | tf_op jit(solution)/shard_map/ppermute | solution.py:773
  58.9 3.4 %collective-permute-start.8 = (f32[64,128]{1,0:T(8,128)S(1)}, f32[64,128]{1,0:T(8,128)S(1)}, u32[]{:S(2)}, u32[]{:S(2)}) collective-permute-start(f32[64,128]{1,0:T(8,128)S(1)} %get-tuple-element.56.refs_0_.refs_4_), channel_id=1, source_target_pairs={{0,3},{1,2},{2,1},{3,0},{4,7},{5,6},{6,5},{7,4},{8,11},{9,10},{10,... | collective-permute-start | bytes 98312 | tf_op jit(solution)/shard_map/ppermute | solution.py:773
  59.6 5.7 %collective-permute-start.7 = (f32[64,128]{1,0:T(8,128)S(1)}, f32[64,128]{1,0:T(8,128)S(1)}, u32[]{:S(2)}, u32[]{:S(2)}) collective-permute-start(f32[64,128]{1,0:T(8,128)S(1)} %get-tuple-element.56.refs_0_.refs_4_), channel_id=1, source_target_pairs={{0,2},{1,3},{2,0},{3,1},{4,6},{5,7},{6,4},{7,5},{8,10},{9,11},{10,... | collective-permute-start | bytes 98312 | tf_op jit(solution)/shard_map/ppermute | solution.py:773
  60.9 5.0 %collective-permute-start.6 = (f32[64,128]{1,0:T(8,128)S(1)}, f32[64,128]{1,0:T(8,128)S(1)}, u32[]{:S(2)}, u32[]{:S(2)}) collective-permute-start(f32[64,128]{1,0:T(8,128)S(1)} %get-tuple-element.56.refs_0_.refs_4_), channel_id=1, source_target_pairs={{0,1},{1,0},{2,3},{3,2},{4,5},{5,4},{6,7},{7,6},{8,9},{9,8},{10,11... | collective-permute-start | bytes 98312 | tf_op jit(solution)/shard_map/ppermute | solution.py:773
  60.9 8.9 %collective-permute-start.20 = (s16[128,512]{1,0:T(8,128)(2,1)S(1)}, s16[128,512]{1,0:T(8,128)(2,1)S(1)}, u32[]{:S(2)}, u32[]{:S(2)}) collective-permute-start(s16[128,512]{1,0:T(8,128)(2,1)S(1)} %get-tuple-element.72), channel_id=1, source_target_pairs={{0,12},{4,8},{8,4},{12,0},{16,28},{20,24},{24,20},{28,16},{1,13},{... | collective-permute-start | bytes 393224 | tf_op jit(solution)/shard_map/ppermute | solution.py:773
  61.5 8.3 %collective-permute-start.21 = (s16[128,512]{1,0:T(8,128)(2,1)S(1)}, s16[128,512]{1,0:T(8,128)(2,1)S(1)}, u32[]{:S(2)}, u32[]{:S(2)}) collective-permute-start(s16[128,512]{1,0:T(8,128)(2,1)S(1)} %get-tuple-element.73), channel_id=1, source_target_pairs={{0,16},{4,20},{8,24},{12,28},{16,0},{20,4},{24,8},{28,12},{1,17},{... | collective-permute-start | bytes 393224 | tf_op jit(solution)/shard_map/ppermute | solution.py:773
  62.3 17.6 %collective-permute-start.22 = (s16[128,512]{1,0:T(8,128)(2,1)S(1)}, s16[128,512]{1,0:T(8,128)(2,1)S(1)}, u32[]{:S(2)}, u32[]{:S(2)}) collective-permute-start(s16[128,512]{1,0:T(8,128)(2,1)S(1)} %get-tuple-element.74), channel_id=1, source_target_pairs={{0,20},{4,16},{8,28},{12,24},{16,4},{20,0},{24,12},{28,8},{1,21},{... | collective-permute-start | bytes 393224 | tf_op jit(solution)/shard_map/ppermute | solution.py:773
  65.4 19.9 %collective-permute-start.23 = (s16[128,512]{1,0:T(8,128)(2,1)S(1)}, s16[128,512]{1,0:T(8,128)(2,1)S(1)}, u32[]{:S(2)}, u32[]{:S(2)}) collective-permute-start(s16[128,512]{1,0:T(8,128)(2,1)S(1)} %get-tuple-element.75), channel_id=1, source_target_pairs={{0,24},{4,28},{8,16},{12,20},{16,8},{20,12},{24,0},{28,4},{1,25},{... | collective-permute-start | bytes 393224 | tf_op jit(solution)/shard_map/ppermute | solution.py:773
  65.9 22.7 %collective-permute-start.24 = (s16[128,512]{1,0:T(8,128)(2,1)S(1)}, s16[128,512]{1,0:T(8,128)(2,1)S(1)}, u32[]{:S(2)}, u32[]{:S(2)}) collective-permute-start(s16[128,512]{1,0:T(8,128)(2,1)S(1)} %get-tuple-element.76), channel_id=1, source_target_pairs={{0,28},{4,24},{8,20},{12,16},{16,12},{20,8},{24,4},{28,0},{1,29},{... | collective-permute-start | bytes 393224 | tf_op jit(solution)/shard_map/ppermute | solution.py:773
  92.0 9.5 %collective-permute-start.28 = (f32[4,48,512]{2,1,0:T(8,128)S(1)}, f32[4,48,512]{2,1,0:T(8,128)S(1)}, u32[]{:S(2)}, u32[]{:S(2)}) collective-permute-start(f32[4,48,512]{2,1,0:T(8,128)S(1)} %get-tuple-element.84), channel_id=1, source_target_pairs={{0,1},{1,0},{2,3},{3,2},{4,5},{5,4},{6,7},{7,6},{8,9},{9,8},{10,11... | collective-permute-start | bytes 1179656 | tf_op jit(solution)/shard_map/ppermute | solution.py:773
  96.6 4.1 %collective-permute-start.17 = (f32[152,128]{1,0:T(8,128)S(1)}, f32[152,128]{1,0:T(8,128)S(1)}, u32[]{:S(2)}, u32[]{:S(2)}) collective-permute-start(f32[152,128]{1,0:T(8,128)S(1)} %get-tuple-element.64.refs_5_), channel_id=1, source_target_pairs={{0,3},{1,2},{2,1},{3,0},{4,7},{5,6},{6,5},{7,4},{8,11},{9,10},{10,... | collective-permute-start | bytes 233480 | tf_op jit(solution)/shard_map/ppermute | solution.py:773
  97.5 5.8 %collective-permute-start.16 = (f32[152,128]{1,0:T(8,128)S(1)}, f32[152,128]{1,0:T(8,128)S(1)}, u32[]{:S(2)}, u32[]{:S(2)}) collective-permute-start(f32[152,128]{1,0:T(8,128)S(1)} %get-tuple-element.64.refs_5_), channel_id=1, source_target_pairs={{0,2},{1,3},{2,0},{3,1},{4,6},{5,7},{6,4},{7,5},{8,10},{9,11},{10,... | collective-permute-start | bytes 233480 | tf_op jit(solution)/shard_map/ppermute | solution.py:773
  98.8 5.3 %collective-permute-start.15 = (f32[152,128]{1,0:T(8,128)S(1)}, f32[152,128]{1,0:T(8,128)S(1)}, u32[]{:S(2)}, u32[]{:S(2)}) collective-permute-start(f32[152,128]{1,0:T(8,128)S(1)} %get-tuple-element.64.refs_5_), channel_id=1, source_target_pairs={{0,1},{1,0},{2,3},{3,2},{4,5},{5,4},{6,7},{7,6},{8,9},{9,8},{10,11... | collective-permute-start | bytes 233480 | tf_op jit(solution)/shard_map/ppermute | solution.py:773
  98.8 5.3 %collective-permute-start.14 = (f32[64,128]{1,0:T(8,128)S(1)}, f32[64,128]{1,0:T(8,128)S(1)}, u32[]{:S(2)}, u32[]{:S(2)}) collective-permute-start(f32[64,128]{1,0:T(8,128)S(1)} %get-tuple-element.62.refs_0_.refs_8_), channel_id=1, source_target_pairs={{0,3},{1,2},{2,1},{3,0},{4,7},{5,6},{6,5},{7,4},{8,11},{9,10},{10,... | collective-permute-start | bytes 98312 | tf_op jit(solution)/shard_map/ppermute | solution.py:773
  100.7 4.2 %collective-permute-start.13 = (f32[64,128]{1,0:T(8,128)S(1)}, f32[64,128]{1,0:T(8,128)S(1)}, u32[]{:S(2)}, u32[]{:S(2)}) collective-permute-start(f32[64,128]{1,0:T(8,128)S(1)} %get-tuple-element.62.refs_0_.refs_8_), channel_id=1, source_target_pairs={{0,2},{1,3},{2,0},{3,1},{4,6},{5,7},{6,4},{7,5},{8,10},{9,11},{10,... | collective-permute-start | bytes 98312 | tf_op jit(solution)/shard_map/ppermute | solution.py:773
  101.5 3.4 %collective-permute-start.12 = (f32[64,128]{1,0:T(8,128)S(1)}, f32[64,128]{1,0:T(8,128)S(1)}, u32[]{:S(2)}, u32[]{:S(2)}) collective-permute-start(f32[64,128]{1,0:T(8,128)S(1)} %get-tuple-element.62.refs_0_.refs_8_), channel_id=1, source_target_pairs={{0,1},{1,0},{2,3},{3,2},{4,5},{5,4},{6,7},{7,6},{8,9},{9,8},{10,11... | collective-permute-start | bytes 98312 | tf_op jit(solution)/shard_map/ppermute | solution.py:773
  103.3 10.6 %collective-permute-start.29 = (f32[4,48,512]{2,1,0:T(8,128)S(1)}, f32[4,48,512]{2,1,0:T(8,128)S(1)}, u32[]{:S(2)}, u32[]{:S(2)}) collective-permute-start(f32[4,48,512]{2,1,0:T(8,128)S(1)} %add.12), channel_id=1, source_target_pairs={{0,2},{1,3},{2,0},{3,1},{4,6},{5,7},{6,4},{7,5},{8,10},{9,11},{10,... | collective-permute-start | bytes 1179656 | tf_op jit(solution)/shard_map/ppermute | solution.py:773
  108.8 1.4 %collective-permute-start.31 = (f32[4,16,512]{2,1,0:T(8,128)S(1)}, f32[4,16,512]{2,1,0:T(8,128)S(1)}, u32[]{:S(2)}, u32[]{:S(2)}) collective-permute-start(f32[4,16,512]{2,1,0:T(8,128)S(1)} %get-tuple-element.87), channel_id=1, source_target_pairs={{0,1},{1,0},{2,3},{3,2},{4,5},{5,4},{6,7},{7,6},{8,9},{9,8},{10,11... | collective-permute-start | bytes 393224 | tf_op jit(solution)/shard_map/ppermute | solution.py:773
  110.2 7.5 %collective-permute-start.32 = (f32[4,16,512]{2,1,0:T(8,128)S(1)}, f32[4,16,512]{2,1,0:T(8,128)S(1)}, u32[]{:S(2)}, u32[]{:S(2)}) collective-permute-start(f32[4,16,512]{2,1,0:T(8,128)S(1)} %add.14), channel_id=1, source_target_pairs={{0,2},{1,3},{2,0},{3,1},{4,6},{5,7},{6,4},{7,5},{8,10},{9,11},{10,... | collective-permute-start | bytes 393224 | tf_op jit(solution)/shard_map/ppermute | solution.py:773
  114.0 8.1 %collective-permute-start.30 = (f32[4,48,512]{2,1,0:T(8,128)S(1)}, f32[4,48,512]{2,1,0:T(8,128)S(1)}, u32[]{:S(2)}, u32[]{:S(2)}) collective-permute-start(f32[4,48,512]{2,1,0:T(8,128)S(1)} %add.13.refs_0_), channel_id=1, source_target_pairs={{0,1},{1,0},{2,3},{3,2},{4,5},{5,4},{6,7},{7,6},{8,9},{9,8},{10,11... | collective-permute-start | bytes 1179656 | tf_op jit(solution)/shard_map/ppermute | solution.py:773
  114.1 4.1 %collective-permute-start.27 = (f32[64,128]{1,0:T(8,128)S(1)}, f32[64,128]{1,0:T(8,128)S(1)}, u32[]{:S(2)}, u32[]{:S(2)}) collective-permute-start(f32[64,128]{1,0:T(8,128)S(1)} %get-tuple-element.81.refs_12_), channel_id=1, source_target_pairs={{0,3},{1,2},{2,1},{3,0},{4,7},{5,6},{6,5},{7,4},{8,11},{9,10},{10,... | collective-permute-start | bytes 98312 | tf_op jit(solution)/shard_map/ppermute | solution.py:773
  115.8 3.9 %collective-permute-start.26 = (f32[64,128]{1,0:T(8,128)S(1)}, f32[64,128]{1,0:T(8,128)S(1)}, u32[]{:S(2)}, u32[]{:S(2)}) collective-permute-start(f32[64,128]{1,0:T(8,128)S(1)} %get-tuple-element.81.refs_12_), channel_id=1, source_target_pairs={{0,2},{1,3},{2,0},{3,1},{4,6},{5,7},{6,4},{7,5},{8,10},{9,11},{10,... | collective-permute-start | bytes 98312 | tf_op jit(solution)/shard_map/ppermute | solution.py:773
  116.3 3.4 %collective-permute-start.25 = (f32[64,128]{1,0:T(8,128)S(1)}, f32[64,128]{1,0:T(8,128)S(1)}, u32[]{:S(2)}, u32[]{:S(2)}) collective-permute-start(f32[64,128]{1,0:T(8,128)S(1)} %get-tuple-element.81.refs_12_), channel_id=1, source_target_pairs={{0,1},{1,0},{2,3},{3,2},{4,5},{5,4},{6,7},{7,6},{8,9},{9,8},{10,11... | collective-permute-start | bytes 98312 | tf_op jit(solution)/shard_map/ppermute | solution.py:773
  117.7 4.4 %collective-permute-start.33 = (f32[4,16,512]{2,1,0:T(8,128)S(1)}, f32[4,16,512]{2,1,0:T(8,128)S(1)}, u32[]{:S(2)}, u32[]{:S(2)}) collective-permute-start(f32[4,16,512]{2,1,0:T(8,128)S(1)} %add.15.refs_2_), channel_id=1, source_target_pairs={{0,1},{1,0},{2,3},{3,2},{4,5},{5,4},{6,7},{7,6},{8,9},{9,8},{10,11... | collective-permute-start | bytes 393224 | tf_op jit(solution)/shard_map/ppermute | solution.py:773

commit v4 on v3

v4 whole, which is shorter than its diff:
```python
import functools

import jax
import jax.numpy as jnp
from jax import lax
from jax.experimental import pallas as pl
from jax.experimental.pallas import tpu as pltpu
from jax.sharding import PartitionSpec as P

GRID = 24
PLANE = GRID * GRID
WIDE = 640
UNROLL = 12
CHUNKS = (4, 4, 4)
K = 16
NMOVE = 4
MOVED = K * NMOVE
CAP = 1
TAU = 0.25
ROOT_TAU = 0.5
F32 = jnp.float32
BF16 = jnp.bfloat16
LEVELS = 32767.0
HIGHEST = lax.Precision.HIGHEST
VMEM = pl.BlockSpec(memory_space=pltpu.VMEM)
SMEM = pl.BlockSpec(memory_space=pltpu.SMEM)
ANY = pl.BlockSpec(memory_space=pl.ANY)
LIMIT = 16 * 2**20
WHOLE = 60 * 2**20
PART = 59500000


def axis_weights(u, with_slopes):
    floors = jnp.floor(u)
    t = u - floors
    remain = 1.0 - t
    square = t * t
    cubed = square * t
    values = (
        remain * remain * remain / 6.0,
        (3.0 * cubed - 6.0 * square + 4.0) / 6.0,
        (-3.0 * cubed + 3.0 * square + 3.0 * t + 1.0) / 6.0,
        cubed / 6.0,
    )
    lanes = u.shape[1]
    line = lax.broadcasted_iota(jnp.int32, (GRID, lanes), 0)
    step = line - (floors.astype(jnp.int32) - 1)
    step = jnp.where(step < 0, step + GRID, step)
    step = jnp.where(step < 0, step + GRID, step)
    step = jnp.where(step >= GRID, step - GRID, step)

    def spread(weights):
        out = jnp.zeros((GRID, lanes), F32)
        for a in range(4):
            out = jnp.where(step == a, jnp.broadcast_to(weights[a], (GRID, lanes)), out)
        return out

    if not with_slopes:
        return spread(values), None
    slopes = (
        -0.5 * remain * remain,
        1.5 * square - 2.0 * t,
        -1.5 * square + t + 0.5,
        0.5 * square,
    )
    return spread(values), spread(slopes)


def halves(first, second):
    product = jnp.concatenate([first[y : y + 1, :] * second for y in range(GRID)], axis=0)
    high = product.astype(BF16)
    return [high, (product - high.astype(F32)).astype(BF16)]


def fill(even_ref, odd_ref, pieces):
    lanes = pieces[0].shape[1]
    pad = jnp.zeros((WIDE - PLANE, lanes), BF16)
    for i, piece in enumerate(pieces):
        at = slice(i * lanes, (i + 1) * lanes)
        even_ref[0:PLANE, at] = piece
        even_ref[PLANE:WIDE, at] = pad
        odd_ref[0 : WIDE - PLANE, at] = pad
        odd_ref[WIDE - PLANE : WIDE, at] = piece


def plane_pair(table_ref, pair, even_ref, odd_ref):
    start = pl.multiple_of(pair * 2 * PLANE, 128)
    even = table_ref[:, pl.ds(start, WIDE)]
    start = pl.multiple_of(pair * 2 * PLANE + 2 * PLANE - WIDE, 128)
    odd = table_ref[:, pl.ds(start, WIDE)]
    return (
        jnp.dot(even, even_ref[...], preferred_element_type=F32),
        jnp.dot(odd, odd_ref[...], preferred_element_type=F32),
    )


def slopes_kernel(
    state_ref, table_ref, phi_ref, grad_ref, even_ref, odd_ref, wx_ref, sx_ref, loads=()
):
    n = state_ref.shape[2]
    wx, sx = axis_weights(state_ref[0, 0:1, :], True)
    wy, sy = axis_weights(state_ref[0, 1:2, :], True)
    wz, sz = axis_weights(state_ref[0, 2:3, :], True)
    wx_ref[...] = wx
    sx_ref[...] = sx
    fill(even_ref, odd_ref, halves(wy, wz) + halves(sy, wz) + halves(wy, sz))
    phi_ref[...] = jnp.zeros_like(phi_ref)
    grad_ref[...] = jnp.zeros_like(grad_ref)

    def body(pair, carry):
        even, odd = plane_pair(table_ref, pair, even_ref, odd_ref)
        w0, w1 = wx_ref[pl.ds(2 * pair, 1), :], wx_ref[pl.ds(2 * pair + 1, 1), :]
        s0, s1 = sx_ref[pl.ds(2 * pair, 1), :], sx_ref[pl.ds(2 * pair + 1, 1), :]

        def both(i):
            at, to = slice(2 * i * n, (2 * i + 1) * n), slice((2 * i + 1) * n, (2 * i + 2) * n)
            return even[:, at] + even[:, to], odd[:, at] + odd[:, to]

        e, o = both(0)
        phi_ref[...] += w0 * e + w1 * o
        grad_ref[:, 0:n] += s0 * e + s1 * o
        for d in (1, 2):
            e, o = both(d)
            grad_ref[:, d * n : (d + 1) * n] += w0 * e + w1 * o
        return carry

    pairs = GRID // 2
    if loads:
        start = 0
        for i, (load, size) in enumerate(zip(loads, CHUNKS)):
            load.wait()
            if i + 1 < len(loads):
                loads[i + 1].start()
            lax.fori_loop(start, start + size, body, 0, unroll=size)
            start += size
    else:
        lax.fori_loop(0, pairs, body, 0, unroll=UNROLL)


def first_kernel(states_ref, table_ref, phi_out, grad_out, held_ref, phi_ref, grad_ref, *refs):
    scratch, (in_sem, out_sem) = refs[:-2], refs[-2:]
    loads = []
    start = 0
    for i, pairs in enumerate(CHUNKS):
        at = pl.ds(start, 2 * PLANE * pairs)
        start += 2 * PLANE * pairs
        loads.append(
            pltpu.make_async_copy(table_ref.at[:, at], held_ref.at[:, at], in_sem.at[i])
        )
    loads[0].start()
    slopes_kernel(states_ref.at[0:1], held_ref, phi_ref, grad_ref, *scratch, loads=loads)
    stores = [
        pltpu.make_async_copy(phi_ref, phi_out, out_sem.at[0]),
        pltpu.make_async_copy(grad_ref, grad_out, out_sem.at[1]),
    ]
    for store in stores:
        store.start()
    for store in stores:
        store.wait()


def slopes_call(states, table):
    orbitals = table.shape[0]
    n = states.shape[2]
    shapes = [(orbitals, n), (orbitals, 3 * n)]
    return pl.pallas_call(
        first_kernel,
        name="slopes",
        out_shape=tuple(jax.ShapeDtypeStruct(shape, F32) for shape in shapes),
        in_specs=[VMEM, ANY],
        out_specs=(ANY, ANY),
        scratch_shapes=[pltpu.VMEM(table.shape, BF16)]
        + [pltpu.VMEM(shape, F32) for shape in shapes]
        + slopes_scratch(n)
        + [pltpu.SemaphoreType.DMA((len(CHUNKS),)), pltpu.SemaphoreType.DMA((2,))],
        compiler_params=params(WHOLE),
        cost_estimate=lasting(5),
    )(states, table)


def slopes_scratch(n):
    return [
        pltpu.VMEM((WIDE, 6 * n), BF16),
        pltpu.VMEM((WIDE, 6 * n), BF16),
        pltpu.VMEM((GRID, n), F32),
        pltpu.VMEM((GRID, n), F32),
    ]


def later_kernel(block, states_ref, table_ref, vm_ref, phi_ref, out_ref, grad_ref, *scratch):
    slopes_kernel(states_ref.at[block : block + 1], table_ref, phi_ref, grad_ref, *scratch)
    drift_rows(block, vm_ref, grad_ref, out_ref, 0)


def later_call(block, states, table, vm):
    orbitals = table.shape[0]
    n = states.shape[2]
    return pl.pallas_call(
        functools.partial(later_kernel, block),
        name="later",
        out_shape=(
            jax.ShapeDtypeStruct((orbitals, n), F32),
            jax.ShapeDtypeStruct((drift_size(block), n), F32),
        ),
        in_specs=[VMEM] * 3,
        out_specs=(VMEM, VMEM),
        scratch_shapes=[pltpu.VMEM((orbitals, 3 * n), F32)] + slopes_scratch(n),
        compiler_params=params(),
        cost_estimate=lasting(5),
    )(states, table, vm)


def split(x):
    high = x.astype(BF16)
    return high, (x - high.astype(F32)).astype(BF16)


def product(a, b, dims):
    (a0, a1), (b0, b1) = split(a), split(b)

    def one(x, y):
        return lax.dot_general(x, y, (dims, ((), ())), preferred_element_type=F32)

    return one(a0, b0) + (one(a0, b1) + one(a1, b0))


def dot(a, b):
    return product(a, b, ((1,), (0,)))


def dot_nt(a, b):
    return product(a, b, ((1,), (1,)))


def own_lanes(n, walker):
    lane = lax.broadcasted_iota(jnp.int32, (MOVED, n), 1)
    return jnp.logical_and(lane >= walker * K, lane < (walker + 1) * K)


def fold(big):
    n = big.shape[1]
    total = jnp.zeros((MOVED, n), F32)
    for w in range(n // K):
        total = jnp.where(own_lanes(n, w), big[w * MOVED : (w + 1) * MOVED, :], total)
    return total


def unit(block, n):
    row = lax.broadcasted_iota(jnp.int32, (MOVED, n), 0)
    lane = lax.broadcasted_iota(jnp.int32, (MOVED, n), 1)
    return jnp.where(row - block * K == lane % K, 1.0, 0.0).astype(F32)


def tree(parts):
    while len(parts) > 1:
        parts = [parts[i] + parts[i + 1] for i in range(0, len(parts), 2)]
    return parts[0]


def total(refs):
    return tree([ref[...] for ref in refs])


def params(limit=LIMIT):
    return pltpu.CompilerParams(vmem_limit_bytes=limit)


def lasting(us):
    return pl.CostEstimate(flops=int(us * 1e8), bytes_accessed=0, transcendentals=0)


def parent_of(meta_ref, walkers, w):
    parent = meta_ref[w]
    group = parent // walkers
    here = group == meta_ref[walkers + NMOVE]
    return here, jnp.where(here, parent % walkers, 0), jnp.where(here, 0, group)


def block_lanes(x, block):
    lane = lax.broadcasted_iota(jnp.int32, x.shape, 1)
    kept = jnp.where(lane // K == block, x, 0.0)
    return tree([kept[:, i : i + 128] for i in range(0, x.shape[1], 128)])


def roll(x, shift):
    if isinstance(shift, int):
        shift = shift % 128
        return x if shift == 0 else pltpu.roll(x, shift, 1)
    return pltpu.roll(x, lax.rem(shift + 1024, 128), 1)


def moved_lanes(x, order_ref):
    line = jnp.zeros((x.shape[0], 128), F32)
    for b in range(NMOVE):
        block = order_ref[b]
        line = line + roll(block_lanes(x, block), (b - block) * K)
    return line


def pack_kernel(parent_ref, order_ref, *refs):
    (out_ref, pos_ref, gauss_ref, acc_ref), sem = refs[3:-1], refs[-1]
    copies = [
        pltpu.make_async_copy(refs[i], refs[i + 4], sem.at[i]) for i in range(3)
    ]
    for copy in copies:
        copy.start()
    for copy in copies:
        copy.wait()
    walkers = pos_ref.shape[1]
    half = jnp.zeros((walkers, 128 - MOVED), F32)
    lane = lax.broadcasted_iota(jnp.int32, (walkers, 128), 1)
    row = lax.broadcasted_iota(jnp.int32, (walkers, 128), 0)
    lines = []
    for d in range(3):
        line = moved_lanes(pos_ref[d], order_ref)
        lines.append(line + jnp.concatenate([half, gauss_ref[d]], axis=1))
    parents = jnp.zeros((walkers, 128), jnp.int32)
    for w in range(walkers):
        parents = jnp.where(row == w, parent_ref[w], parents)
    decided = jnp.concatenate([acc_ref[...].astype(F32), half], axis=1)
    lines.append(jnp.where(lane < MOVED, decided, parents.astype(F32)))
    for g in range(out_ref.shape[0]):
        for d in range(4):
            out_ref[g, d * walkers : (d + 1) * walkers, :] = lines[d]


def pack_call(parent, order, positions, gaussian, accepted, groups):
    walkers = positions.shape[1]
    held = [positions, gaussian, accepted]
    return pl.pallas_call(
        pack_kernel,
        name="pack",
        out_shape=jax.ShapeDtypeStruct((groups, 4 * walkers, 128), F32),
        in_specs=[SMEM, SMEM, ANY, ANY, ANY],
        out_specs=VMEM,
        scratch_shapes=[pltpu.VMEM(x.shape, x.dtype) for x in held]
        + [pltpu.SemaphoreType.DMA((3,))],
        compiler_params=params(WHOLE),
        cost_estimate=lasting(1),
    )(parent, order, *held)


def columns_kernel(order_ref, v_in, pos_in, own_out, code_out, v_ref, pos_ref, own_ref, code_ref, sem):
    walkers, orbitals, electrons = v_ref.shape

    def load(w):
        return pltpu.make_async_copy(v_in.at[w], v_ref.at[w], sem.at[0, w])

    def store(w):
        return (
            pltpu.make_async_copy(own_ref.at[w], own_out.at[w], sem.at[1, w]),
            pltpu.make_async_copy(code_ref.at[w], code_out.at[w], sem.at[2, w]),
        )

    first = pltpu.make_async_copy(pos_in, pos_ref, sem.at[0, walkers])
    first.start()
    for w in range(walkers):
        load(w).start()
    first.wait()

    def body(w, carry):
        load(w).wait()
        v = v_ref[w]
        own_ref[w, 0:MOVED, :] = jnp.transpose(moved_lanes(v, order_ref))[0:MOVED, :]
        size = jnp.abs(v)
        scale = jnp.max(size, axis=0, keepdims=True)
        at = MOVED
        for line in [scale] + [pos_ref[d, pl.ds(w, 1), :] for d in range(3)]:
            for i in range(0, electrons, orbitals):
                own_ref[w, at : at + 1, :] = line[:, i : i + orbitals]
                at += 1
        some = scale > 0.0
        step = jnp.where(some, LEVELS / jnp.sqrt(jnp.where(some, scale, 1.0)), 0.0)
        level = jnp.minimum(jnp.floor(jnp.sqrt(size) * step + 0.5), LEVELS)
        code_ref[w] = jnp.where(v < 0.0, -level, level).astype(jnp.int32).astype(jnp.int16)
        for copy in store(w):
            copy.start()
        return carry

    lax.fori_loop(0, walkers, body, 0)
    for w in range(walkers):
        for copy in store(w):
            copy.wait()


def payload_rows(orbitals, electrons):
    return MOVED + 4 * electrons // orbitals


def columns_call(order, inverse, positions):
    walkers, orbitals, electrons = inverse.shape
    own = (walkers, payload_rows(orbitals, electrons), orbitals)
    return pl.pallas_call(
        columns_kernel,
        name="columns",
        out_shape=(
            jax.ShapeDtypeStruct(own, F32),
            jax.ShapeDtypeStruct(inverse.shape, jnp.int16),
        ),
        in_specs=[SMEM, ANY, ANY],
        out_specs=(ANY, ANY),
        scratch_shapes=[
            pltpu.VMEM(inverse.shape, F32),
            pltpu.VMEM(positions.shape, F32),
            pltpu.VMEM(own, F32),
            pltpu.VMEM(inverse.shape, jnp.int16),
            pltpu.SemaphoreType.DMA((3, walkers + 1)),
        ],
        compiler_params=params(WHOLE),
        cost_estimate=lasting(3),
    )(order, inverse, positions)


def route_kernel(meta_ref, info_in, own_in, code_in, states_ref, out_ref, outcode_ref, *refs):
    info_ref, own_ref, code_ref, parents_ref, sem, out_sem = refs
    walkers = own_ref.shape[0]
    groups = out_ref.shape[0]
    rows = 3 * walkers
    asked = []
    for g in range(groups):
        at = pl.ds(rows, walkers)
        asked.append(pltpu.make_async_copy(info_in.at[g, at], parents_ref.at[g], sem.at[3]))
    for each in asked:
        each.start()
    loads = [
        pltpu.make_async_copy(info_in, info_ref, sem.at[0]),
        pltpu.make_async_copy(own_in, own_ref, sem.at[1]),
        pltpu.make_async_copy(code_in, code_ref, sem.at[2]),
    ]
    for load in loads:
        load.start()
    for each in asked:
        each.wait()
    me = meta_ref[walkers + NMOVE]
    sending = []
    for g in range(groups):
        wanted = jnp.int32(0)
        for s in range(walkers):
            within = parents_ref[g, s, MOVED].astype(jnp.int32) - me * walkers
            mine = jnp.logical_and(within >= 0, within < walkers)
            wanted = jnp.where(mine, within, wanted)
        sending.append(jnp.where(me == g, 0, wanted))
    for load in loads[1:]:
        load.wait()
    stores = []
    for g in range(groups):
        source = sending[g]
        stores.append(pltpu.make_async_copy(own_ref.at[source], out_ref.at[g], out_sem.at[0, g]))
        stores.append(
            pltpu.make_async_copy(code_ref.at[source], outcode_ref.at[g], out_sem.at[1, g])
        )
    for store in stores:
        store.start()
    loads[0].wait()
    lane = lax.broadcasted_iota(jnp.int32, (8, 128), 1)
    tiles = []
    for w in range(walkers):
        group, place = meta_ref[w] // walkers, meta_ref[w] % walkers
        line = [info_ref[group, pl.ds(d * walkers + place, 1), :] for d in range(4)]
        line = jnp.concatenate(line, axis=0)
        tiles.append(jnp.concatenate([line, roll(line, 128 - MOVED)], axis=0))
    for b in range(NMOVE):
        state = jnp.zeros((8, 128), F32)
        for w in range(walkers):
            state = jnp.where(lane // K == w, roll(tiles[w], (w - b) * K), state)
        states_ref[b] = state
    for store in stores:
        store.wait()


def route_call(meta, info, own, code):
    groups = info.shape[0]
    shapes = [(groups, *own.shape[1:]), (groups, *code.shape[1:])]
    return pl.pallas_call(
        route_kernel,
        name="route",
        out_shape=(
            jax.ShapeDtypeStruct((NMOVE, 8, 128), F32),
            jax.ShapeDtypeStruct(shapes[0], F32),
            jax.ShapeDtypeStruct(shapes[1], code.dtype),
        ),
        in_specs=[SMEM, ANY, ANY, ANY],
        out_specs=(VMEM, ANY, ANY),
        scratch_shapes=[
            pltpu.VMEM(info.shape, F32),
            pltpu.VMEM(own.shape, F32),
            pltpu.VMEM(code.shape, code.dtype),
            pltpu.SMEM((groups, own.shape[0], 128), F32),
            pltpu.SemaphoreType.DMA((4,)),
            pltpu.SemaphoreType.DMA((2, groups)),
        ],
        compiler_params=params(WHOLE),
        cost_estimate=lasting(3),
    )(meta, info, own, code)


def select_kernel(meta_ref, own_ref, got_ref, grad_in, vm_ref, out_ref, grad_ref, sem):
    walkers = own_ref.shape[0]
    load = pltpu.make_async_copy(grad_in, grad_ref, sem.at[walkers])
    load.start()

    def copy(w, source):
        to = vm_ref.at[w * MOVED : (w + 1) * MOVED]
        return pltpu.make_async_copy(source.at[0:MOVED], to, sem.at[w])

    for w in range(walkers):
        here, place, group = parent_of(meta_ref, walkers, w)

        @pl.when(here)
        def _():
            copy(w, own_ref.at[place]).start()

        @pl.when(jnp.logical_not(here))
        def _():
            copy(w, got_ref.at[group]).start()

    for w in range(walkers):
        copy(w, own_ref.at[0]).wait()
    load.wait()
    drift_rows(0, vm_ref, grad_ref, out_ref, 0)


def drift_size(block):
    return 8 + 3 * K * block


def drift_rows(block, vm_ref, grad_ref, out_ref, at):
    n = grad_ref.shape[1] // 3
    size = K * block
    out_ref[at + 3 : at + 8, :] = jnp.zeros((5, n), F32)
    for d in range(3):
        q = fold(dot(vm_ref[...], grad_ref[:, d * n : (d + 1) * n]))
        out_ref[at + d : at + d + 1, :] = jnp.sum(q * unit(block, n), axis=0, keepdims=True)
        if block:
            out_ref[at + 8 + d * size : at + 8 + (d + 1) * size, :] = q[0:size, :]


def drift_of(block, q, t):
    size = K * block
    lines = [q[0:3, :]]
    if block:
        lines[0] += jnp.concatenate(
            [
                jnp.sum(q[8 + d * size : 8 + (d + 1) * size, :] * t[0:size, :], axis=0)[None]
                for d in range(3)
            ],
            axis=0,
        )
    return lines[0]


def select_call(meta, own, got, grad):
    walkers, _, orbitals = own.shape
    n = grad.shape[1] // 3
    return pl.pallas_call(
        select_kernel,
        name="select",
        out_shape=(
            jax.ShapeDtypeStruct((walkers * MOVED, orbitals), F32),
            jax.ShapeDtypeStruct((drift_size(0), n), F32),
        ),
        in_specs=[SMEM, ANY, ANY, ANY],
        out_specs=(VMEM, VMEM),
        scratch_shapes=[
            pltpu.VMEM(grad.shape, F32),
            pltpu.SemaphoreType.DMA((walkers + 1,)),
        ],
        compiler_params=params(PART),
        cost_estimate=lasting(2),
    )(meta, own, got, grad)


def spread(x):
    n = x.shape[1]
    return jnp.concatenate([jnp.where(own_lanes(n, w), x, 0.0) for w in range(n // K)], axis=0)


def step_kernel(block, count, *refs):
    refs = list(refs)
    parts = [refs.pop(0) for _ in range(count)]
    later_ref = refs.pop(0) if block < NMOVE - 1 else None
    if block:
        t_before = refs.pop(0)
    if block > 1:
        y_before = refs.pop(0)
    states_ref, phi_ref, vm_ref, table_ref = [refs.pop(0) for _ in range(4)]
    s_ref, moved_ref, d_ref, t_ref = [refs.pop(0) for _ in range(4)]
    y_ref = refs.pop(0) if block else None
    sum_ref, big_ref, even_ref, odd_ref, wx_ref = refs
    if later_ref is not None:
        s_ref[MOVED:, :] = later_ref[...]
    n = sum_ref.shape[1]
    state = states_ref[block]
    if block == 0:
        t_ref[...] = unit(0, n)
        drifts = drift_of(0, total(parts), None)
    else:
        s = tree([ref[0:MOVED, :] for ref in parts])
        if block > 1:
            s_ref[0:MOVED, :] = s
            big_ref[...] = dot(y_before[...], s_ref[0:MOVED, :])
            s = s - fold(big_ref[...])
        s_ref[0:MOVED, :] = s
        y_all = dot_nt(spread(s_ref[0:MOVED, :]), t_before[...])
        if block > 1:
            y_all = y_all + y_before[...]
        y_ref[...] = y_all
        rows = jnp.concatenate(
            [
                y_ref[w * MOVED + block * K : w * MOVED + (block + 1) * K, :]
                for w in range(n // K)
            ],
            axis=0,
        )
        t_ref[...] = unit(block, n) - jnp.transpose(rows)
        q = tree([ref[MOVED:, :] for ref in parts])
        drifts = drift_of(block, q, t_ref[...])
    speeds = jnp.sum(drifts * drifts, axis=0, keepdims=True)
    capped = drifts / jnp.sqrt(1.0 + TAU * speeds)
    moved = state[0:3, :] + state[3:4, :] * (TAU * capped + ROOT_TAU * state[4:7, :])
    moved_ref[0:3, :] = moved
    moved_ref[3:8, :] = jnp.zeros((5, n), F32)
    wx, _ = axis_weights(moved[0:1, :], False)
    wy, _ = axis_weights(moved[1:2, :], False)
    wz, _ = axis_weights(moved[2:3, :], False)
    wx_ref[...] = wx
    fill(even_ref, odd_ref, halves(wy, wz))
    sum_ref[...] = jnp.zeros_like(sum_ref)

    def body(pair, carry):
        even, odd = plane_pair(table_ref, pair, even_ref, odd_ref)
        w0, w1 = wx_ref[pl.ds(2 * pair, 1), :], wx_ref[pl.ds(2 * pair + 1, 1), :]
        sum_ref[...] += w0 * (even[:, 0:n] + even[:, n:]) + w1 * (odd[:, 0:n] + odd[:, n:])
        return carry

    lax.fori_loop(0, GRID // 2, body, 0, unroll=UNROLL)
    change = sum_ref[...] - phi_ref[...]
    d_ref[...] = jnp.transpose(change)
    s_ref[0:MOVED, :] = fold(dot(vm_ref[...], change))


def step_call(block, parts, later, carried, states, phi, vm, table):
    orbitals, n = table.shape[0], states.shape[2]
    rows = vm.shape[0]
    operands = [*parts, *later, *carried, states, phi, vm, table]
    sums = (MOVED + later[0].shape[0] if later else MOVED, n)
    shapes = [sums, (8, n), (n, orbitals), (MOVED, n)] + [(rows, MOVED)] * (block > 0)
    return pl.pallas_call(
        functools.partial(step_kernel, block, len(parts)),
        name="step",
        out_shape=tuple(jax.ShapeDtypeStruct(shape, F32) for shape in shapes),
        in_specs=[VMEM] * len(operands),
        out_specs=(VMEM,) * len(shapes),
        scratch_shapes=[
            pltpu.VMEM((orbitals, n), F32),
            pltpu.VMEM((rows, n), F32),
            pltpu.VMEM((WIDE, 2 * n), BF16),
            pltpu.VMEM((WIDE, 2 * n), BF16),
            pltpu.VMEM((GRID, n), F32),
        ],
        compiler_params=params(),
        cost_estimate=lasting(3),
    )(*operands)


def last_kernel(counts, *refs):
    refs = list(refs)
    sums = [[refs.pop(0) for _ in range(count)] for count in counts]
    ts = [refs.pop(0)[...] for _ in range(NMOVE)]
    vm_ref, out_ref, l_ref = refs
    for block in range(NMOVE - 1):
        r = unit(block, ts[block].shape[1])
        if block:
            sums_of = tree([ref[0:MOVED, :] for ref in sums[block - 1]])
            r = r - fold(dot(l_ref[...], sums_of))
        more = dot_nt(spread(r), ts[block])
        l_ref[...] = l_ref[...] + more if block else more
    t = jnp.transpose(ts[-1])
    for w in range(out_ref.shape[0]):
        at = slice(w * MOVED, (w + 1) * MOVED)
        early = l_ref[w * MOVED : (w + 1) * MOVED - K, :]
        factor = jnp.concatenate([early, t[w * K : (w + 1) * K, :]], axis=0)
        out_ref[w] = jnp.transpose(dot(factor, vm_ref[at, :]))


def last_call(s_parts, ts, vm):
    rows, orbitals = vm.shape
    operands = [part for parts in s_parts for part in parts] + list(ts) + [vm]
    return pl.pallas_call(
        functools.partial(last_kernel, [len(parts) for parts in s_parts]),
        name="last",
        out_shape=(
            jax.ShapeDtypeStruct((rows // MOVED, orbitals, MOVED), F32),
            jax.ShapeDtypeStruct((rows, MOVED), F32),
        ),
        in_specs=[VMEM] * len(operands),
        out_specs=(VMEM, VMEM),
        compiler_params=params(),
        cost_estimate=lasting(2),
    )(*operands)


def both_halves(meta_ref, walkers, i):
    parity = meta_ref[meta_ref.shape[0] - 1]
    half = walkers // 2
    return i + half * parity, i + half * (1 - parity)


def assemble_kernel(meta_ref, own_ref, got_ref, code_ref, *refs):
    change_refs = refs[: NMOVE - 1]
    v_ref, mine_ref, give_ref, held_ref, sem = refs[NMOVE - 1 :]
    walkers, orbitals, electrons = own_ref.shape
    load = pltpu.make_async_copy(code_ref, held_ref, sem)
    load.start()
    load.wait()

    def body(i, carry):
        for w, out_ref in zip(both_halves(meta_ref, walkers, i), (mine_ref, give_ref)):
            here, place, group = parent_of(meta_ref, walkers, w)
            scale = jnp.concatenate(
                [
                    got_ref[group, MOVED + j : MOVED + j + 1, :]
                    for j in range(electrons // orbitals)
                ],
                axis=1,
            )
            level = held_ref[group].astype(jnp.int32).astype(F32) * (1.0 / LEVELS)
            v = jnp.where(here, own_ref[place], level * jnp.abs(level) * scale)
            v_ref[w] = v
            at = pl.ds(pl.multiple_of(w * K, K), K)
            change = jnp.concatenate([ref[at, :] for ref in change_refs], axis=0)
            out_ref[i] = dot(change, v)
        return carry

    lax.fori_loop(0, walkers // 2, body, 0)


def assemble_call(meta, inverse, got, code, changes):
    walkers, orbitals, electrons = inverse.shape
    half = (walkers // 2, (NMOVE - 1) * K, electrons)
    return pl.pallas_call(
        assemble_kernel,
        name="assemble",
        out_shape=(
            jax.ShapeDtypeStruct(inverse.shape, F32),
            jax.ShapeDtypeStruct(half, F32),
            jax.ShapeDtypeStruct(half, F32),
        ),
        in_specs=[SMEM, VMEM, VMEM, ANY] + [VMEM] * len(changes),
        out_specs=(VMEM,) * 3,
        scratch_shapes=[
            pltpu.VMEM(code.shape, code.dtype),
            pltpu.SemaphoreType.DMA(()),
        ],
        compiler_params=params(),
        cost_estimate=lasting(4),
    )(meta, inverse, got, code, *changes)


def sums_kernel(meta_ref, v_ref, change_ref, mine_ref, give_ref):
    walkers = v_ref.shape[0]

    def body(i, carry):
        for w, out_ref in zip(both_halves(meta_ref, walkers, i), (mine_ref, give_ref)):
            at = pl.ds(pl.multiple_of(w * K, K), K)
            out_ref[i] = dot(change_ref[at, :], v_ref[w])
        return carry

    lax.fori_loop(0, walkers // 2, body, 0)


def sums_call(meta, inverse, change):
    walkers, _, electrons = inverse.shape
    half = jax.ShapeDtypeStruct((walkers // 2, K, electrons), F32)
    return pl.pallas_call(
        sums_kernel,
        name="sums",
        out_shape=(half, half),
        in_specs=[SMEM, VMEM, VMEM],
        out_specs=(VMEM, VMEM),
        compiler_params=params(),
        cost_estimate=lasting(1),
    )(meta, inverse, change)


def update_kernel(order_ref, meta_ref, v_ref, factor_ref, l_ref, *refs):
    sums_refs, (out_ref, new_ref, sem) = refs[:4], refs[4:]
    walkers = v_ref.shape[0]

    def store(w):
        return pltpu.make_async_copy(new_ref.at[w], out_ref.at[w], sem.at[w])

    half = walkers // 2
    own = [both_halves(meta_ref, walkers, i) for i in range(half)]
    places = [(own[i][h], i, sums_refs[2 * h : 2 * h + 2]) for i in range(half) for h in range(2)]
    lates = []
    for w, i, (early_ref, late_ref) in places:
        moved = moved_lanes(late_ref[i], order_ref)[:, 0:MOVED]
        rows = l_ref[pl.ds(pl.multiple_of(w * MOVED, MOVED), MOVED), :]
        lates.append(dot_nt(moved, rows)[:, 0 : MOVED - K])
    for n, (w, i, (early_ref, late_ref)) in enumerate(places):
        lates[n] = late_ref[i] - dot(lates[n], early_ref[i])
    for late, (w, i, (early_ref, _)) in zip(lates, places):
        sums = jnp.concatenate([early_ref[i], late], axis=0)
        new_ref[w] = v_ref[w] - dot(factor_ref[w], sums)
        store(w).start()
    for w in range(walkers):
        store(w).wait()


def update_call(order, meta, inverse, factor, rows, sums):
    return pl.pallas_call(
        update_kernel,
        name="update",
        out_shape=jax.ShapeDtypeStruct(inverse.shape, F32),
        in_specs=[SMEM] * 2 + [VMEM] * 7,
        out_specs=ANY,
        scratch_shapes=[
            pltpu.VMEM(inverse.shape, F32),
            pltpu.SemaphoreType.DMA((inverse.shape[0],)),
        ],
        compiler_params=params(),
        cost_estimate=lasting(2),
    )(order, meta, inverse, factor, rows, *sums)


def place_kernel(meta_ref, own_ref, got_ref, *refs):
    out_ref = refs[NMOVE]
    _, walkers, electrons = own_ref.shape
    parts = electrons // got_ref.shape[2]
    lane = lax.broadcasted_iota(jnp.int32, (1, electrons), 1)
    for w in range(walkers):
        here, place, group = parent_of(meta_ref, walkers, w)
        fresh = []
        for b in range(NMOVE):
            block = meta_ref[walkers + b]
            fresh.append((block, roll(refs[b][...], (block - w) * K)))
        for d in range(3):
            at = MOVED + (d + 1) * parts
            far = jnp.concatenate(
                [got_ref[group, at + i : at + i + 1, :] for i in range(parts)], axis=1
            )
            line = jnp.where(here, own_ref[d, pl.ds(place, 1), :], far)
            for block, moved in fresh:
                moved = jnp.concatenate([moved[d : d + 1, :]] * (electrons // 128), axis=1)
                line = jnp.where(lane // K == block, moved, line)
            out_ref[d, w : w + 1, :] = line


def place_call(meta, positions, got, moved):
    return pl.pallas_call(
        place_kernel,
        name="place",
        out_shape=jax.ShapeDtypeStruct(positions.shape, F32),
        in_specs=[SMEM] + [VMEM] * (2 + NMOVE),
        out_specs=VMEM,
        compiler_params=params(),
        cost_estimate=lasting(1),
    )(meta, positions, got, *moved)


def swap(x, axis, k):
    return lax.ppermute(x, axis, [(i, i ^ k) for i in range(lax.axis_size(axis))])


def exchange(part, axis):
    return [part] + [swap(part, axis, k) for k in range(1, lax.axis_size(axis))]


def add_up(mine, axis, done):
    k = 2
    while k < lax.axis_size(axis):
        *others, done = together(*[swap(x, axis, k) for x in mine], done)
        mine = [x + other for x, other in zip(mine, others)]
        k *= 2
    return [(x, swap(x, axis, 1)) for x in mine], done


def together(*values):
    return lax.optimization_barrier(values)


def alltoall(x):
    return lax.all_to_all(x, "walker", split_axis=0, concat_axis=0, tiled=True)


def local(positions, inverse, spline_table, gaussian, accepted, block_order, parent):
    groups = lax.axis_size("walker")
    me = lax.axis_index("walker").astype(jnp.int32)
    parity = lax.rem(lax.axis_index("orb"), 2).astype(jnp.int32)
    meta = jnp.concatenate([parent, block_order[:NMOVE], me[None], parity[None]])
    positions = jnp.transpose(positions, (1, 0, 2))
    gaussian = jnp.transpose(gaussian, (1, 0, 2))

    info = alltoall(pack_call(parent, block_order, positions, gaussian, accepted, groups))
    own, code = columns_call(block_order, inverse, positions)
    states, outgoing, code = route_call(meta, info, own, code)
    got = alltoall(outgoing)
    phi, grad = slopes_call(states, spline_table)
    got, code, phi, grad = together(got, code, phi, grad)
    code = alltoall(code)
    vm, first = select_call(meta, own, got, grad)
    p0 = exchange(first, "orb")

    def step(b, parts, later, carried, phi):
        return step_call(b, parts, later, carried, states, phi, vm, spline_table)

    phi1, later1 = later_call(1, states, spline_table, vm)
    p1, new0, change0, t0 = step(0, p0, [later1], [], phi)
    p1 = exchange(p1, "orb")
    phi2, later2 = later_call(2, states, spline_table, vm)
    p2, new1, change1, t1, y = step(1, p1, [later2], [t0], phi1)
    p2 = exchange(p2, "orb")
    phi3, later3 = later_call(3, states, spline_table, vm)
    p3, new2, change2, t2, y = step(2, p2, [later3], [t1, y], phi2)
    p3 = exchange(p3, "orb")
    whole, mine, give = assemble_call(meta, inverse, got, code, [change0, change1, change2])
    p3, mine, give = together(p3, mine, give)
    early = mine + swap(give, "orb", 1)
    _, new3, change3, t3, _ = step(3, p3, [], [t2, y], phi3)
    mine, give = sums_call(meta, whole, change3)
    late = mine + swap(give, "orb", 1)
    factor, rows = last_call([p2, p3], [t0, t1, t2, t3], vm)
    new_positions = place_call(meta, positions, got, [new0, new1, new2, new3])
    factor, new_positions = together(factor, new_positions)
    (early, late), factor = add_up([early, late], "orb", factor)
    new_inverse = update_call(block_order, meta, whole, factor, rows, [early[0], late[0], early[1], late[1]])
    return jnp.transpose(new_positions, (1, 0, 2)), new_inverse


def solution(mesh):
    return jax.shard_map(
        local,
        mesh=mesh,
        in_specs=(
            P("walker", None, None),
            P("walker", "orb", None),
            P("orb", None),
            P("walker", None, None),
            P("walker", None),
            P(),
            P("walker"),
        ),
        out_specs=(P("walker", None, None), P("walker", "orb", None)),
        check_vma=False,
    )
```

time: 126 us -> 108 us (0.86)
  the two profiles are of different devices: /device:TPU:18 before, /device:TPU:0 now
where the time goes in v4:
time: 108 us
  Pallas kernels  59.8 us (55%)
  starting transfers between devices  28.2 us (26%)
  local copies, waits for them, and re-layouts  9.62 us (9%)
  waiting for transfers between devices  7.76 us (7%)
  between operations  1.42 us (1%)
    all_to_all x3, starting transfers between devices, alltoall(): return lax.all_to_all(x, 'walker', split_axis=0, concat_axis=0, tiled=True)  16.5 us
    pallas_call x3, Pallas kernels, later_call(): pl.pallas_call(functools.partial(later_kernel, block), name='later', out_...  13.6 us
    ppermute x18, starting transfers between devices, swap(): lax.ppermute(x, axis, [(i, i ^ k) for i in range(lax.axis_size(axis))])  11.7 us
    pallas_call x4, Pallas kernels, step_call(): pl.pallas_call(functools.partial(step_kernel, block, len(parts)), name='s...  11.5 us
    unnamed x88, local copies, waits for them, and re-layouts  9.62 us
    pallas_call x1, Pallas kernels, slopes_call(): pl.pallas_call(first_kernel, name='slopes', out_shape=tuple((jax.ShapeDty...  7.25 us
    pallas_call x1, Pallas kernels, columns_call(): pl.pallas_call(columns_kernel, name='columns', out_shape=(jax.ShapeDtypeS...  5.4 us
    ppermute x18, waiting for transfers between devices, swap(): lax.ppermute(x, axis, [(i, i ^ k) for i in range(lax.axis_size(axis))])  3.97 us
  transfers between devices with their start and end apart: 21, of which 5 were waited for; matrix products, arithmetic and copies ran while one was open for 1% of the time, Pallas kernels for 47%

profile of v4, /device:TPU:0, one launch (start us, length us, event | category | flops | bytes accessed | tf_op | source)
XLA Modules:
  0.0 107.5 jit_solution(4648322611895683761)
XLA Ops:
  0.6 0.0 copy-start.33
  0.7 2.4 %pack.1 = f32[8,32,128]{2,1,0:T(8,128)} custom-call(s32[8]{0:T(128)} %parent_ref.1, s32[32]{0:T(128)} %order_ref.5, f32[3,8,512]{2,1,0:T(8,128)} %bitcast.6, f32[3,8,64]{2,1,0:T(8,128)} %bitcast.11, s32[8,64]{1,0:T(8,128)} %refs_2_.1), custom_call_target="tpu_custom_call" | custom-call | flops 100000000 | tf_op jit(solution)/shard_map/pack/pallas_call | solution.py:330
  3.0 7.3 %all-to-all-start = ((f32[8,32,128]{2,1,0:T(8,128)}), f32[8,32,128]{2,1,0:T(8,128)S(1)}, u32[]{:S(2)}, u32[]{:S(2)}) async-start(f32[8,32,128]{2,1,0:T(8,128)} %pack.1), calls=%async_computation | async-start | bytes 262144 | tf_op jit(solution)/shard_map/all_to_all | solution.py:884
  10.3 5.4 %columns.1 = (f32[8,80,128]{2,1,0:T(8,128)}, s16[8,128,512]{2,1,0:T(8,128)(2,1)}) custom-call(s32[32]{0:T(128)} %order_ref.5, f32[8,128,512]{2,1,0:T(8,128)} %own_ref.1, f32[3,8,512]{2,1,0:T(8,128)} %bitcast.7), custom_call_target="tpu_custom_call" | custom-call | flops 300000000 | tf_op jit(solution)/shard_map/columns/pallas_call | solution.py:393
  15.8 0.7 pad_add_fusion.meta_ref
  16.4 1.3 %all-to-all-done.info_in = f32[8,32,128]{2,1,0:T(8,128)S(1)} async-done(((f32[8,32,128]{2,1,0:T(8,128)}), f32[8,32,128]{2,1,0:T(8,128)S(1)}, u32[]{:S(2)}, u32[]{:S(2)}) %all-to-all-start) | async-done | bytes 131104 | tf_op jit(solution)/shard_map/all_to_all | solution.py:884
  17.7 0.6 copy-done.42
  18.3 4.0 %route.1 = (f32[4,8,128]{2,1,0:T(8,128)}, f32[8,80,128]{2,1,0:T(8,128)}, s16[8,128,512]{2,1,0:T(8,128)(2,1)}) custom-call(s32[14]{0:T(128)} %pad_add_fusion.meta_ref, f32[8,32,128]{2,1,0:T(8,128)} %copy-done.42, f32[8,80,128]{2,1,0:T(8,128)} %get-tuple-element.56.own_in.own_ref, s16[8,128,512]{2,1,0:T(8,128)(2,1)} %get-tuple-element.57.code_in), custom_call_target="tpu_custom_call" | custom-call | flops 300000000 | tf_op jit(solution)/shard_map/route/pallas_call | solution.py:474
  22.3 4.8 %all-to-all-start.1 = ((f32[8,80,128]{2,1,0:T(8,128)}), f32[8,80,128]{2,1,0:T(8,128)}, u32[]{:S(2)}, u32[]{:S(2)}) async-start(f32[8,80,128]{2,1,0:T(8,128)} %get-tuple-element.58), calls=%async_computation.1 | async-start | bytes 655360 | tf_op jit(solution)/shard_map/all_to_all | solution.py:884
  27.1 7.3 %slopes.1 = (f32[128,128]{1,0:T(8,128)}, f32[128,384]{1,0:T(8,128)}) custom-call(f32[4,8,128]{2,1,0:T(8,128)} %get-tuple-element.60.states_ref.refs_5_.refs_6_.refs_7_, bf16[128,13824]{1,0:T(8,128)(2,1)} %refs_9_.3), custom_call_target="tpu_custom_call" | custom-call | flops 500000000 | tf_op jit(solution)/shard_map/slopes/pallas_call | solution.py:166
  34.3 0.0 copy-start.4
  34.3 2.5 %all-to-all-done.1.got_ref = f32[8,80,128]{2,1,0:T(8,128)} async-done(((f32[8,80,128]{2,1,0:T(8,128)}), f32[8,80,128]{2,1,0:T(8,128)}, u32[]{:S(2)}, u32[]{:S(2)}) %all-to-all-start.1) | async-done | bytes 327712 | tf_op jit(solution)/shard_map/all_to_all | solution.py:884
  36.9 4.4 %all-to-all-start.2 = ((s16[8,128,512]{2,1,0:T(8,128)(2,1)}), s16[8,128,512]{2,1,0:T(8,128)(2,1)}, u32[]{:S(2)}, u32[]{:S(2)}) async-start(s16[8,128,512]{2,1,0:T(8,128)(2,1)} %get-tuple-element.79), calls=%async_computation.2 | async-start | bytes 2097152 | tf_op jit(solution)/shard_map/all_to_all | solution.py:884
  41.3 2.9 %select.3 = (f32[512,128]{1,0:T(8,128)}, f32[8,128]{1,0:T(8,128)}) custom-call(s32[14]{0:T(128)} %pad_add_fusion.meta_ref, f32[8,80,128]{2,1,0:T(8,128)} %get-tuple-element.56.own_in.own_ref, f32[8,80,128]{2,1,0:T(8,128)} %all-to-all-done.1.got_ref, f32[128,384]{1,0:T(8,128)} %get-tuple-element.64.grad_in), custom_call_target="tpu_custom_call" | custom-call | flops 200000000 | tf_op jit(solution)/shard_map/select/pallas_call | solution.py:555
  44.2 0.1 collective-permute-start.2
  44.3 1.6 %collective-permute-start.1 = (f32[8,128]{1,0:T(8,128)}, f32[8,128]{1,0:T(8,128)S(1)}, u32[]{:S(2)}, u32[]{:S(2)}) collective-permute-start(f32[8,128]{1,0:T(8,128)} %get-tuple-element.65.refs_0_), channel_id=1, source_target_pairs={{0,2},{1,3},{2,0},{3,1},{4,6},{5,7},{6,4},{7,5},{8,10},{9,11},{10,... | collective-permute-start | bytes 12296 | tf_op jit(solution)/shard_map/ppermute | solution.py:863
  45.9 0.3 collective-permute-start
  46.2 0.9 copy-done.1
  47.1 4.5 %later.3 = (f32[128,128]{1,0:T(8,128)S(1)}, f32[56,128]{1,0:T(8,128)S(1)}) custom-call(f32[4,8,128]{2,1,0:T(8,128)S(1)} %copy-done.4, bf16[128,13824]{1,0:T(8,128)(2,1)S(1)} %copy-done, f32[512,128]{1,0:T(8,128)S(1)} %copy-done.1), custom_call_target="tpu_custom_call" | custom-call | flops 500000000 | tf_op jit(solution)/shard_map/later/pallas_call | solution.py:198
  51.7 0.0 collective-permute-done.1.refs_2_
  51.7 0.0 collective-permute-done.refs_1_
  51.7 1.8 %step.4 = (f32[120,128]{1,0:T(8,128)S(1)}, f32[8,128]{1,0:T(8,128)S(1)}, f32[128,128]{1,0:T(8,128)S(1)}, f32[64,128]{1,0:T(8,128)S(1)}) custom-call(f32[8,128]{1,0:T(8,128)S(1)} %copy-done.41, f32[8,128]{1,0:T(8,128)S(1)} %collective-permute-done.refs_1_, f32[8,128]{1,0:T(8,128)S(1)} %collective-permute-done.1.refs_2_, ...), custom_call_target="tpu_custom_call" | custom-call | flops 300000000 | tf_op jit(solution)/shard_map/step/pallas_call | solution.py:648
  53.6 1.2 %collective-permute-start.5 = (f32[120,128]{1,0:T(8,128)S(1)}, f32[120,128]{1,0:T(8,128)S(1)}, u32[]{:S(2)}, u32[]{:S(2)}) collective-permute-start(f32[120,128]{1,0:T(8,128)S(1)} %get-tuple-element.69.refs_0_), channel_id=1, source_target_pairs={{0,3},{1,2},{2,1},{3,0},{4,7},{5,6},{6,5},{7,4},{8,11},{9,10},{10,... | collective-permute-start | bytes 184328 | tf_op jit(solution)/shard_map/ppermute | solution.py:863
  54.7 0.7 collective-permute-start.4
  55.5 0.0 collective-permute-start.3
  55.5 4.5 %later.4 = (f32[128,128]{1,0:T(8,128)S(1)}, f32[104,128]{1,0:T(8,128)S(1)}) custom-call(f32[4,8,128]{2,1,0:T(8,128)S(1)} %copy-done.4, bf16[128,13824]{1,0:T(8,128)(2,1)S(1)} %copy-done, f32[512,128]{1,0:T(8,128)S(1)} %copy-done.1), custom_call_target="tpu_custom_call" | custom-call | flops 500000000 | tf_op jit(solution)/shard_map/later/pallas_call | solution.py:198
  60.0 0.0 collective-permute-done.5.refs_3_
  60.0 0.0 collective-permute-done.4.refs_2_
  60.1 2.5 %step.5 = (f32[168,128]{1,0:T(8,128)S(1)}, f32[8,128]{1,0:T(8,128)S(1)}, f32[128,128]{1,0:T(8,128)S(1)}, f32[64,128]{1,0:T(8,128)S(1)}, f32[512,64]{1,0:T(8,128)S(1)}) custom-call(f32[120,128]{1,0:T(8,128)S(1)} %get-tuple-element.69.refs_0_, f32[120,128]{1,0:T(8,128)S(1)} %collective-permute-done.3.refs_1_, f32[120,128]{1,0:T(8,128)S(1)} %collective-permute-done.4.refs_2_, ...), custom_call_target="tpu_custom_call" | custom-call | flops 300000000 | tf_op jit(solution)/shard_map/step/pallas_call | solution.py:648
  62.6 1.4 %collective-permute-start.8 = (f32[168,128]{1,0:T(8,128)S(1)}, f32[168,128]{1,0:T(8,128)S(1)}, u32[]{:S(2)}, u32[]{:S(2)}) collective-permute-start(f32[168,128]{1,0:T(8,128)S(1)} %get-tuple-element.73.refs_0_), channel_id=1, source_target_pairs={{0,3},{1,2},{2,1},{3,0},{4,7},{5,6},{6,5},{7,4},{8,11},{9,10},{10,... | collective-permute-start | bytes 258056 | tf_op jit(solution)/shard_map/ppermute | solution.py:863
  64.1 0.7 collective-permute-start.7
  64.8 0.0 collective-permute-start.6
  64.8 4.5 %later.5 = (f32[128,128]{1,0:T(8,128)S(1)}, f32[152,128]{1,0:T(8,128)S(1)}) custom-call(f32[4,8,128]{2,1,0:T(8,128)S(1)} %copy-done.4, bf16[128,13824]{1,0:T(8,128)(2,1)S(1)} %copy-done, f32[512,128]{1,0:T(8,128)S(1)} %copy-done.1), custom_call_target="tpu_custom_call" | custom-call | flops 500000000 | tf_op jit(solution)/shard_map/later/pallas_call | solution.py:198
  69.3 0.6 copy-done.24
  70.0 3.1 %step.6 = (f32[216,128]{1,0:T(8,128)}, f32[8,128]{1,0:T(8,128)S(1)}, f32[128,128]{1,0:T(8,128)S(1)}, f32[64,128]{1,0:T(8,128)S(1)}, f32[512,64]{1,0:T(8,128)S(1)}) custom-call(f32[168,128]{1,0:T(8,128)S(1)} %get-tuple-element.73.refs_0_, f32[168,128]{1,0:T(8,128)S(1)} %collective-permute-done.6.refs_1_, f32[168,128]{1,0:T(8,128)S(1)} %collective-permute-done.7.refs_2_, ...), custom_call_target="tpu_custom_call" | custom-call | flops 300000000 | tf_op jit(solution)/shard_map/step/pallas_call | solution.py:648
  73.2 0.7 copy-done.13
  73.8 0.6 copy-done.20
  74.4 0.6 copy-done.29
  75.1 0.6 copy-done.39
  75.6 1.4 %collective-permute-start.11 = (f32[216,128]{1,0:T(8,128)}, f32[216,128]{1,0:T(8,128)}, u32[]{:S(2)}, u32[]{:S(2)}) collective-permute-start(f32[216,128]{1,0:T(8,128)} %get-tuple-element.85.refs_0_.refs_4_), channel_id=1, source_target_pairs={{0,3},{1,2},{2,1},{3,0},{4,7},{5,6},{6,5},{7,4},{8,11},{9,10},{10,... | collective-permute-start | bytes 331784 | tf_op jit(solution)/shard_map/ppermute | solution.py:863
  77.0 0.7 collective-permute-start.10
  77.8 1.6 %copy-done.3 = f32[8,128,512]{2,1,0:T(8,128)S(1)} copy-done((f32[8,128,512]{2,1,0:T(8,128)S(1)}, f32[8,128,512]{2,1,0:T(8,128)}, u32[]{:S(2)}) %copy-start.3) | copy-done | bytes 2097176
  79.4 0.8 copy-done.23
  80.2 0.8 copy-done.27
  81.1 0.8 copy-done.30
  81.9 0.7 copy-done.31
  82.6 3.7 %assemble.1 = (f32[8,128,512]{2,1,0:T(8,128)S(1)}, f32[4,48,512]{2,1,0:T(8,128)S(1)}, f32[4,48,512]{2,1,0:T(8,128)S(1)}) custom-call(s32[14]{0:T(128)S(1)} %copy-done.31, f32[8,128,512]{2,1,0:T(8,128)S(1)} %copy-done.3, f32[8,80,128]{2,1,0:T(8,128)} %all-to-all-done.1.got_ref, s16[8,128,512]{2,1,0:T(8,128)(2,1)} %all-to-all-done.2.code_ref, ...), custom_call_target="tpu_custom_call" | custom-call | flops 400000000 | tf_op jit(solution)/shard_map/assemble/pallas_call | solution.py:741
  86.3 0.6 collective-permute-start.12
  86.8 1.3 %collective-permute-done.12 = f32[4,48,512]{2,1,0:T(8,128)S(1)} collective-permute-done((f32[4,48,512]{2,1,0:T(8,128)S(1)}, f32[4,48,512]{2,1,0:T(8,128)S(1)}, u32[]{:S(2)}, u32[]{:S(2)}) %collective-permute-start.12) | collective-permute-done | bytes 393248 | tf_op jit(solution)/shard_map/ppermute | solution.py:863
  88.2 0.1 add.12
  88.3 1.4 %collective-permute-start.13 = (f32[4,48,512]{2,1,0:T(8,128)S(1)}, f32[4,48,512]{2,1,0:T(8,128)S(1)}, u32[]{:S(2)}, u32[]{:S(2)}) collective-permute-start(f32[4,48,512]{2,1,0:T(8,128)S(1)} %add.12), channel_id=1, source_target_pairs={{0,2},{1,3},{2,0},{3,1},{4,6},{5,7},{6,4},{7,5},{8,10},{9,11},{10,... | collective-permute-start | bytes 1179656 | tf_op jit(solution)/shard_map/ppermute | solution.py:863
  89.6 4.1 %step.7 = (f32[64,128]{1,0:T(8,128)}, f32[8,128]{1,0:T(8,128)S(1)}, f32[128,128]{1,0:T(8,128)S(1)}, f32[64,128]{1,0:T(8,128)S(1)}, f32[512,64]{1,0:T(8,128)}) custom-call(f32[216,128]{1,0:T(8,128)} %get-tuple-element.85.refs_0_.refs_4_, f32[216,128]{1,0:T(8,128)} %collective-permute-done.9.refs_1_.refs_5_, ...), custom_call_target="tpu_custom_call" | custom-call | flops 300000000 | tf_op jit(solution)/shard_map/step/pallas_call | solution.py:648
  93.9 1.6 %sums.1 = (f32[4,16,512]{2,1,0:T(8,128)S(1)}, f32[4,16,512]{2,1,0:T(8,128)S(1)}) custom-call(s32[14]{0:T(128)S(1)} %copy-done.32, f32[8,128,512]{2,1,0:T(8,128)S(1)} %get-tuple-element.99.v_ref, f32[128,128]{1,0:T(8,128)S(1)} %get-tuple-element.102.change_ref), custom_call_target="tpu_custom_call" | custom-call | flops 100000000 | tf_op jit(solution)/shard_map/sums/pallas_call | solution.py:775
  95.5 0.0 copy-start.34
  95.5 0.1 collective-permute-start.14
  95.6 1.3 %collective-permute-done.14 = f32[4,16,512]{2,1,0:T(8,128)S(1)} collective-permute-done((f32[4,16,512]{2,1,0:T(8,128)S(1)}, f32[4,16,512]{2,1,0:T(8,128)S(1)}, u32[]{:S(2)}, u32[]{:S(2)}) %collective-permute-start.14) | collective-permute-done | bytes 131104 | tf_op jit(solution)/shard_map/ppermute | solution.py:863
  96.9 0.8 collective-permute-start.15
  97.7 1.8 %place.1 = f32[3,8,512]{2,1,0:T(8,128)} custom-call(s32[14]{0:T(128)S(1)} %copy-done.32, f32[3,8,512]{2,1,0:T(8,128)S(1)} %bitcast.8, f32[8,80,128]{2,1,0:T(8,128)} %all-to-all-done.1.got_ref, f32[8,128]{1,0:T(8,128)S(1)} %copy-done.36, f32[8,128]{1,0:T(8,128)S(1)} %copy-done.38, f32[8,128]{1,0:T(8,128)S(1)} %copy-done.40, ...), custom_call_target="tpu_custom_call" | custom-call | flops 100000000 | tf_op jit(solution)/shard_map/place/pallas_call | solution.py:851
  99.6 3.0 %last.1 = (f32[8,128,64]{2,1,0:T(8,128)S(1)}, f32[512,64]{1,0:T(8,128)S(1)}) custom-call(f32[168,128]{1,0:T(8,128)S(1)} %copy-done.6, f32[168,128]{1,0:T(8,128)S(1)} %copy-done.12, f32[168,128]{1,0:T(8,128)S(1)} %copy-done.10, f32[168,128]{1,0:T(8,128)S(1)} %copy-done.8, f32[216,128]{1,0:T(8,128)} %get-tuple-element.85.refs_0_.refs_4_, ...), custom_call_target="tpu_custom_call" | custom-call | flops 200000000 | tf_op jit(solution)/shard_map/last/pallas_call | solution.py:689
  102.6 0.1 add.14.refs_0_
  102.6 0.1 collective-permute-start.16
  102.8 0.6 collective-permute-start.17
  103.3 1.3 %collective-permute-done.17.refs_3_ = f32[4,16,512]{2,1,0:T(8,128)S(1)} collective-permute-done((f32[4,16,512]{2,1,0:T(8,128)S(1)}, f32[4,16,512]{2,1,0:T(8,128)S(1)}, u32[]{:S(2)}, u32[]{:S(2)}) %collective-permute-start.17) | collective-permute-done | bytes 131104 | tf_op jit(solution)/shard_map/ppermute | solution.py:863
  104.6 2.7 %update.1 = f32[8,128,512]{2,1,0:T(8,128)} custom-call(s32[32]{0:T(128)S(1)} %copy-done.34, s32[14]{0:T(128)S(1)} %copy-done.32, f32[8,128,512]{2,1,0:T(8,128)S(1)} %get-tuple-element.99.v_ref, f32[8,128,64]{2,1,0:T(8,128)S(1)} %get-tuple-element.106.factor_ref, f32[512,64]{1,0:T(8,128)S(1)} %get-tuple-element.107.l_ref, f32[4,48,512]{2,1,0:T(8,128)S(1)} %add.14.refs_0_, ...), custom_call_target="tpu_custom_call" | custom-call | flops 200000000 | tf_op jit(solution)/shard_map/update/pallas_call | solution.py:812
  (88 shorter events, 0.2 us)
Async XLA Ops:
  0.6 15.1 %copy-start.33 = (s32[32]{0:T(128)S(1)}, s32[32]{0:T(128)}, u32[]{:S(2)}) copy-start(s32[32]{0:T(128)} %order_ref.5) | copy-start | bytes 388
  0.6 15.1 %copy-start.43 = (s32[8]{0:T(128)S(1)}, s32[8]{0:T(128)}, u32[]{:S(2)}) copy-start(s32[8]{0:T(128)} %parent_ref.1) | copy-start | bytes 100
  3.0 14.6 %all-to-all-start = ((f32[8,32,128]{2,1,0:T(8,128)}), f32[8,32,128]{2,1,0:T(8,128)S(1)}, u32[]{:S(2)}, u32[]{:S(2)}) async-start(f32[8,32,128]{2,1,0:T(8,128)} %pack.1), calls=%async_computation | async-start | bytes 262144 | tf_op jit(solution)/shard_map/all_to_all | solution.py:884
  17.7 0.6 copy-start.42
  22.3 14.6 %all-to-all-start.1 = ((f32[8,80,128]{2,1,0:T(8,128)}), f32[8,80,128]{2,1,0:T(8,128)}, u32[]{:S(2)}, u32[]{:S(2)}) async-start(f32[8,80,128]{2,1,0:T(8,128)} %get-tuple-element.58), calls=%async_computation.1 | async-start | bytes 655360 | tf_op jit(solution)/shard_map/all_to_all | solution.py:884
  27.1 19.1 %copy-start = (bf16[128,13824]{1,0:T(8,128)(2,1)S(1)}, bf16[128,13824]{1,0:T(8,128)(2,1)}, u32[]{:S(2)}) copy-start(bf16[128,13824]{1,0:T(8,128)(2,1)} %refs_9_.3) | copy-start | bytes 10616836
  34.3 11.8 %copy-start.4 = (f32[4,8,128]{2,1,0:T(8,128)S(1)}, f32[4,8,128]{2,1,0:T(8,128)}, u32[]{:S(2)}) copy-start(f32[4,8,128]{2,1,0:T(8,128)} %get-tuple-element.60.states_ref.refs_5_.refs_6_.refs_7_) | copy-start | bytes 49156
  36.9 40.9 %all-to-all-start.2 = ((s16[8,128,512]{2,1,0:T(8,128)(2,1)}), s16[8,128,512]{2,1,0:T(8,128)(2,1)}, u32[]{:S(2)}, u32[]{:S(2)}) async-start(s16[8,128,512]{2,1,0:T(8,128)(2,1)} %get-tuple-element.79), calls=%async_computation.2 | async-start | bytes 2097152 | tf_op jit(solution)/shard_map/all_to_all | solution.py:884
  41.3 10.4 %copy-start.28 = (f32[128,128]{1,0:T(8,128)S(1)}, f32[128,128]{1,0:T(8,128)}, u32[]{:S(2)}) copy-start(f32[128,128]{1,0:T(8,128)} %get-tuple-element.68.refs_6_) | copy-start | bytes 196612
  44.2 7.4 %collective-permute-start.2 = (f32[8,128]{1,0:T(8,128)}, f32[8,128]{1,0:T(8,128)S(1)}, u32[]{:S(2)}, u32[]{:S(2)}) collective-permute-start(f32[8,128]{1,0:T(8,128)} %get-tuple-element.65.refs_0_), channel_id=1, source_target_pairs={{0,3},{1,2},{2,1},{3,0},{4,7},{5,6},{6,5},{7,4},{8,11},{9,10},{10,... | collective-permute-start | bytes 12296 | tf_op jit(solution)/shard_map/ppermute | solution.py:863
  44.3 7.3 %collective-permute-start.1 = (f32[8,128]{1,0:T(8,128)}, f32[8,128]{1,0:T(8,128)S(1)}, u32[]{:S(2)}, u32[]{:S(2)}) collective-permute-start(f32[8,128]{1,0:T(8,128)} %get-tuple-element.65.refs_0_), channel_id=1, source_target_pairs={{0,2},{1,3},{2,0},{3,1},{4,6},{5,7},{6,4},{7,5},{8,10},{9,11},{10,... | collective-permute-start | bytes 12296 | tf_op jit(solution)/shard_map/ppermute | solution.py:863
  45.9 5.8 %collective-permute-start = (f32[8,128]{1,0:T(8,128)}, f32[8,128]{1,0:T(8,128)S(1)}, u32[]{:S(2)}, u32[]{:S(2)}) collective-permute-start(f32[8,128]{1,0:T(8,128)} %get-tuple-element.65.refs_0_), channel_id=1, source_target_pairs={{0,1},{1,0},{2,3},{3,2},{4,5},{5,4},{6,7},{7,6},{8,9},{9,8},{10,11... | collective-permute-start | bytes 12296 | tf_op jit(solution)/shard_map/ppermute | solution.py:863
  46.2 1.0 copy-start.1
  47.1 4.6 %copy-start.41 = (f32[8,128]{1,0:T(8,128)S(1)}, f32[8,128]{1,0:T(8,128)}, u32[]{:S(2)}) copy-start(f32[8,128]{1,0:T(8,128)} %get-tuple-element.65.refs_0_) | copy-start | bytes 12292
  53.5 6.5 %copy-start.22 = (f32[128,128]{1,0:T(8,128)}, f32[128,128]{1,0:T(8,128)S(1)}, u32[]{:S(2)}) copy-start(f32[128,128]{1,0:T(8,128)S(1)} %get-tuple-element.80.refs_0_) | copy-start | bytes 196612
  53.5 9.0 %copy-start.16 = (f32[64,128]{1,0:T(8,128)}, f32[64,128]{1,0:T(8,128)S(1)}, u32[]{:S(2)}) copy-start(f32[64,128]{1,0:T(8,128)S(1)} %get-tuple-element.71.refs_5_.refs_8_) | copy-start | bytes 98308
  53.6 9.0 %copy-start.35 = (f32[8,128]{1,0:T(8,128)}, f32[8,128]{1,0:T(8,128)S(1)}, u32[]{:S(2)}) copy-start(f32[8,128]{1,0:T(8,128)S(1)} %get-tuple-element.94.refs_0_) | copy-start | bytes 12292
  53.6 6.5 %collective-permute-start.5 = (f32[120,128]{1,0:T(8,128)S(1)}, f32[120,128]{1,0:T(8,128)S(1)}, u32[]{:S(2)}, u32[]{:S(2)}) collective-permute-start(f32[120,128]{1,0:T(8,128)S(1)} %get-tuple-element.69.refs_0_), channel_id=1, source_target_pairs={{0,3},{1,2},{2,1},{3,0},{4,7},{5,6},{6,5},{7,4},{8,11},{9,10},{10,... | collective-permute-start | bytes 184328 | tf_op jit(solution)/shard_map/ppermute | solution.py:863
  54.7 5.3 %collective-permute-start.4 = (f32[120,128]{1,0:T(8,128)S(1)}, f32[120,128]{1,0:T(8,128)S(1)}, u32[]{:S(2)}, u32[]{:S(2)}) collective-permute-start(f32[120,128]{1,0:T(8,128)S(1)} %get-tuple-element.69.refs_0_), channel_id=1, source_target_pairs={{0,2},{1,3},{2,0},{3,1},{4,6},{5,7},{6,4},{7,5},{8,10},{9,11},{10,... | collective-permute-start | bytes 184328 | tf_op jit(solution)/shard_map/ppermute | solution.py:863
  55.5 4.6 %collective-permute-start.3 = (f32[120,128]{1,0:T(8,128)S(1)}, f32[120,128]{1,0:T(8,128)S(1)}, u32[]{:S(2)}, u32[]{:S(2)}) collective-permute-start(f32[120,128]{1,0:T(8,128)S(1)} %get-tuple-element.69.refs_0_), channel_id=1, source_target_pairs={{0,1},{1,0},{2,3},{3,2},{4,5},{5,4},{6,7},{7,6},{8,9},{9,8},{10,11... | collective-permute-start | bytes 184328 | tf_op jit(solution)/shard_map/ppermute | solution.py:863
  62.6 10.5 %copy-start.5 = (f32[168,128]{1,0:T(8,128)}, f32[168,128]{1,0:T(8,128)S(1)}, u32[]{:S(2)}) copy-start(f32[168,128]{1,0:T(8,128)S(1)} %get-tuple-element.73.refs_0_) | copy-start | bytes 258052
  62.6 10.5 %copy-start.18 = (f32[64,128]{1,0:T(8,128)}, f32[64,128]{1,0:T(8,128)S(1)}, u32[]{:S(2)}) copy-start(f32[64,128]{1,0:T(8,128)S(1)} %get-tuple-element.75.refs_5_.refs_9_) | copy-start | bytes 98308
  62.6 10.5 %copy-start.26 = (f32[128,128]{1,0:T(8,128)}, f32[128,128]{1,0:T(8,128)S(1)}, u32[]{:S(2)}) copy-start(f32[128,128]{1,0:T(8,128)S(1)} %get-tuple-element.81.refs_1_) | copy-start | bytes 196612
  62.6 10.5 %copy-start.37 = (f32[8,128]{1,0:T(8,128)}, f32[8,128]{1,0:T(8,128)S(1)}, u32[]{:S(2)}) copy-start(f32[8,128]{1,0:T(8,128)S(1)} %get-tuple-element.95.refs_1_) | copy-start | bytes 12292
  62.6 7.3 %collective-permute-start.8 = (f32[168,128]{1,0:T(8,128)S(1)}, f32[168,128]{1,0:T(8,128)S(1)}, u32[]{:S(2)}, u32[]{:S(2)}) collective-permute-start(f32[168,128]{1,0:T(8,128)S(1)} %get-tuple-element.73.refs_0_), channel_id=1, source_target_pairs={{0,3},{1,2},{2,1},{3,0},{4,7},{5,6},{6,5},{7,4},{8,11},{9,10},{10,... | collective-permute-start | bytes 258056 | tf_op jit(solution)/shard_map/ppermute | solution.py:863
  64.1 5.9 %collective-permute-start.7 = (f32[168,128]{1,0:T(8,128)S(1)}, f32[168,128]{1,0:T(8,128)S(1)}, u32[]{:S(2)}, u32[]{:S(2)}) collective-permute-start(f32[168,128]{1,0:T(8,128)S(1)} %get-tuple-element.73.refs_0_), channel_id=1, source_target_pairs={{0,2},{1,3},{2,0},{3,1},{4,6},{5,7},{6,4},{7,5},{8,10},{9,11},{10,... | collective-permute-start | bytes 258056 | tf_op jit(solution)/shard_map/ppermute | solution.py:863
  64.8 5.2 %collective-permute-start.6 = (f32[168,128]{1,0:T(8,128)S(1)}, f32[168,128]{1,0:T(8,128)S(1)}, u32[]{:S(2)}, u32[]{:S(2)}) collective-permute-start(f32[168,128]{1,0:T(8,128)S(1)} %get-tuple-element.73.refs_0_), channel_id=1, source_target_pairs={{0,1},{1,0},{2,3},{3,2},{4,5},{5,4},{6,7},{7,6},{8,9},{9,8},{10,11... | collective-permute-start | bytes 258056 | tf_op jit(solution)/shard_map/ppermute | solution.py:863
  69.3 0.6 copy-start.24
  69.9 3.2 %copy-start.7 = (f32[168,128]{1,0:T(8,128)}, f32[168,128]{1,0:T(8,128)S(1)}, u32[]{:S(2)}) copy-start(f32[168,128]{1,0:T(8,128)S(1)} %collective-permute-done.8.refs_3_) | copy-start | bytes 258052
  70.0 3.2 %copy-start.9 = (f32[168,128]{1,0:T(8,128)}, f32[168,128]{1,0:T(8,128)S(1)}, u32[]{:S(2)}) copy-start(f32[168,128]{1,0:T(8,128)S(1)} %collective-permute-done.7.refs_2_) | copy-start | bytes 258052
  70.0 3.2 %copy-start.11 = (f32[168,128]{1,0:T(8,128)}, f32[168,128]{1,0:T(8,128)S(1)}, u32[]{:S(2)}) copy-start(f32[168,128]{1,0:T(8,128)S(1)} %collective-permute-done.6.refs_1_) | copy-start | bytes 258052
  73.1 0.7 copy-start.13
  73.8 0.6 copy-start.20
  74.4 0.6 copy-start.29
  75.6 10.6 %collective-permute-start.11 = (f32[216,128]{1,0:T(8,128)}, f32[216,128]{1,0:T(8,128)}, u32[]{:S(2)}, u32[]{:S(2)}) collective-permute-start(f32[216,128]{1,0:T(8,128)} %get-tuple-element.85.refs_0_.refs_4_), channel_id=1, source_target_pairs={{0,3},{1,2},{2,1},{3,0},{4,7},{5,6},{6,5},{7,4},{8,11},{9,10},{10,... | collective-permute-start | bytes 331784 | tf_op jit(solution)/shard_map/ppermute | solution.py:863
  77.0 9.2 %collective-permute-start.10 = (f32[216,128]{1,0:T(8,128)}, f32[216,128]{1,0:T(8,128)}, u32[]{:S(2)}, u32[]{:S(2)}) collective-permute-start(f32[216,128]{1,0:T(8,128)} %get-tuple-element.85.refs_0_.refs_4_), channel_id=1, source_target_pairs={{0,2},{1,3},{2,0},{3,1},{4,6},{5,7},{6,4},{7,5},{8,10},{9,11},{10,... | collective-permute-start | bytes 331784 | tf_op jit(solution)/shard_map/ppermute | solution.py:863
  77.8 8.5 %collective-permute-start.9 = (f32[216,128]{1,0:T(8,128)}, f32[216,128]{1,0:T(8,128)}, u32[]{:S(2)}, u32[]{:S(2)}) collective-permute-start(f32[216,128]{1,0:T(8,128)} %get-tuple-element.85.refs_0_.refs_4_), channel_id=1, source_target_pairs={{0,1},{1,0},{2,3},{3,2},{4,5},{5,4},{6,7},{7,6},{8,9},{9,8},{10,11... | collective-permute-start | bytes 331784 | tf_op jit(solution)/shard_map/ppermute | solution.py:863
  77.8 1.6 %copy-start.3 = (f32[8,128,512]{2,1,0:T(8,128)S(1)}, f32[8,128,512]{2,1,0:T(8,128)}, u32[]{:S(2)}) copy-start(f32[8,128,512]{2,1,0:T(8,128)} %own_ref.1) | copy-start | bytes 6291460
  79.4 0.8 copy-start.23
  80.2 0.8 copy-start.27
  81.1 0.8 copy-start.30
  81.9 0.7 copy-start.31
  82.6 7.1 %copy-start.2 = (f32[512,128]{1,0:T(8,128)S(1)}, f32[512,128]{1,0:T(8,128)}, u32[]{:S(2)}) copy-start(f32[512,128]{1,0:T(8,128)} %get-tuple-element.66.vm_ref.refs_7_.refs_8_.refs_9_.refs_12_) | copy-start | bytes 786436
  82.6 7.1 %copy-start.14 = (f32[512,64]{1,0:T(8,128)S(1)}, f32[512,64]{1,0:T(8,128)}, u32[]{:S(2)}) copy-start(f32[512,64]{1,0:T(8,128)} %copy-done.13) | copy-start | bytes 393220
  82.6 7.1 %copy-start.21 = (f32[64,128]{1,0:T(8,128)S(1)}, f32[64,128]{1,0:T(8,128)}, u32[]{:S(2)}) copy-start(f32[64,128]{1,0:T(8,128)} %copy-done.20) | copy-start | bytes 98308
  82.6 7.1 %copy-start.25 = (f32[128,128]{1,0:T(8,128)S(1)}, f32[128,128]{1,0:T(8,128)}, u32[]{:S(2)}) copy-start(f32[128,128]{1,0:T(8,128)} %copy-done.24) | copy-start | bytes 196612
  86.3 1.9 %collective-permute-start.12 = (f32[4,48,512]{2,1,0:T(8,128)S(1)}, f32[4,48,512]{2,1,0:T(8,128)S(1)}, u32[]{:S(2)}, u32[]{:S(2)}) collective-permute-start(f32[4,48,512]{2,1,0:T(8,128)S(1)} %get-tuple-element.101), channel_id=1, source_target_pairs={{0,1},{1,0},{2,3},{3,2},{4,5},{5,4},{6,7},{7,6},{8,9},{9,8},{10,11... | collective-permute-start | bytes 1179656 | tf_op jit(solution)/shard_map/ppermute | solution.py:863
  88.3 14.3 %collective-permute-start.13 = (f32[4,48,512]{2,1,0:T(8,128)S(1)}, f32[4,48,512]{2,1,0:T(8,128)S(1)}, u32[]{:S(2)}, u32[]{:S(2)}) collective-permute-start(f32[4,48,512]{2,1,0:T(8,128)S(1)} %add.12), channel_id=1, source_target_pairs={{0,2},{1,3},{2,0},{3,1},{4,6},{5,7},{6,4},{7,5},{8,10},{9,11},{10,... | collective-permute-start | bytes 1179656 | tf_op jit(solution)/shard_map/ppermute | solution.py:863
  89.6 4.2 %copy-start.32 = (s32[14]{0:T(128)S(1)}, s32[14]{0:T(128)}, u32[]{:S(2)}) copy-start(s32[14]{0:T(128)} %pad_add_fusion.meta_ref) | copy-start | bytes 172
  93.8 3.9 %copy-start.15 = (f32[8,3,512]{2,0,1:T(8,128)S(1)}, f32[8,3,512]{2,0,1:T(8,128)}, u32[]{:S(2)}) copy-start(f32[8,3,512]{2,0,1:T(8,128)} %param.7) | copy-start | bytes 147460
  93.8 3.9 %copy-start.36 = (f32[8,128]{1,0:T(8,128)S(1)}, f32[8,128]{1,0:T(8,128)}, u32[]{:S(2)}) copy-start(f32[8,128]{1,0:T(8,128)} %copy-done.35) | copy-start | bytes 12292
  93.8 3.9 %copy-start.38 = (f32[8,128]{1,0:T(8,128)S(1)}, f32[8,128]{1,0:T(8,128)}, u32[]{:S(2)}) copy-start(f32[8,128]{1,0:T(8,128)} %copy-done.37) | copy-start | bytes 12292
  93.8 3.9 %copy-start.40 = (f32[8,128]{1,0:T(8,128)S(1)}, f32[8,128]{1,0:T(8,128)}, u32[]{:S(2)}) copy-start(f32[8,128]{1,0:T(8,128)} %copy-done.39) | copy-start | bytes 12292
  93.8 5.8 %copy-start.6 = (f32[168,128]{1,0:T(8,128)S(1)}, f32[168,128]{1,0:T(8,128)}, u32[]{:S(2)}) copy-start(f32[168,128]{1,0:T(8,128)} %copy-done.5) | copy-start | bytes 258052
  93.8 5.8 %copy-start.8 = (f32[168,128]{1,0:T(8,128)S(1)}, f32[168,128]{1,0:T(8,128)}, u32[]{:S(2)}) copy-start(f32[168,128]{1,0:T(8,128)} %copy-done.7) | copy-start | bytes 258052
  93.8 5.7 %copy-start.10 = (f32[168,128]{1,0:T(8,128)S(1)}, f32[168,128]{1,0:T(8,128)}, u32[]{:S(2)}) copy-start(f32[168,128]{1,0:T(8,128)} %copy-done.9) | copy-start | bytes 258052
  93.8 5.7 %copy-start.12 = (f32[168,128]{1,0:T(8,128)S(1)}, f32[168,128]{1,0:T(8,128)}, u32[]{:S(2)}) copy-start(f32[168,128]{1,0:T(8,128)} %copy-done.11) | copy-start | bytes 258052
  93.8 5.7 %copy-start.17 = (f32[64,128]{1,0:T(8,128)S(1)}, f32[64,128]{1,0:T(8,128)}, u32[]{:S(2)}) copy-start(f32[64,128]{1,0:T(8,128)} %copy-done.16) | copy-start | bytes 98308
  93.8 5.7 %copy-start.19 = (f32[64,128]{1,0:T(8,128)S(1)}, f32[64,128]{1,0:T(8,128)}, u32[]{:S(2)}) copy-start(f32[64,128]{1,0:T(8,128)} %copy-done.18) | copy-start | bytes 98308
  95.5 9.2 %copy-start.34 = (s32[32]{0:T(128)S(1)}, s32[32]{0:T(128)}, u32[]{:S(2)}) copy-start(s32[32]{0:T(128)} %order_ref.5) | copy-start | bytes 388
  95.5 1.4 %collective-permute-start.14 = (f32[4,16,512]{2,1,0:T(8,128)S(1)}, f32[4,16,512]{2,1,0:T(8,128)S(1)}, u32[]{:S(2)}, u32[]{:S(2)}) collective-permute-start(f32[4,16,512]{2,1,0:T(8,128)S(1)} %get-tuple-element.104), channel_id=1, source_target_pairs={{0,1},{1,0},{2,3},{3,2},{4,5},{5,4},{6,7},{7,6},{8,9},{9,8},{10,11... | collective-permute-start | bytes 393224 | tf_op jit(solution)/shard_map/ppermute | solution.py:863
  96.9 5.7 %collective-permute-start.15 = (f32[4,16,512]{2,1,0:T(8,128)S(1)}, f32[4,16,512]{2,1,0:T(8,128)S(1)}, u32[]{:S(2)}, u32[]{:S(2)}) collective-permute-start(f32[4,16,512]{2,1,0:T(8,128)S(1)} %add.13), channel_id=1, source_target_pairs={{0,2},{1,3},{2,0},{3,1},{4,6},{5,7},{6,4},{7,5},{8,10},{9,11},{10,... | collective-permute-start | bytes 393224 | tf_op jit(solution)/shard_map/ppermute | solution.py:863
  102.6 2.0 %collective-permute-start.16 = (f32[4,48,512]{2,1,0:T(8,128)S(1)}, f32[4,48,512]{2,1,0:T(8,128)S(1)}, u32[]{:S(2)}, u32[]{:S(2)}) collective-permute-start(f32[4,48,512]{2,1,0:T(8,128)S(1)} %add.14.refs_0_), channel_id=1, source_target_pairs={{0,1},{1,0},{2,3},{3,2},{4,5},{5,4},{6,7},{7,6},{8,9},{9,8},{10,11... | collective-permute-start | bytes 1179656 | tf_op jit(solution)/shard_map/ppermute | solution.py:863
  102.8 1.9 %collective-permute-start.17 = (f32[4,16,512]{2,1,0:T(8,128)S(1)}, f32[4,16,512]{2,1,0:T(8,128)S(1)}, u32[]{:S(2)}, u32[]{:S(2)}) collective-permute-start(f32[4,16,512]{2,1,0:T(8,128)S(1)} %add.15.refs_1_), channel_id=1, source_target_pairs={{0,1},{1,0},{2,3},{3,2},{4,5},{5,4},{6,7},{7,6},{8,9},{9,8},{10,11... | collective-permute-start | bytes 393224 | tf_op jit(solution)/shard_map/ppermute | solution.py:863
  (1 other events, 0.6 us)

commit v5 on v4

--- a/solution.py
+++ b/solution.py
@@ -28,6 +28,7 @@
 LIMIT = 16 * 2**20
 WHOLE = 60 * 2**20
 PART = 59500000
+ALMOST = 63300000
 
 
 def axis_weights(u, with_slopes):
@@ -95,7 +96,7 @@
 
 
 def slopes_kernel(
-    state_ref, table_ref, phi_ref, grad_ref, even_ref, odd_ref, wx_ref, sx_ref, loads=()
+    state_ref, table_ref, phi_ref, grad_ref, even_ref, odd_ref, wx_ref, sx_ref, loads=(), beside=()
 ):
     n = state_ref.shape[2]
     wx, sx = axis_weights(state_ref[0, 0:1, :], True)
@@ -131,14 +132,20 @@
             load.wait()
             if i + 1 < len(loads):
                 loads[i + 1].start()
+            if beside[i] is not None:
+                beside[i]()
             lax.fori_loop(start, start + size, body, 0, unroll=size)
             start += size
     else:
         lax.fori_loop(0, pairs, body, 0, unroll=UNROLL)
 
 
-def first_kernel(states_ref, table_ref, phi_out, grad_out, held_ref, phi_ref, grad_ref, *refs):
-    scratch, (in_sem, out_sem) = refs[:-2], refs[-2:]
+def first_kernel(
+    sending_ref, states_ref, table_ref, code_in, phi_out, grad_out, code_out, *refs
+):
+    held_ref, phi_ref, grad_ref, code_ref = refs[:4]
+    scratch, (in_sem, out_sem, code_sem) = refs[4:-3], refs[-3:]
+    groups = code_out.shape[0]
     loads = []
     start = 0
     for i, pairs in enumerate(CHUNKS):
@@ -148,34 +155,55 @@
             pltpu.make_async_copy(table_ref.at[:, at], held_ref.at[:, at], in_sem.at[i])
         )
     loads[0].start()
-    slopes_kernel(states_ref.at[0:1], held_ref, phi_ref, grad_ref, *scratch, loads=loads)
+    codes = pltpu.make_async_copy(code_in, code_ref, code_sem.at[groups])
+    picks = []
+    for g in range(groups):
+        source = code_ref.at[sending_ref[g]]
+        picks.append(pltpu.make_async_copy(source, code_out.at[g], code_sem.at[g]))
+
+    def pick():
+        codes.wait()
+        for copy in picks:
+            copy.start()
+
+    beside = (None, codes.start, pick)
+    slopes_kernel(
+        states_ref.at[0:1], held_ref, phi_ref, grad_ref, *scratch, loads=loads, beside=beside
+    )
     stores = [
         pltpu.make_async_copy(phi_ref, phi_out, out_sem.at[0]),
         pltpu.make_async_copy(grad_ref, grad_out, out_sem.at[1]),
     ]
     for store in stores:
         store.start()
-    for store in stores:
+    for store in stores + picks:
         store.wait()
 
 
-def slopes_call(states, table):
+def slopes_call(sending, states, table, code):
     orbitals = table.shape[0]
     n = states.shape[2]
+    groups = sending.shape[0]
     shapes = [(orbitals, n), (orbitals, 3 * n)]
     return pl.pallas_call(
         first_kernel,
         name="slopes",
-        out_shape=tuple(jax.ShapeDtypeStruct(shape, F32) for shape in shapes),
-        in_specs=[VMEM, ANY],
-        out_specs=(ANY, ANY),
+        out_shape=tuple(jax.ShapeDtypeStruct(shape, F32) for shape in shapes)
+        + (jax.ShapeDtypeStruct((groups, *code.shape[1:]), code.dtype),),
+        in_specs=[SMEM, VMEM, ANY, ANY],
+        out_specs=(ANY, ANY, ANY),
         scratch_shapes=[pltpu.VMEM(table.shape, BF16)]
         + [pltpu.VMEM(shape, F32) for shape in shapes]
+        + [pltpu.VMEM(code.shape, code.dtype)]
         + slopes_scratch(n)
-        + [pltpu.SemaphoreType.DMA((len(CHUNKS),)), pltpu.SemaphoreType.DMA((2,))],
+        + [
+            pltpu.SemaphoreType.DMA((len(CHUNKS),)),
+            pltpu.SemaphoreType.DMA((2,)),
+            pltpu.SemaphoreType.DMA((groups + 1,)),
+        ],
         compiler_params=params(WHOLE),
         cost_estimate=lasting(5),
-    )(states, table)
+    )(sending, states, table, code)
 
 
 def slopes_scratch(n):
@@ -187,9 +215,11 @@
     ]
 
 
-def later_kernel(block, states_ref, table_ref, vm_ref, phi_ref, out_ref, grad_ref, *scratch):
+def later_kernel(block, states_ref, table_ref, vm_ref, out_ref, grad_ref, *scratch):
+    orbitals = table_ref.shape[0]
+    phi_ref = out_ref.at[0:orbitals]
     slopes_kernel(states_ref.at[block : block + 1], table_ref, phi_ref, grad_ref, *scratch)
-    drift_rows(block, vm_ref, grad_ref, out_ref, 0)
+    drift_rows(block, vm_ref, grad_ref, out_ref, orbitals)
 
 
 def later_call(block, states, table, vm):
@@ -198,12 +228,9 @@
     return pl.pallas_call(
         functools.partial(later_kernel, block),
         name="later",
-        out_shape=(
-            jax.ShapeDtypeStruct((orbitals, n), F32),
-            jax.ShapeDtypeStruct((drift_size(block), n), F32),
-        ),
+        out_shape=jax.ShapeDtypeStruct((orbitals + drift_size(block), n), F32),
         in_specs=[VMEM] * 3,
-        out_specs=(VMEM, VMEM),
+        out_specs=VMEM,
         scratch_shapes=[pltpu.VMEM((orbitals, 3 * n), F32)] + slopes_scratch(n),
         compiler_params=params(),
         cost_estimate=lasting(5),
@@ -411,21 +438,20 @@
     )(order, inverse, positions)
 
 
-def route_kernel(meta_ref, info_in, own_in, code_in, states_ref, out_ref, outcode_ref, *refs):
-    info_ref, own_ref, code_ref, parents_ref, sem, out_sem = refs
+def route_kernel(meta_ref, info_in, own_in, states_ref, out_ref, sending_ref, *refs):
+    info_ref, own_ref, parents_ref, sem, out_sem = refs
     walkers = own_ref.shape[0]
     groups = out_ref.shape[0]
     rows = 3 * walkers
     asked = []
     for g in range(groups):
         at = pl.ds(rows, walkers)
-        asked.append(pltpu.make_async_copy(info_in.at[g, at], parents_ref.at[g], sem.at[3]))
+        asked.append(pltpu.make_async_copy(info_in.at[g, at], parents_ref.at[g], sem.at[2]))
     for each in asked:
         each.start()
     loads = [
         pltpu.make_async_copy(info_in, info_ref, sem.at[0]),
         pltpu.make_async_copy(own_in, own_ref, sem.at[1]),
-        pltpu.make_async_copy(code_in, code_ref, sem.at[2]),
     ]
     for load in loads:
         load.start()
@@ -440,15 +466,13 @@
             mine = jnp.logical_and(within >= 0, within < walkers)
             wanted = jnp.where(mine, within, wanted)
         sending.append(jnp.where(me == g, 0, wanted))
+        sending_ref[g] = sending[g]
     for load in loads[1:]:
         load.wait()
     stores = []
     for g in range(groups):
         source = sending[g]
-        stores.append(pltpu.make_async_copy(own_ref.at[source], out_ref.at[g], out_sem.at[0, g]))
-        stores.append(
-            pltpu.make_async_copy(code_ref.at[source], outcode_ref.at[g], out_sem.at[1, g])
-        )
+        stores.append(pltpu.make_async_copy(own_ref.at[source], out_ref.at[g], out_sem.at[g]))
     for store in stores:
         store.start()
     loads[0].wait()
@@ -468,30 +492,28 @@
         store.wait()
 
 
-def route_call(meta, info, own, code):
+def route_call(meta, info, own):
     groups = info.shape[0]
-    shapes = [(groups, *own.shape[1:]), (groups, *code.shape[1:])]
     return pl.pallas_call(
         route_kernel,
         name="route",
         out_shape=(
             jax.ShapeDtypeStruct((NMOVE, 8, 128), F32),
-            jax.ShapeDtypeStruct(shapes[0], F32),
-            jax.ShapeDtypeStruct(shapes[1], code.dtype),
+            jax.ShapeDtypeStruct((groups, *own.shape[1:]), F32),
+            jax.ShapeDtypeStruct((groups,), jnp.int32),
         ),
-        in_specs=[SMEM, ANY, ANY, ANY],
-        out_specs=(VMEM, ANY, ANY),
+        in_specs=[SMEM, ANY, ANY],
+        out_specs=(VMEM, ANY, SMEM),
         scratch_shapes=[
             pltpu.VMEM(info.shape, F32),
             pltpu.VMEM(own.shape, F32),
-            pltpu.VMEM(code.shape, code.dtype),
             pltpu.SMEM((groups, own.shape[0], 128), F32),
-            pltpu.SemaphoreType.DMA((4,)),
-            pltpu.SemaphoreType.DMA((2, groups)),
+            pltpu.SemaphoreType.DMA((3,)),
+            pltpu.SemaphoreType.DMA((groups,)),
         ],
-        compiler_params=params(WHOLE),
+        compiler_params=params(ALMOST),
         cost_estimate=lasting(3),
-    )(meta, info, own, code)
+    )(meta, info, own)
 
 
 def select_kernel(meta_ref, own_ref, got_ref, grad_in, vm_ref, out_ref, grad_ref, sem):
@@ -575,51 +597,82 @@
     return jnp.concatenate([jnp.where(own_lanes(n, w), x, 0.0) for w in range(n // K)], axis=0)
 
 
+BLOCK_ROWS = 8 + MOVED
+
+
+def log_rows(block, n, kind):
+    start = block * (BLOCK_ROWS + n)
+    if kind == "moved":
+        return slice(start, start + 8)
+    if kind == "t":
+        return slice(start + 8, start + BLOCK_ROWS)
+    return slice(start + BLOCK_ROWS, start + BLOCK_ROWS + n)
+
+
+def log_y(n):
+    start = NMOVE * (BLOCK_ROWS + n)
+    return slice(start, start + n // K * MOVED)
+
+
 def step_kernel(block, count, *refs):
     refs = list(refs)
+    last = block == NMOVE - 1
     parts = [refs.pop(0) for _ in range(count)]
-    later_ref = refs.pop(0) if block < NMOVE - 1 else None
-    if block:
-        t_before = refs.pop(0)
-    if block > 1:
-        y_before = refs.pop(0)
-    states_ref, phi_ref, vm_ref, table_ref = [refs.pop(0) for _ in range(4)]
-    s_ref, moved_ref, d_ref, t_ref = [refs.pop(0) for _ in range(4)]
-    y_ref = refs.pop(0) if block else None
-    sum_ref, big_ref, even_ref, odd_ref, wx_ref = refs
-    if later_ref is not None:
-        s_ref[MOVED:, :] = later_ref[...]
-    n = sum_ref.shape[1]
+    before_ref = refs.pop(0)
+    if last:
+        meta_ref, whole_ref = refs.pop(0), refs.pop(0)
+    else:
+        later_ref = refs.pop(0)
+    states_ref, vm_ref, table_ref = [refs.pop(0) for _ in range(3)]
+    if last:
+        mine_ref, give_ref = refs.pop(0), refs.pop(0)
+    else:
+        s_ref = refs.pop(0)
+    log_ref, sum_ref, big_ref, even_ref, odd_ref, wx_ref = refs
+    orbitals, n = sum_ref.shape
+    y_rows = log_y(n)
+    phi_rows = slice(y_rows.stop, y_rows.stop + orbitals)
+    if not last:
+        s_ref[MOVED:, :] = later_ref[orbitals:, :]
+        log_ref[phi_rows, :] = later_ref[0:orbitals, :]
     state = states_ref[block]
     if block == 0:
-        t_ref[...] = unit(0, n)
+        phi_ref = before_ref
+        t = unit(0, n)
         drifts = drift_of(0, total(parts), None)
     else:
-        s = tree([ref[0:MOVED, :] for ref in parts])
+        phi_ref = before_ref.at[phi_rows]
+        done = slice(0, block * (BLOCK_ROWS + n))
+        log_ref[done, :] = before_ref[done, :]
+        t_before = before_ref[log_rows(block - 1, n, "t"), :]
+        big_ref[0:MOVED, :] = tree([ref[0:MOVED, :] for ref in parts])
         if block > 1:
-            s_ref[0:MOVED, :] = s
-            big_ref[...] = dot(y_before[...], s_ref[0:MOVED, :])
-            s = s - fold(big_ref[...])
-        s_ref[0:MOVED, :] = s
-        y_all = dot_nt(spread(s_ref[0:MOVED, :]), t_before[...])
+            y_before = before_ref[y_rows, 0:MOVED]
+            big_ref[MOVED:, :] = dot(y_before, big_ref[0:MOVED, :])
+            big_ref[0:MOVED, :] = big_ref[0:MOVED, :] - fold(big_ref[MOVED:, :])
+        y_all = dot_nt(spread(big_ref[0:MOVED, :]), t_before)
         if block > 1:
-            y_all = y_all + y_before[...]
-        y_ref[...] = y_all
+            y_all = y_all + before_ref[y_rows, 0:MOVED]
+        log_ref[y_rows, 0:MOVED] = y_all
+        start = y_rows.start + block * K
         rows = jnp.concatenate(
             [
-                y_ref[w * MOVED + block * K : w * MOVED + (block + 1) * K, :]
+                log_ref[start + w * MOVED : start + w * MOVED + K, 0:MOVED]
                 for w in range(n // K)
             ],
             axis=0,
         )
-        t_ref[...] = unit(block, n) - jnp.transpose(rows)
+        log_ref[log_rows(block, n, "t"), :] = unit(block, n) - jnp.transpose(rows)
+        t = log_ref[log_rows(block, n, "t"), :]
         q = tree([ref[MOVED:, :] for ref in parts])
-        drifts = drift_of(block, q, t_ref[...])
+        drifts = drift_of(block, q, t)
+    if block == 0:
+        log_ref[log_rows(0, n, "t"), :] = t
     speeds = jnp.sum(drifts * drifts, axis=0, keepdims=True)
     capped = drifts / jnp.sqrt(1.0 + TAU * speeds)
     moved = state[0:3, :] + state[3:4, :] * (TAU * capped + ROOT_TAU * state[4:7, :])
-    moved_ref[0:3, :] = moved
-    moved_ref[3:8, :] = jnp.zeros((5, n), F32)
+    moved_rows = log_rows(block, n, "moved")
+    log_ref[moved_rows, :] = jnp.concatenate([moved, jnp.zeros((5, n), F32)], axis=0)
     wx, _ = axis_weights(moved[0:1, :], False)
     wy, _ = axis_weights(moved[1:2, :], False)
     wz, _ = axis_weights(moved[2:3, :], False)
@@ -635,25 +688,39 @@
 
     lax.fori_loop(0, GRID // 2, body, 0, unroll=UNROLL)
     change = sum_ref[...] - phi_ref[...]
-    d_ref[...] = jnp.transpose(change)
-    s_ref[0:MOVED, :] = fold(dot(vm_ref[...], change))
-
-
-def step_call(block, parts, later, carried, states, phi, vm, table):
+    change_rows = log_rows(block, n, "change")
+    log_ref[change_rows, 0:orbitals] = jnp.transpose(change)
+    if not last:
+        s_ref[0:MOVED, :] = fold(dot(vm_ref[...], change))
+        return
+    walkers = whole_ref.shape[0]
+    for i in range(walkers // 2):
+        for w, out_ref in zip(both_halves(meta_ref, walkers, i), (mine_ref, give_ref)):
+            at = pl.ds(pl.multiple_of(change_rows.start + w * K, 8), K)
+            out_ref[i] = dot(log_ref[at, 0:orbitals], whole_ref[w])
+
+
+def step_call(block, parts, before, more, states, vm, table):
     orbitals, n = table.shape[0], states.shape[2]
     rows = vm.shape[0]
-    operands = [*parts, *later, *carried, states, phi, vm, table]
-    sums = (MOVED + later[0].shape[0] if later else MOVED, n)
-    shapes = [sums, (8, n), (n, orbitals), (MOVED, n)] + [(rows, MOVED)] * (block > 0)
+    operands = [*parts, before, *more, states, vm, table]
+    specs = [VMEM] * len(operands)
+    log = (log_y(n).stop + orbitals, 128)
+    if block == NMOVE - 1:
+        specs[len(parts) + 1] = SMEM
+        walkers, _, electrons = more[1].shape
+        shapes = [(walkers // 2, K, electrons)] * 2 + [log]
+    else:
+        shapes = [(MOVED + more[0].shape[0] - orbitals, n), log]
     return pl.pallas_call(
         functools.partial(step_kernel, block, len(parts)),
         name="step",
         out_shape=tuple(jax.ShapeDtypeStruct(shape, F32) for shape in shapes),
-        in_specs=[VMEM] * len(operands),
+        in_specs=specs,
         out_specs=(VMEM,) * len(shapes),
         scratch_shapes=[
             pltpu.VMEM((orbitals, n), F32),
-            pltpu.VMEM((rows, n), F32),
+            pltpu.VMEM((MOVED + rows, n), F32),
             pltpu.VMEM((WIDE, 2 * n), BF16),
             pltpu.VMEM((WIDE, 2 * n), BF16),
             pltpu.VMEM((GRID, n), F32),
@@ -666,8 +733,9 @@
 def last_kernel(counts, *refs):
     refs = list(refs)
     sums = [[refs.pop(0) for _ in range(count)] for count in counts]
-    ts = [refs.pop(0)[...] for _ in range(NMOVE)]
-    vm_ref, out_ref, l_ref = refs
+    log_ref, vm_ref, out_ref, l_ref = refs
+    n = log_ref.shape[1]
+    ts = [log_ref[log_rows(block, n, "t"), :] for block in range(NMOVE)]
     for block in range(NMOVE - 1):
         r = unit(block, ts[block].shape[1])
         if block:
@@ -683,9 +751,9 @@
         out_ref[w] = jnp.transpose(dot(factor, vm_ref[at, :]))
 
 
-def last_call(s_parts, ts, vm):
+def last_call(s_parts, log, vm):
     rows, orbitals = vm.shape
-    operands = [part for parts in s_parts for part in parts] + list(ts) + [vm]
+    operands = [part for parts in s_parts for part in parts] + [log, vm]
     return pl.pallas_call(
         functools.partial(last_kernel, [len(parts) for parts in s_parts]),
         name="last",
@@ -707,8 +775,8 @@
 
 
 def assemble_kernel(meta_ref, own_ref, got_ref, code_ref, *refs):
-    change_refs = refs[: NMOVE - 1]
-    v_ref, mine_ref, give_ref, held_ref, sem = refs[NMOVE - 1 :]
+    log_ref, v_ref, mine_ref, give_ref, held_ref, sem = refs
+    n = log_ref.shape[1]
     walkers, orbitals, electrons = own_ref.shape
     load = pltpu.make_async_copy(code_ref, held_ref, sem)
     load.start()
@@ -727,15 +795,18 @@
             level = held_ref[group].astype(jnp.int32).astype(F32) * (1.0 / LEVELS)
             v = jnp.where(here, own_ref[place], level * jnp.abs(level) * scale)
             v_ref[w] = v
-            at = pl.ds(pl.multiple_of(w * K, K), K)
-            change = jnp.concatenate([ref[at, :] for ref in change_refs], axis=0)
+            change = []
+            for b in range(NMOVE - 1):
+                at = log_rows(b, n, "change").start + w * K
+                change.append(log_ref[pl.ds(pl.multiple_of(at, 8), K), 0:orbitals])
+            change = jnp.concatenate(change, axis=0)
             out_ref[i] = dot(change, v)
         return carry
 
     lax.fori_loop(0, walkers // 2, body, 0)
 
 
-def assemble_call(meta, inverse, got, code, changes):
+def assemble_call(meta, inverse, got, code, log):
     walkers, orbitals, electrons = inverse.shape
     half = (walkers // 2, (NMOVE - 1) * K, electrons)
     return pl.pallas_call(
@@ -746,7 +817,7 @@
             jax.ShapeDtypeStruct(half, F32),
             jax.ShapeDtypeStruct(half, F32),
         ),
-        in_specs=[SMEM, VMEM, VMEM, ANY] + [VMEM] * len(changes),
+        in_specs=[SMEM, VMEM, VMEM, ANY, VMEM],
         out_specs=(VMEM,) * 3,
         scratch_shapes=[
             pltpu.VMEM(code.shape, code.dtype),
@@ -754,33 +825,7 @@
         ],
         compiler_params=params(),
         cost_estimate=lasting(4),
-    )(meta, inverse, got, code, *changes)
-
-
-def sums_kernel(meta_ref, v_ref, change_ref, mine_ref, give_ref):
-    walkers = v_ref.shape[0]
-
-    def body(i, carry):
-        for w, out_ref in zip(both_halves(meta_ref, walkers, i), (mine_ref, give_ref)):
-            at = pl.ds(pl.multiple_of(w * K, K), K)
-            out_ref[i] = dot(change_ref[at, :], v_ref[w])
-        return carry
-
-    lax.fori_loop(0, walkers // 2, body, 0)
-
-
-def sums_call(meta, inverse, change):
-    walkers, _, electrons = inverse.shape
-    half = jax.ShapeDtypeStruct((walkers // 2, K, electrons), F32)
-    return pl.pallas_call(
-        sums_kernel,
-        name="sums",
-        out_shape=(half, half),
-        in_specs=[SMEM, VMEM, VMEM],
-        out_specs=(VMEM, VMEM),
-        compiler_params=params(),
-        cost_estimate=lasting(1),
-    )(meta, inverse, change)
+    )(meta, inverse, got, code, log)
 
 
 def update_kernel(order_ref, meta_ref, v_ref, factor_ref, l_ref, *refs):
@@ -824,8 +869,7 @@
     )(order, meta, inverse, factor, rows, *sums)
 
 
-def place_kernel(meta_ref, own_ref, got_ref, *refs):
-    out_ref = refs[NMOVE]
+def place_kernel(meta_ref, own_ref, got_ref, log_ref, out_ref):
     _, walkers, electrons = own_ref.shape
     parts = electrons // got_ref.shape[2]
     lane = lax.broadcasted_iota(jnp.int32, (1, electrons), 1)
@@ -834,7 +878,8 @@
         fresh = []
         for b in range(NMOVE):
             block = meta_ref[walkers + b]
-            fresh.append((block, roll(refs[b][...], (block - w) * K)))
+            moved = log_ref[log_rows(b, log_ref.shape[1], "moved"), :]
+            fresh.append((block, roll(moved, (block - w) * K)))
         for d in range(3):
             at = MOVED + (d + 1) * parts
             far = jnp.concatenate(
@@ -847,16 +892,16 @@
             out_ref[d, w : w + 1, :] = line
 
 
-def place_call(meta, positions, got, moved):
+def place_call(meta, positions, got, log):
     return pl.pallas_call(
         place_kernel,
         name="place",
         out_shape=jax.ShapeDtypeStruct(positions.shape, F32),
-        in_specs=[SMEM] + [VMEM] * (2 + NMOVE),
+        in_specs=[SMEM] + [VMEM] * 3,
         out_specs=VMEM,
         compiler_params=params(),
         cost_estimate=lasting(1),
-    )(meta, positions, got, *moved)
+    )(meta, positions, got, log)
 
 
 def swap(x, axis, k):
@@ -894,34 +939,34 @@
 
     info = alltoall(pack_call(parent, block_order, positions, gaussian, accepted, groups))
     own, code = columns_call(block_order, inverse, positions)
-    states, outgoing, code = route_call(meta, info, own, code)
+    states, outgoing, sending = route_call(meta, info, own)
     got = alltoall(outgoing)
-    phi, grad = slopes_call(states, spline_table)
+    phi, grad, code = slopes_call(sending, states, spline_table, code)
     got, code, phi, grad = together(got, code, phi, grad)
     code = alltoall(code)
     vm, first = select_call(meta, own, got, grad)
     p0 = exchange(first, "orb")
 
-    def step(b, parts, later, carried, phi):
-        return step_call(b, parts, later, carried, states, phi, vm, spline_table)
-
-    phi1, later1 = later_call(1, states, spline_table, vm)
-    p1, new0, change0, t0 = step(0, p0, [later1], [], phi)
+    def step(b, parts, before, more):
+        return step_call(b, parts, before, more, states, vm, spline_table)
+
+    later = later_call(1, states, spline_table, vm)
+    p1, log = step(0, p0, phi, [later])
     p1 = exchange(p1, "orb")
-    phi2, later2 = later_call(2, states, spline_table, vm)
-    p2, new1, change1, t1, y = step(1, p1, [later2], [t0], phi1)
+    later = later_call(2, states, spline_table, vm)
+    p2, log = step(1, p1, log, [later])
     p2 = exchange(p2, "orb")
-    phi3, later3 = later_call(3, states, spline_table, vm)
-    p3, new2, change2, t2, y = step(2, p2, [later3], [t1, y], phi2)
+    held, code = together(states, code)
+    later = later_call(3, held, spline_table, vm)
+    p3, log = step(2, p2, log, [later])
     p3 = exchange(p3, "orb")
-    whole, mine, give = assemble_call(meta, inverse, got, code, [change0, change1, change2])
+    whole, mine, give = assemble_call(meta, inverse, got, code, log)
     p3, mine, give = together(p3, mine, give)
     early = mine + swap(give, "orb", 1)
-    _, new3, change3, t3, _ = step(3, p3, [], [t2, y], phi3)
-    mine, give = sums_call(meta, whole, change3)
+    mine, give, log = step(3, p3, log, [meta, whole])
     late = mine + swap(give, "orb", 1)
-    factor, rows = last_call([p2, p3], [t0, t1, t2, t3], vm)
-    new_positions = place_call(meta, positions, got, [new0, new1, new2, new3])
+    factor, rows = last_call([p2, p3], log, vm)
+    new_positions = place_call(meta, positions, got, log)
     factor, new_positions = together(factor, new_positions)
     (early, late), factor = add_up([early, late], "orb", factor)
     new_inverse = update_call(block_order, meta, whole, factor, rows, [early[0], late[0], early[1], late[1]])

time: 108 us -> 104 us (0.963)
  local copies, waits for them, and re-layouts: 9.62 us -> 3.47 us
  waiting for transfers between devices: 7.76 us -> 12.1 us
  Pallas kernels: 59.8 us -> 58.6 us
    unnamed x88 -> x32, local copies, waits for them, and re-layouts: 9.62 us -> 3.47 us
    ppermute x18, waiting for transfers between devices: 3.97 us -> 8.49 us  [swap(): lax.ppermute(x, axis, [(i, i ^ k) for i in range(lax.axis_size(axis))])]
    pallas_call x1 -> x0, Pallas kernels: 1.58 us -> none  [sums_call(): pl.pallas_call(sums_kernel, name='sums', out_shape=(half, half), in_specs...]
  transfers between devices with their start and end apart: 21 -> 21, of which waited for: 5 -> 7; matrix products, arithmetic and copies ran while one was open for 1% -> 1% of each run, Pallas kernels for 47% -> 45%
where the time goes in v5:
time: 104 us; the launch traced here: 103 us
  Pallas kernels  58.6 us (56%)
  starting transfers between devices  27.3 us (26%)
  waiting for transfers between devices  12.1 us (12%)
  local copies, waits for them, and re-layouts  3.47 us (3%)
  between operations  1.16 us (1%)
    all_to_all x3, starting transfers between devices, alltoall(): return lax.all_to_all(x, 'walker', split_axis=0, concat_axis=0, tiled=True)  16.4 us
    pallas_call x3, Pallas kernels, later_call(): pl.pallas_call(functools.partial(later_kernel, block), name='later', out_...  13.6 us
    pallas_call x4, Pallas kernels, step_call(): pl.pallas_call(functools.partial(step_kernel, block, len(parts)), name='s...  11.9 us
    ppermute x18, starting transfers between devices, swap(): lax.ppermute(x, axis, [(i, i ^ k) for i in range(lax.axis_size(axis))])  11 us
    ppermute x18, waiting for transfers between devices, swap(): lax.ppermute(x, axis, [(i, i ^ k) for i in range(lax.axis_size(axis))])  8.49 us
    pallas_call x1, Pallas kernels, slopes_call(): pl.pallas_call(first_kernel, name='slopes', out_shape=tuple((jax.ShapeDty...  7.53 us
    pallas_call x1, Pallas kernels, columns_call(): pl.pallas_call(columns_kernel, name='columns', out_shape=(jax.ShapeDtypeS...  5.4 us
    pallas_call x1, Pallas kernels, assemble_call(): pl.pallas_call(assemble_kernel, name='assemble', out_shape=(jax.ShapeDtyp...  3.86 us
  transfers between devices with their start and end apart: 21, of which 7 were waited for; matrix products, arithmetic and copies ran while one was open for 1% of the time, Pallas kernels for 45%

profile of v5, /device:TPU:0, one launch (start us, length us, event | category | flops | bytes accessed | tf_op | source)
XLA Modules:
  0.0 103.4 jit_solution(13568677750705534657)
XLA Ops:
  0.6 0.0 copy-start.11
  0.7 2.4 %pack.1 = f32[8,32,128]{2,1,0:T(8,128)} custom-call(s32[8]{0:T(128)} %parent_ref.1, s32[32]{0:T(128)} %order_ref.5, f32[3,8,512]{2,1,0:T(8,128)} %bitcast.6, f32[3,8,64]{2,1,0:T(8,128)} %bitcast.11, s32[8,64]{1,0:T(8,128)} %refs_2_.1), custom_call_target="tpu_custom_call" | custom-call | flops 100000000 | tf_op jit(solution)/shard_map/pack/pallas_call | solution.py:357
  3.0 7.3 %all-to-all-start = ((f32[8,32,128]{2,1,0:T(8,128)}), f32[8,32,128]{2,1,0:T(8,128)S(1)}, u32[]{:S(2)}, u32[]{:S(2)}) async-start(f32[8,32,128]{2,1,0:T(8,128)} %pack.1), calls=%async_computation | async-start | bytes 262144 | tf_op jit(solution)/shard_map/all_to_all | solution.py:929
  10.3 5.4 %columns.1 = (f32[8,80,128]{2,1,0:T(8,128)}, s16[8,128,512]{2,1,0:T(8,128)(2,1)}) custom-call(s32[32]{0:T(128)} %order_ref.5, f32[8,128,512]{2,1,0:T(8,128)} %own_ref.1, f32[3,8,512]{2,1,0:T(8,128)} %bitcast.7), custom_call_target="tpu_custom_call" | custom-call | flops 300000000 | tf_op jit(solution)/shard_map/columns/pallas_call | solution.py:420
  15.8 0.6 pad_add_fusion.meta_ref.refs_5_
  16.3 1.4 %all-to-all-done.info_in = f32[8,32,128]{2,1,0:T(8,128)S(1)} async-done(((f32[8,32,128]{2,1,0:T(8,128)}), f32[8,32,128]{2,1,0:T(8,128)S(1)}, u32[]{:S(2)}, u32[]{:S(2)}) %all-to-all-start) | async-done | bytes 131104 | tf_op jit(solution)/shard_map/all_to_all | solution.py:929
  17.7 0.6 copy-done.14
  18.3 3.5 %route.1 = (f32[4,8,128]{2,1,0:T(8,128)}, f32[8,80,128]{2,1,0:T(8,128)}, s32[8]{0:T(128)}) custom-call(s32[14]{0:T(128)} %pad_add_fusion.meta_ref.refs_5_, f32[8,32,128]{2,1,0:T(8,128)} %copy-done.14, f32[8,80,128]{2,1,0:T(8,128)} %get-tuple-element.43.own_in.own_ref), custom_call_target="tpu_custom_call" | custom-call | flops 300000000 | tf_op jit(solution)/shard_map/route/pallas_call | solution.py:497
  21.8 4.7 %all-to-all-start.1 = ((f32[8,80,128]{2,1,0:T(8,128)}), f32[8,80,128]{2,1,0:T(8,128)}, u32[]{:S(2)}, u32[]{:S(2)}) async-start(f32[8,80,128]{2,1,0:T(8,128)} %get-tuple-element.44), calls=%async_computation.1 | async-start | bytes 655360 | tf_op jit(solution)/shard_map/all_to_all | solution.py:929
  26.5 7.5 %slopes.1 = (f32[128,128]{1,0:T(8,128)}, f32[128,384]{1,0:T(8,128)}, s16[8,128,512]{2,1,0:T(8,128)(2,1)}) custom-call(s32[8]{0:T(128)} %get-tuple-element.45.sending_ref, f32[4,8,128]{2,1,0:T(8,128)} %get-tuple-element.61.states_ref.refs_6_.refs_7_, bf16[128,13824]{1,0:T(8,128)(2,1)} %refs_9_.1, s16[8,128,512]{2,1,0:T(8,128)(2,1)} %get-tuple-element.47.code_in), custom_call_target="tpu_custom_call" | custom-call | flops 500000000 | tf_op jit(solution)/shard_map/slopes/pallas_call | solution.py:188
  34.0 0.0 copy-start.5
  34.0 2.3 %all-to-all-done.1.got_ref = f32[8,80,128]{2,1,0:T(8,128)} async-done(((f32[8,80,128]{2,1,0:T(8,128)}), f32[8,80,128]{2,1,0:T(8,128)}, u32[]{:S(2)}, u32[]{:S(2)}) %all-to-all-start.1) | async-done | bytes 327712 | tf_op jit(solution)/shard_map/all_to_all | solution.py:929
  36.3 4.4 %all-to-all-start.2 = ((s16[8,128,512]{2,1,0:T(8,128)(2,1)}), s16[8,128,512]{2,1,0:T(8,128)(2,1)}, u32[]{:S(2)}, u32[]{:S(2)}) async-start(s16[8,128,512]{2,1,0:T(8,128)(2,1)} %get-tuple-element.60), calls=%async_computation.2 | async-start | bytes 2097152 | tf_op jit(solution)/shard_map/all_to_all | solution.py:929
  40.7 2.9 %select.3 = (f32[512,128]{1,0:T(8,128)}, f32[8,128]{1,0:T(8,128)}) custom-call(s32[14]{0:T(128)} %pad_add_fusion.meta_ref.refs_5_, f32[8,80,128]{2,1,0:T(8,128)} %get-tuple-element.43.own_in.own_ref, f32[8,80,128]{2,1,0:T(8,128)} %all-to-all-done.1.got_ref, f32[128,384]{1,0:T(8,128)} %get-tuple-element.52.grad_in), custom_call_target="tpu_custom_call" | custom-call | flops 200000000 | tf_op jit(solution)/shard_map/select/pallas_call | solution.py:577
  43.6 0.1 collective-permute-start.2
  43.7 1.6 %collective-permute-start.1 = (f32[8,128]{1,0:T(8,128)}, f32[8,128]{1,0:T(8,128)S(1)}, u32[]{:S(2)}, u32[]{:S(2)}) collective-permute-start(f32[8,128]{1,0:T(8,128)} %get-tuple-element.53.refs_0_), channel_id=1, source_target_pairs={{0,2},{1,3},{2,0},{3,1},{4,6},{5,7},{6,4},{7,5},{8,10},{9,11},{10,... | collective-permute-start | bytes 12296 | tf_op jit(solution)/shard_map/ppermute | solution.py:908
  45.3 0.3 collective-permute-start
  45.6 0.9 copy-done.1
  46.5 4.5 %later.3.refs_5_ = f32[184,128]{1,0:T(8,128)S(1)} custom-call(f32[4,8,128]{2,1,0:T(8,128)S(1)} %copy-done.5, bf16[128,13824]{1,0:T(8,128)(2,1)S(1)} %copy-done, f32[512,128]{1,0:T(8,128)S(1)} %copy-done.1), custom_call_target="tpu_custom_call" | custom-call | flops 500000000 | tf_op jit(solution)/shard_map/later/pallas_call | solution.py:228
  51.1 0.0 collective-permute-done.2.refs_3_
  51.1 0.0 collective-permute-done.1.refs_2_
  51.1 0.0 collective-permute-done.refs_1_
  51.1 1.8 %step.4 = (f32[120,128]{1,0:T(8,128)S(1)}, f32[1440,128]{1,0:T(8,128)S(1)}) custom-call(f32[8,128]{1,0:T(8,128)S(1)} %copy-done.13, f32[8,128]{1,0:T(8,128)S(1)} %collective-permute-done.refs_1_, f32[8,128]{1,0:T(8,128)S(1)} %collective-permute-done.1.refs_2_, f32[8,128]{1,0:T(8,128)S(1)} %collective-permute-done.2.refs_3_, f32[128,128]{1,0:T(8,128)S(1)} %copy-done.9, ...), custom_call_target="tpu_custom_call" | custom-call | flops 300000000 | tf_op jit(solution)/shard_map/step/pallas_call | solution.py:715
  53.0 1.2 %collective-permute-start.5 = (f32[120,128]{1,0:T(8,128)S(1)}, f32[120,128]{1,0:T(8,128)S(1)}, u32[]{:S(2)}, u32[]{:S(2)}) collective-permute-start(f32[120,128]{1,0:T(8,128)S(1)} %get-tuple-element.56.refs_0_), channel_id=1, source_target_pairs={{0,3},{1,2},{2,1},{3,0},{4,7},{5,6},{6,5},{7,4},{8,11},{9,10},{10,... | collective-permute-start | bytes 184328 | tf_op jit(solution)/shard_map/ppermute | solution.py:908
  54.1 0.7 collective-permute-start.4
  54.9 0.0 collective-permute-start.3
  54.9 4.6 %later.4.refs_5_ = f32[232,128]{1,0:T(8,128)S(1)} custom-call(f32[4,8,128]{2,1,0:T(8,128)S(1)} %copy-done.5, bf16[128,13824]{1,0:T(8,128)(2,1)S(1)} %copy-done, f32[512,128]{1,0:T(8,128)S(1)} %copy-done.1), custom_call_target="tpu_custom_call" | custom-call | flops 500000000 | tf_op jit(solution)/shard_map/later/pallas_call | solution.py:228
  59.5 0.0 collective-permute-done.5.refs_3_
  59.5 0.0 collective-permute-done.4.refs_2_
  59.5 0.0 collective-permute-done.3.refs_1_
  59.5 3.1 %step.5 = (f32[168,128]{1,0:T(8,128)}, f32[1440,128]{1,0:T(8,128)S(1)}) custom-call(f32[120,128]{1,0:T(8,128)S(1)} %get-tuple-element.56.refs_0_, f32[120,128]{1,0:T(8,128)S(1)} %collective-permute-done.3.refs_1_, f32[120,128]{1,0:T(8,128)S(1)} %collective-permute-done.4.refs_2_, f32[120,128]{1,0:T(8,128)S(1)} %collective-permute-done.5.refs_3_, ...), custom_call_target="tpu_custom_call" | custom-call | flops 300000000 | tf_op jit(solution)/shard_map/step/pallas_call | solution.py:715
  62.6 0.9 copy-done.6
  63.5 1.4 %collective-permute-start.8 = (f32[168,128]{1,0:T(8,128)}, f32[168,128]{1,0:T(8,128)}, u32[]{:S(2)}, u32[]{:S(2)}) collective-permute-start(f32[168,128]{1,0:T(8,128)} %get-tuple-element.58.refs_0_), channel_id=1, source_target_pairs={{0,3},{1,2},{2,1},{3,0},{4,7},{5,6},{6,5},{7,4},{8,11},{9,10},{10,... | collective-permute-start | bytes 258056 | tf_op jit(solution)/shard_map/ppermute | solution.py:908
  64.9 0.7 collective-permute-start.7
  65.6 0.0 collective-permute-start.6
  65.6 0.0 all-to-all-done.2.code_ref
  65.6 0.9 copy-done.2
  66.6 4.5 %later.5.refs_5_ = f32[280,128]{1,0:T(8,128)S(1)} custom-call(f32[4,8,128]{2,1,0:T(8,128)S(1)} %copy-done.5, bf16[128,13824]{1,0:T(8,128)(2,1)S(1)} %copy-done, f32[512,128]{1,0:T(8,128)S(1)} %copy-done.2), custom_call_target="tpu_custom_call" | custom-call | flops 500000000 | tf_op jit(solution)/shard_map/later/pallas_call | solution.py:228
  71.1 0.0 collective-permute-done.8.refs_3_
  71.1 0.0 collective-permute-done.7.refs_2_
  71.1 0.0 collective-permute-done.6.refs_1_
  71.1 0.0 copy-start.4
  71.1 3.6 %step.6 = (f32[216,128]{1,0:T(8,128)S(1)}, f32[1440,128]{1,0:T(8,128)S(1)}) custom-call(f32[168,128]{1,0:T(8,128)} %get-tuple-element.58.refs_0_, f32[168,128]{1,0:T(8,128)} %collective-permute-done.6.refs_1_, f32[168,128]{1,0:T(8,128)} %collective-permute-done.7.refs_2_, f32[168,128]{1,0:T(8,128)} %collective-permute-done.8.refs_3_, ...), custom_call_target="tpu_custom_call" | custom-call | flops 300000000 | tf_op jit(solution)/shard_map/step/pallas_call | solution.py:715
  74.8 1.5 %collective-permute-start.11 = (f32[216,128]{1,0:T(8,128)S(1)}, f32[216,128]{1,0:T(8,128)S(1)}, u32[]{:S(2)}, u32[]{:S(2)}) collective-permute-start(f32[216,128]{1,0:T(8,128)S(1)} %get-tuple-element.67.refs_0_.refs_4_), channel_id=1, source_target_pairs={{0,3},{1,2},{2,1},{3,0},{4,7},{5,6},{6,5},{7,4},{8,11},{9,10},{10,... | collective-permute-start | bytes 331784 | tf_op jit(solution)/shard_map/ppermute | solution.py:908
  76.2 0.7 collective-permute-start.10
  77.0 3.9 %assemble.1 = (f32[8,128,512]{2,1,0:T(8,128)S(1)}, f32[4,48,512]{2,1,0:T(8,128)S(1)}, f32[4,48,512]{2,1,0:T(8,128)S(1)}) custom-call(s32[14]{0:T(128)S(1)} %copy-done.10, f32[8,128,512]{2,1,0:T(8,128)S(1)} %copy-done.4, f32[8,80,128]{2,1,0:T(8,128)} %all-to-all-done.1.got_ref, s16[8,128,512]{2,1,0:T(8,128)(2,1)} %all-to-all-done.2.code_ref, ...), custom_call_target="tpu_custom_call" | custom-call | flops 400000000 | tf_op jit(solution)/shard_map/assemble/pallas_call | solution.py:812
  80.9 1.7 %collective-permute-done.10.refs_2_.refs_6_ = f32[216,128]{1,0:T(8,128)S(1)} collective-permute-done((f32[216,128]{1,0:T(8,128)S(1)}, f32[216,128]{1,0:T(8,128)S(1)}, u32[]{:S(2)}, u32[]{:S(2)}) %collective-permute-start.10) | collective-permute-done | bytes 110624 | tf_op jit(solution)/shard_map/ppermute | solution.py:908
  82.6 0.0 collective-permute-done.9.refs_1_.refs_5_
  82.6 0.0 collective-permute-start.12
  82.6 1.7 %collective-permute-done.12 = f32[4,48,512]{2,1,0:T(8,128)S(1)} collective-permute-done((f32[4,48,512]{2,1,0:T(8,128)S(1)}, f32[4,48,512]{2,1,0:T(8,128)S(1)}, u32[]{:S(2)}, u32[]{:S(2)}) %collective-permute-start.12) | collective-permute-done | bytes 393248 | tf_op jit(solution)/shard_map/ppermute | solution.py:908
  84.3 0.1 add.12
  84.4 1.5 %collective-permute-start.13 = (f32[4,48,512]{2,1,0:T(8,128)S(1)}, f32[4,48,512]{2,1,0:T(8,128)S(1)}, u32[]{:S(2)}, u32[]{:S(2)}) collective-permute-start(f32[4,48,512]{2,1,0:T(8,128)S(1)} %add.12), channel_id=1, source_target_pairs={{0,2},{1,3},{2,0},{3,1},{4,6},{5,7},{6,4},{7,5},{8,10},{9,11},{10,... | collective-permute-start | bytes 1179656 | tf_op jit(solution)/shard_map/ppermute | solution.py:908
  85.9 3.3 %step.7 = (f32[4,16,512]{2,1,0:T(8,128)S(1)}, f32[4,16,512]{2,1,0:T(8,128)S(1)}, f32[1440,128]{1,0:T(8,128)S(1)}) custom-call(f32[216,128]{1,0:T(8,128)S(1)} %get-tuple-element.67.refs_0_.refs_4_, f32[216,128]{1,0:T(8,128)S(1)} %collective-permute-done.9.refs_1_.refs_5_, f32[216,128]{1,0:T(8,128)S(1)} %collective-permute-done.10.refs_2_.refs_6_, ...), custom_call_target="tpu_custom_call" | custom-call | flops 300000000 | tf_op jit(solution)/shard_map/step/pallas_call | solution.py:715
  89.2 1.4 %collective-permute-done.14 = f32[4,16,512]{2,1,0:T(8,128)S(1)} collective-permute-done((f32[4,16,512]{2,1,0:T(8,128)S(1)}, f32[4,16,512]{2,1,0:T(8,128)S(1)}, u32[]{:S(2)}, u32[]{:S(2)}) %collective-permute-start.14) | collective-permute-done | bytes 131104 | tf_op jit(solution)/shard_map/ppermute | solution.py:908
  90.6 0.6 collective-permute-start.15
  91.3 1.8 %place.1 = f32[3,8,512]{2,1,0:T(8,128)} custom-call(s32[14]{0:T(128)S(1)} %copy-done.10, f32[3,8,512]{2,1,0:T(8,128)S(1)} %bitcast.8, f32[8,80,128]{2,1,0:T(8,128)} %all-to-all-done.1.got_ref, f32[1440,128]{1,0:T(8,128)S(1)} %get-tuple-element.72.refs_8_.log_ref), custom_call_target="tpu_custom_call" | custom-call | flops 100000000 | tf_op jit(solution)/shard_map/place/pallas_call | solution.py:896
  93.1 2.9 %last.1 = (f32[8,128,64]{2,1,0:T(8,128)S(1)}, f32[512,64]{1,0:T(8,128)S(1)}) custom-call(f32[168,128]{1,0:T(8,128)} %get-tuple-element.58.refs_0_, f32[168,128]{1,0:T(8,128)} %collective-permute-done.6.refs_1_, f32[168,128]{1,0:T(8,128)} %collective-permute-done.7.refs_2_, f32[168,128]{1,0:T(8,128)} %collective-permute-done.8.refs_3_, ...), custom_call_target="tpu_custom_call" | custom-call | flops 200000000 | tf_op jit(solution)/shard_map/last/pallas_call | solution.py:757
  96.0 2.4 %collective-permute-done.15 = f32[4,16,512]{2,1,0:T(8,128)S(1)} collective-permute-done((f32[4,16,512]{2,1,0:T(8,128)S(1)}, f32[4,16,512]{2,1,0:T(8,128)S(1)}, u32[]{:S(2)}, u32[]{:S(2)}) %collective-permute-start.15) | collective-permute-done | bytes 131104 | tf_op jit(solution)/shard_map/ppermute | solution.py:908
  98.4 0.0 collective-permute-done.13
  98.4 0.1 add.14.refs_0_
  98.5 0.1 collective-permute-start.16
  98.6 0.6 collective-permute-start.17
  99.1 1.3 %collective-permute-done.17.refs_3_ = f32[4,16,512]{2,1,0:T(8,128)S(1)} collective-permute-done((f32[4,16,512]{2,1,0:T(8,128)S(1)}, f32[4,16,512]{2,1,0:T(8,128)S(1)}, u32[]{:S(2)}, u32[]{:S(2)}) %collective-permute-start.17) | collective-permute-done | bytes 131104 | tf_op jit(solution)/shard_map/ppermute | solution.py:908
  100.4 2.7 %update.1 = f32[8,128,512]{2,1,0:T(8,128)} custom-call(s32[32]{0:T(128)S(1)} %copy-done.12, s32[14]{0:T(128)S(1)} %copy-done.10, f32[8,128,512]{2,1,0:T(8,128)S(1)} %get-tuple-element.71.refs_6_.v_ref, f32[8,128,64]{2,1,0:T(8,128)S(1)} %get-tuple-element.80.factor_ref, f32[512,64]{1,0:T(8,128)S(1)} %get-tuple-element.81.l_ref, ...), custom_call_target="tpu_custom_call" | custom-call | flops 200000000 | tf_op jit(solution)/shard_map/update/pallas_call | solution.py:857
  (31 shorter events, 0.1 us)
Async XLA Ops:
  0.6 15.1 %copy-start.11 = (s32[32]{0:T(128)S(1)}, s32[32]{0:T(128)}, u32[]{:S(2)}) copy-start(s32[32]{0:T(128)} %order_ref.5) | copy-start | bytes 388
  0.6 15.1 %copy-start.15 = (s32[8]{0:T(128)S(1)}, s32[8]{0:T(128)}, u32[]{:S(2)}) copy-start(s32[8]{0:T(128)} %parent_ref.1) | copy-start | bytes 100
  3.0 14.6 %all-to-all-start = ((f32[8,32,128]{2,1,0:T(8,128)}), f32[8,32,128]{2,1,0:T(8,128)S(1)}, u32[]{:S(2)}, u32[]{:S(2)}) async-start(f32[8,32,128]{2,1,0:T(8,128)} %pack.1), calls=%async_computation | async-start | bytes 262144 | tf_op jit(solution)/shard_map/all_to_all | solution.py:929
  17.7 0.7 copy-start.14
  21.8 14.5 %all-to-all-start.1 = ((f32[8,80,128]{2,1,0:T(8,128)}), f32[8,80,128]{2,1,0:T(8,128)}, u32[]{:S(2)}, u32[]{:S(2)}) async-start(f32[8,80,128]{2,1,0:T(8,128)} %get-tuple-element.44), calls=%async_computation.1 | async-start | bytes 655360 | tf_op jit(solution)/shard_map/all_to_all | solution.py:929
  26.5 19.1 %copy-start = (bf16[128,13824]{1,0:T(8,128)(2,1)S(1)}, bf16[128,13824]{1,0:T(8,128)(2,1)}, u32[]{:S(2)}) copy-start(bf16[128,13824]{1,0:T(8,128)(2,1)} %refs_9_.1) | copy-start | bytes 10616836
  34.0 11.6 %copy-start.5 = (f32[4,8,128]{2,1,0:T(8,128)S(1)}, f32[4,8,128]{2,1,0:T(8,128)}, u32[]{:S(2)}) copy-start(f32[4,8,128]{2,1,0:T(8,128)} %get-tuple-element.61.states_ref.refs_6_.refs_7_) | copy-start | bytes 49156
  36.3 29.3 %all-to-all-start.2 = ((s16[8,128,512]{2,1,0:T(8,128)(2,1)}), s16[8,128,512]{2,1,0:T(8,128)(2,1)}, u32[]{:S(2)}, u32[]{:S(2)}) async-start(s16[8,128,512]{2,1,0:T(8,128)(2,1)} %get-tuple-element.60), calls=%async_computation.2 | async-start | bytes 2097152 | tf_op jit(solution)/shard_map/all_to_all | solution.py:929
  40.7 10.4 %copy-start.9 = (f32[128,128]{1,0:T(8,128)S(1)}, f32[128,128]{1,0:T(8,128)}, u32[]{:S(2)}) copy-start(f32[128,128]{1,0:T(8,128)} %get-tuple-element.54.refs_4_) | copy-start | bytes 196612
  43.6 7.4 %collective-permute-start.2 = (f32[8,128]{1,0:T(8,128)}, f32[8,128]{1,0:T(8,128)S(1)}, u32[]{:S(2)}, u32[]{:S(2)}) collective-permute-start(f32[8,128]{1,0:T(8,128)} %get-tuple-element.53.refs_0_), channel_id=1, source_target_pairs={{0,3},{1,2},{2,1},{3,0},{4,7},{5,6},{6,5},{7,4},{8,11},{9,10},{10,... | collective-permute-start | bytes 12296 | tf_op jit(solution)/shard_map/ppermute | solution.py:908
  43.7 7.4 %collective-permute-start.1 = (f32[8,128]{1,0:T(8,128)}, f32[8,128]{1,0:T(8,128)S(1)}, u32[]{:S(2)}, u32[]{:S(2)}) collective-permute-start(f32[8,128]{1,0:T(8,128)} %get-tuple-element.53.refs_0_), channel_id=1, source_target_pairs={{0,2},{1,3},{2,0},{3,1},{4,6},{5,7},{6,4},{7,5},{8,10},{9,11},{10,... | collective-permute-start | bytes 12296 | tf_op jit(solution)/shard_map/ppermute | solution.py:908
  45.3 5.8 %collective-permute-start = (f32[8,128]{1,0:T(8,128)}, f32[8,128]{1,0:T(8,128)S(1)}, u32[]{:S(2)}, u32[]{:S(2)}) collective-permute-start(f32[8,128]{1,0:T(8,128)} %get-tuple-element.53.refs_0_), channel_id=1, source_target_pairs={{0,1},{1,0},{2,3},{3,2},{4,5},{5,4},{6,7},{7,6},{8,9},{9,8},{10,11... | collective-permute-start | bytes 12296 | tf_op jit(solution)/shard_map/ppermute | solution.py:908
  45.6 1.0 copy-start.1
  46.5 4.6 %copy-start.13 = (f32[8,128]{1,0:T(8,128)S(1)}, f32[8,128]{1,0:T(8,128)}, u32[]{:S(2)}) copy-start(f32[8,128]{1,0:T(8,128)} %get-tuple-element.53.refs_0_) | copy-start | bytes 12292
  53.0 6.5 %collective-permute-start.5 = (f32[120,128]{1,0:T(8,128)S(1)}, f32[120,128]{1,0:T(8,128)S(1)}, u32[]{:S(2)}, u32[]{:S(2)}) collective-permute-start(f32[120,128]{1,0:T(8,128)S(1)} %get-tuple-element.56.refs_0_), channel_id=1, source_target_pairs={{0,3},{1,2},{2,1},{3,0},{4,7},{5,6},{6,5},{7,4},{8,11},{9,10},{10,... | collective-permute-start | bytes 184328 | tf_op jit(solution)/shard_map/ppermute | solution.py:908
  54.1 5.3 %collective-permute-start.4 = (f32[120,128]{1,0:T(8,128)S(1)}, f32[120,128]{1,0:T(8,128)S(1)}, u32[]{:S(2)}, u32[]{:S(2)}) collective-permute-start(f32[120,128]{1,0:T(8,128)S(1)} %get-tuple-element.56.refs_0_), channel_id=1, source_target_pairs={{0,2},{1,3},{2,0},{3,1},{4,6},{5,7},{6,4},{7,5},{8,10},{9,11},{10,... | collective-permute-start | bytes 184328 | tf_op jit(solution)/shard_map/ppermute | solution.py:908
  54.9 4.6 %collective-permute-start.3 = (f32[120,128]{1,0:T(8,128)S(1)}, f32[120,128]{1,0:T(8,128)S(1)}, u32[]{:S(2)}, u32[]{:S(2)}) collective-permute-start(f32[120,128]{1,0:T(8,128)S(1)} %get-tuple-element.56.refs_0_), channel_id=1, source_target_pairs={{0,1},{1,0},{2,3},{3,2},{4,5},{5,4},{6,7},{7,6},{8,9},{9,8},{10,11... | collective-permute-start | bytes 184328 | tf_op jit(solution)/shard_map/ppermute | solution.py:908
  62.6 0.9 copy-start.6
  63.5 7.6 %collective-permute-start.8 = (f32[168,128]{1,0:T(8,128)}, f32[168,128]{1,0:T(8,128)}, u32[]{:S(2)}, u32[]{:S(2)}) collective-permute-start(f32[168,128]{1,0:T(8,128)} %get-tuple-element.58.refs_0_), channel_id=1, source_target_pairs={{0,3},{1,2},{2,1},{3,0},{4,7},{5,6},{6,5},{7,4},{8,11},{9,10},{10,... | collective-permute-start | bytes 258056 | tf_op jit(solution)/shard_map/ppermute | solution.py:908
  64.9 6.2 %collective-permute-start.7 = (f32[168,128]{1,0:T(8,128)}, f32[168,128]{1,0:T(8,128)}, u32[]{:S(2)}, u32[]{:S(2)}) collective-permute-start(f32[168,128]{1,0:T(8,128)} %get-tuple-element.58.refs_0_), channel_id=1, source_target_pairs={{0,2},{1,3},{2,0},{3,1},{4,6},{5,7},{6,4},{7,5},{8,10},{9,11},{10,... | collective-permute-start | bytes 258056 | tf_op jit(solution)/shard_map/ppermute | solution.py:908
  65.6 5.5 %collective-permute-start.6 = (f32[168,128]{1,0:T(8,128)}, f32[168,128]{1,0:T(8,128)}, u32[]{:S(2)}, u32[]{:S(2)}) collective-permute-start(f32[168,128]{1,0:T(8,128)} %get-tuple-element.58.refs_0_), channel_id=1, source_target_pairs={{0,1},{1,0},{2,3},{3,2},{4,5},{5,4},{6,7},{7,6},{8,9},{9,8},{10,11... | collective-permute-start | bytes 258056 | tf_op jit(solution)/shard_map/ppermute | solution.py:908
  65.6 1.0 copy-start.2
  66.6 4.6 %copy-start.7 = (f32[1440,128]{1,0:T(8,128)S(1)}, f32[1440,128]{1,0:T(8,128)}, u32[]{:S(2)}) copy-start(f32[1440,128]{1,0:T(8,128)} %copy-done.6) | copy-start | bytes 2211844
  71.1 5.9 %copy-start.4 = (f32[8,128,512]{2,1,0:T(8,128)S(1)}, f32[8,128,512]{2,1,0:T(8,128)}, u32[]{:S(2)}) copy-start(f32[8,128,512]{2,1,0:T(8,128)} %own_ref.1) | copy-start | bytes 6291460
  71.1 5.9 %copy-start.10 = (s32[14]{0:T(128)S(1)}, s32[14]{0:T(128)}, u32[]{:S(2)}) copy-start(s32[14]{0:T(128)} %pad_add_fusion.meta_ref.refs_5_) | copy-start | bytes 172
  74.8 6.1 %collective-permute-start.11 = (f32[216,128]{1,0:T(8,128)S(1)}, f32[216,128]{1,0:T(8,128)S(1)}, u32[]{:S(2)}, u32[]{:S(2)}) collective-permute-start(f32[216,128]{1,0:T(8,128)S(1)} %get-tuple-element.67.refs_0_.refs_4_), channel_id=1, source_target_pairs={{0,3},{1,2},{2,1},{3,0},{4,7},{5,6},{6,5},{7,4},{8,11},{9,10},{10,... | collective-permute-start | bytes 331784 | tf_op jit(solution)/shard_map/ppermute | solution.py:908
  76.2 6.3 %collective-permute-start.10 = (f32[216,128]{1,0:T(8,128)S(1)}, f32[216,128]{1,0:T(8,128)S(1)}, u32[]{:S(2)}, u32[]{:S(2)}) collective-permute-start(f32[216,128]{1,0:T(8,128)S(1)} %get-tuple-element.67.refs_0_.refs_4_), channel_id=1, source_target_pairs={{0,2},{1,3},{2,0},{3,1},{4,6},{5,7},{6,4},{7,5},{8,10},{9,11},{10,... | collective-permute-start | bytes 331784 | tf_op jit(solution)/shard_map/ppermute | solution.py:908
  77.0 5.6 %collective-permute-start.9 = (f32[216,128]{1,0:T(8,128)S(1)}, f32[216,128]{1,0:T(8,128)S(1)}, u32[]{:S(2)}, u32[]{:S(2)}) collective-permute-start(f32[216,128]{1,0:T(8,128)S(1)} %get-tuple-element.67.refs_0_.refs_4_), channel_id=1, source_target_pairs={{0,1},{1,0},{2,3},{3,2},{4,5},{5,4},{6,7},{7,6},{8,9},{9,8},{10,11... | collective-permute-start | bytes 331784 | tf_op jit(solution)/shard_map/ppermute | solution.py:908
  77.0 8.9 %copy-start.3 = (f32[512,128]{1,0:T(8,128)S(1)}, f32[512,128]{1,0:T(8,128)}, u32[]{:S(2)}) copy-start(f32[512,128]{1,0:T(8,128)} %get-tuple-element.55.vm_ref.refs_7_.refs_8_.refs_9_) | copy-start | bytes 786436
  82.6 1.7 %collective-permute-start.12 = (f32[4,48,512]{2,1,0:T(8,128)S(1)}, f32[4,48,512]{2,1,0:T(8,128)S(1)}, u32[]{:S(2)}, u32[]{:S(2)}) collective-permute-start(f32[4,48,512]{2,1,0:T(8,128)S(1)} %get-tuple-element.76), channel_id=1, source_target_pairs={{0,1},{1,0},{2,3},{3,2},{4,5},{5,4},{6,7},{7,6},{8,9},{9,8},{10,11... | collective-permute-start | bytes 1179656 | tf_op jit(solution)/shard_map/ppermute | solution.py:908
  84.4 14.0 %collective-permute-start.13 = (f32[4,48,512]{2,1,0:T(8,128)S(1)}, f32[4,48,512]{2,1,0:T(8,128)S(1)}, u32[]{:S(2)}, u32[]{:S(2)}) collective-permute-start(f32[4,48,512]{2,1,0:T(8,128)S(1)} %add.12), channel_id=1, source_target_pairs={{0,2},{1,3},{2,0},{3,1},{4,6},{5,7},{6,4},{7,5},{8,10},{9,11},{10,... | collective-permute-start | bytes 1179656 | tf_op jit(solution)/shard_map/ppermute | solution.py:908
  85.9 5.4 %copy-start.8 = (f32[8,3,512]{2,0,1:T(8,128)S(1)}, f32[8,3,512]{2,0,1:T(8,128)}, u32[]{:S(2)}) copy-start(f32[8,3,512]{2,0,1:T(8,128)} %param.7) | copy-start | bytes 147460
  89.2 1.4 %collective-permute-start.14 = (f32[4,16,512]{2,1,0:T(8,128)S(1)}, f32[4,16,512]{2,1,0:T(8,128)S(1)}, u32[]{:S(2)}, u32[]{:S(2)}) collective-permute-start(f32[4,16,512]{2,1,0:T(8,128)S(1)} %get-tuple-element.78), channel_id=1, source_target_pairs={{0,1},{1,0},{2,3},{3,2},{4,5},{5,4},{6,7},{7,6},{8,9},{9,8},{10,11... | collective-permute-start | bytes 393224 | tf_op jit(solution)/shard_map/ppermute | solution.py:908
  90.6 7.8 %collective-permute-start.15 = (f32[4,16,512]{2,1,0:T(8,128)S(1)}, f32[4,16,512]{2,1,0:T(8,128)S(1)}, u32[]{:S(2)}, u32[]{:S(2)}) collective-permute-start(f32[4,16,512]{2,1,0:T(8,128)S(1)} %add.13), channel_id=1, source_target_pairs={{0,2},{1,3},{2,0},{3,1},{4,6},{5,7},{6,4},{7,5},{8,10},{9,11},{10,... | collective-permute-start | bytes 393224 | tf_op jit(solution)/shard_map/ppermute | solution.py:908
  91.3 9.2 %copy-start.12 = (s32[32]{0:T(128)S(1)}, s32[32]{0:T(128)}, u32[]{:S(2)}) copy-start(s32[32]{0:T(128)} %order_ref.5) | copy-start | bytes 388
  98.5 2.0 %collective-permute-start.16 = (f32[4,48,512]{2,1,0:T(8,128)S(1)}, f32[4,48,512]{2,1,0:T(8,128)S(1)}, u32[]{:S(2)}, u32[]{:S(2)}) collective-permute-start(f32[4,48,512]{2,1,0:T(8,128)S(1)} %add.14.refs_0_), channel_id=1, source_target_pairs={{0,1},{1,0},{2,3},{3,2},{4,5},{5,4},{6,7},{7,6},{8,9},{9,8},{10,11... | collective-permute-start | bytes 1179656 | tf_op jit(solution)/shard_map/ppermute | solution.py:908
  98.6 1.9 %collective-permute-start.17 = (f32[4,16,512]{2,1,0:T(8,128)S(1)}, f32[4,16,512]{2,1,0:T(8,128)S(1)}, u32[]{:S(2)}, u32[]{:S(2)}) collective-permute-start(f32[4,16,512]{2,1,0:T(8,128)S(1)} %add.15.refs_1_), channel_id=1, source_target_pairs={{0,1},{1,0},{2,3},{3,2},{4,5},{5,4},{6,7},{7,6},{8,9},{9,8},{10,11... | collective-permute-start | bytes 393224 | tf_op jit(solution)/shard_map/ppermute | solution.py:908

commit v6 on v5

--- a/solution.py
+++ b/solution.py
@@ -9,7 +9,8 @@
 
 GRID = 24
 PLANE = GRID * GRID
-WIDE = 640
+MAIN = 512
+EDGE = PLANE - MAIN
 UNROLL = 12
 CHUNKS = (4, 4, 4)
 K = 16
@@ -21,6 +22,7 @@
 F32 = jnp.float32
 BF16 = jnp.bfloat16
 LEVELS = 32767.0
+LOG2_E = 1.4426950408889634
 HIGHEST = lax.Precision.HIGHEST
 VMEM = pl.BlockSpec(memory_space=pltpu.VMEM)
 SMEM = pl.BlockSpec(memory_space=pltpu.SMEM)
@@ -67,36 +69,57 @@
     return spread(values), spread(slopes)
 
 
-def halves(first, second):
-    product = jnp.concatenate([first[y : y + 1, :] * second for y in range(GRID)], axis=0)
-    high = product.astype(BF16)
-    return [high, (product - high.astype(F32)).astype(BF16)]
-
-
-def fill(even_ref, odd_ref, pieces):
-    lanes = pieces[0].shape[1]
-    pad = jnp.zeros((WIDE - PLANE, lanes), BF16)
-    for i, piece in enumerate(pieces):
-        at = slice(i * lanes, (i + 1) * lanes)
-        even_ref[0:PLANE, at] = piece
-        even_ref[PLANE:WIDE, at] = pad
-        odd_ref[0 : WIDE - PLANE, at] = pad
-        odd_ref[WIDE - PLANE : WIDE, at] = piece
-
-
-def plane_pair(table_ref, pair, even_ref, odd_ref):
+def products(first, second):
+    return jnp.concatenate([first[y : y + 1, :] * second for y in range(GRID)], axis=0)
+
+
+def fill(whole_ref, edge_ref, weights):
+    n = edge_ref.shape[1]
+    for i, weight in enumerate(weights):
+        for j, piece in enumerate(split(weight)):
+            whole_ref[:, (2 * i + j) * n : (2 * i + j + 1) * n] = piece
+        edge_ref[2 * EDGE * i : 2 * EDGE * i + EDGE, :] = weight[MAIN:PLANE, :]
+        edge_ref[2 * EDGE * i + EDGE : 2 * EDGE * (i + 1), :] = weight[0:EDGE, :]
+
+
+def plane_pair(table_ref, pair, whole_ref):
     start = pl.multiple_of(pair * 2 * PLANE, 128)
-    even = table_ref[:, pl.ds(start, WIDE)]
-    start = pl.multiple_of(pair * 2 * PLANE + 2 * PLANE - WIDE, 128)
-    odd = table_ref[:, pl.ds(start, WIDE)]
+    even = table_ref[:, pl.ds(start, MAIN)]
+    start = pl.multiple_of(pair * 2 * PLANE + MAIN + 128, 128)
+    odd = table_ref[:, pl.ds(start, MAIN)]
     return (
-        jnp.dot(even, even_ref[...], preferred_element_type=F32),
-        jnp.dot(odd, odd_ref[...], preferred_element_type=F32),
+        jnp.dot(even, whole_ref[0:MAIN, :], preferred_element_type=F32),
+        jnp.dot(odd, whole_ref[EDGE:PLANE, :], preferred_element_type=F32),
     )
 
 
+def middle_weights(mid_ref, edge_ref, pair, terms):
+    n = edge_ref.shape[1]
+    at = pl.ds(pl.multiple_of(pair * 128, 128), 128)
+    for i, (kind, w0, w1) in enumerate(terms):
+        start = 2 * EDGE * kind
+        part = jnp.concatenate(
+            [
+                w0 * edge_ref[start : start + EDGE, :],
+                w1 * edge_ref[start + EDGE : start + 2 * EDGE, :],
+            ],
+            axis=0,
+        )
+        for j, piece in enumerate(split(part)):
+            mid_ref[at, (2 * i + j) * n : (2 * i + j + 1) * n] = piece
+
+
+def middle(table_ref, mid_ref):
+    lanes = [
+        table_ref[:, q * 2 * PLANE + MAIN : q * 2 * PLANE + MAIN + 128] for q in range(GRID // 2)
+    ]
+    lanes = jnp.concatenate(lanes, axis=1)
+    return jnp.dot(lanes, mid_ref[...], preferred_element_type=F32)
+
+
 def slopes_kernel(
-    state_ref, table_ref, phi_ref, grad_ref, even_ref, odd_ref, wx_ref, sx_ref, loads=(), beside=()
+    state_ref, table_ref, phi_ref, grad_ref, whole_ref, mid_ref, edge_ref, wx_ref, sx_ref,
+    loads=(), beside=()
 ):
     n = state_ref.shape[2]
     wx, sx = axis_weights(state_ref[0, 0:1, :], True)
@@ -104,14 +127,16 @@
     wz, sz = axis_weights(state_ref[0, 2:3, :], True)
     wx_ref[...] = wx
     sx_ref[...] = sx
-    fill(even_ref, odd_ref, halves(wy, wz) + halves(sy, wz) + halves(wy, sz))
+    fill(whole_ref, edge_ref, [products(wy, wz), products(sy, wz), products(wy, sz)])
     phi_ref[...] = jnp.zeros_like(phi_ref)
     grad_ref[...] = jnp.zeros_like(grad_ref)
 
     def body(pair, carry):
-        even, odd = plane_pair(table_ref, pair, even_ref, odd_ref)
+        even, odd = plane_pair(table_ref, pair, whole_ref)
         w0, w1 = wx_ref[pl.ds(2 * pair, 1), :], wx_ref[pl.ds(2 * pair + 1, 1), :]
         s0, s1 = sx_ref[pl.ds(2 * pair, 1), :], sx_ref[pl.ds(2 * pair + 1, 1), :]
+        terms = [(0, w0, w1), (0, s0, s1), (1, w0, w1), (2, w0, w1)]
+        middle_weights(mid_ref, edge_ref, pair, terms)
 
         def both(i):
             at, to = slice(2 * i * n, (2 * i + 1) * n), slice((2 * i + 1) * n, (2 * i + 2) * n)
@@ -138,6 +163,11 @@
             start += size
     else:
         lax.fori_loop(0, pairs, body, 0, unroll=UNROLL)
+    rest = middle(table_ref, mid_ref)
+    phi_ref[...] += rest[:, 0:n] + rest[:, n : 2 * n]
+    for d in range(3):
+        at = 2 * (d + 1) * n
+        grad_ref[:, d * n : (d + 1) * n] += rest[:, at : at + n] + rest[:, at + n : at + 2 * n]
 
 
 def first_kernel(
@@ -207,10 +237,14 @@
 
 
 def slopes_scratch(n):
+    return weights_scratch(n, 3, 4) + [pltpu.VMEM((GRID, n), F32)]
+
+
+def weights_scratch(n, kinds, terms):
     return [
-        pltpu.VMEM((WIDE, 6 * n), BF16),
-        pltpu.VMEM((WIDE, 6 * n), BF16),
-        pltpu.VMEM((GRID, n), F32),
+        pltpu.VMEM((PLANE, 2 * kinds * n), BF16),
+        pltpu.VMEM((GRID // 2 * 128, 2 * terms * n), BF16),
+        pltpu.VMEM((2 * EDGE * kinds, n), F32),
         pltpu.VMEM((GRID, n), F32),
     ]
 
@@ -259,16 +293,17 @@
     return product(a, b, ((1,), (1,)))
 
 
-def own_lanes(n, walker):
-    lane = lax.broadcasted_iota(jnp.int32, (MOVED, n), 1)
+def own_lanes(rows, n, walker):
+    lane = lax.broadcasted_iota(jnp.int32, (rows, n), 1)
     return jnp.logical_and(lane >= walker * K, lane < (walker + 1) * K)
 
 
 def fold(big):
     n = big.shape[1]
-    total = jnp.zeros((MOVED, n), F32)
+    rows = big.shape[0] // (n // K)
+    total = jnp.zeros((rows, n), F32)
     for w in range(n // K):
-        total = jnp.where(own_lanes(n, w), big[w * MOVED : (w + 1) * MOVED, :], total)
+        total = jnp.where(own_lanes(rows, n, w), big[w * rows : (w + 1) * rows, :], total)
     return total
 
 
@@ -549,10 +584,14 @@
 def drift_rows(block, vm_ref, grad_ref, out_ref, at):
     n = grad_ref.shape[1] // 3
     size = K * block
+    used = size + K
+    rows = [vm_ref[w * MOVED : w * MOVED + used, :] for w in range(n // K)]
+    big = dot(jnp.concatenate(rows, axis=0), grad_ref[...])
     out_ref[at + 3 : at + 8, :] = jnp.zeros((5, n), F32)
     for d in range(3):
-        q = fold(dot(vm_ref[...], grad_ref[:, d * n : (d + 1) * n]))
-        out_ref[at + d : at + d + 1, :] = jnp.sum(q * unit(block, n), axis=0, keepdims=True)
+        q = fold(big[:, d * n : (d + 1) * n])
+        own = q[size:used, :] * unit(0, n)[0:K, :]
+        out_ref[at + d : at + d + 1, :] = jnp.sum(own, axis=0, keepdims=True)
         if block:
             out_ref[at + 8 + d * size : at + 8 + (d + 1) * size, :] = q[0:size, :]
 
@@ -594,7 +633,7 @@
 
 def spread(x):
     n = x.shape[1]
-    return jnp.concatenate([jnp.where(own_lanes(n, w), x, 0.0) for w in range(n // K)], axis=0)
+    return jnp.concatenate([jnp.where(own_lanes(x.shape[0], n, w), x, 0.0) for w in range(n // K)], axis=0)
 
 
 BLOCK_ROWS = 8 + MOVED
@@ -628,7 +667,7 @@
         mine_ref, give_ref = refs.pop(0), refs.pop(0)
     else:
         s_ref = refs.pop(0)
-    log_ref, sum_ref, big_ref, even_ref, odd_ref, wx_ref = refs
+    log_ref, sum_ref, big_ref, wide_ref, mid_ref, edge_ref, wx_ref = refs
     orbitals, n = sum_ref.shape
     y_rows = log_y(n)
     phi_rows = slice(y_rows.stop, y_rows.stop + orbitals)
@@ -677,17 +716,19 @@
     wy, _ = axis_weights(moved[1:2, :], False)
     wz, _ = axis_weights(moved[2:3, :], False)
     wx_ref[...] = wx
-    fill(even_ref, odd_ref, halves(wy, wz))
+    fill(wide_ref, edge_ref, [products(wy, wz)])
     sum_ref[...] = jnp.zeros_like(sum_ref)
 
     def body(pair, carry):
-        even, odd = plane_pair(table_ref, pair, even_ref, odd_ref)
+        even, odd = plane_pair(table_ref, pair, wide_ref)
         w0, w1 = wx_ref[pl.ds(2 * pair, 1), :], wx_ref[pl.ds(2 * pair + 1, 1), :]
+        middle_weights(mid_ref, edge_ref, pair, [(0, w0, w1)])
         sum_ref[...] += w0 * (even[:, 0:n] + even[:, n:]) + w1 * (odd[:, 0:n] + odd[:, n:])
         return carry
 
     lax.fori_loop(0, GRID // 2, body, 0, unroll=UNROLL)
-    change = sum_ref[...] - phi_ref[...]
+    rest = middle(table_ref, mid_ref)
+    change = sum_ref[...] + (rest[:, 0:n] + rest[:, n:]) - phi_ref[...]
     change_rows = log_rows(block, n, "change")
     log_ref[change_rows, 0:orbitals] = jnp.transpose(change)
     if not last:
@@ -721,9 +762,7 @@
         scratch_shapes=[
             pltpu.VMEM((orbitals, n), F32),
             pltpu.VMEM((MOVED + rows, n), F32),
-            pltpu.VMEM((WIDE, 2 * n), BF16),
-            pltpu.VMEM((WIDE, 2 * n), BF16),
-            pltpu.VMEM((GRID, n), F32),
+            *weights_scratch(n, 1, 1),
         ],
         compiler_params=params(),
         cost_estimate=lasting(3),
@@ -828,19 +867,57 @@
     )(meta, inverse, got, code, log)
 
 
-def update_kernel(order_ref, meta_ref, v_ref, factor_ref, l_ref, *refs):
+def join_kernel(mine_ref, got_ref, sum_ref, code_ref, power_ref):
+    for i in range(mine_ref.shape[0]):
+        x = mine_ref[i] + got_ref[i]
+        sum_ref[i] = x
+        size = jnp.abs(x)
+        top = jnp.max(size, axis=0, keepdims=True)
+        power = jnp.ceil(jnp.log(jnp.where(top > 0.0, top, 1.0)) * LOG2_E)
+        power = jnp.where(top > 0.0, jnp.maximum(power, -126.0), 0.0)
+        level = jnp.floor(jnp.sqrt(size) * (LEVELS * jnp.exp2(-0.5 * power)) + 0.5)
+        level = jnp.minimum(level, LEVELS)
+        code_ref[i] = jnp.where(x < 0.0, -level, level).astype(jnp.int32).astype(jnp.int16)
+        power_ref[i : i + 1, :] = power
+
+
+def join_call(mine, got):
+    half, _, electrons = mine.shape
+    return pl.pallas_call(
+        join_kernel,
+        name="join",
+        out_shape=(
+            jax.ShapeDtypeStruct(mine.shape, F32),
+            jax.ShapeDtypeStruct(mine.shape, jnp.int16),
+            jax.ShapeDtypeStruct((half, electrons), F32),
+        ),
+        in_specs=[VMEM, VMEM],
+        out_specs=(VMEM,) * 3,
+        compiler_params=params(),
+        cost_estimate=lasting(1),
+    )(mine, got)
+
+
+def decode(code, power):
+    root = jnp.exp2(0.5 * power[:, None, :]) * (1.0 / LEVELS)
+    level = code.astype(F32)
+    return (level * root) * (jnp.abs(level) * root)
+
+
+def update_kernel(meta_ref, v_ref, factor_ref, l_ref, *refs):
     sums_refs, (out_ref, new_ref, sem) = refs[:4], refs[4:]
     walkers = v_ref.shape[0]
 
     def store(w):
         return pltpu.make_async_copy(new_ref.at[w], out_ref.at[w], sem.at[w])
 
+    order = [meta_ref[walkers + b] for b in range(NMOVE)]
     half = walkers // 2
     own = [both_halves(meta_ref, walkers, i) for i in range(half)]
     places = [(own[i][h], i, sums_refs[2 * h : 2 * h + 2]) for i in range(half) for h in range(2)]
     lates = []
     for w, i, (early_ref, late_ref) in places:
-        moved = moved_lanes(late_ref[i], order_ref)[:, 0:MOVED]
+        moved = moved_lanes(late_ref[i], order)[:, 0:MOVED]
         rows = l_ref[pl.ds(pl.multiple_of(w * MOVED, MOVED), MOVED), :]
         lates.append(dot_nt(moved, rows)[:, 0 : MOVED - K])
     for n, (w, i, (early_ref, late_ref)) in enumerate(places):
@@ -853,12 +930,12 @@
         store(w).wait()
 
 
-def update_call(order, meta, inverse, factor, rows, sums):
+def update_call(meta, inverse, factor, rows, sums):
     return pl.pallas_call(
         update_kernel,
         name="update",
         out_shape=jax.ShapeDtypeStruct(inverse.shape, F32),
-        in_specs=[SMEM] * 2 + [VMEM] * 7,
+        in_specs=[SMEM] + [VMEM] * 7,
         out_specs=ANY,
         scratch_shapes=[
             pltpu.VMEM(inverse.shape, F32),
@@ -866,7 +943,7 @@
         ],
         compiler_params=params(),
         cost_estimate=lasting(2),
-    )(order, meta, inverse, factor, rows, *sums)
+    )(meta, inverse, factor, rows, *sums)
 
 
 def place_kernel(meta_ref, own_ref, got_ref, log_ref, out_ref):
@@ -912,13 +989,20 @@
     return [part] + [swap(part, axis, k) for k in range(1, lax.axis_size(axis))]
 
 
-def add_up(mine, axis, done):
+def add_up(early, late, axis, done):
+    parts = [early, late]
     k = 2
-    while k < lax.axis_size(axis):
-        *others, done = together(*[swap(x, axis, k) for x in mine], done)
-        mine = [x + other for x, other in zip(mine, others)]
+    size = lax.axis_size(axis)
+    while k < size:
+        got = [[swap(x, axis, k) for x in part[1:]] for part in parts]
+        got, done = together(got, done)
+        added = [decode(*x) for x in got]
+        if 2 * k < size:
+            parts = [join_call(part[0], x) for part, x in zip(parts, added)]
+        else:
+            parts = [[part[0] + x] for part, x in zip(parts, added)]
         k *= 2
-    return [(x, swap(x, axis, 1)) for x in mine], done
+    return [(x, swap(x, axis, 1)) for (x,) in parts], done
 
 
 def together(*values):
@@ -962,14 +1046,14 @@
     p3 = exchange(p3, "orb")
     whole, mine, give = assemble_call(meta, inverse, got, code, log)
     p3, mine, give = together(p3, mine, give)
-    early = mine + swap(give, "orb", 1)
+    early = join_call(mine, swap(give, "orb", 1))
     mine, give, log = step(3, p3, log, [meta, whole])
-    late = mine + swap(give, "orb", 1)
+    late = join_call(mine, swap(give, "orb", 1))
     factor, rows = last_call([p2, p3], log, vm)
     new_positions = place_call(meta, positions, got, log)
     factor, new_positions = together(factor, new_positions)
-    (early, late), factor = add_up([early, late], "orb", factor)
-    new_inverse = update_call(block_order, meta, whole, factor, rows, [early[0], late[0], early[1], late[1]])
+    (early, late), factor = add_up(early, late, "orb", factor)
+    new_inverse = update_call(meta, whole, factor, rows, [early[0], late[0], early[1], late[1]])
     return jnp.transpose(new_positions, (1, 0, 2)), new_inverse
 
 

time: 104 us -> 102 us (0.981)
  waiting for transfers between devices: 12.1 us -> 9.18 us
  starting transfers between devices: 27.3 us -> 29.2 us
  Pallas kernels: 58.6 us -> 57.5 us
    ppermute x18 -> x20, waiting for transfers between devices: 8.49 us -> 4.5 us  [swap(): lax.ppermute(x, axis, [(i, i ^ k) for i in range(lax.axis_size(axis))])]
    ppermute x18 -> x20, starting transfers between devices: 11 us -> 12.7 us  [swap(): lax.ppermute(x, axis, [(i, i ^ k) for i in range(lax.axis_size(axis))])]
    all_to_all x3, waiting for transfers between devices: 3.62 us -> 4.68 us  [alltoall(): return lax.all_to_all(x, 'walker', split_axis=0, concat_axis=0, tiled=True)]
    unnamed x32 -> x30, local copies, waits for them, and re-layouts: 3.47 us -> 3.46 us
  transfers between devices with their start and end apart: 21 -> 23, of which waited for: 7 -> 7; matrix products, arithmetic and copies ran while one was open for 1% -> 1% of each run, Pallas kernels for 45% -> 45%
where the time goes in v6:
time: 102 us; the launch traced here: 101 us
  Pallas kernels  57.5 us (56%)
  starting transfers between devices  29.2 us (29%)
  waiting for transfers between devices  9.18 us (9%)
  local copies, waits for them, and re-layouts  3.46 us (3%)
  between operations  1.16 us (1%)
    all_to_all x3, starting transfers between devices, alltoall(): return lax.all_to_all(x, 'walker', split_axis=0, concat_axis=0, tiled=True)  16.5 us
    pallas_call x3, Pallas kernels, later_call(): pl.pallas_call(functools.partial(later_kernel, block), name='later', out_...  13.3 us
    ppermute x20, starting transfers between devices, swap(): lax.ppermute(x, axis, [(i, i ^ k) for i in range(lax.axis_size(axis))])  12.7 us
    pallas_call x4, Pallas kernels, step_call(): pl.pallas_call(functools.partial(step_kernel, block, len(parts)), name='s...  11.1 us
    pallas_call x1, Pallas kernels, slopes_call(): pl.pallas_call(first_kernel, name='slopes', out_shape=tuple((jax.ShapeDty...  7.63 us
    pallas_call x1, Pallas kernels, columns_call(): pl.pallas_call(columns_kernel, name='columns', out_shape=(jax.ShapeDtypeS...  5.4 us
    all_to_all x3, waiting for transfers between devices, alltoall(): return lax.all_to_all(x, 'walker', split_axis=0, concat_axis=0, tiled=True)  4.68 us
    ppermute x20, waiting for transfers between devices, swap(): lax.ppermute(x, axis, [(i, i ^ k) for i in range(lax.axis_size(axis))])  4.5 us
  transfers between devices with their start and end apart: 23, of which 7 were waited for; matrix products, arithmetic and copies ran while one was open for 1% of the time, Pallas kernels for 45%

profile of v6, /device:TPU:0, one launch (start us, length us, event | category | flops | bytes accessed | tf_op | source)
XLA Modules:
  0.0 101.4 jit_solution(16065662577134310905)
XLA Ops:
  0.6 0.0 copy-start.13
  0.7 2.4 %pack.1 = f32[8,32,128]{2,1,0:T(8,128)} custom-call(s32[8]{0:T(128)} %parent_ref.1, s32[32]{0:T(128)} %order_ref.3, f32[3,8,512]{2,1,0:T(8,128)} %bitcast.6, f32[3,8,64]{2,1,0:T(8,128)} %bitcast.11, s32[8,64]{1,0:T(8,128)} %refs_2_.1), custom_call_target="tpu_custom_call" | custom-call | flops 100000000 | tf_op jit(solution)/shard_map/pack/pallas_call | solution.py:392
  3.0 7.3 %all-to-all-start = ((f32[8,32,128]{2,1,0:T(8,128)}), f32[8,32,128]{2,1,0:T(8,128)S(1)}, u32[]{:S(2)}, u32[]{:S(2)}) async-start(f32[8,32,128]{2,1,0:T(8,128)} %pack.1), calls=%async_computation | async-start | bytes 262144 | tf_op jit(solution)/shard_map/all_to_all | solution.py:1013
  10.3 5.4 %columns.1 = (f32[8,80,128]{2,1,0:T(8,128)}, s16[8,128,512]{2,1,0:T(8,128)(2,1)}) custom-call(s32[32]{0:T(128)} %order_ref.3, f32[8,128,512]{2,1,0:T(8,128)} %own_ref.1, f32[3,8,512]{2,1,0:T(8,128)} %bitcast.7), custom_call_target="tpu_custom_call" | custom-call | flops 300000000 | tf_op jit(solution)/shard_map/columns/pallas_call | solution.py:455
  15.8 0.7 pad_add_fusion.meta_ref.refs_5_
  16.4 1.2 %all-to-all-done.info_in = f32[8,32,128]{2,1,0:T(8,128)S(1)} async-done(((f32[8,32,128]{2,1,0:T(8,128)}), f32[8,32,128]{2,1,0:T(8,128)S(1)}, u32[]{:S(2)}, u32[]{:S(2)}) %all-to-all-start) | async-done | bytes 131104 | tf_op jit(solution)/shard_map/all_to_all | solution.py:1013
  17.7 0.6 copy-done.12
  18.3 3.5 %route.1 = (f32[4,8,128]{2,1,0:T(8,128)}, f32[8,80,128]{2,1,0:T(8,128)}, s32[8]{0:T(128)}) custom-call(s32[14]{0:T(128)} %pad_add_fusion.meta_ref.refs_5_, f32[8,32,128]{2,1,0:T(8,128)} %copy-done.12, f32[8,80,128]{2,1,0:T(8,128)} %get-tuple-element.51.own_in.own_ref), custom_call_target="tpu_custom_call" | custom-call | flops 300000000 | tf_op jit(solution)/shard_map/route/pallas_call | solution.py:532
  21.8 4.8 %all-to-all-start.1 = ((f32[8,80,128]{2,1,0:T(8,128)}), f32[8,80,128]{2,1,0:T(8,128)}, u32[]{:S(2)}, u32[]{:S(2)}) async-start(f32[8,80,128]{2,1,0:T(8,128)} %get-tuple-element.52), calls=%async_computation.1 | async-start | bytes 655360 | tf_op jit(solution)/shard_map/all_to_all | solution.py:1013
  26.6 7.6 %slopes.1 = (f32[128,128]{1,0:T(8,128)}, f32[128,384]{1,0:T(8,128)}, s16[8,128,512]{2,1,0:T(8,128)(2,1)}) custom-call(s32[8]{0:T(128)} %get-tuple-element.53.sending_ref, f32[4,8,128]{2,1,0:T(8,128)} %get-tuple-element.69.states_ref.refs_6_.refs_7_, bf16[128,13824]{1,0:T(8,128)(2,1)} %refs_9_.1, s16[8,128,512]{2,1,0:T(8,128)(2,1)} %get-tuple-element.55.code_in), custom_call_target="tpu_custom_call" | custom-call | flops 500000000 | tf_op jit(solution)/shard_map/slopes/pallas_call | solution.py:218
  34.2 0.0 copy-start.5
  34.3 2.2 %all-to-all-done.1.got_ref = f32[8,80,128]{2,1,0:T(8,128)} async-done(((f32[8,80,128]{2,1,0:T(8,128)}), f32[8,80,128]{2,1,0:T(8,128)}, u32[]{:S(2)}, u32[]{:S(2)}) %all-to-all-start.1) | async-done | bytes 327712 | tf_op jit(solution)/shard_map/all_to_all | solution.py:1013
  36.4 4.4 %all-to-all-start.2 = ((s16[8,128,512]{2,1,0:T(8,128)(2,1)}), s16[8,128,512]{2,1,0:T(8,128)(2,1)}, u32[]{:S(2)}, u32[]{:S(2)}) async-start(s16[8,128,512]{2,1,0:T(8,128)(2,1)} %get-tuple-element.68), calls=%async_computation.2 | async-start | bytes 2097152 | tf_op jit(solution)/shard_map/all_to_all | solution.py:1013
  40.9 2.7 %select.3 = (f32[512,128]{1,0:T(8,128)}, f32[8,128]{1,0:T(8,128)}) custom-call(s32[14]{0:T(128)} %pad_add_fusion.meta_ref.refs_5_, f32[8,80,128]{2,1,0:T(8,128)} %get-tuple-element.51.own_in.own_ref, f32[8,80,128]{2,1,0:T(8,128)} %all-to-all-done.1.got_ref, f32[128,384]{1,0:T(8,128)} %get-tuple-element.60.grad_in), custom_call_target="tpu_custom_call" | custom-call | flops 200000000 | tf_op jit(solution)/shard_map/select/pallas_call | solution.py:616
  43.6 0.1 collective-permute-start.2
  43.6 1.6 %collective-permute-start.1 = (f32[8,128]{1,0:T(8,128)}, f32[8,128]{1,0:T(8,128)S(1)}, u32[]{:S(2)}, u32[]{:S(2)}) collective-permute-start(f32[8,128]{1,0:T(8,128)} %get-tuple-element.61.refs_0_), channel_id=1, source_target_pairs={{0,2},{1,3},{2,0},{3,1},{4,6},{5,7},{6,4},{7,5},{8,10},{9,11},{10,... | collective-permute-start | bytes 12296 | tf_op jit(solution)/shard_map/ppermute | solution.py:985
  45.2 0.3 collective-permute-start
  45.5 0.9 copy-done.1
  46.4 4.3 %later.3.refs_5_ = f32[184,128]{1,0:T(8,128)S(1)} custom-call(f32[4,8,128]{2,1,0:T(8,128)S(1)} %copy-done.5, bf16[128,13824]{1,0:T(8,128)(2,1)S(1)} %copy-done, f32[512,128]{1,0:T(8,128)S(1)} %copy-done.1), custom_call_target="tpu_custom_call" | custom-call | flops 500000000 | tf_op jit(solution)/shard_map/later/pallas_call | solution.py:262
  50.8 0.0 collective-permute-done.refs_1_
  50.8 1.6 %step.4 = (f32[120,128]{1,0:T(8,128)S(1)}, f32[1440,128]{1,0:T(8,128)S(1)}) custom-call(f32[8,128]{1,0:T(8,128)S(1)} %copy-done.11, f32[8,128]{1,0:T(8,128)S(1)} %collective-permute-done.refs_1_, f32[8,128]{1,0:T(8,128)S(1)} %collective-permute-done.1.refs_2_, f32[8,128]{1,0:T(8,128)S(1)} %collective-permute-done.2.refs_3_, f32[128,128]{1,0:T(8,128)S(1)} %copy-done.9, ...), custom_call_target="tpu_custom_call" | custom-call | flops 300000000 | tf_op jit(solution)/shard_map/step/pallas_call | solution.py:756
  52.4 1.2 %collective-permute-start.5 = (f32[120,128]{1,0:T(8,128)S(1)}, f32[120,128]{1,0:T(8,128)S(1)}, u32[]{:S(2)}, u32[]{:S(2)}) collective-permute-start(f32[120,128]{1,0:T(8,128)S(1)} %get-tuple-element.64.refs_0_), channel_id=1, source_target_pairs={{0,3},{1,2},{2,1},{3,0},{4,7},{5,6},{6,5},{7,4},{8,11},{9,10},{10,... | collective-permute-start | bytes 184328 | tf_op jit(solution)/shard_map/ppermute | solution.py:985
  53.6 0.7 collective-permute-start.4
  54.3 0.0 collective-permute-start.3
  54.3 4.4 %later.4.refs_5_ = f32[232,128]{1,0:T(8,128)S(1)} custom-call(f32[4,8,128]{2,1,0:T(8,128)S(1)} %copy-done.5, bf16[128,13824]{1,0:T(8,128)(2,1)S(1)} %copy-done, f32[512,128]{1,0:T(8,128)S(1)} %copy-done.1), custom_call_target="tpu_custom_call" | custom-call | flops 500000000 | tf_op jit(solution)/shard_map/later/pallas_call | solution.py:262
  58.7 0.0 collective-permute-done.4.refs_2_
  58.7 0.0 collective-permute-done.3.refs_1_
  58.7 2.7 %step.5 = (f32[168,128]{1,0:T(8,128)}, f32[1440,128]{1,0:T(8,128)S(1)}) custom-call(f32[120,128]{1,0:T(8,128)S(1)} %get-tuple-element.64.refs_0_, f32[120,128]{1,0:T(8,128)S(1)} %collective-permute-done.3.refs_1_, f32[120,128]{1,0:T(8,128)S(1)} %collective-permute-done.4.refs_2_, f32[120,128]{1,0:T(8,128)S(1)} %collective-permute-done.5.refs_3_, ...), custom_call_target="tpu_custom_call" | custom-call | flops 300000000 | tf_op jit(solution)/shard_map/step/pallas_call | solution.py:756
  61.4 0.9 copy-done.6
  62.3 1.4 %collective-permute-start.8 = (f32[168,128]{1,0:T(8,128)}, f32[168,128]{1,0:T(8,128)}, u32[]{:S(2)}, u32[]{:S(2)}) collective-permute-start(f32[168,128]{1,0:T(8,128)} %get-tuple-element.66.refs_0_), channel_id=1, source_target_pairs={{0,3},{1,2},{2,1},{3,0},{4,7},{5,6},{6,5},{7,4},{8,11},{9,10},{10,... | collective-permute-start | bytes 258056 | tf_op jit(solution)/shard_map/ppermute | solution.py:985
  63.7 0.7 collective-permute-start.7
  64.4 0.0 collective-permute-start.6
  64.4 1.3 %all-to-all-done.2.code_ref = s16[8,128,512]{2,1,0:T(8,128)(2,1)} async-done(((s16[8,128,512]{2,1,0:T(8,128)(2,1)}), s16[8,128,512]{2,1,0:T(8,128)(2,1)}, u32[]{:S(2)}, u32[]{:S(2)}) %all-to-all-start.2) | async-done | bytes 1048608 | tf_op jit(solution)/shard_map/all_to_all | solution.py:1013
  65.7 0.9 copy-done.2
  66.7 4.7 %later.5.refs_5_ = f32[280,128]{1,0:T(8,128)S(1)} custom-call(f32[4,8,128]{2,1,0:T(8,128)S(1)} %copy-done.5, bf16[128,13824]{1,0:T(8,128)(2,1)S(1)} %copy-done, f32[512,128]{1,0:T(8,128)S(1)} %copy-done.2), custom_call_target="tpu_custom_call" | custom-call | flops 500000000 | tf_op jit(solution)/shard_map/later/pallas_call | solution.py:262
  71.3 0.0 collective-permute-done.8.refs_3_
  71.4 0.0 copy-start.4
  71.4 3.5 %step.6 = (f32[216,128]{1,0:T(8,128)S(1)}, f32[1440,128]{1,0:T(8,128)S(1)}) custom-call(f32[168,128]{1,0:T(8,128)} %get-tuple-element.66.refs_0_, f32[168,128]{1,0:T(8,128)} %collective-permute-done.6.refs_1_, f32[168,128]{1,0:T(8,128)} %collective-permute-done.7.refs_2_, f32[168,128]{1,0:T(8,128)} %collective-permute-done.8.refs_3_, ...), custom_call_target="tpu_custom_call" | custom-call | flops 300000000 | tf_op jit(solution)/shard_map/step/pallas_call | solution.py:756
  74.9 0.2 collective-permute-start.11
  75.1 1.5 %collective-permute-start.10 = (f32[216,128]{1,0:T(8,128)S(1)}, f32[216,128]{1,0:T(8,128)S(1)}, u32[]{:S(2)}, u32[]{:S(2)}) collective-permute-start(f32[216,128]{1,0:T(8,128)S(1)} %get-tuple-element.75.refs_0_.refs_4_), channel_id=1, source_target_pairs={{0,2},{1,3},{2,0},{3,1},{4,6},{5,7},{6,4},{7,5},{8,10},{9,11},{10,... | collective-permute-start | bytes 331784 | tf_op jit(solution)/shard_map/ppermute | solution.py:985
  76.5 0.3 collective-permute-start.9
  76.8 3.6 %assemble.1 = (f32[8,128,512]{2,1,0:T(8,128)S(1)}, f32[4,48,512]{2,1,0:T(8,128)S(1)}, f32[4,48,512]{2,1,0:T(8,128)S(1)}) custom-call(s32[14]{0:T(128)S(1)} %copy-done.10, f32[8,128,512]{2,1,0:T(8,128)S(1)} %copy-done.4, f32[8,80,128]{2,1,0:T(8,128)} %all-to-all-done.1.got_ref, s16[8,128,512]{2,1,0:T(8,128)(2,1)} %all-to-all-done.2.code_ref, ...), custom_call_target="tpu_custom_call" | custom-call | flops 400000000 | tf_op jit(solution)/shard_map/assemble/pallas_call | solution.py:851
  80.5 0.0 collective-permute-done.11.refs_3_.refs_7_
  80.5 2.2 %collective-permute-done.10.refs_2_.refs_6_ = f32[216,128]{1,0:T(8,128)S(1)} collective-permute-done((f32[216,128]{1,0:T(8,128)S(1)}, f32[216,128]{1,0:T(8,128)S(1)}, u32[]{:S(2)}, u32[]{:S(2)}) %collective-permute-start.10) | collective-permute-done | bytes 110624 | tf_op jit(solution)/shard_map/ppermute | solution.py:985
  82.7 0.0 collective-permute-done.9.refs_1_.refs_5_
  82.7 0.1 collective-permute-start.12
  82.7 3.3 %step.7 = (f32[4,16,512]{2,1,0:T(8,128)S(1)}, f32[4,16,512]{2,1,0:T(8,128)S(1)}, f32[1440,128]{1,0:T(8,128)S(1)}) custom-call(f32[216,128]{1,0:T(8,128)S(1)} %get-tuple-element.75.refs_0_.refs_4_, f32[216,128]{1,0:T(8,128)S(1)} %collective-permute-done.9.refs_1_.refs_5_, f32[216,128]{1,0:T(8,128)S(1)} %collective-permute-done.10.refs_2_.refs_6_, ...), custom_call_target="tpu_custom_call" | custom-call | flops 300000000 | tf_op jit(solution)/shard_map/step/pallas_call | solution.py:756
  86.0 0.5 collective-permute-start.15
  86.5 0.3 join.2
  86.8 0.1 collective-permute-start.13
  86.9 0.6 collective-permute-done.15.got_ref
  87.5 0.1 join.3
  87.6 1.5 %collective-permute-start.16 = (s16[4,16,512]{2,1,0:T(8,128)(2,1)S(1)}, s16[4,16,512]{2,1,0:T(8,128)(2,1)S(1)}, u32[]{:S(2)}, u32[]{:S(2)}) collective-permute-start(s16[4,16,512]{2,1,0:T(8,128)(2,1)S(1)} %get-tuple-element.89), channel_id=1, source_target_pairs={{0,2},{1,3},{2,0},{3,1},{4,6},{5,7},{6,4},{7,5},{8,10},{9,11},{10,... | collective-permute-start | bytes 196616 | tf_op jit(solution)/shard_map/ppermute | solution.py:985
  89.1 2.9 %last.1 = (f32[8,128,64]{2,1,0:T(8,128)S(1)}, f32[512,64]{1,0:T(8,128)S(1)}) custom-call(f32[168,128]{1,0:T(8,128)} %get-tuple-element.66.refs_0_, f32[168,128]{1,0:T(8,128)} %collective-permute-done.6.refs_1_, f32[168,128]{1,0:T(8,128)} %collective-permute-done.7.refs_2_, f32[168,128]{1,0:T(8,128)} %collective-permute-done.8.refs_3_, ...), custom_call_target="tpu_custom_call" | custom-call | flops 200000000 | tf_op jit(solution)/shard_map/last/pallas_call | solution.py:796
  92.0 0.7 collective-permute-start.17
  92.7 1.4 %collective-permute-start.14 = (f32[4,512]{1,0:T(4,128)S(1)}, f32[4,512]{1,0:T(4,128)S(1)}, u32[]{:S(2)}, u32[]{:S(2)}) collective-permute-start(f32[4,512]{1,0:T(4,128)S(1)} %get-tuple-element.86), channel_id=1, source_target_pairs={{0,2},{1,3},{2,0},{3,1},{4,6},{5,7},{6,4},{7,5},{8,10},{9,11},{10,... | collective-permute-start | bytes 24584 | tf_op jit(solution)/shard_map/ppermute | solution.py:985
  94.1 1.8 %place.1 = f32[3,8,512]{2,1,0:T(8,128)} custom-call(s32[14]{0:T(128)S(1)} %copy-done.10, f32[3,8,512]{2,1,0:T(8,128)S(1)} %bitcast.8, f32[8,80,128]{2,1,0:T(8,128)} %all-to-all-done.1.got_ref, f32[1440,128]{1,0:T(8,128)S(1)} %get-tuple-element.80.refs_8_.log_ref), custom_call_target="tpu_custom_call" | custom-call | flops 100000000 | tf_op jit(solution)/shard_map/place/pallas_call | solution.py:973
  95.9 0.0 collective-permute-done.16
  95.9 0.4 collective-permute-done.14
  96.4 0.1 fusion.1.refs_0_
  96.5 0.1 collective-permute-start.18
  96.6 0.6 collective-permute-start.19
  97.2 1.3 %collective-permute-done.19.refs_3_ = f32[4,16,512]{2,1,0:T(8,128)S(1)} collective-permute-done((f32[4,16,512]{2,1,0:T(8,128)S(1)}, f32[4,16,512]{2,1,0:T(8,128)S(1)}, u32[]{:S(2)}, u32[]{:S(2)}) %collective-permute-start.19) | collective-permute-done | bytes 131104 | tf_op jit(solution)/shard_map/ppermute | solution.py:985
  98.5 2.7 %update.1 = f32[8,128,512]{2,1,0:T(8,128)} custom-call(s32[14]{0:T(128)S(1)} %copy-done.10, f32[8,128,512]{2,1,0:T(8,128)S(1)} %get-tuple-element.79.refs_6_.v_ref, f32[8,128,64]{2,1,0:T(8,128)S(1)} %get-tuple-element.92.factor_ref, f32[512,64]{1,0:T(8,128)S(1)} %get-tuple-element.93.l_ref, f32[4,48,512]{2,1,0:T(8,128)S(1)} %fusion.1.refs_0_, ...), custom_call_target="tpu_custom_call" | custom-call | flops 200000000 | tf_op jit(solution)/shard_map/update/pallas_call | solution.py:934
  (35 shorter events, 0.1 us)
Async XLA Ops:
  0.6 15.1 %copy-start.13 = (s32[32]{0:T(128)S(1)}, s32[32]{0:T(128)}, u32[]{:S(2)}) copy-start(s32[32]{0:T(128)} %order_ref.3) | copy-start | bytes 388
  0.6 15.1 %copy-start.14 = (s32[8]{0:T(128)S(1)}, s32[8]{0:T(128)}, u32[]{:S(2)}) copy-start(s32[8]{0:T(128)} %parent_ref.1) | copy-start | bytes 100
  3.0 14.6 %all-to-all-start = ((f32[8,32,128]{2,1,0:T(8,128)}), f32[8,32,128]{2,1,0:T(8,128)S(1)}, u32[]{:S(2)}, u32[]{:S(2)}) async-start(f32[8,32,128]{2,1,0:T(8,128)} %pack.1), calls=%async_computation | async-start | bytes 262144 | tf_op jit(solution)/shard_map/all_to_all | solution.py:1013
  17.7 0.7 copy-start.12
  21.8 14.6 %all-to-all-start.1 = ((f32[8,80,128]{2,1,0:T(8,128)}), f32[8,80,128]{2,1,0:T(8,128)}, u32[]{:S(2)}, u32[]{:S(2)}) async-start(f32[8,80,128]{2,1,0:T(8,128)} %get-tuple-element.52), calls=%async_computation.1 | async-start | bytes 655360 | tf_op jit(solution)/shard_map/all_to_all | solution.py:1013
  26.6 18.9 %copy-start = (bf16[128,13824]{1,0:T(8,128)(2,1)S(1)}, bf16[128,13824]{1,0:T(8,128)(2,1)}, u32[]{:S(2)}) copy-start(bf16[128,13824]{1,0:T(8,128)(2,1)} %refs_9_.1) | copy-start | bytes 10616836
  34.2 11.2 %copy-start.5 = (f32[4,8,128]{2,1,0:T(8,128)S(1)}, f32[4,8,128]{2,1,0:T(8,128)}, u32[]{:S(2)}) copy-start(f32[4,8,128]{2,1,0:T(8,128)} %get-tuple-element.69.states_ref.refs_6_.refs_7_) | copy-start | bytes 49156
  36.4 29.3 %all-to-all-start.2 = ((s16[8,128,512]{2,1,0:T(8,128)(2,1)}), s16[8,128,512]{2,1,0:T(8,128)(2,1)}, u32[]{:S(2)}, u32[]{:S(2)}) async-start(s16[8,128,512]{2,1,0:T(8,128)(2,1)} %get-tuple-element.68), calls=%async_computation.2 | async-start | bytes 2097152 | tf_op jit(solution)/shard_map/all_to_all | solution.py:1013
  40.9 9.9 %copy-start.9 = (f32[128,128]{1,0:T(8,128)S(1)}, f32[128,128]{1,0:T(8,128)}, u32[]{:S(2)}) copy-start(f32[128,128]{1,0:T(8,128)} %get-tuple-element.62.refs_4_) | copy-start | bytes 196612
  43.6 7.2 %collective-permute-start.2 = (f32[8,128]{1,0:T(8,128)}, f32[8,128]{1,0:T(8,128)S(1)}, u32[]{:S(2)}, u32[]{:S(2)}) collective-permute-start(f32[8,128]{1,0:T(8,128)} %get-tuple-element.61.refs_0_), channel_id=1, source_target_pairs={{0,3},{1,2},{2,1},{3,0},{4,7},{5,6},{6,5},{7,4},{8,11},{9,10},{10,... | collective-permute-start | bytes 12296 | tf_op jit(solution)/shard_map/ppermute | solution.py:985
  43.6 7.1 %collective-permute-start.1 = (f32[8,128]{1,0:T(8,128)}, f32[8,128]{1,0:T(8,128)S(1)}, u32[]{:S(2)}, u32[]{:S(2)}) collective-permute-start(f32[8,128]{1,0:T(8,128)} %get-tuple-element.61.refs_0_), channel_id=1, source_target_pairs={{0,2},{1,3},{2,0},{3,1},{4,6},{5,7},{6,4},{7,5},{8,10},{9,11},{10,... | collective-permute-start | bytes 12296 | tf_op jit(solution)/shard_map/ppermute | solution.py:985
  45.2 5.6 %collective-permute-start = (f32[8,128]{1,0:T(8,128)}, f32[8,128]{1,0:T(8,128)S(1)}, u32[]{:S(2)}, u32[]{:S(2)}) collective-permute-start(f32[8,128]{1,0:T(8,128)} %get-tuple-element.61.refs_0_), channel_id=1, source_target_pairs={{0,1},{1,0},{2,3},{3,2},{4,5},{5,4},{6,7},{7,6},{8,9},{9,8},{10,11... | collective-permute-start | bytes 12296 | tf_op jit(solution)/shard_map/ppermute | solution.py:985
  45.5 1.0 copy-start.1
  46.4 4.3 %copy-start.11 = (f32[8,128]{1,0:T(8,128)S(1)}, f32[8,128]{1,0:T(8,128)}, u32[]{:S(2)}) copy-start(f32[8,128]{1,0:T(8,128)} %get-tuple-element.61.refs_0_) | copy-start | bytes 12292
  52.4 6.3 %collective-permute-start.5 = (f32[120,128]{1,0:T(8,128)S(1)}, f32[120,128]{1,0:T(8,128)S(1)}, u32[]{:S(2)}, u32[]{:S(2)}) collective-permute-start(f32[120,128]{1,0:T(8,128)S(1)} %get-tuple-element.64.refs_0_), channel_id=1, source_target_pairs={{0,3},{1,2},{2,1},{3,0},{4,7},{5,6},{6,5},{7,4},{8,11},{9,10},{10,... | collective-permute-start | bytes 184328 | tf_op jit(solution)/shard_map/ppermute | solution.py:985
  53.6 5.1 %collective-permute-start.4 = (f32[120,128]{1,0:T(8,128)S(1)}, f32[120,128]{1,0:T(8,128)S(1)}, u32[]{:S(2)}, u32[]{:S(2)}) collective-permute-start(f32[120,128]{1,0:T(8,128)S(1)} %get-tuple-element.64.refs_0_), channel_id=1, source_target_pairs={{0,2},{1,3},{2,0},{3,1},{4,6},{5,7},{6,4},{7,5},{8,10},{9,11},{10,... | collective-permute-start | bytes 184328 | tf_op jit(solution)/shard_map/ppermute | solution.py:985
  54.3 4.4 %collective-permute-start.3 = (f32[120,128]{1,0:T(8,128)S(1)}, f32[120,128]{1,0:T(8,128)S(1)}, u32[]{:S(2)}, u32[]{:S(2)}) collective-permute-start(f32[120,128]{1,0:T(8,128)S(1)} %get-tuple-element.64.refs_0_), channel_id=1, source_target_pairs={{0,1},{1,0},{2,3},{3,2},{4,5},{5,4},{6,7},{7,6},{8,9},{9,8},{10,11... | collective-permute-start | bytes 184328 | tf_op jit(solution)/shard_map/ppermute | solution.py:985
  61.4 0.9 copy-start.6
  62.3 9.0 %collective-permute-start.8 = (f32[168,128]{1,0:T(8,128)}, f32[168,128]{1,0:T(8,128)}, u32[]{:S(2)}, u32[]{:S(2)}) collective-permute-start(f32[168,128]{1,0:T(8,128)} %get-tuple-element.66.refs_0_), channel_id=1, source_target_pairs={{0,3},{1,2},{2,1},{3,0},{4,7},{5,6},{6,5},{7,4},{8,11},{9,10},{10,... | collective-permute-start | bytes 258056 | tf_op jit(solution)/shard_map/ppermute | solution.py:985
  63.7 7.7 %collective-permute-start.7 = (f32[168,128]{1,0:T(8,128)}, f32[168,128]{1,0:T(8,128)}, u32[]{:S(2)}, u32[]{:S(2)}) collective-permute-start(f32[168,128]{1,0:T(8,128)} %get-tuple-element.66.refs_0_), channel_id=1, source_target_pairs={{0,2},{1,3},{2,0},{3,1},{4,6},{5,7},{6,4},{7,5},{8,10},{9,11},{10,... | collective-permute-start | bytes 258056 | tf_op jit(solution)/shard_map/ppermute | solution.py:985
  64.4 6.9 %collective-permute-start.6 = (f32[168,128]{1,0:T(8,128)}, f32[168,128]{1,0:T(8,128)}, u32[]{:S(2)}, u32[]{:S(2)}) collective-permute-start(f32[168,128]{1,0:T(8,128)} %get-tuple-element.66.refs_0_), channel_id=1, source_target_pairs={{0,1},{1,0},{2,3},{3,2},{4,5},{5,4},{6,7},{7,6},{8,9},{9,8},{10,11... | collective-permute-start | bytes 258056 | tf_op jit(solution)/shard_map/ppermute | solution.py:985
  65.7 1.0 copy-start.2
  66.6 4.7 %copy-start.7 = (f32[1440,128]{1,0:T(8,128)S(1)}, f32[1440,128]{1,0:T(8,128)}, u32[]{:S(2)}) copy-start(f32[1440,128]{1,0:T(8,128)} %copy-done.6) | copy-start | bytes 2211844
  71.4 5.5 %copy-start.4 = (f32[8,128,512]{2,1,0:T(8,128)S(1)}, f32[8,128,512]{2,1,0:T(8,128)}, u32[]{:S(2)}) copy-start(f32[8,128,512]{2,1,0:T(8,128)} %own_ref.1) | copy-start | bytes 6291460
  71.4 5.5 %copy-start.10 = (s32[14]{0:T(128)S(1)}, s32[14]{0:T(128)}, u32[]{:S(2)}) copy-start(s32[14]{0:T(128)} %pad_add_fusion.meta_ref.refs_5_) | copy-start | bytes 172
  74.9 5.6 %collective-permute-start.11 = (f32[216,128]{1,0:T(8,128)S(1)}, f32[216,128]{1,0:T(8,128)S(1)}, u32[]{:S(2)}, u32[]{:S(2)}) collective-permute-start(f32[216,128]{1,0:T(8,128)S(1)} %get-tuple-element.75.refs_0_.refs_4_), channel_id=1, source_target_pairs={{0,3},{1,2},{2,1},{3,0},{4,7},{5,6},{6,5},{7,4},{8,11},{9,10},{10,... | collective-permute-start | bytes 331784 | tf_op jit(solution)/shard_map/ppermute | solution.py:985
  75.1 7.6 %collective-permute-start.10 = (f32[216,128]{1,0:T(8,128)S(1)}, f32[216,128]{1,0:T(8,128)S(1)}, u32[]{:S(2)}, u32[]{:S(2)}) collective-permute-start(f32[216,128]{1,0:T(8,128)S(1)} %get-tuple-element.75.refs_0_.refs_4_), channel_id=1, source_target_pairs={{0,2},{1,3},{2,0},{3,1},{4,6},{5,7},{6,4},{7,5},{8,10},{9,11},{10,... | collective-permute-start | bytes 331784 | tf_op jit(solution)/shard_map/ppermute | solution.py:985
  76.5 6.2 %collective-permute-start.9 = (f32[216,128]{1,0:T(8,128)S(1)}, f32[216,128]{1,0:T(8,128)S(1)}, u32[]{:S(2)}, u32[]{:S(2)}) collective-permute-start(f32[216,128]{1,0:T(8,128)S(1)} %get-tuple-element.75.refs_0_.refs_4_), channel_id=1, source_target_pairs={{0,1},{1,0},{2,3},{3,2},{4,5},{5,4},{6,7},{7,6},{8,9},{9,8},{10,11... | collective-permute-start | bytes 331784 | tf_op jit(solution)/shard_map/ppermute | solution.py:985
  76.8 5.9 %copy-start.3 = (f32[512,128]{1,0:T(8,128)S(1)}, f32[512,128]{1,0:T(8,128)}, u32[]{:S(2)}) copy-start(f32[512,128]{1,0:T(8,128)} %get-tuple-element.63.vm_ref.refs_7_.refs_8_.refs_9_) | copy-start | bytes 786436
  82.7 3.8 %collective-permute-start.12 = (f32[4,48,512]{2,1,0:T(8,128)S(1)}, f32[4,48,512]{2,1,0:T(8,128)S(1)}, u32[]{:S(2)}, u32[]{:S(2)}) collective-permute-start(f32[4,48,512]{2,1,0:T(8,128)S(1)} %get-tuple-element.84), channel_id=1, source_target_pairs={{0,1},{1,0},{2,3},{3,2},{4,5},{5,4},{6,7},{7,6},{8,9},{9,8},{10,11... | collective-permute-start | bytes 1179656 | tf_op jit(solution)/shard_map/ppermute | solution.py:985
  86.0 8.1 %copy-start.8 = (f32[8,3,512]{2,0,1:T(8,128)S(1)}, f32[8,3,512]{2,0,1:T(8,128)}, u32[]{:S(2)}) copy-start(f32[8,3,512]{2,0,1:T(8,128)} %param.7) | copy-start | bytes 147460
  86.0 1.4 %collective-permute-start.15 = (f32[4,16,512]{2,1,0:T(8,128)S(1)}, f32[4,16,512]{2,1,0:T(8,128)S(1)}, u32[]{:S(2)}, u32[]{:S(2)}) collective-permute-start(f32[4,16,512]{2,1,0:T(8,128)S(1)} %get-tuple-element.88), channel_id=1, source_target_pairs={{0,1},{1,0},{2,3},{3,2},{4,5},{5,4},{6,7},{7,6},{8,9},{9,8},{10,11... | collective-permute-start | bytes 393224 | tf_op jit(solution)/shard_map/ppermute | solution.py:985
  86.8 9.6 %collective-permute-start.13 = (s16[4,48,512]{2,1,0:T(8,128)(2,1)S(1)}, s16[4,48,512]{2,1,0:T(8,128)(2,1)S(1)}, u32[]{:S(2)}, u32[]{:S(2)}) collective-permute-start(s16[4,48,512]{2,1,0:T(8,128)(2,1)S(1)} %get-tuple-element.85), channel_id=1, source_target_pairs={{0,2},{1,3},{2,0},{3,1},{4,6},{5,7},{6,4},{7,5},{8,10},{9,11},{10,... | collective-permute-start | bytes 589832 | tf_op jit(solution)/shard_map/ppermute | solution.py:985
  87.6 8.3 %collective-permute-start.16 = (s16[4,16,512]{2,1,0:T(8,128)(2,1)S(1)}, s16[4,16,512]{2,1,0:T(8,128)(2,1)S(1)}, u32[]{:S(2)}, u32[]{:S(2)}) collective-permute-start(s16[4,16,512]{2,1,0:T(8,128)(2,1)S(1)} %get-tuple-element.89), channel_id=1, source_target_pairs={{0,2},{1,3},{2,0},{3,1},{4,6},{5,7},{6,4},{7,5},{8,10},{9,11},{10,... | collective-permute-start | bytes 196616 | tf_op jit(solution)/shard_map/ppermute | solution.py:985
  92.0 3.9 %collective-permute-start.17 = (f32[4,512]{1,0:T(4,128)S(1)}, f32[4,512]{1,0:T(4,128)S(1)}, u32[]{:S(2)}, u32[]{:S(2)}) collective-permute-start(f32[4,512]{1,0:T(4,128)S(1)} %get-tuple-element.90), channel_id=1, source_target_pairs={{0,2},{1,3},{2,0},{3,1},{4,6},{5,7},{6,4},{7,5},{8,10},{9,11},{10,... | collective-permute-start | bytes 24584 | tf_op jit(solution)/shard_map/ppermute | solution.py:985
  92.7 3.7 %collective-permute-start.14 = (f32[4,512]{1,0:T(4,128)S(1)}, f32[4,512]{1,0:T(4,128)S(1)}, u32[]{:S(2)}, u32[]{:S(2)}) collective-permute-start(f32[4,512]{1,0:T(4,128)S(1)} %get-tuple-element.86), channel_id=1, source_target_pairs={{0,2},{1,3},{2,0},{3,1},{4,6},{5,7},{6,4},{7,5},{8,10},{9,11},{10,... | collective-permute-start | bytes 24584 | tf_op jit(solution)/shard_map/ppermute | solution.py:985
  96.5 2.0 %collective-permute-start.18 = (f32[4,48,512]{2,1,0:T(8,128)S(1)}, f32[4,48,512]{2,1,0:T(8,128)S(1)}, u32[]{:S(2)}, u32[]{:S(2)}) collective-permute-start(f32[4,48,512]{2,1,0:T(8,128)S(1)} %fusion.1.refs_0_), channel_id=1, source_target_pairs={{0,1},{1,0},{2,3},{3,2},{4,5},{5,4},{6,7},{7,6},{8,9},{9,8},{10,11... | collective-permute-start | bytes 1179656 | tf_op jit(solution)/shard_map/ppermute | solution.py:985
  96.6 1.8 %collective-permute-start.19 = (f32[4,16,512]{2,1,0:T(8,128)S(1)}, f32[4,16,512]{2,1,0:T(8,128)S(1)}, u32[]{:S(2)}, u32[]{:S(2)}) collective-permute-start(f32[4,16,512]{2,1,0:T(8,128)S(1)} %fusion.4.refs_1_), channel_id=1, source_target_pairs={{0,1},{1,0},{2,3},{3,2},{4,5},{5,4},{6,7},{7,6},{8,9},{9,8},{10,11... | collective-permute-start | bytes 393224 | tf_op jit(solution)/shard_map/ppermute | solution.py:985

commit v7 on v6

--- a/solution.py
+++ b/solution.py
@@ -328,7 +328,7 @@
 
 
 def lasting(us):
-    return pl.CostEstimate(flops=int(us * 1e8), bytes_accessed=0, transcendentals=0)
+    return pl.CostEstimate(flops=int(us * 1e9), bytes_accessed=0, transcendentals=0)
 
 
 def parent_of(meta_ref, walkers, w):

time: 102 us -> 101 us (level)
  Pallas kernels: 57.5 us -> 52.6 us
  waiting for transfers between devices: 9.18 us -> 12.9 us
    all_to_all x3, waiting for transfers between devices: 4.68 us -> 6.72 us  [alltoall(): return lax.all_to_all(x, 'walker', split_axis=0, concat_axis=0, tiled=True)]
    pallas_call x4, Pallas kernels: 11.1 us -> 9.29 us  [step_call(): pl.pallas_call(functools.partial(step_kernel, block, len(parts)), name='s...]
    ppermute x20, waiting for transfers between devices: 4.5 us -> 6.18 us  [swap(): lax.ppermute(x, axis, [(i, i ^ k) for i in range(lax.axis_size(axis))])]
    pallas_call x1, Pallas kernels: 3.64 us -> 2.03 us  [assemble_call(): pl.pallas_call(assemble_kernel, name='assemble', out_shape=(jax.ShapeDtyp...]
    unnamed x30 -> x32, local copies, waits for them, and re-layouts: 3.46 us -> 3.67 us
  transfers between devices with their start and end apart: 23 -> 23, of which waited for: 7 -> 9; matrix products, arithmetic and copies ran while one was open for 1% -> 1% of each run, Pallas kernels for 45% -> 42%
where the time goes in v7:
time: 101 us; the launch traced here: 100 us
  Pallas kernels  52.6 us (52%)
  starting transfers between devices  29 us (29%)
  waiting for transfers between devices  12.9 us (13%)
  local copies, waits for them, and re-layouts  3.67 us (4%)
  between operations  1.19 us (1%)
    all_to_all x3, starting transfers between devices, alltoall(): return lax.all_to_all(x, 'walker', split_axis=0, concat_axis=0, tiled=True)  15.7 us
    pallas_call x3, Pallas kernels, later_call(): pl.pallas_call(functools.partial(later_kernel, block), name='later', out_...  13.4 us
    ppermute x20, starting transfers between devices, swap(): lax.ppermute(x, axis, [(i, i ^ k) for i in range(lax.axis_size(axis))])  13.3 us
    pallas_call x4, Pallas kernels, step_call(): pl.pallas_call(functools.partial(step_kernel, block, len(parts)), name='s...  9.29 us
    pallas_call x1, Pallas kernels, slopes_call(): pl.pallas_call(first_kernel, name='slopes', out_shape=tuple((jax.ShapeDty...  7.28 us
    all_to_all x3, waiting for transfers between devices, alltoall(): return lax.all_to_all(x, 'walker', split_axis=0, concat_axis=0, tiled=True)  6.72 us
    ppermute x20, waiting for transfers between devices, swap(): lax.ppermute(x, axis, [(i, i ^ k) for i in range(lax.axis_size(axis))])  6.18 us
    pallas_call x1, Pallas kernels, columns_call(): pl.pallas_call(columns_kernel, name='columns', out_shape=(jax.ShapeDtypeS...  5.4 us
  transfers between devices with their start and end apart: 23, of which 9 were waited for; matrix products, arithmetic and copies ran while one was open for 1% of the time, Pallas kernels for 42%

profile of v7, /device:TPU:0, one launch (start us, length us, event | category | flops | bytes accessed | tf_op | source)
XLA Modules:
  0.0 100.1 jit_solution(5586004080099608004)
XLA Ops:
  0.6 0.0 copy-start.15
  0.7 2.4 %pack.1 = f32[8,32,128]{2,1,0:T(8,128)} custom-call(s32[8]{0:T(128)} %parent_ref.1, s32[32]{0:T(128)} %order_ref.3, f32[3,8,512]{2,1,0:T(8,128)} %bitcast.6, f32[3,8,64]{2,1,0:T(8,128)} %bitcast.10, s32[8,64]{1,0:T(8,128)} %refs_2_.1), custom_call_target="tpu_custom_call" | custom-call | flops 1000000000 | tf_op jit(solution)/shard_map/pack/pallas_call | solution.py:392
  3.0 7.3 %all-to-all-start = ((f32[8,32,128]{2,1,0:T(8,128)}), f32[8,32,128]{2,1,0:T(8,128)S(1)}, u32[]{:S(2)}, u32[]{:S(2)}) async-start(f32[8,32,128]{2,1,0:T(8,128)} %pack.1), calls=%async_computation | async-start | bytes 262144 | tf_op jit(solution)/shard_map/all_to_all | solution.py:1013
  10.3 0.6 pad_add_fusion.meta_ref.refs_5_
  10.9 5.4 %columns.1 = (f32[8,80,128]{2,1,0:T(8,128)}, s16[8,128,512]{2,1,0:T(8,128)(2,1)}) custom-call(s32[32]{0:T(128)} %order_ref.3, f32[8,128,512]{2,1,0:T(8,128)} %own_ref.1, f32[3,8,512]{2,1,0:T(8,128)} %bitcast.7), custom_call_target="tpu_custom_call" | custom-call | flops 3000000000 | tf_op jit(solution)/shard_map/columns/pallas_call | solution.py:455
  16.3 1.4 %all-to-all-done.info_in = f32[8,32,128]{2,1,0:T(8,128)S(1)} async-done(((f32[8,32,128]{2,1,0:T(8,128)}), f32[8,32,128]{2,1,0:T(8,128)S(1)}, u32[]{:S(2)}, u32[]{:S(2)}) %all-to-all-start) | async-done | bytes 131104 | tf_op jit(solution)/shard_map/all_to_all | solution.py:1013
  17.7 0.7 copy-done.13
  18.3 3.5 %route.1 = (f32[4,8,128]{2,1,0:T(8,128)}, f32[8,80,128]{2,1,0:T(8,128)}, s32[8]{0:T(128)}) custom-call(s32[14]{0:T(128)} %pad_add_fusion.meta_ref.refs_5_, f32[8,32,128]{2,1,0:T(8,128)} %copy-done.13, f32[8,80,128]{2,1,0:T(8,128)} %get-tuple-element.51.own_in.own_ref), custom_call_target="tpu_custom_call" | custom-call | flops 3000000000 | tf_op jit(solution)/shard_map/route/pallas_call | solution.py:532
  21.8 4.6 %all-to-all-start.1 = ((f32[8,80,128]{2,1,0:T(8,128)}), f32[8,80,128]{2,1,0:T(8,128)S(1)}, u32[]{:S(2)}, u32[]{:S(2)}) async-start(f32[8,80,128]{2,1,0:T(8,128)} %get-tuple-element.52), calls=%async_computation.1 | async-start | bytes 655360 | tf_op jit(solution)/shard_map/all_to_all | solution.py:1013
  26.5 7.3 %slopes.1 = (f32[128,128]{1,0:T(8,128)}, f32[128,384]{1,0:T(8,128)}, s16[8,128,512]{2,1,0:T(8,128)(2,1)}) custom-call(s32[8]{0:T(128)} %get-tuple-element.53.sending_ref, f32[4,8,128]{2,1,0:T(8,128)} %get-tuple-element.69.states_ref.refs_6_.refs_7_, bf16[128,13824]{1,0:T(8,128)(2,1)} %refs_9_.1, s16[8,128,512]{2,1,0:T(8,128)(2,1)} %get-tuple-element.55.code_in), custom_call_target="tpu_custom_call" | custom-call | flops 5000000000 | tf_op jit(solution)/shard_map/slopes/pallas_call | solution.py:218
  33.8 2.4 %all-to-all-done.1.got_ref = f32[8,80,128]{2,1,0:T(8,128)S(1)} async-done(((f32[8,80,128]{2,1,0:T(8,128)}), f32[8,80,128]{2,1,0:T(8,128)S(1)}, u32[]{:S(2)}, u32[]{:S(2)}) %all-to-all-start.1) | async-done | bytes 327712 | tf_op jit(solution)/shard_map/all_to_all | solution.py:1013
  36.2 3.7 %all-to-all-start.2 = ((s16[8,128,512]{2,1,0:T(8,128)(2,1)}), s16[8,128,512]{2,1,0:T(8,128)(2,1)S(1)}, u32[]{:S(2)}, u32[]{:S(2)}) async-start(s16[8,128,512]{2,1,0:T(8,128)(2,1)} %get-tuple-element.68), calls=%async_computation.2 | async-start | bytes 2097152 | tf_op jit(solution)/shard_map/all_to_all | solution.py:1013
  39.9 0.0 copy-start.3
  40.0 0.0 copy-start.12
  40.0 2.9 %select.3 = (f32[512,128]{1,0:T(8,128)}, f32[8,128]{1,0:T(8,128)}) custom-call(s32[14]{0:T(128)} %pad_add_fusion.meta_ref.refs_5_, f32[8,80,128]{2,1,0:T(8,128)} %get-tuple-element.51.own_in.own_ref, f32[8,80,128]{2,1,0:T(8,128)} %copy-done, f32[128,384]{1,0:T(8,128)} %get-tuple-element.60.grad_in), custom_call_target="tpu_custom_call" | custom-call | flops 2000000000 | tf_op jit(solution)/shard_map/select/pallas_call | solution.py:616
  42.9 0.2 collective-permute-start.2
  43.0 1.5 %collective-permute-start.1 = (f32[8,128]{1,0:T(8,128)}, f32[8,128]{1,0:T(8,128)S(1)}, u32[]{:S(2)}, u32[]{:S(2)}) collective-permute-start(f32[8,128]{1,0:T(8,128)} %get-tuple-element.61.refs_0_), channel_id=1, source_target_pairs={{0,2},{1,3},{2,0},{3,1},{4,6},{5,7},{6,4},{7,5},{8,10},{9,11},{10,... | collective-permute-start | bytes 12296 | tf_op jit(solution)/shard_map/ppermute | solution.py:985
  44.5 0.3 collective-permute-start
  44.8 0.9 copy-done.9
  45.8 4.3 %later.3.refs_5_ = f32[184,128]{1,0:T(8,128)S(1)} custom-call(f32[4,8,128]{2,1,0:T(8,128)S(1)} %copy-done.12, bf16[128,13824]{1,0:T(8,128)(2,1)S(1)} %copy-done.3, f32[512,128]{1,0:T(8,128)S(1)} %copy-done.9), custom_call_target="tpu_custom_call" | custom-call | flops 5000000000 | tf_op jit(solution)/shard_map/later/pallas_call | solution.py:262
  50.1 0.0 collective-permute-done.2.refs_3_
  50.1 0.0 collective-permute-done.refs_1_
  50.2 1.6 %step.4 = (f32[120,128]{1,0:T(8,128)S(1)}, f32[1440,128]{1,0:T(8,128)S(1)}) custom-call(f32[8,128]{1,0:T(8,128)S(1)} %copy-done.8, f32[8,128]{1,0:T(8,128)S(1)} %collective-permute-done.refs_1_, f32[8,128]{1,0:T(8,128)S(1)} %collective-permute-done.1.refs_2_, f32[8,128]{1,0:T(8,128)S(1)} %collective-permute-done.2.refs_3_, f32[128,128]{1,0:T(8,128)S(1)} %copy-done.11, ...), custom_call_target="tpu_custom_call" | custom-call | flops 3000000000 | tf_op jit(solution)/shard_map/step/pallas_call | solution.py:756
  51.8 1.2 %collective-permute-start.5 = (f32[120,128]{1,0:T(8,128)S(1)}, f32[120,128]{1,0:T(8,128)S(1)}, u32[]{:S(2)}, u32[]{:S(2)}) collective-permute-start(f32[120,128]{1,0:T(8,128)S(1)} %get-tuple-element.64.refs_0_), channel_id=1, source_target_pairs={{0,3},{1,2},{2,1},{3,0},{4,7},{5,6},{6,5},{7,4},{8,11},{9,10},{10,... | collective-permute-start | bytes 184328 | tf_op jit(solution)/shard_map/ppermute | solution.py:985
  53.0 0.7 collective-permute-start.4
  53.7 0.0 collective-permute-start.3
  53.7 4.4 %later.4.refs_5_ = f32[232,128]{1,0:T(8,128)S(1)} custom-call(f32[4,8,128]{2,1,0:T(8,128)S(1)} %copy-done.12, bf16[128,13824]{1,0:T(8,128)(2,1)S(1)} %copy-done.3, f32[512,128]{1,0:T(8,128)S(1)} %copy-done.10), custom_call_target="tpu_custom_call" | custom-call | flops 5000000000 | tf_op jit(solution)/shard_map/later/pallas_call | solution.py:262
  58.1 0.0 collective-permute-done.5.refs_3_
  58.1 0.0 collective-permute-done.4.refs_2_
  58.2 2.1 %step.5 = (f32[168,128]{1,0:T(8,128)S(1)}, f32[1440,128]{1,0:T(8,128)S(1)}) custom-call(f32[120,128]{1,0:T(8,128)S(1)} %get-tuple-element.64.refs_0_, f32[120,128]{1,0:T(8,128)S(1)} %collective-permute-done.3.refs_1_, f32[120,128]{1,0:T(8,128)S(1)} %collective-permute-done.4.refs_2_, f32[120,128]{1,0:T(8,128)S(1)} %collective-permute-done.5.refs_3_, ...), custom_call_target="tpu_custom_call" | custom-call | flops 3000000000 | tf_op jit(solution)/shard_map/step/pallas_call | solution.py:756
  60.2 1.4 %collective-permute-start.8 = (f32[168,128]{1,0:T(8,128)S(1)}, f32[168,128]{1,0:T(8,128)S(1)}, u32[]{:S(2)}, u32[]{:S(2)}) collective-permute-start(f32[168,128]{1,0:T(8,128)S(1)} %get-tuple-element.66.refs_0_), channel_id=1, source_target_pairs={{0,3},{1,2},{2,1},{3,0},{4,7},{5,6},{6,5},{7,4},{8,11},{9,10},{10,... | collective-permute-start | bytes 258056 | tf_op jit(solution)/shard_map/ppermute | solution.py:985
  61.7 0.7 collective-permute-start.7
  62.4 2.9 %all-to-all-done.2.code_ref = s16[8,128,512]{2,1,0:T(8,128)(2,1)S(1)} async-done(((s16[8,128,512]{2,1,0:T(8,128)(2,1)}), s16[8,128,512]{2,1,0:T(8,128)(2,1)S(1)}, u32[]{:S(2)}, u32[]{:S(2)}) %all-to-all-start.2) | async-done | bytes 1048608 | tf_op jit(solution)/shard_map/all_to_all | solution.py:1013
  65.4 2.0 %copy-done.4 = bf16[128,13824]{1,0:T(8,128)(2,1)S(1)} copy-done((bf16[128,13824]{1,0:T(8,128)(2,1)S(1)}, bf16[128,13824]{1,0:T(8,128)(2,1)}, u32[]{:S(2)}) %copy-start.4) | copy-done | bytes 3538968
  67.4 4.7 %later.5.refs_5_ = f32[280,128]{1,0:T(8,128)S(1)} custom-call(f32[4,8,128]{2,1,0:T(8,128)S(1)} %copy-done.12, bf16[128,13824]{1,0:T(8,128)(2,1)S(1)} %copy-done.4, f32[512,128]{1,0:T(8,128)S(1)} %copy-done.10), custom_call_target="tpu_custom_call" | custom-call | flops 5000000000 | tf_op jit(solution)/shard_map/later/pallas_call | solution.py:262
  72.1 0.0 copy-start.1
  72.1 0.0 copy-start.6
  72.1 2.3 %step.6 = (f32[216,128]{1,0:T(8,128)S(1)}, f32[1440,128]{1,0:T(8,128)S(1)}) custom-call(f32[168,128]{1,0:T(8,128)S(1)} %get-tuple-element.66.refs_0_, f32[168,128]{1,0:T(8,128)S(1)} %collective-permute-done.6.refs_1_, f32[168,128]{1,0:T(8,128)S(1)} %collective-permute-done.7.refs_2_, f32[168,128]{1,0:T(8,128)S(1)} %collective-permute-done.8.refs_3_, ...), custom_call_target="tpu_custom_call" | custom-call | flops 3000000000 | tf_op jit(solution)/shard_map/step/pallas_call | solution.py:756
  74.5 0.1 collective-permute-start.11
  74.6 1.6 %collective-permute-start.10 = (f32[216,128]{1,0:T(8,128)S(1)}, f32[216,128]{1,0:T(8,128)S(1)}, u32[]{:S(2)}, u32[]{:S(2)}) collective-permute-start(f32[216,128]{1,0:T(8,128)S(1)} %get-tuple-element.75.refs_0_.refs_4_), channel_id=1, source_target_pairs={{0,2},{1,3},{2,0},{3,1},{4,6},{5,7},{6,4},{7,5},{8,10},{9,11},{10,... | collective-permute-start | bytes 331784 | tf_op jit(solution)/shard_map/ppermute | solution.py:985
  76.1 0.3 collective-permute-start.9
  76.4 2.0 %assemble.1 = (f32[8,128,512]{2,1,0:T(8,128)S(1)}, f32[4,48,512]{2,1,0:T(8,128)S(1)}, f32[4,48,512]{2,1,0:T(8,128)S(1)}) custom-call(s32[14]{0:T(128)S(1)} %copy-done.2, f32[8,128,512]{2,1,0:T(8,128)S(1)} %copy-done.6, f32[8,80,128]{2,1,0:T(8,128)S(1)} %copy-done.1, s16[8,128,512]{2,1,0:T(8,128)(2,1)S(1)} %all-to-all-done.2.code_ref, ...), custom_call_target="tpu_custom_call" | custom-call | flops 4000000000 | tf_op jit(solution)/shard_map/assemble/pallas_call | solution.py:851
  78.5 1.4 %collective-permute-done.11.refs_3_.refs_7_ = f32[216,128]{1,0:T(8,128)S(1)} collective-permute-done((f32[216,128]{1,0:T(8,128)S(1)}, f32[216,128]{1,0:T(8,128)S(1)}, u32[]{:S(2)}, u32[]{:S(2)}) %collective-permute-start.11) | collective-permute-done | bytes 110624 | tf_op jit(solution)/shard_map/ppermute | solution.py:985
  79.9 2.4 %collective-permute-done.10.refs_2_.refs_6_ = f32[216,128]{1,0:T(8,128)S(1)} collective-permute-done((f32[216,128]{1,0:T(8,128)S(1)}, f32[216,128]{1,0:T(8,128)S(1)}, u32[]{:S(2)}, u32[]{:S(2)}) %collective-permute-start.10) | collective-permute-done | bytes 110624 | tf_op jit(solution)/shard_map/ppermute | solution.py:985
  82.3 0.1 collective-permute-start.12
  82.4 3.3 %step.7 = (f32[4,16,512]{2,1,0:T(8,128)S(1)}, f32[4,16,512]{2,1,0:T(8,128)S(1)}, f32[1440,128]{1,0:T(8,128)S(1)}) custom-call(f32[216,128]{1,0:T(8,128)S(1)} %get-tuple-element.75.refs_0_.refs_4_, f32[216,128]{1,0:T(8,128)S(1)} %collective-permute-done.9.refs_1_.refs_5_, f32[216,128]{1,0:T(8,128)S(1)} %collective-permute-done.10.refs_2_.refs_6_, ...), custom_call_target="tpu_custom_call" | custom-call | flops 3000000000 | tf_op jit(solution)/shard_map/step/pallas_call | solution.py:756
  85.6 0.5 collective-permute-start.15
  86.1 0.3 join.2
  86.4 0.1 collective-permute-start.13
  86.5 1.9 %last.1 = (f32[8,128,64]{2,1,0:T(8,128)S(1)}, f32[512,64]{1,0:T(8,128)S(1)}) custom-call(f32[168,128]{1,0:T(8,128)S(1)} %get-tuple-element.66.refs_0_, f32[168,128]{1,0:T(8,128)S(1)} %collective-permute-done.6.refs_1_, f32[168,128]{1,0:T(8,128)S(1)} %collective-permute-done.7.refs_2_, f32[168,128]{1,0:T(8,128)S(1)} %collective-permute-done.8.refs_3_, ...), custom_call_target="tpu_custom_call" | custom-call | flops 2000000000 | tf_op jit(solution)/shard_map/last/pallas_call | solution.py:796
  88.4 0.0 copy-start.7
  88.4 0.1 join.3
  88.5 2.1 %collective-permute-start.17 = (f32[4,512]{1,0:T(4,128)S(1)}, f32[4,512]{1,0:T(4,128)S(1)}, u32[]{:S(2)}, u32[]{:S(2)}) collective-permute-start(f32[4,512]{1,0:T(4,128)S(1)} %get-tuple-element.90), channel_id=1, source_target_pairs={{0,2},{1,3},{2,0},{3,1},{4,6},{5,7},{6,4},{7,5},{8,10},{9,11},{10,... | collective-permute-start | bytes 24584 | tf_op jit(solution)/shard_map/ppermute | solution.py:985
  90.6 0.1 collective-permute-start.16
  90.7 1.9 %collective-permute-start.14 = (f32[4,512]{1,0:T(4,128)S(1)}, f32[4,512]{1,0:T(4,128)S(1)}, u32[]{:S(2)}, u32[]{:S(2)}) collective-permute-start(f32[4,512]{1,0:T(4,128)S(1)} %get-tuple-element.86), channel_id=1, source_target_pairs={{0,2},{1,3},{2,0},{3,1},{4,6},{5,7},{6,4},{7,5},{8,10},{9,11},{10,... | collective-permute-start | bytes 24584 | tf_op jit(solution)/shard_map/ppermute | solution.py:985
  92.7 1.4 %place.1 = f32[3,8,512]{2,1,0:T(8,128)} custom-call(s32[14]{0:T(128)S(1)} %copy-done.2, f32[3,8,512]{2,1,0:T(8,128)S(1)} %bitcast.8, f32[8,80,128]{2,1,0:T(8,128)S(1)} %copy-done.1, f32[1440,128]{1,0:T(8,128)S(1)} %get-tuple-element.80.refs_8_.log_ref), custom_call_target="tpu_custom_call" | custom-call | flops 1000000000 | tf_op jit(solution)/shard_map/place/pallas_call | solution.py:973
  94.0 0.2 collective-permute-done.17
  94.2 0.8 collective-permute-done.16
  95.0 0.1 collective-permute-done.14
  95.1 0.1 fusion.1.refs_0_
  95.2 0.1 collective-permute-start.18
  95.4 0.6 collective-permute-start.19
  95.9 1.3 %collective-permute-done.19.refs_3_ = f32[4,16,512]{2,1,0:T(8,128)S(1)} collective-permute-done((f32[4,16,512]{2,1,0:T(8,128)S(1)}, f32[4,16,512]{2,1,0:T(8,128)S(1)}, u32[]{:S(2)}, u32[]{:S(2)}) %collective-permute-start.19) | collective-permute-done | bytes 131104 | tf_op jit(solution)/shard_map/ppermute | solution.py:985
  97.2 2.7 %update.1 = f32[8,128,512]{2,1,0:T(8,128)} custom-call(s32[14]{0:T(128)S(1)} %copy-done.2, f32[8,128,512]{2,1,0:T(8,128)S(1)} %get-tuple-element.79.refs_6_.v_ref, f32[8,128,64]{2,1,0:T(8,128)S(1)} %get-tuple-element.92.factor_ref, f32[512,64]{1,0:T(8,128)S(1)} %get-tuple-element.93.l_ref, f32[4,48,512]{2,1,0:T(8,128)S(1)} %fusion.1.refs_0_, ...), custom_call_target="tpu_custom_call" | custom-call | flops 2000000000 | tf_op jit(solution)/shard_map/update/pallas_call | solution.py:934
  (37 shorter events, 0.1 us)
Async XLA Ops:
  0.6 9.7 %copy-start.15 = (s32[32]{0:T(128)S(1)}, s32[32]{0:T(128)}, u32[]{:S(2)}) copy-start(s32[32]{0:T(128)} %order_ref.3) | copy-start | bytes 388
  0.6 9.7 %copy-start.14 = (s32[8]{0:T(128)S(1)}, s32[8]{0:T(128)}, u32[]{:S(2)}) copy-start(s32[8]{0:T(128)} %parent_ref.1) | copy-start | bytes 100
  3.0 14.6 %all-to-all-start = ((f32[8,32,128]{2,1,0:T(8,128)}), f32[8,32,128]{2,1,0:T(8,128)S(1)}, u32[]{:S(2)}, u32[]{:S(2)}) async-start(f32[8,32,128]{2,1,0:T(8,128)} %pack.1), calls=%async_computation | async-start | bytes 262144 | tf_op jit(solution)/shard_map/all_to_all | solution.py:1013
  17.7 0.7 copy-start.13
  21.8 14.4 %all-to-all-start.1 = ((f32[8,80,128]{2,1,0:T(8,128)}), f32[8,80,128]{2,1,0:T(8,128)S(1)}, u32[]{:S(2)}, u32[]{:S(2)}) async-start(f32[8,80,128]{2,1,0:T(8,128)} %get-tuple-element.52), calls=%async_computation.1 | async-start | bytes 655360 | tf_op jit(solution)/shard_map/all_to_all | solution.py:1013
  36.2 3.7 %copy-start = (f32[8,80,128]{2,1,0:T(8,128)}, f32[8,80,128]{2,1,0:T(8,128)S(1)}, u32[]{:S(2)}) copy-start(f32[8,80,128]{2,1,0:T(8,128)S(1)} %all-to-all-done.1.got_ref) | copy-start | bytes 983044
  36.2 29.2 %all-to-all-start.2 = ((s16[8,128,512]{2,1,0:T(8,128)(2,1)}), s16[8,128,512]{2,1,0:T(8,128)(2,1)S(1)}, u32[]{:S(2)}, u32[]{:S(2)}) async-start(s16[8,128,512]{2,1,0:T(8,128)(2,1)} %get-tuple-element.68), calls=%async_computation.2 | async-start | bytes 2097152 | tf_op jit(solution)/shard_map/all_to_all | solution.py:1013
  39.9 4.9 %copy-start.3 = (bf16[128,13824]{1,0:T(8,128)(2,1)S(1)}, bf16[128,13824]{1,0:T(8,128)(2,1)}, u32[]{:S(2)}) copy-start(bf16[128,13824]{1,0:T(8,128)(2,1)} %refs_9_.1) | copy-start | bytes 10616836
  40.0 4.9 %copy-start.12 = (f32[4,8,128]{2,1,0:T(8,128)S(1)}, f32[4,8,128]{2,1,0:T(8,128)}, u32[]{:S(2)}) copy-start(f32[4,8,128]{2,1,0:T(8,128)} %get-tuple-element.69.states_ref.refs_6_.refs_7_) | copy-start | bytes 49156
  42.9 7.2 %collective-permute-start.2 = (f32[8,128]{1,0:T(8,128)}, f32[8,128]{1,0:T(8,128)S(1)}, u32[]{:S(2)}, u32[]{:S(2)}) collective-permute-start(f32[8,128]{1,0:T(8,128)} %get-tuple-element.61.refs_0_), channel_id=1, source_target_pairs={{0,3},{1,2},{2,1},{3,0},{4,7},{5,6},{6,5},{7,4},{8,11},{9,10},{10,... | collective-permute-start | bytes 12296 | tf_op jit(solution)/shard_map/ppermute | solution.py:985
  43.0 7.1 %collective-permute-start.1 = (f32[8,128]{1,0:T(8,128)}, f32[8,128]{1,0:T(8,128)S(1)}, u32[]{:S(2)}, u32[]{:S(2)}) collective-permute-start(f32[8,128]{1,0:T(8,128)} %get-tuple-element.61.refs_0_), channel_id=1, source_target_pairs={{0,2},{1,3},{2,0},{3,1},{4,6},{5,7},{6,4},{7,5},{8,10},{9,11},{10,... | collective-permute-start | bytes 12296 | tf_op jit(solution)/shard_map/ppermute | solution.py:985
  44.5 5.6 %collective-permute-start = (f32[8,128]{1,0:T(8,128)}, f32[8,128]{1,0:T(8,128)S(1)}, u32[]{:S(2)}, u32[]{:S(2)}) collective-permute-start(f32[8,128]{1,0:T(8,128)} %get-tuple-element.61.refs_0_), channel_id=1, source_target_pairs={{0,1},{1,0},{2,3},{3,2},{4,5},{5,4},{6,7},{7,6},{8,9},{9,8},{10,11... | collective-permute-start | bytes 12296 | tf_op jit(solution)/shard_map/ppermute | solution.py:985
  44.8 1.0 copy-start.9
  45.8 4.4 %copy-start.8 = (f32[8,128]{1,0:T(8,128)S(1)}, f32[8,128]{1,0:T(8,128)}, u32[]{:S(2)}) copy-start(f32[8,128]{1,0:T(8,128)} %get-tuple-element.61.refs_0_) | copy-start | bytes 12292
  45.8 4.4 %copy-start.11 = (f32[128,128]{1,0:T(8,128)S(1)}, f32[128,128]{1,0:T(8,128)}, u32[]{:S(2)}) copy-start(f32[128,128]{1,0:T(8,128)} %get-tuple-element.62.refs_4_) | copy-start | bytes 196612
  50.1 3.6 %copy-start.10 = (f32[512,128]{1,0:T(8,128)S(1)}, f32[512,128]{1,0:T(8,128)}, u32[]{:S(2)}) copy-start(f32[512,128]{1,0:T(8,128)} %get-tuple-element.63.vm_ref.refs_7_.refs_8_.refs_9_) | copy-start | bytes 786436
  51.8 6.3 %collective-permute-start.5 = (f32[120,128]{1,0:T(8,128)S(1)}, f32[120,128]{1,0:T(8,128)S(1)}, u32[]{:S(2)}, u32[]{:S(2)}) collective-permute-start(f32[120,128]{1,0:T(8,128)S(1)} %get-tuple-element.64.refs_0_), channel_id=1, source_target_pairs={{0,3},{1,2},{2,1},{3,0},{4,7},{5,6},{6,5},{7,4},{8,11},{9,10},{10,... | collective-permute-start | bytes 184328 | tf_op jit(solution)/shard_map/ppermute | solution.py:985
  53.0 5.2 %collective-permute-start.4 = (f32[120,128]{1,0:T(8,128)S(1)}, f32[120,128]{1,0:T(8,128)S(1)}, u32[]{:S(2)}, u32[]{:S(2)}) collective-permute-start(f32[120,128]{1,0:T(8,128)S(1)} %get-tuple-element.64.refs_0_), channel_id=1, source_target_pairs={{0,2},{1,3},{2,0},{3,1},{4,6},{5,7},{6,4},{7,5},{8,10},{9,11},{10,... | collective-permute-start | bytes 184328 | tf_op jit(solution)/shard_map/ppermute | solution.py:985
  53.7 4.4 %collective-permute-start.3 = (f32[120,128]{1,0:T(8,128)S(1)}, f32[120,128]{1,0:T(8,128)S(1)}, u32[]{:S(2)}, u32[]{:S(2)}) collective-permute-start(f32[120,128]{1,0:T(8,128)S(1)} %get-tuple-element.64.refs_0_), channel_id=1, source_target_pairs={{0,1},{1,0},{2,3},{3,2},{4,5},{5,4},{6,7},{7,6},{8,9},{9,8},{10,11... | collective-permute-start | bytes 184328 | tf_op jit(solution)/shard_map/ppermute | solution.py:985
  60.2 11.8 %collective-permute-start.8 = (f32[168,128]{1,0:T(8,128)S(1)}, f32[168,128]{1,0:T(8,128)S(1)}, u32[]{:S(2)}, u32[]{:S(2)}) collective-permute-start(f32[168,128]{1,0:T(8,128)S(1)} %get-tuple-element.66.refs_0_), channel_id=1, source_target_pairs={{0,3},{1,2},{2,1},{3,0},{4,7},{5,6},{6,5},{7,4},{8,11},{9,10},{10,... | collective-permute-start | bytes 258056 | tf_op jit(solution)/shard_map/ppermute | solution.py:985
  61.7 10.4 %collective-permute-start.7 = (f32[168,128]{1,0:T(8,128)S(1)}, f32[168,128]{1,0:T(8,128)S(1)}, u32[]{:S(2)}, u32[]{:S(2)}) collective-permute-start(f32[168,128]{1,0:T(8,128)S(1)} %get-tuple-element.66.refs_0_), channel_id=1, source_target_pairs={{0,2},{1,3},{2,0},{3,1},{4,6},{5,7},{6,4},{7,5},{8,10},{9,11},{10,... | collective-permute-start | bytes 258056 | tf_op jit(solution)/shard_map/ppermute | solution.py:985
  62.4 9.7 %collective-permute-start.6 = (f32[168,128]{1,0:T(8,128)S(1)}, f32[168,128]{1,0:T(8,128)S(1)}, u32[]{:S(2)}, u32[]{:S(2)}) collective-permute-start(f32[168,128]{1,0:T(8,128)S(1)} %get-tuple-element.66.refs_0_), channel_id=1, source_target_pairs={{0,1},{1,0},{2,3},{3,2},{4,5},{5,4},{6,7},{7,6},{8,9},{9,8},{10,11... | collective-permute-start | bytes 258056 | tf_op jit(solution)/shard_map/ppermute | solution.py:985
  65.4 2.0 %copy-start.4 = (bf16[128,13824]{1,0:T(8,128)(2,1)S(1)}, bf16[128,13824]{1,0:T(8,128)(2,1)}, u32[]{:S(2)}) copy-start(bf16[128,13824]{1,0:T(8,128)(2,1)} %refs_9_.1) | copy-start | bytes 10616836
  72.1 4.3 %copy-start.1 = (f32[8,80,128]{2,1,0:T(8,128)S(1)}, f32[8,80,128]{2,1,0:T(8,128)}, u32[]{:S(2)}) copy-start(f32[8,80,128]{2,1,0:T(8,128)} %copy-done) | copy-start | bytes 983044
  72.1 4.3 %copy-start.2 = (s32[14]{0:T(128)S(1)}, s32[14]{0:T(128)}, u32[]{:S(2)}) copy-start(s32[14]{0:T(128)} %pad_add_fusion.meta_ref.refs_5_) | copy-start | bytes 172
  72.1 4.3 %copy-start.6 = (f32[8,128,512]{2,1,0:T(8,128)S(1)}, f32[8,128,512]{2,1,0:T(8,128)}, u32[]{:S(2)}) copy-start(f32[8,128,512]{2,1,0:T(8,128)} %own_ref.1) | copy-start | bytes 6291460
  74.5 5.4 %collective-permute-start.11 = (f32[216,128]{1,0:T(8,128)S(1)}, f32[216,128]{1,0:T(8,128)S(1)}, u32[]{:S(2)}, u32[]{:S(2)}) collective-permute-start(f32[216,128]{1,0:T(8,128)S(1)} %get-tuple-element.75.refs_0_.refs_4_), channel_id=1, source_target_pairs={{0,3},{1,2},{2,1},{3,0},{4,7},{5,6},{6,5},{7,4},{8,11},{9,10},{10,... | collective-permute-start | bytes 331784 | tf_op jit(solution)/shard_map/ppermute | solution.py:985
  74.6 7.7 %collective-permute-start.10 = (f32[216,128]{1,0:T(8,128)S(1)}, f32[216,128]{1,0:T(8,128)S(1)}, u32[]{:S(2)}, u32[]{:S(2)}) collective-permute-start(f32[216,128]{1,0:T(8,128)S(1)} %get-tuple-element.75.refs_0_.refs_4_), channel_id=1, source_target_pairs={{0,2},{1,3},{2,0},{3,1},{4,6},{5,7},{6,4},{7,5},{8,10},{9,11},{10,... | collective-permute-start | bytes 331784 | tf_op jit(solution)/shard_map/ppermute | solution.py:985
  76.1 6.2 %collective-permute-start.9 = (f32[216,128]{1,0:T(8,128)S(1)}, f32[216,128]{1,0:T(8,128)S(1)}, u32[]{:S(2)}, u32[]{:S(2)}) collective-permute-start(f32[216,128]{1,0:T(8,128)S(1)} %get-tuple-element.75.refs_0_.refs_4_), channel_id=1, source_target_pairs={{0,1},{1,0},{2,3},{3,2},{4,5},{5,4},{6,7},{7,6},{8,9},{9,8},{10,11... | collective-permute-start | bytes 331784 | tf_op jit(solution)/shard_map/ppermute | solution.py:985
  76.4 5.9 %copy-start.5 = (bf16[128,13824]{1,0:T(8,128)(2,1)S(1)}, bf16[128,13824]{1,0:T(8,128)(2,1)}, u32[]{:S(2)}) copy-start(bf16[128,13824]{1,0:T(8,128)(2,1)} %refs_9_.1) | copy-start | bytes 10616836
  82.3 3.8 %collective-permute-start.12 = (f32[4,48,512]{2,1,0:T(8,128)S(1)}, f32[4,48,512]{2,1,0:T(8,128)S(1)}, u32[]{:S(2)}, u32[]{:S(2)}) collective-permute-start(f32[4,48,512]{2,1,0:T(8,128)S(1)} %get-tuple-element.84), channel_id=1, source_target_pairs={{0,1},{1,0},{2,3},{3,2},{4,5},{5,4},{6,7},{7,6},{8,9},{9,8},{10,11... | collective-permute-start | bytes 1179656 | tf_op jit(solution)/shard_map/ppermute | solution.py:985
  85.6 2.8 %collective-permute-start.15 = (f32[4,16,512]{2,1,0:T(8,128)S(1)}, f32[4,16,512]{2,1,0:T(8,128)S(1)}, u32[]{:S(2)}, u32[]{:S(2)}) collective-permute-start(f32[4,16,512]{2,1,0:T(8,128)S(1)} %get-tuple-element.88), channel_id=1, source_target_pairs={{0,1},{1,0},{2,3},{3,2},{4,5},{5,4},{6,7},{7,6},{8,9},{9,8},{10,11... | collective-permute-start | bytes 393224 | tf_op jit(solution)/shard_map/ppermute | solution.py:985
  86.4 8.7 %collective-permute-start.13 = (s16[4,48,512]{2,1,0:T(8,128)(2,1)S(1)}, s16[4,48,512]{2,1,0:T(8,128)(2,1)S(1)}, u32[]{:S(2)}, u32[]{:S(2)}) collective-permute-start(s16[4,48,512]{2,1,0:T(8,128)(2,1)S(1)} %get-tuple-element.85), channel_id=1, source_target_pairs={{0,2},{1,3},{2,0},{3,1},{4,6},{5,7},{6,4},{7,5},{8,10},{9,11},{10,... | collective-permute-start | bytes 589832 | tf_op jit(solution)/shard_map/ppermute | solution.py:985
  88.4 4.3 %copy-start.7 = (f32[8,3,512]{2,0,1:T(8,128)S(1)}, f32[8,3,512]{2,0,1:T(8,128)}, u32[]{:S(2)}) copy-start(f32[8,3,512]{2,0,1:T(8,128)} %param.7) | copy-start | bytes 147460
  88.5 5.7 %collective-permute-start.17 = (f32[4,512]{1,0:T(4,128)S(1)}, f32[4,512]{1,0:T(4,128)S(1)}, u32[]{:S(2)}, u32[]{:S(2)}) collective-permute-start(f32[4,512]{1,0:T(4,128)S(1)} %get-tuple-element.90), channel_id=1, source_target_pairs={{0,2},{1,3},{2,0},{3,1},{4,6},{5,7},{6,4},{7,5},{8,10},{9,11},{10,... | collective-permute-start | bytes 24584 | tf_op jit(solution)/shard_map/ppermute | solution.py:985
  90.6 4.4 %collective-permute-start.16 = (s16[4,16,512]{2,1,0:T(8,128)(2,1)S(1)}, s16[4,16,512]{2,1,0:T(8,128)(2,1)S(1)}, u32[]{:S(2)}, u32[]{:S(2)}) collective-permute-start(s16[4,16,512]{2,1,0:T(8,128)(2,1)S(1)} %get-tuple-element.89), channel_id=1, source_target_pairs={{0,2},{1,3},{2,0},{3,1},{4,6},{5,7},{6,4},{7,5},{8,10},{9,11},{10,... | collective-permute-start | bytes 196616 | tf_op jit(solution)/shard_map/ppermute | solution.py:985
  90.7 4.4 %collective-permute-start.14 = (f32[4,512]{1,0:T(4,128)S(1)}, f32[4,512]{1,0:T(4,128)S(1)}, u32[]{:S(2)}, u32[]{:S(2)}) collective-permute-start(f32[4,512]{1,0:T(4,128)S(1)} %get-tuple-element.86), channel_id=1, source_target_pairs={{0,2},{1,3},{2,0},{3,1},{4,6},{5,7},{6,4},{7,5},{8,10},{9,11},{10,... | collective-permute-start | bytes 24584 | tf_op jit(solution)/shard_map/ppermute | solution.py:985
  95.2 2.0 %collective-permute-start.18 = (f32[4,48,512]{2,1,0:T(8,128)S(1)}, f32[4,48,512]{2,1,0:T(8,128)S(1)}, u32[]{:S(2)}, u32[]{:S(2)}) collective-permute-start(f32[4,48,512]{2,1,0:T(8,128)S(1)} %fusion.1.refs_0_), channel_id=1, source_target_pairs={{0,1},{1,0},{2,3},{3,2},{4,5},{5,4},{6,7},{7,6},{8,9},{9,8},{10,11... | collective-permute-start | bytes 1179656 | tf_op jit(solution)/shard_map/ppermute | solution.py:985
  95.4 1.8 %collective-permute-start.19 = (f32[4,16,512]{2,1,0:T(8,128)S(1)}, f32[4,16,512]{2,1,0:T(8,128)S(1)}, u32[]{:S(2)}, u32[]{:S(2)}) collective-permute-start(f32[4,16,512]{2,1,0:T(8,128)S(1)} %fusion.4.refs_1_), channel_id=1, source_target_pairs={{0,1},{1,0},{2,3},{3,2},{4,5},{5,4},{6,7},{7,6},{8,9},{9,8},{10,11... | collective-permute-start | bytes 393224 | tf_op jit(solution)/shard_map/ppermute | solution.py:985

commit v8 on v7

--- a/solution.py
+++ b/solution.py
@@ -478,20 +478,16 @@
     walkers = own_ref.shape[0]
     groups = out_ref.shape[0]
     rows = 3 * walkers
-    asked = []
-    for g in range(groups):
-        at = pl.ds(rows, walkers)
-        asked.append(pltpu.make_async_copy(info_in.at[g, at], parents_ref.at[g], sem.at[2]))
-    for each in asked:
-        each.start()
+    at = pl.ds(rows, walkers)
+    asked = pltpu.make_async_copy(info_in.at[:, at], parents_ref, sem.at[2])
+    asked.start()
     loads = [
         pltpu.make_async_copy(info_in, info_ref, sem.at[0]),
         pltpu.make_async_copy(own_in, own_ref, sem.at[1]),
     ]
     for load in loads:
         load.start()
-    for each in asked:
-        each.wait()
+    asked.wait()
     me = meta_ref[walkers + NMOVE]
     sending = []
     for g in range(groups):

time: 101 us -> 101 us (level)
  no operation moved by 1% of the time
where the time goes in v8:
time: 101 us; the launch traced here: 100 us
  Pallas kernels  52.6 us (52%)
  starting transfers between devices  29 us (29%)
  waiting for transfers between devices  12.9 us (13%)
  local copies, waits for them, and re-layouts  3.67 us (4%)
  between operations  1.19 us (1%)
    all_to_all x3, starting transfers between devices, alltoall(): return lax.all_to_all(x, 'walker', split_axis=0, concat_axis=0, tiled=True)  15.7 us
    pallas_call x3, Pallas kernels, later_call(): pl.pallas_call(functools.partial(later_kernel, block), name='later', out_...  13.4 us
    ppermute x20, starting transfers between devices, swap(): lax.ppermute(x, axis, [(i, i ^ k) for i in range(lax.axis_size(axis))])  13.3 us
    pallas_call x4, Pallas kernels, step_call(): pl.pallas_call(functools.partial(step_kernel, block, len(parts)), name='s...  9.29 us
    pallas_call x1, Pallas kernels, slopes_call(): pl.pallas_call(first_kernel, name='slopes', out_shape=tuple((jax.ShapeDty...  7.28 us
    all_to_all x3, waiting for transfers between devices, alltoall(): return lax.all_to_all(x, 'walker', split_axis=0, concat_axis=0, tiled=True)  6.73 us
    ppermute x20, waiting for transfers between devices, swap(): lax.ppermute(x, axis, [(i, i ^ k) for i in range(lax.axis_size(axis))])  6.18 us
    pallas_call x1, Pallas kernels, columns_call(): pl.pallas_call(columns_kernel, name='columns', out_shape=(jax.ShapeDtypeS...  5.4 us
  transfers between devices with their start and end apart: 23, of which 9 were waited for; matrix products, arithmetic and copies ran while one was open for 1% of the time, Pallas kernels for 42%

profile of v8, /device:TPU:0, one launch (start us, length us, event | category | flops | bytes accessed | tf_op | source)
XLA Modules:
  0.0 100.1 jit_solution(15142107110029033332)
XLA Ops:
  0.6 0.0 copy-start.15
  0.7 2.4 %pack.1 = f32[8,32,128]{2,1,0:T(8,128)} custom-call(s32[8]{0:T(128)} %parent_ref.1, s32[32]{0:T(128)} %order_ref.3, f32[3,8,512]{2,1,0:T(8,128)} %bitcast.6, f32[3,8,64]{2,1,0:T(8,128)} %bitcast.10, s32[8,64]{1,0:T(8,128)} %refs_2_.1), custom_call_target="tpu_custom_call" | custom-call | flops 1000000000 | tf_op jit(solution)/shard_map/pack/pallas_call | solution.py:392
  3.0 7.3 %all-to-all-start = ((f32[8,32,128]{2,1,0:T(8,128)}), f32[8,32,128]{2,1,0:T(8,128)S(1)}, u32[]{:S(2)}, u32[]{:S(2)}) async-start(f32[8,32,128]{2,1,0:T(8,128)} %pack.1), calls=%async_computation | async-start | bytes 262144 | tf_op jit(solution)/shard_map/all_to_all | solution.py:1009
  10.3 0.6 pad_add_fusion.meta_ref.refs_5_
  10.9 5.4 %columns.1 = (f32[8,80,128]{2,1,0:T(8,128)}, s16[8,128,512]{2,1,0:T(8,128)(2,1)}) custom-call(s32[32]{0:T(128)} %order_ref.3, f32[8,128,512]{2,1,0:T(8,128)} %own_ref.1, f32[3,8,512]{2,1,0:T(8,128)} %bitcast.7), custom_call_target="tpu_custom_call" | custom-call | flops 3000000000 | tf_op jit(solution)/shard_map/columns/pallas_call | solution.py:455
  16.3 1.4 %all-to-all-done.info_in = f32[8,32,128]{2,1,0:T(8,128)S(1)} async-done(((f32[8,32,128]{2,1,0:T(8,128)}), f32[8,32,128]{2,1,0:T(8,128)S(1)}, u32[]{:S(2)}, u32[]{:S(2)}) %all-to-all-start) | async-done | bytes 131104 | tf_op jit(solution)/shard_map/all_to_all | solution.py:1009
  17.7 0.7 copy-done.13
  18.3 3.5 %route.1 = (f32[4,8,128]{2,1,0:T(8,128)}, f32[8,80,128]{2,1,0:T(8,128)}, s32[8]{0:T(128)}) custom-call(s32[14]{0:T(128)} %pad_add_fusion.meta_ref.refs_5_, f32[8,32,128]{2,1,0:T(8,128)} %copy-done.13, f32[8,80,128]{2,1,0:T(8,128)} %get-tuple-element.51.own_in.own_ref), custom_call_target="tpu_custom_call" | custom-call | flops 3000000000 | tf_op jit(solution)/shard_map/route/pallas_call | solution.py:528
  21.8 4.6 %all-to-all-start.1 = ((f32[8,80,128]{2,1,0:T(8,128)}), f32[8,80,128]{2,1,0:T(8,128)S(1)}, u32[]{:S(2)}, u32[]{:S(2)}) async-start(f32[8,80,128]{2,1,0:T(8,128)} %get-tuple-element.52), calls=%async_computation.1 | async-start | bytes 655360 | tf_op jit(solution)/shard_map/all_to_all | solution.py:1009
  26.5 7.3 %slopes.1 = (f32[128,128]{1,0:T(8,128)}, f32[128,384]{1,0:T(8,128)}, s16[8,128,512]{2,1,0:T(8,128)(2,1)}) custom-call(s32[8]{0:T(128)} %get-tuple-element.53.sending_ref, f32[4,8,128]{2,1,0:T(8,128)} %get-tuple-element.69.states_ref.refs_6_.refs_7_, bf16[128,13824]{1,0:T(8,128)(2,1)} %refs_9_.1, s16[8,128,512]{2,1,0:T(8,128)(2,1)} %get-tuple-element.55.code_in), custom_call_target="tpu_custom_call" | custom-call | flops 5000000000 | tf_op jit(solution)/shard_map/slopes/pallas_call | solution.py:218
  33.8 2.4 %all-to-all-done.1.got_ref = f32[8,80,128]{2,1,0:T(8,128)S(1)} async-done(((f32[8,80,128]{2,1,0:T(8,128)}), f32[8,80,128]{2,1,0:T(8,128)S(1)}, u32[]{:S(2)}, u32[]{:S(2)}) %all-to-all-start.1) | async-done | bytes 327712 | tf_op jit(solution)/shard_map/all_to_all | solution.py:1009
  36.2 3.7 %all-to-all-start.2 = ((s16[8,128,512]{2,1,0:T(8,128)(2,1)}), s16[8,128,512]{2,1,0:T(8,128)(2,1)S(1)}, u32[]{:S(2)}, u32[]{:S(2)}) async-start(s16[8,128,512]{2,1,0:T(8,128)(2,1)} %get-tuple-element.68), calls=%async_computation.2 | async-start | bytes 2097152 | tf_op jit(solution)/shard_map/all_to_all | solution.py:1009
  39.9 0.0 copy-start.3
  40.0 0.0 copy-start.12
  40.0 2.9 %select.3 = (f32[512,128]{1,0:T(8,128)}, f32[8,128]{1,0:T(8,128)}) custom-call(s32[14]{0:T(128)} %pad_add_fusion.meta_ref.refs_5_, f32[8,80,128]{2,1,0:T(8,128)} %get-tuple-element.51.own_in.own_ref, f32[8,80,128]{2,1,0:T(8,128)} %copy-done, f32[128,384]{1,0:T(8,128)} %get-tuple-element.60.grad_in), custom_call_target="tpu_custom_call" | custom-call | flops 2000000000 | tf_op jit(solution)/shard_map/select/pallas_call | solution.py:612
  42.9 0.2 collective-permute-start.2
  43.0 1.5 %collective-permute-start.1 = (f32[8,128]{1,0:T(8,128)}, f32[8,128]{1,0:T(8,128)S(1)}, u32[]{:S(2)}, u32[]{:S(2)}) collective-permute-start(f32[8,128]{1,0:T(8,128)} %get-tuple-element.61.refs_0_), channel_id=1, source_target_pairs={{0,2},{1,3},{2,0},{3,1},{4,6},{5,7},{6,4},{7,5},{8,10},{9,11},{10,... | collective-permute-start | bytes 12296 | tf_op jit(solution)/shard_map/ppermute | solution.py:981
  44.5 0.3 collective-permute-start
  44.8 0.9 copy-done.9
  45.8 4.3 %later.3.refs_5_ = f32[184,128]{1,0:T(8,128)S(1)} custom-call(f32[4,8,128]{2,1,0:T(8,128)S(1)} %copy-done.12, bf16[128,13824]{1,0:T(8,128)(2,1)S(1)} %copy-done.3, f32[512,128]{1,0:T(8,128)S(1)} %copy-done.9), custom_call_target="tpu_custom_call" | custom-call | flops 5000000000 | tf_op jit(solution)/shard_map/later/pallas_call | solution.py:262
  50.1 0.0 collective-permute-done.2.refs_3_
  50.1 0.0 collective-permute-done.1.refs_2_
  50.2 1.6 %step.4 = (f32[120,128]{1,0:T(8,128)S(1)}, f32[1440,128]{1,0:T(8,128)S(1)}) custom-call(f32[8,128]{1,0:T(8,128)S(1)} %copy-done.8, f32[8,128]{1,0:T(8,128)S(1)} %collective-permute-done.refs_1_, f32[8,128]{1,0:T(8,128)S(1)} %collective-permute-done.1.refs_2_, f32[8,128]{1,0:T(8,128)S(1)} %collective-permute-done.2.refs_3_, f32[128,128]{1,0:T(8,128)S(1)} %copy-done.11, ...), custom_call_target="tpu_custom_call" | custom-call | flops 3000000000 | tf_op jit(solution)/shard_map/step/pallas_call | solution.py:752
  51.8 1.2 %collective-permute-start.5 = (f32[120,128]{1,0:T(8,128)S(1)}, f32[120,128]{1,0:T(8,128)S(1)}, u32[]{:S(2)}, u32[]{:S(2)}) collective-permute-start(f32[120,128]{1,0:T(8,128)S(1)} %get-tuple-element.64.refs_0_), channel_id=1, source_target_pairs={{0,3},{1,2},{2,1},{3,0},{4,7},{5,6},{6,5},{7,4},{8,11},{9,10},{10,... | collective-permute-start | bytes 184328 | tf_op jit(solution)/shard_map/ppermute | solution.py:981
  53.0 0.7 collective-permute-start.4
  53.7 0.0 collective-permute-start.3
  53.7 4.4 %later.4.refs_5_ = f32[232,128]{1,0:T(8,128)S(1)} custom-call(f32[4,8,128]{2,1,0:T(8,128)S(1)} %copy-done.12, bf16[128,13824]{1,0:T(8,128)(2,1)S(1)} %copy-done.3, f32[512,128]{1,0:T(8,128)S(1)} %copy-done.10), custom_call_target="tpu_custom_call" | custom-call | flops 5000000000 | tf_op jit(solution)/shard_map/later/pallas_call | solution.py:262
  58.1 0.0 collective-permute-done.5.refs_3_
  58.1 0.0 collective-permute-done.4.refs_2_
  58.2 2.1 %step.5 = (f32[168,128]{1,0:T(8,128)S(1)}, f32[1440,128]{1,0:T(8,128)S(1)}) custom-call(f32[120,128]{1,0:T(8,128)S(1)} %get-tuple-element.64.refs_0_, f32[120,128]{1,0:T(8,128)S(1)} %collective-permute-done.3.refs_1_, f32[120,128]{1,0:T(8,128)S(1)} %collective-permute-done.4.refs_2_, f32[120,128]{1,0:T(8,128)S(1)} %collective-permute-done.5.refs_3_, ...), custom_call_target="tpu_custom_call" | custom-call | flops 3000000000 | tf_op jit(solution)/shard_map/step/pallas_call | solution.py:752
  60.2 1.4 %collective-permute-start.8 = (f32[168,128]{1,0:T(8,128)S(1)}, f32[168,128]{1,0:T(8,128)S(1)}, u32[]{:S(2)}, u32[]{:S(2)}) collective-permute-start(f32[168,128]{1,0:T(8,128)S(1)} %get-tuple-element.66.refs_0_), channel_id=1, source_target_pairs={{0,3},{1,2},{2,1},{3,0},{4,7},{5,6},{6,5},{7,4},{8,11},{9,10},{10,... | collective-permute-start | bytes 258056 | tf_op jit(solution)/shard_map/ppermute | solution.py:981
  61.7 0.7 collective-permute-start.7
  62.4 2.9 %all-to-all-done.2.code_ref = s16[8,128,512]{2,1,0:T(8,128)(2,1)S(1)} async-done(((s16[8,128,512]{2,1,0:T(8,128)(2,1)}), s16[8,128,512]{2,1,0:T(8,128)(2,1)S(1)}, u32[]{:S(2)}, u32[]{:S(2)}) %all-to-all-start.2) | async-done | bytes 1048608 | tf_op jit(solution)/shard_map/all_to_all | solution.py:1009
  65.4 2.0 %copy-done.4 = bf16[128,13824]{1,0:T(8,128)(2,1)S(1)} copy-done((bf16[128,13824]{1,0:T(8,128)(2,1)S(1)}, bf16[128,13824]{1,0:T(8,128)(2,1)}, u32[]{:S(2)}) %copy-start.4) | copy-done | bytes 3538968
  67.4 4.7 %later.5.refs_5_ = f32[280,128]{1,0:T(8,128)S(1)} custom-call(f32[4,8,128]{2,1,0:T(8,128)S(1)} %copy-done.12, bf16[128,13824]{1,0:T(8,128)(2,1)S(1)} %copy-done.4, f32[512,128]{1,0:T(8,128)S(1)} %copy-done.10), custom_call_target="tpu_custom_call" | custom-call | flops 5000000000 | tf_op jit(solution)/shard_map/later/pallas_call | solution.py:262
  72.1 0.0 copy-start.1
  72.1 0.0 copy-start.6
  72.1 2.4 %step.6 = (f32[216,128]{1,0:T(8,128)S(1)}, f32[1440,128]{1,0:T(8,128)S(1)}) custom-call(f32[168,128]{1,0:T(8,128)S(1)} %get-tuple-element.66.refs_0_, f32[168,128]{1,0:T(8,128)S(1)} %collective-permute-done.6.refs_1_, f32[168,128]{1,0:T(8,128)S(1)} %collective-permute-done.7.refs_2_, f32[168,128]{1,0:T(8,128)S(1)} %collective-permute-done.8.refs_3_, ...), custom_call_target="tpu_custom_call" | custom-call | flops 3000000000 | tf_op jit(solution)/shard_map/step/pallas_call | solution.py:752
  74.5 0.1 collective-permute-start.11
  74.6 1.6 %collective-permute-start.10 = (f32[216,128]{1,0:T(8,128)S(1)}, f32[216,128]{1,0:T(8,128)S(1)}, u32[]{:S(2)}, u32[]{:S(2)}) collective-permute-start(f32[216,128]{1,0:T(8,128)S(1)} %get-tuple-element.75.refs_0_.refs_4_), channel_id=1, source_target_pairs={{0,2},{1,3},{2,0},{3,1},{4,6},{5,7},{6,4},{7,5},{8,10},{9,11},{10,... | collective-permute-start | bytes 331784 | tf_op jit(solution)/shard_map/ppermute | solution.py:981
  76.1 0.3 collective-permute-start.9
  76.4 2.0 %assemble.1 = (f32[8,128,512]{2,1,0:T(8,128)S(1)}, f32[4,48,512]{2,1,0:T(8,128)S(1)}, f32[4,48,512]{2,1,0:T(8,128)S(1)}) custom-call(s32[14]{0:T(128)S(1)} %copy-done.2, f32[8,128,512]{2,1,0:T(8,128)S(1)} %copy-done.6, f32[8,80,128]{2,1,0:T(8,128)S(1)} %copy-done.1, s16[8,128,512]{2,1,0:T(8,128)(2,1)S(1)} %all-to-all-done.2.code_ref, ...), custom_call_target="tpu_custom_call" | custom-call | flops 4000000000 | tf_op jit(solution)/shard_map/assemble/pallas_call | solution.py:847
  78.5 1.4 %collective-permute-done.11.refs_3_.refs_7_ = f32[216,128]{1,0:T(8,128)S(1)} collective-permute-done((f32[216,128]{1,0:T(8,128)S(1)}, f32[216,128]{1,0:T(8,128)S(1)}, u32[]{:S(2)}, u32[]{:S(2)}) %collective-permute-start.11) | collective-permute-done | bytes 110624 | tf_op jit(solution)/shard_map/ppermute | solution.py:981
  79.9 2.4 %collective-permute-done.10.refs_2_.refs_6_ = f32[216,128]{1,0:T(8,128)S(1)} collective-permute-done((f32[216,128]{1,0:T(8,128)S(1)}, f32[216,128]{1,0:T(8,128)S(1)}, u32[]{:S(2)}, u32[]{:S(2)}) %collective-permute-start.10) | collective-permute-done | bytes 110624 | tf_op jit(solution)/shard_map/ppermute | solution.py:981
  82.3 0.1 collective-permute-start.12
  82.4 3.3 %step.7 = (f32[4,16,512]{2,1,0:T(8,128)S(1)}, f32[4,16,512]{2,1,0:T(8,128)S(1)}, f32[1440,128]{1,0:T(8,128)S(1)}) custom-call(f32[216,128]{1,0:T(8,128)S(1)} %get-tuple-element.75.refs_0_.refs_4_, f32[216,128]{1,0:T(8,128)S(1)} %collective-permute-done.9.refs_1_.refs_5_, f32[216,128]{1,0:T(8,128)S(1)} %collective-permute-done.10.refs_2_.refs_6_, ...), custom_call_target="tpu_custom_call" | custom-call | flops 3000000000 | tf_op jit(solution)/shard_map/step/pallas_call | solution.py:752
  85.6 0.5 collective-permute-start.15
  86.1 0.3 join.2
  86.4 0.1 collective-permute-start.13
  86.5 1.9 %last.1 = (f32[8,128,64]{2,1,0:T(8,128)S(1)}, f32[512,64]{1,0:T(8,128)S(1)}) custom-call(f32[168,128]{1,0:T(8,128)S(1)} %get-tuple-element.66.refs_0_, f32[168,128]{1,0:T(8,128)S(1)} %collective-permute-done.6.refs_1_, f32[168,128]{1,0:T(8,128)S(1)} %collective-permute-done.7.refs_2_, f32[168,128]{1,0:T(8,128)S(1)} %collective-permute-done.8.refs_3_, ...), custom_call_target="tpu_custom_call" | custom-call | flops 2000000000 | tf_op jit(solution)/shard_map/last/pallas_call | solution.py:792
  88.4 0.0 copy-start.7
  88.4 0.1 join.3
  88.6 2.1 %collective-permute-start.17 = (f32[4,512]{1,0:T(4,128)S(1)}, f32[4,512]{1,0:T(4,128)S(1)}, u32[]{:S(2)}, u32[]{:S(2)}) collective-permute-start(f32[4,512]{1,0:T(4,128)S(1)} %get-tuple-element.90), channel_id=1, source_target_pairs={{0,2},{1,3},{2,0},{3,1},{4,6},{5,7},{6,4},{7,5},{8,10},{9,11},{10,... | collective-permute-start | bytes 24584 | tf_op jit(solution)/shard_map/ppermute | solution.py:981
  90.6 0.1 collective-permute-start.16
  90.7 1.9 %collective-permute-start.14 = (f32[4,512]{1,0:T(4,128)S(1)}, f32[4,512]{1,0:T(4,128)S(1)}, u32[]{:S(2)}, u32[]{:S(2)}) collective-permute-start(f32[4,512]{1,0:T(4,128)S(1)} %get-tuple-element.86), channel_id=1, source_target_pairs={{0,2},{1,3},{2,0},{3,1},{4,6},{5,7},{6,4},{7,5},{8,10},{9,11},{10,... | collective-permute-start | bytes 24584 | tf_op jit(solution)/shard_map/ppermute | solution.py:981
  92.7 1.4 %place.1 = f32[3,8,512]{2,1,0:T(8,128)} custom-call(s32[14]{0:T(128)S(1)} %copy-done.2, f32[3,8,512]{2,1,0:T(8,128)S(1)} %bitcast.8, f32[8,80,128]{2,1,0:T(8,128)S(1)} %copy-done.1, f32[1440,128]{1,0:T(8,128)S(1)} %get-tuple-element.80.refs_8_.log_ref), custom_call_target="tpu_custom_call" | custom-call | flops 1000000000 | tf_op jit(solution)/shard_map/place/pallas_call | solution.py:969
  94.0 0.2 collective-permute-done.17
  94.2 0.8 collective-permute-done.16
  95.0 0.1 collective-permute-done.14
  95.1 0.1 fusion.1.refs_0_
  95.2 0.1 collective-permute-start.18
  95.4 0.6 collective-permute-start.19
  96.0 1.3 %collective-permute-done.19.refs_3_ = f32[4,16,512]{2,1,0:T(8,128)S(1)} collective-permute-done((f32[4,16,512]{2,1,0:T(8,128)S(1)}, f32[4,16,512]{2,1,0:T(8,128)S(1)}, u32[]{:S(2)}, u32[]{:S(2)}) %collective-permute-start.19) | collective-permute-done | bytes 131104 | tf_op jit(solution)/shard_map/ppermute | solution.py:981
  97.2 2.7 %update.1 = f32[8,128,512]{2,1,0:T(8,128)} custom-call(s32[14]{0:T(128)S(1)} %copy-done.2, f32[8,128,512]{2,1,0:T(8,128)S(1)} %get-tuple-element.79.refs_6_.v_ref, f32[8,128,64]{2,1,0:T(8,128)S(1)} %get-tuple-element.92.factor_ref, f32[512,64]{1,0:T(8,128)S(1)} %get-tuple-element.93.l_ref, f32[4,48,512]{2,1,0:T(8,128)S(1)} %fusion.1.refs_0_, ...), custom_call_target="tpu_custom_call" | custom-call | flops 2000000000 | tf_op jit(solution)/shard_map/update/pallas_call | solution.py:930
  (37 shorter events, 0.1 us)
Async XLA Ops:
  0.6 9.7 %copy-start.15 = (s32[32]{0:T(128)S(1)}, s32[32]{0:T(128)}, u32[]{:S(2)}) copy-start(s32[32]{0:T(128)} %order_ref.3) | copy-start | bytes 388
  0.6 9.7 %copy-start.14 = (s32[8]{0:T(128)S(1)}, s32[8]{0:T(128)}, u32[]{:S(2)}) copy-start(s32[8]{0:T(128)} %parent_ref.1) | copy-start | bytes 100
  3.0 14.6 %all-to-all-start = ((f32[8,32,128]{2,1,0:T(8,128)}), f32[8,32,128]{2,1,0:T(8,128)S(1)}, u32[]{:S(2)}, u32[]{:S(2)}) async-start(f32[8,32,128]{2,1,0:T(8,128)} %pack.1), calls=%async_computation | async-start | bytes 262144 | tf_op jit(solution)/shard_map/all_to_all | solution.py:1009
  17.7 0.7 copy-start.13
  21.8 14.4 %all-to-all-start.1 = ((f32[8,80,128]{2,1,0:T(8,128)}), f32[8,80,128]{2,1,0:T(8,128)S(1)}, u32[]{:S(2)}, u32[]{:S(2)}) async-start(f32[8,80,128]{2,1,0:T(8,128)} %get-tuple-element.52), calls=%async_computation.1 | async-start | bytes 655360 | tf_op jit(solution)/shard_map/all_to_all | solution.py:1009
  36.2 3.7 %copy-start = (f32[8,80,128]{2,1,0:T(8,128)}, f32[8,80,128]{2,1,0:T(8,128)S(1)}, u32[]{:S(2)}) copy-start(f32[8,80,128]{2,1,0:T(8,128)S(1)} %all-to-all-done.1.got_ref) | copy-start | bytes 983044
  36.2 29.2 %all-to-all-start.2 = ((s16[8,128,512]{2,1,0:T(8,128)(2,1)}), s16[8,128,512]{2,1,0:T(8,128)(2,1)S(1)}, u32[]{:S(2)}, u32[]{:S(2)}) async-start(s16[8,128,512]{2,1,0:T(8,128)(2,1)} %get-tuple-element.68), calls=%async_computation.2 | async-start | bytes 2097152 | tf_op jit(solution)/shard_map/all_to_all | solution.py:1009
  39.9 4.9 %copy-start.3 = (bf16[128,13824]{1,0:T(8,128)(2,1)S(1)}, bf16[128,13824]{1,0:T(8,128)(2,1)}, u32[]{:S(2)}) copy-start(bf16[128,13824]{1,0:T(8,128)(2,1)} %refs_9_.1) | copy-start | bytes 10616836
  40.0 4.9 %copy-start.12 = (f32[4,8,128]{2,1,0:T(8,128)S(1)}, f32[4,8,128]{2,1,0:T(8,128)}, u32[]{:S(2)}) copy-start(f32[4,8,128]{2,1,0:T(8,128)} %get-tuple-element.69.states_ref.refs_6_.refs_7_) | copy-start | bytes 49156
  42.9 7.2 %collective-permute-start.2 = (f32[8,128]{1,0:T(8,128)}, f32[8,128]{1,0:T(8,128)S(1)}, u32[]{:S(2)}, u32[]{:S(2)}) collective-permute-start(f32[8,128]{1,0:T(8,128)} %get-tuple-element.61.refs_0_), channel_id=1, source_target_pairs={{0,3},{1,2},{2,1},{3,0},{4,7},{5,6},{6,5},{7,4},{8,11},{9,10},{10,... | collective-permute-start | bytes 12296 | tf_op jit(solution)/shard_map/ppermute | solution.py:981
  43.0 7.1 %collective-permute-start.1 = (f32[8,128]{1,0:T(8,128)}, f32[8,128]{1,0:T(8,128)S(1)}, u32[]{:S(2)}, u32[]{:S(2)}) collective-permute-start(f32[8,128]{1,0:T(8,128)} %get-tuple-element.61.refs_0_), channel_id=1, source_target_pairs={{0,2},{1,3},{2,0},{3,1},{4,6},{5,7},{6,4},{7,5},{8,10},{9,11},{10,... | collective-permute-start | bytes 12296 | tf_op jit(solution)/shard_map/ppermute | solution.py:981
  44.5 5.6 %collective-permute-start = (f32[8,128]{1,0:T(8,128)}, f32[8,128]{1,0:T(8,128)S(1)}, u32[]{:S(2)}, u32[]{:S(2)}) collective-permute-start(f32[8,128]{1,0:T(8,128)} %get-tuple-element.61.refs_0_), channel_id=1, source_target_pairs={{0,1},{1,0},{2,3},{3,2},{4,5},{5,4},{6,7},{7,6},{8,9},{9,8},{10,11... | collective-permute-start | bytes 12296 | tf_op jit(solution)/shard_map/ppermute | solution.py:981
  44.8 1.0 copy-start.9
  45.8 4.4 %copy-start.8 = (f32[8,128]{1,0:T(8,128)S(1)}, f32[8,128]{1,0:T(8,128)}, u32[]{:S(2)}) copy-start(f32[8,128]{1,0:T(8,128)} %get-tuple-element.61.refs_0_) | copy-start | bytes 12292
  45.8 4.4 %copy-start.11 = (f32[128,128]{1,0:T(8,128)S(1)}, f32[128,128]{1,0:T(8,128)}, u32[]{:S(2)}) copy-start(f32[128,128]{1,0:T(8,128)} %get-tuple-element.62.refs_4_) | copy-start | bytes 196612
  50.1 3.6 %copy-start.10 = (f32[512,128]{1,0:T(8,128)S(1)}, f32[512,128]{1,0:T(8,128)}, u32[]{:S(2)}) copy-start(f32[512,128]{1,0:T(8,128)} %get-tuple-element.63.vm_ref.refs_7_.refs_8_.refs_9_) | copy-start | bytes 786436
  51.8 6.3 %collective-permute-start.5 = (f32[120,128]{1,0:T(8,128)S(1)}, f32[120,128]{1,0:T(8,128)S(1)}, u32[]{:S(2)}, u32[]{:S(2)}) collective-permute-start(f32[120,128]{1,0:T(8,128)S(1)} %get-tuple-element.64.refs_0_), channel_id=1, source_target_pairs={{0,3},{1,2},{2,1},{3,0},{4,7},{5,6},{6,5},{7,4},{8,11},{9,10},{10,... | collective-permute-start | bytes 184328 | tf_op jit(solution)/shard_map/ppermute | solution.py:981
  53.0 5.2 %collective-permute-start.4 = (f32[120,128]{1,0:T(8,128)S(1)}, f32[120,128]{1,0:T(8,128)S(1)}, u32[]{:S(2)}, u32[]{:S(2)}) collective-permute-start(f32[120,128]{1,0:T(8,128)S(1)} %get-tuple-element.64.refs_0_), channel_id=1, source_target_pairs={{0,2},{1,3},{2,0},{3,1},{4,6},{5,7},{6,4},{7,5},{8,10},{9,11},{10,... | collective-permute-start | bytes 184328 | tf_op jit(solution)/shard_map/ppermute | solution.py:981
  53.7 4.4 %collective-permute-start.3 = (f32[120,128]{1,0:T(8,128)S(1)}, f32[120,128]{1,0:T(8,128)S(1)}, u32[]{:S(2)}, u32[]{:S(2)}) collective-permute-start(f32[120,128]{1,0:T(8,128)S(1)} %get-tuple-element.64.refs_0_), channel_id=1, source_target_pairs={{0,1},{1,0},{2,3},{3,2},{4,5},{5,4},{6,7},{7,6},{8,9},{9,8},{10,11... | collective-permute-start | bytes 184328 | tf_op jit(solution)/shard_map/ppermute | solution.py:981
  60.2 11.8 %collective-permute-start.8 = (f32[168,128]{1,0:T(8,128)S(1)}, f32[168,128]{1,0:T(8,128)S(1)}, u32[]{:S(2)}, u32[]{:S(2)}) collective-permute-start(f32[168,128]{1,0:T(8,128)S(1)} %get-tuple-element.66.refs_0_), channel_id=1, source_target_pairs={{0,3},{1,2},{2,1},{3,0},{4,7},{5,6},{6,5},{7,4},{8,11},{9,10},{10,... | collective-permute-start | bytes 258056 | tf_op jit(solution)/shard_map/ppermute | solution.py:981
  61.7 10.4 %collective-permute-start.7 = (f32[168,128]{1,0:T(8,128)S(1)}, f32[168,128]{1,0:T(8,128)S(1)}, u32[]{:S(2)}, u32[]{:S(2)}) collective-permute-start(f32[168,128]{1,0:T(8,128)S(1)} %get-tuple-element.66.refs_0_), channel_id=1, source_target_pairs={{0,2},{1,3},{2,0},{3,1},{4,6},{5,7},{6,4},{7,5},{8,10},{9,11},{10,... | collective-permute-start | bytes 258056 | tf_op jit(solution)/shard_map/ppermute | solution.py:981
  62.4 9.7 %collective-permute-start.6 = (f32[168,128]{1,0:T(8,128)S(1)}, f32[168,128]{1,0:T(8,128)S(1)}, u32[]{:S(2)}, u32[]{:S(2)}) collective-permute-start(f32[168,128]{1,0:T(8,128)S(1)} %get-tuple-element.66.refs_0_), channel_id=1, source_target_pairs={{0,1},{1,0},{2,3},{3,2},{4,5},{5,4},{6,7},{7,6},{8,9},{9,8},{10,11... | collective-permute-start | bytes 258056 | tf_op jit(solution)/shard_map/ppermute | solution.py:981
  65.4 2.0 %copy-start.4 = (bf16[128,13824]{1,0:T(8,128)(2,1)S(1)}, bf16[128,13824]{1,0:T(8,128)(2,1)}, u32[]{:S(2)}) copy-start(bf16[128,13824]{1,0:T(8,128)(2,1)} %refs_9_.1) | copy-start | bytes 10616836
  72.1 4.3 %copy-start.1 = (f32[8,80,128]{2,1,0:T(8,128)S(1)}, f32[8,80,128]{2,1,0:T(8,128)}, u32[]{:S(2)}) copy-start(f32[8,80,128]{2,1,0:T(8,128)} %copy-done) | copy-start | bytes 983044
  72.1 4.3 %copy-start.2 = (s32[14]{0:T(128)S(1)}, s32[14]{0:T(128)}, u32[]{:S(2)}) copy-start(s32[14]{0:T(128)} %pad_add_fusion.meta_ref.refs_5_) | copy-start | bytes 172
  72.1 4.3 %copy-start.6 = (f32[8,128,512]{2,1,0:T(8,128)S(1)}, f32[8,128,512]{2,1,0:T(8,128)}, u32[]{:S(2)}) copy-start(f32[8,128,512]{2,1,0:T(8,128)} %own_ref.1) | copy-start | bytes 6291460
  74.5 5.4 %collective-permute-start.11 = (f32[216,128]{1,0:T(8,128)S(1)}, f32[216,128]{1,0:T(8,128)S(1)}, u32[]{:S(2)}, u32[]{:S(2)}) collective-permute-start(f32[216,128]{1,0:T(8,128)S(1)} %get-tuple-element.75.refs_0_.refs_4_), channel_id=1, source_target_pairs={{0,3},{1,2},{2,1},{3,0},{4,7},{5,6},{6,5},{7,4},{8,11},{9,10},{10,... | collective-permute-start | bytes 331784 | tf_op jit(solution)/shard_map/ppermute | solution.py:981
  74.6 7.7 %collective-permute-start.10 = (f32[216,128]{1,0:T(8,128)S(1)}, f32[216,128]{1,0:T(8,128)S(1)}, u32[]{:S(2)}, u32[]{:S(2)}) collective-permute-start(f32[216,128]{1,0:T(8,128)S(1)} %get-tuple-element.75.refs_0_.refs_4_), channel_id=1, source_target_pairs={{0,2},{1,3},{2,0},{3,1},{4,6},{5,7},{6,4},{7,5},{8,10},{9,11},{10,... | collective-permute-start | bytes 331784 | tf_op jit(solution)/shard_map/ppermute | solution.py:981
  76.1 6.2 %collective-permute-start.9 = (f32[216,128]{1,0:T(8,128)S(1)}, f32[216,128]{1,0:T(8,128)S(1)}, u32[]{:S(2)}, u32[]{:S(2)}) collective-permute-start(f32[216,128]{1,0:T(8,128)S(1)} %get-tuple-element.75.refs_0_.refs_4_), channel_id=1, source_target_pairs={{0,1},{1,0},{2,3},{3,2},{4,5},{5,4},{6,7},{7,6},{8,9},{9,8},{10,11... | collective-permute-start | bytes 331784 | tf_op jit(solution)/shard_map/ppermute | solution.py:981
  76.4 5.9 %copy-start.5 = (bf16[128,13824]{1,0:T(8,128)(2,1)S(1)}, bf16[128,13824]{1,0:T(8,128)(2,1)}, u32[]{:S(2)}) copy-start(bf16[128,13824]{1,0:T(8,128)(2,1)} %refs_9_.1) | copy-start | bytes 10616836
  82.3 3.8 %collective-permute-start.12 = (f32[4,48,512]{2,1,0:T(8,128)S(1)}, f32[4,48,512]{2,1,0:T(8,128)S(1)}, u32[]{:S(2)}, u32[]{:S(2)}) collective-permute-start(f32[4,48,512]{2,1,0:T(8,128)S(1)} %get-tuple-element.84), channel_id=1, source_target_pairs={{0,1},{1,0},{2,3},{3,2},{4,5},{5,4},{6,7},{7,6},{8,9},{9,8},{10,11... | collective-permute-start | bytes 1179656 | tf_op jit(solution)/shard_map/ppermute | solution.py:981
  85.6 2.8 %collective-permute-start.15 = (f32[4,16,512]{2,1,0:T(8,128)S(1)}, f32[4,16,512]{2,1,0:T(8,128)S(1)}, u32[]{:S(2)}, u32[]{:S(2)}) collective-permute-start(f32[4,16,512]{2,1,0:T(8,128)S(1)} %get-tuple-element.88), channel_id=1, source_target_pairs={{0,1},{1,0},{2,3},{3,2},{4,5},{5,4},{6,7},{7,6},{8,9},{9,8},{10,11... | collective-permute-start | bytes 393224 | tf_op jit(solution)/shard_map/ppermute | solution.py:981
  86.4 8.7 %collective-permute-start.13 = (s16[4,48,512]{2,1,0:T(8,128)(2,1)S(1)}, s16[4,48,512]{2,1,0:T(8,128)(2,1)S(1)}, u32[]{:S(2)}, u32[]{:S(2)}) collective-permute-start(s16[4,48,512]{2,1,0:T(8,128)(2,1)S(1)} %get-tuple-element.85), channel_id=1, source_target_pairs={{0,2},{1,3},{2,0},{3,1},{4,6},{5,7},{6,4},{7,5},{8,10},{9,11},{10,... | collective-permute-start | bytes 589832 | tf_op jit(solution)/shard_map/ppermute | solution.py:981
  88.4 4.3 %copy-start.7 = (f32[8,3,512]{2,0,1:T(8,128)S(1)}, f32[8,3,512]{2,0,1:T(8,128)}, u32[]{:S(2)}) copy-start(f32[8,3,512]{2,0,1:T(8,128)} %param.7) | copy-start | bytes 147460
  88.6 5.7 %collective-permute-start.17 = (f32[4,512]{1,0:T(4,128)S(1)}, f32[4,512]{1,0:T(4,128)S(1)}, u32[]{:S(2)}, u32[]{:S(2)}) collective-permute-start(f32[4,512]{1,0:T(4,128)S(1)} %get-tuple-element.90), channel_id=1, source_target_pairs={{0,2},{1,3},{2,0},{3,1},{4,6},{5,7},{6,4},{7,5},{8,10},{9,11},{10,... | collective-permute-start | bytes 24584 | tf_op jit(solution)/shard_map/ppermute | solution.py:981
  90.6 4.4 %collective-permute-start.16 = (s16[4,16,512]{2,1,0:T(8,128)(2,1)S(1)}, s16[4,16,512]{2,1,0:T(8,128)(2,1)S(1)}, u32[]{:S(2)}, u32[]{:S(2)}) collective-permute-start(s16[4,16,512]{2,1,0:T(8,128)(2,1)S(1)} %get-tuple-element.89), channel_id=1, source_target_pairs={{0,2},{1,3},{2,0},{3,1},{4,6},{5,7},{6,4},{7,5},{8,10},{9,11},{10,... | collective-permute-start | bytes 196616 | tf_op jit(solution)/shard_map/ppermute | solution.py:981
  90.7 4.4 %collective-permute-start.14 = (f32[4,512]{1,0:T(4,128)S(1)}, f32[4,512]{1,0:T(4,128)S(1)}, u32[]{:S(2)}, u32[]{:S(2)}) collective-permute-start(f32[4,512]{1,0:T(4,128)S(1)} %get-tuple-element.86), channel_id=1, source_target_pairs={{0,2},{1,3},{2,0},{3,1},{4,6},{5,7},{6,4},{7,5},{8,10},{9,11},{10,... | collective-permute-start | bytes 24584 | tf_op jit(solution)/shard_map/ppermute | solution.py:981
  95.2 2.0 %collective-permute-start.18 = (f32[4,48,512]{2,1,0:T(8,128)S(1)}, f32[4,48,512]{2,1,0:T(8,128)S(1)}, u32[]{:S(2)}, u32[]{:S(2)}) collective-permute-start(f32[4,48,512]{2,1,0:T(8,128)S(1)} %fusion.1.refs_0_), channel_id=1, source_target_pairs={{0,1},{1,0},{2,3},{3,2},{4,5},{5,4},{6,7},{7,6},{8,9},{9,8},{10,11... | collective-permute-start | bytes 1179656 | tf_op jit(solution)/shard_map/ppermute | solution.py:981
  95.4 1.8 %collective-permute-start.19 = (f32[4,16,512]{2,1,0:T(8,128)S(1)}, f32[4,16,512]{2,1,0:T(8,128)S(1)}, u32[]{:S(2)}, u32[]{:S(2)}) collective-permute-start(f32[4,16,512]{2,1,0:T(8,128)S(1)} %fusion.4.refs_1_), channel_id=1, source_target_pairs={{0,1},{1,0},{2,3},{3,2},{4,5},{5,4},{6,7},{7,6},{8,9},{9,8},{10,11... | collective-permute-start | bytes 393224 | tf_op jit(solution)/shard_map/ppermute | solution.py:981
